TPU v7x, 32 devices: a whole 2x2x4 slice. The times are simulated.
32 devices in a mesh: dp: 4 (over y, x), fsdp: 8 (over z, core).
Axes of the slice: x: 2, y: 2, z: 4, core: 2. Of those that a mesh axis runs over, the one named last changes fastest.
Arguments:
- grads: bfloat16 [4, 32, 512, 4096], P('dp', None, None, 'fsdp'), may hold values from -5 to 5
- left_stats: float32 [32, 8, 512, 512], P('fsdp', 'dp'), as said below
- right_stats: float32 [32, 8, 512, 512], P('fsdp', 'dp'), as said below
- left_root: float32 [32, 8, 512, 512], P('fsdp', 'dp'), as said below
- right_root: float32 [32, 8, 512, 512], P('fsdp', 'dp'), as said below
Outputs:
- update: bfloat16 [32, 512, 4096], P(None, None, 'fsdp')
Inputs may be any that keep to these rules, and one draw needn't show every extreme that they name: `left_stats`: symmetric. `right_stats`: symmetric. `left_root`: symmetric. `right_root`: symmetric.
All inputs are finite; a program needn't handle non-finite values.
Results may differ from a plain program's by a relative error of at most 0.012.
Values may be sent and summed in bfloat16 or wider, within the bound.
No kernel may reach another device: no remote copies, remote signals or barrier semaphores. Data moves between devices by JAX's collectives and lax.ppermute only.
A program may use at most 256 MiB of HBM per device.

v0:
```python
import jax
import jax.numpy as jnp
from jax import lax
from jax.sharding import PartitionSpec as P

EXACT = lax.Precision.HIGHEST
ema_decay = 0.999


def fourth_power(root):
    square = jnp.einsum("bij,bjk->bik", root, root, precision=EXACT)
    return jnp.einsum("bij,bjk->bik", square, square, precision=EXACT)


def refine(root, fourth, stats):
    coupled = jnp.einsum("bij,bjk->bik", fourth, stats, precision=EXACT)
    identity = jnp.eye(root.shape[-1], dtype=jnp.float32)
    factor = (5.0 * identity - coupled) * 0.25
    return jnp.einsum("bij,bjk->bik", root, factor, precision=EXACT)


def shards(grads, left_stats, right_stats, left_root, right_root):
    slab_count = left_stats.shape[0]
    col_blocks = left_stats.shape[1]
    order = left_stats.shape[2]
    block_count = slab_count * col_blocks
    left_prior = left_root.reshape(block_count, order, order)
    right_prior = right_root.reshape(block_count, order, order)
    left_fourth = fourth_power(left_prior)
    right_fourth = fourth_power(right_prior)
    regrouped = lax.all_to_all(grads, "fsdp", split_axis=1, concat_axis=3, tiled=True)
    summed = lax.psum_scatter(
        regrouped.astype(jnp.float32).astype(jnp.bfloat16), "dp", scatter_dimension=3, tiled=True
    )
    blocks = (
        summed.reshape(slab_count, order, col_blocks, order)
        .transpose(0, 2, 1, 3)
        .reshape(block_count, order, order)
    )
    gram_left = jnp.einsum("bik,bjk->bij", blocks, blocks, preferred_element_type=jnp.float32)
    gram_right = jnp.einsum("bki,bkj->bij", blocks, blocks, preferred_element_type=jnp.float32)
    left = ema_decay * left_stats.reshape(block_count, order, order) + (1.0 - ema_decay) * gram_left
    right = (
        ema_decay * right_stats.reshape(block_count, order, order) + (1.0 - ema_decay) * gram_right
    )
    new_left = refine(left_prior, left_fourth, left)
    new_right = refine(right_prior, right_fourth, right)
    halfway = jnp.einsum("bij,bjk->bik", new_left, blocks.astype(jnp.float32), precision=EXACT)
    result = jnp.einsum("bij,bjk->bik", halfway, new_right, precision=EXACT).astype(jnp.bfloat16)
    local_slabs = result.reshape(slab_count, col_blocks, order, order).transpose(0, 2, 1, 3)
    local_slabs = local_slabs.reshape(1, slab_count, order, col_blocks * order)
    copied = lax.all_gather(local_slabs, "dp", axis=3, tiled=True)
    finished = lax.all_to_all(copied, "fsdp", split_axis=3, concat_axis=1, tiled=True)
    return finished[0]


def solution(mesh):
    placed = (
        P("dp", None, None, "fsdp"),
        P("fsdp", "dp", None, None),
        P("fsdp", "dp", None, None),
        P("fsdp", "dp", None, None),
        P("fsdp", "dp", None, None),
    )
    return jax.shard_map(
        shards, mesh=mesh, in_specs=placed, out_specs=P(None, None, "fsdp"), check_vma=False
    )
```

profile of v0, /device:TPU:0, one launch (start us, length us, event | category | flops | bytes accessed | tf_op | source)
XLA Modules:
  0.0 1272.3 jit_solution(14108685856933971557)
XLA Ops:
  6.5 0.0 reduce-scatter.2.cloned.1.call-start
  6.5 372.0 %all_to_all.33 = bf16[1,32,512,512]{3,2,0,1:T(8,128)(2,1)} all-to-all(bf16[1,32,512,512]{3,2,0,1:T(8,128)(2,1)} %bitcast.66), channel_id=1, replica_groups=mesh['dp'=4,'fsdp'=8] {'fsdp'}, dimensions={1} | all-to-all | bytes 33554432 | tf_op jit(solution)/shard_map/all_to_all | solution.py:31
  378.5 22.2 %copy.25 = bf16[1,4,512,8,512]{2,4,3,1,0:T(8,128)(2,1)} copy(bf16[1,4,512,8,512]{4,2,1,3,0:T(8,128)(2,1)} %bitcast.64) | data formatting | bytes 33554432 | tf_op jit(solution)/shard_map/all_to_all | solution.py:31
  400.7 0.0 reduce-scatter.2.cloned.1.call-update
  400.7 0.0 all-gather.2.cloned.1.call-start
  400.8 0.1 fusion.10
  400.9 0.0 slice-start
  400.9 8.6 broadcast_multiply_fusion.1
  409.5 0.0 slice-start.1
  409.5 8.3 broadcast_multiply_fusion
  417.8 0.0 slice-done
  417.8 0.0 slice-done.1
  417.8 0.0 slice-start.4
  417.8 15.5 %fusion.13 = f32[8,512,512]{2,1,0:T(8,128)S(1)} fusion(f32[8,512,512]{2,1,0:T(8,128)S(1)} %bitcast.52), kind=kOutput, calls=%fused_computation.19 | convolution fusion | flops 12884901888 | bytes 16777216 | tf_op jit(solution)/shard_map/bij,bjk->bik/dot_general | solution.py:11
  433.3 0.0 slice-start.5
  433.3 16.3 %fusion.14 = f32[8,512,512]{2,1,0:T(8,128)} fusion(f32[8,512,512]{2,1,0:T(8,128)S(1)} %fusion.13), kind=kOutput, calls=%fused_computation.20 | convolution fusion | flops 12884901888 | bytes 16777216 | tf_op jit(solution)/shard_map/bij,bjk->bik/dot_general | solution.py:12
  449.6 0.0 slice-done.4
  449.6 0.0 slice-done.5
  449.7 15.3 %fusion.17 = f32[8,512,512]{2,1,0:T(8,128)S(1)} fusion(f32[8,512,512]{2,1,0:T(8,128)S(1)} %bitcast.58), kind=kOutput, calls=%fused_computation.23 | convolution fusion | flops 12884901888 | bytes 16777216 | tf_op jit(solution)/shard_map/bij,bjk->bik/dot_general | solution.py:11
  464.9 16.2 %fusion.18 = f32[8,512,512]{2,1,0:T(8,128)} fusion(f32[8,512,512]{2,1,0:T(8,128)S(1)} %fusion.17), kind=kOutput, calls=%fused_computation.24 | convolution fusion | flops 12884901888 | bytes 16777216 | tf_op jit(solution)/shard_map/bij,bjk->bik/dot_general | solution.py:12
  481.1 73.2 %reduce-scatter.2.cloned.1.call-done = bf16[1,4,512,1024]{2,3,1,0:T(8,128)(2,1)} async-done(((bf16[1,4,512,4096]{2,3,1,0:T(8,128)(2,1)}), bf16[1,4,512,1024]{2,3,1,0:T(8,128)(2,1)}) %reduce-scatter.2.cloned.1.call-update) | async-done | bytes 4194320 | tf_op jit(solution)/shard_map/reduce_scatter | solution.py:32
  554.3 7.3 copy.26
  561.6 0.0 slice-start.2
  561.6 11.8 bitcast_add_fusion.1
  573.4 0.0 slice-start.3
  573.4 20.0 %fusion.15 = f32[8,512,512]{2,1,0:T(8,128)} fusion(f32[8,512,512]{2,1,0:T(8,128)} %fusion.14, f32[8,512,512]{2,1,0:T(8,128)} %bitcast_add_fusion.1), kind=kOutput, calls=%fused_computation.21 | convolution fusion | flops 12884901888 | bytes 25165824 | tf_op jit(solution)/shard_map/bij,bjk->bik/dot_general | solution.py:16
  593.4 0.0 slice-done.2
  593.4 0.0 slice-done.3
  593.4 0.0 copy-start
  593.4 17.9 %fusion.3 = f32[8,512,512]{1,2,0:T(8,128)} fusion(f32[8,512,512]{2,1,0:T(8,128)S(1)} %bitcast.55, f32[8,512,512]{2,1,0:T(8,128)} %fusion.15, f32[512,512]{1,0:T(8,128)S(1)} %fusion.10), kind=kOutput, calls=%fused_computation.5 | convolution fusion | flops 12889096192 | bytes 26214400 | tf_op jit(solution)/shard_map/bij,bjk->bik/dot_general | solution.py:19
  611.3 0.0 copy-done
  611.3 0.0 copy-start.1
  611.3 9.6 fusion.16
  620.9 0.0 copy-done.1
  620.9 0.0 slice-start.6
  621.0 9.3 bitcast_add_fusion
  630.2 0.0 slice-start.7
  630.2 19.6 %fusion.19 = f32[8,512,512]{2,1,0:T(8,128)} fusion(f32[8,512,512]{2,1,0:T(8,128)} %fusion.18, f32[8,512,512]{2,1,0:T(8,128)} %bitcast_add_fusion), kind=kOutput, calls=%fused_computation.25 | convolution fusion | flops 12884901888 | bytes 25165824 | tf_op jit(solution)/shard_map/bij,bjk->bik/dot_general | solution.py:16
  649.8 0.0 slice-done.6
  649.8 0.0 slice-done.7
  649.9 30.4 %fusion = f32[8,512,512]{2,1,0:T(8,128)} fusion(f32[8,512,512]{2,1,0:T(8,128)S(1)} %bitcast.61, f32[8,512,512]{2,1,0:T(8,128)} %fusion.19, f32[512,512]{1,0:T(8,128)S(1)} %fusion.10), kind=kOutput, calls=%fused_computation.2 | convolution fusion | flops 12889096192 | bytes 26214400 | tf_op jit(solution)/shard_map/bij,bjk->bik/dot_general | solution.py:19
  680.3 16.0 %convolution_convert_fusion = bf16[8,512,512]{1,2,0:T(8,128)(2,1)S(1)} fusion(f32[8,512,512]{2,1,0:T(8,128)S(1)} %fusion.16, f32[8,512,512]{2,1,0:T(8,128)} %fusion), kind=kOutput, calls=%fused_computation.14 | convolution fusion | flops 12886999040 | bytes 20971520 | tf_op jit(solution)/shard_map/bij,bjk->bik/dot_general | solution.py:49
  696.3 5.3 copy.31
  701.5 0.0 all-gather.2.cloned.1.call-update
  701.5 157.6 %all-gather.2.cloned.1.call-done = bf16[1,4,512,4096]{2,1,0,3:T(4,128)(2,1)} async-done(((bf16[1,4,512,1024]{2,1,0,3:T(4,128)(2,1)}), bf16[1,4,512,4096]{2,1,0,3:T(4,128)(2,1)}) %all-gather.2.cloned.1.call-update) | async-done | bytes 16777232 | tf_op jit(solution)/shard_map/all_gather | solution.py:52
  859.1 369.0 %all_to_all.34 = bf16[1,4,512,4096]{2,1,0,3:T(4,128)(2,1)S(1)} all-to-all(bf16[1,4,512,4096]{2,1,0,3:T(4,128)(2,1)} %all-gather.2.cloned.1.call-done), channel_id=1, replica_groups=mesh['dp'=4,'fsdp'=8] {'fsdp'}, dimensions={3} | all-to-all | bytes 33554432 | tf_op jit(solution)/shard_map/all_to_all | solution.py:53
  1228.1 13.6 %copy.32 = bf16[1,4,512,4096]{2,3,1,0:T(8,128)(2,1)} copy(bf16[1,4,512,4096]{2,1,0,3:T(4,128)(2,1)S(1)} %all_to_all.34) | data formatting | bytes 33554432 | tf_op jit(solution)/shard_map/all_to_all | solution.py:53
  1241.7 23.3 %copy.33 = bf16[1,8,4,512,512]{4,3,2,1,0:T(8,128)(2,1)} copy(bf16[1,8,4,512,512]{3,4,1,2,0:T(8,128)(2,1)} %bitcast.63) | data formatting | bytes 33554432 | tf_op jit(solution)/shard_map/all_to_all | solution.py:53
  (4 shorter events, 0.0 us)
Async XLA Ops:
  6.5 547.7 %reduce-scatter.2.cloned.1.call-start = ((), (), s32[]{:S(2)}) async-start(), calls=%async_computation.3 | async-start | bytes 20971520 | tf_op jit(solution)/shard_map/reduce_scatter | solution.py:32
  400.7 458.4 %all-gather.2.cloned.1.call-start = ((), (), s32[]{:S(2)}) async-start(), calls=%async_computation.4 | async-start | bytes 20971520 | tf_op jit(solution)/shard_map/all_gather | solution.py:52
  400.9 16.9 %slice-start = ((s8[8388608]{0:T(1024)(128)(4,1)}), s8[4194304]{0:T(1024)(128)(4,1)S(1)}, s32[]{:S(2)}) async-start(s8[8388608]{0:T(1024)(128)(4,1)} %bitcast.50), calls=%async_computation.5 | async-start | bytes 8388608
  409.5 8.3 slice-start.1
  417.8 31.9 %slice-start.4 = ((s8[8388608]{0:T(1024)(128)(4,1)}), s8[4194304]{0:T(1024)(128)(4,1)S(1)}, s32[]{:S(2)}) async-start(s8[8388608]{0:T(1024)(128)(4,1)} %bitcast.56), calls=%async_computation.9 | async-start | bytes 8388608
  433.3 16.3 %slice-start.5 = ((s8[8388608]{0:T(1024)(128)(4,1)}), s8[4194304]{0:T(1024)(128)(4,1)S(1)}, s32[]{:S(2)}) async-start(s8[8388608]{0:T(1024)(128)(4,1)} %bitcast.56), calls=%async_computation.10 | async-start | bytes 8388608
  561.6 31.8 %slice-start.2 = ((s8[8388608]{0:T(1024)(128)(4,1)}), s8[4194304]{0:T(1024)(128)(4,1)S(1)}, s32[]{:S(2)}) async-start(s8[8388608]{0:T(1024)(128)(4,1)} %bitcast.53), calls=%async_computation.7 | async-start | bytes 8388608
  573.4 20.0 %slice-start.3 = ((s8[8388608]{0:T(1024)(128)(4,1)}), s8[4194304]{0:T(1024)(128)(4,1)S(1)}, s32[]{:S(2)}) async-start(s8[8388608]{0:T(1024)(128)(4,1)} %bitcast.53), calls=%async_computation.8 | async-start | bytes 8388608
  593.4 17.9 %copy-start = (bf16[4,512,2,512]{3,1,2,0:T(8,128)(2,1)S(1)}, bf16[4,512,2,512]{3,1,2,0:T(8,128)(2,1)}, u32[]{:S(2)}) copy-start(bf16[4,512,2,512]{3,1,2,0:T(8,128)(2,1)} %copy.26) | copy-start | bytes 12582916
  611.3 9.6 copy-start.1
  620.9 28.9 %slice-start.6 = ((s8[8388608]{0:T(1024)(128)(4,1)}), s8[4194304]{0:T(1024)(128)(4,1)S(1)}, s32[]{:S(2)}) async-start(s8[8388608]{0:T(1024)(128)(4,1)} %bitcast.59), calls=%async_computation.11 | async-start | bytes 8388608
  630.2 19.6 %slice-start.7 = ((s8[8388608]{0:T(1024)(128)(4,1)}), s8[4194304]{0:T(1024)(128)(4,1)S(1)}, s32[]{:S(2)}) async-start(s8[8388608]{0:T(1024)(128)(4,1)} %bitcast.59), calls=%async_computation.12 | async-start | bytes 8388608
Sparse Core Ops, SparseCore 0:
  400.8 153.4 reduce-scatter.1
  701.6 157.4 all-gather.1
where the time goes:
time: 1280 us; the launch traced here: 1270 us
  blocking collectives  741 us (58%)
  waiting for transfers between devices  231 us (18%)
  matrix products  198 us (15%)
  local copies, waits for them, and re-layouts  71.7 us (6%)
  other arithmetic  17 us (1%)
  between operations  14 us (1%)
    all_to_all x1, blocking collectives, shards(): lax.all_to_all(grads, 'fsdp', split_axis=1, concat_axis=3, tiled=True)  372 us
    all_to_all x1, blocking collectives, shards(): lax.all_to_all(copied, 'fsdp', split_axis=3, concat_axis=1, tiled=True)  369 us
    all_gather x1, waiting for transfers between devices, shards(): copied = lax.all_gather(local_slabs, 'dp', axis=3, tiled=True)  158 us
    reduce_scatter x1, waiting for transfers between devices, shards(): lax.psum_scatter(regrouped.astype(jnp.float32).astype(jnp.bfloat16), 'dp'...  73.2 us
    dot_general x2, matrix products, refine(): return jnp.einsum('bij,bjk->bik', root, factor, precision=EXACT)  48.3 us
    dot_general x2, matrix products, refine(): coupled = jnp.einsum('bij,bjk->bik', fourth, stats, precision=EXACT)  39.6 us
    all_to_all x2, local copies, waits for them, and re-layouts, shards(): lax.all_to_all(copied, 'fsdp', split_axis=3, concat_axis=1, tiled=True)  36.9 us
    dot_general x2, matrix products, fourth_power(): return jnp.einsum('bij,bjk->bik', square, square, precision=EXACT)  32.5 us
  transfers between devices with their start and end apart: 2, of which 2 were waited for; matrix products, arithmetic and copies ran while one was open for 6% of the time, Pallas kernels for 0%

commit v1 on v0

v1 whole, which is shorter than its diff:
```python
import functools

import jax
import jax.numpy as jnp
from jax import lax
from jax.experimental import pallas as pl
from jax.experimental.pallas import tpu as pltpu
from jax.sharding import PartitionSpec as P

ema_decay = 0.999
MESH_AXES = ("dp", "fsdp")
VMEM_LIMIT = 60 * 1024 * 1024


def split(x):
    high = x.astype(jnp.bfloat16)
    low = (x - high.astype(jnp.float32)).astype(jnp.bfloat16)
    return high, low


def mm(a, b):
    return jnp.dot(a, b, preferred_element_type=jnp.float32)


def dot3(a, b):
    a_high, a_low = split(a)
    b_high, b_low = split(b)
    return mm(a_high, b_high) + (mm(a_high, b_low) + mm(a_low, b_high))


def fourth_kernel(left_ref, right_ref, left_out, right_out):
    for ref, out in ((left_ref, left_out), (right_ref, right_out)):
        root = ref[0, 0]
        square = dot3(root, root)
        out[0, 0] = dot3(square, square)


def fourth_powers(left_root, right_root):
    slabs, col_blocks, order, _ = left_root.shape
    spec = pl.BlockSpec((1, 1, order, order), lambda i, j: (i, j, 0, 0))
    shape = jax.ShapeDtypeStruct(left_root.shape, jnp.float32)
    count = slabs * col_blocks
    return pl.pallas_call(
        fourth_kernel,
        grid=(slabs, col_blocks),
        in_specs=[spec, spec],
        out_specs=[spec, spec],
        out_shape=[shape, shape],
        compiler_params=pltpu.CompilerParams(vmem_limit_bytes=VMEM_LIMIT),
        cost_estimate=pl.CostEstimate(
            flops=count * 4 * 3 * 2 * order**3, bytes_accessed=count * 16 * order**2, transcendentals=0
        ),
        name="fourth_powers",
    )(left_root, right_root)


def copy_all(copies):
    for copy in copies:
        copy.start()
    for copy in copies:
        copy.wait()


def pieces_of(ranks, inner):
    return [(d, k, e) for d in range(ranks) for k in range(ranks) for e in range(inner)]


def pack_kernel(ranks, inner, slot, per, inner_ref, grads_ref, out_ref, sems):
    rows = grads_ref.shape[1] // ranks
    mine = inner_ref[0]
    copies = []
    for at, (d, k, e) in enumerate(pieces_of(ranks, inner)):
        slab = ((d ^ k) * inner + (mine ^ e)) * per + slot
        copies.append(
            pltpu.make_async_copy(
                grads_ref.at[slab, pl.ds(d * rows, rows), :],
                out_ref.at[pl.ds(at * rows, rows), :],
                sems.at[at],
            )
        )
    copy_all(copies)


def pack(ranks, inner, slot, per, my_inner, grads):
    slabs, order, width = grads.shape
    count = ranks * ranks * inner
    return pl.pallas_call(
        functools.partial(pack_kernel, ranks, inner, slot, per),
        in_specs=[pl.BlockSpec(memory_space=pltpu.SMEM), pl.BlockSpec(memory_space=pl.ANY)],
        out_specs=pl.BlockSpec(memory_space=pl.ANY),
        out_shape=jax.ShapeDtypeStruct((slabs // per * order, width), grads.dtype),
        scratch_shapes=[pltpu.SemaphoreType.DMA((count,))],
        compiler_params=pltpu.CompilerParams(vmem_limit_bytes=VMEM_LIMIT),
        cost_estimate=pl.CostEstimate(
            flops=0, bytes_accessed=4 * slabs // per * order * width, transcendentals=0
        ),
        name="pack_slabs",
    )(my_inner, grads)


def unpack_kernel(ranks, inner, slot, per, inner_ref, got_ref, *rest):
    out_ref, sems = rest[-2], rest[-1]
    rows = out_ref.shape[1] // ranks
    mine = inner_ref[0]
    copies = []
    for at, (d, k, e) in enumerate(pieces_of(ranks, inner)):
        slab = ((d ^ k) * inner + (mine ^ e)) * per + slot
        copies.append(
            pltpu.make_async_copy(
                got_ref.at[pl.ds(at * rows, rows), :],
                out_ref.at[slab, pl.ds(d * rows, rows), :],
                sems.at[at],
            )
        )
    copy_all(copies)


def unpack(ranks, inner, slot, per, my_inner, got, shape, so_far):
    anywhere = pl.BlockSpec(memory_space=pl.ANY)
    operands = [my_inner, got] + ([] if so_far is None else [so_far])
    return pl.pallas_call(
        functools.partial(unpack_kernel, ranks, inner, slot, per),
        in_specs=[pl.BlockSpec(memory_space=pltpu.SMEM)] + [anywhere] * (len(operands) - 1),
        out_specs=anywhere,
        out_shape=jax.ShapeDtypeStruct(shape, got.dtype),
        scratch_shapes=[pltpu.SemaphoreType.DMA((ranks * ranks * inner,))],
        input_output_aliases={} if so_far is None else {2: 0},
        compiler_params=pltpu.CompilerParams(vmem_limit_bytes=VMEM_LIMIT),
        cost_estimate=pl.CostEstimate(flops=0, bytes_accessed=4 * got.size, transcendentals=0),
        name="unpack_slabs",
    )(*operands)


def refine(root, fourth, stats):
    order = root.shape[0]
    coupled = dot3(fourth, stats)
    on_diagonal = lax.broadcasted_iota(jnp.int32, (order, order), 0) == lax.broadcasted_iota(
        jnp.int32, (order, order), 1
    )
    factor = (jnp.where(on_diagonal, 5.0, 0.0) - coupled) * 0.25
    return dot3(root, factor)


def block_kernel(ranks, inner, steps, place_ref, *refs):
    count = ranks * inner
    pieces = refs[:count]
    left_stats, right_stats, left_root, right_root, left_fourth, right_fourth = refs[count : count + 6]
    outs = refs[count + 6 : 2 * count + 6]
    blocks, results = refs[2 * count + 6 :]
    rows, width = pieces[0].shape
    order = blocks.shape[1]
    outer_place, inner_place = place_ref[0], place_ref[1]
    step = pl.program_id(0)
    per_block = order // width

    def spot(k, e):
        shard = inner_place ^ e
        row = pl.multiple_of((outer_place ^ k) * rows, rows)
        column = pl.multiple_of((shard % per_block) * width, width)
        return shard // per_block, pl.ds(row, rows), pl.ds(column, width)

    @pl.when(step == 0)
    def _():
        for k in range(ranks):
            for e in range(inner):
                blocks[spot(k, e)] = pieces[k * inner + e][...]

    block = blocks[step]
    turned = block.T
    left = ema_decay * left_stats[0, 0] + (1.0 - ema_decay) * mm(block, turned)
    right = ema_decay * right_stats[0, 0] + (1.0 - ema_decay) * mm(turned, block)
    new_left = refine(left_root[0, 0], left_fourth[0, 0], left)
    new_right = refine(right_root[0, 0], right_fourth[0, 0], right)
    high, low = split(new_left)
    halfway = mm(high, block) + mm(low, block)
    results[step] = dot3(halfway, new_right).astype(results.dtype)

    @pl.when(step == steps - 1)
    def _():
        for k in range(ranks):
            for e in range(inner):
                outs[k * inner + e][...] = results[spot(k, e)]


def precondition(ranks, inner, slot, place, pieces, stats_and_roots):
    _, col_blocks, order, _ = stats_and_roots[0].shape
    rows, width = pieces[0].shape
    count = ranks * inner
    piece = pl.BlockSpec((rows, width), lambda j: (0, 0))
    matrix = pl.BlockSpec((1, 1, order, order), lambda j: (slot, j, 0, 0))
    return pl.pallas_call(
        functools.partial(block_kernel, ranks, inner, col_blocks),
        grid=(col_blocks,),
        in_specs=[pl.BlockSpec(memory_space=pltpu.SMEM)] + [piece] * count + [matrix] * 6,
        out_specs=[piece] * count,
        out_shape=[jax.ShapeDtypeStruct((rows, width), jnp.bfloat16)] * count,
        scratch_shapes=[pltpu.VMEM((col_blocks, order, order), jnp.bfloat16)] * 2,
        compiler_params=pltpu.CompilerParams(vmem_limit_bytes=VMEM_LIMIT),
        cost_estimate=pl.CostEstimate(
            flops=col_blocks * 19 * 2 * order**3,
            bytes_accessed=col_blocks * 28 * order**2,
            transcendentals=0,
        ),
        name="precondition",
    )(place, *pieces, *stats_and_roots)


def shards(ranks, fsdp, grads, left_stats, right_stats, left_root, right_root):
    per = left_stats.shape[0]
    inner = fsdp // ranks
    grads = grads[0]
    slabs, order, width = grads.shape
    rows = order // ranks
    f = lax.axis_index("fsdp")
    place = jnp.stack([f // inner, f % inner]).astype(jnp.int32)
    my_inner = place[1:]
    rounds = [(k, e) for k in range(ranks) for e in range(inner)]

    def number(d, a, b):
        return (d * ranks + a) * inner + b

    sources = [(d, a, b) for d in range(ranks) for a in range(ranks) for b in range(inner)]
    to_owner = {
        (k, e): [(number(d, a, b), number(a, d ^ k, b ^ e)) for d, a, b in sources] for k, e in rounds
    }
    to_column = {key: [(y, x) for x, y in pairs] for key, pairs in to_owner.items()}

    summed = []
    for slot in range(per):
        packed = pack(ranks, inner, slot, per, my_inner, grads)
        summed.append(lax.psum_scatter(packed, "dp", scatter_dimension=0, tiled=True))
    left_fourth, right_fourth = fourth_powers(left_root, right_root)
    summed[0], left_fourth, right_fourth = lax.optimization_barrier((summed[0], left_fourth, right_fourth))
    matrices = (left_stats, right_stats, left_root, right_root, left_fourth, right_fourth)
    out = None
    for slot in range(per):
        arrived = [
            lax.ppermute(summed[slot][at * rows : (at + 1) * rows], MESH_AXES, to_owner[key])
            for at, key in enumerate(rounds)
        ]
        done = precondition(ranks, inner, slot, place, arrived, matrices)
        back = [lax.ppermute(piece, MESH_AXES, to_column[key]) for piece, key in zip(done, rounds)]
        gathered = lax.all_gather(jnp.concatenate(back, axis=0), "dp", axis=0, tiled=True)
        out = unpack(ranks, inner, slot, per, my_inner, gathered, grads.shape, out)
    return out


def solution(mesh):
    placed = (
        P("dp", None, None, "fsdp"),
        P("fsdp", "dp", None, None),
        P("fsdp", "dp", None, None),
        P("fsdp", "dp", None, None),
        P("fsdp", "dp", None, None),
    )
    run = functools.partial(shards, mesh.shape["dp"], mesh.shape["fsdp"])
    return jax.shard_map(
        run, mesh=mesh, in_specs=placed, out_specs=P(None, None, "fsdp"), check_vma=False
    )
```

time: 1280 us -> 1560 us (1.22)
  Pallas kernels: 0 us -> 1120 us
  blocking collectives: 741 us -> 0 us
  starting transfers between devices: 0.04 us -> 296 us
  matrix products: 198 us -> 0 us
  waiting for transfers between devices: 231 us -> 103 us
  local copies, waits for them, and re-layouts: 71.7 us -> 14.9 us
  other arithmetic: 17 us -> 0.61 us
    pallas_call x0 -> x13, Pallas kernels: none -> 1120 us  [the longest x4 514 us: unpack(): pl.pallas_call(functools.partial(unpack_kernel, ranks, inner, slot, per),...]
    all_to_all x2 -> x0, blocking collectives: 741 us -> none  [the longest x1 372 us: shards(): lax.all_to_all(grads, 'fsdp', split_axis=1, concat_axis=3, tiled=True)]
    ppermute x0 -> x64, starting transfers between devices: none -> 296 us  [the longest x32 199 us: shards(): lax.ppermute(piece, MESH_AXES, to_column[key])]
    dot_general x12 -> x0, matrix products: 198 us -> none  [the longest x2 48.3 us: refine(): return jnp.einsum('bij,bjk->bik', root, factor, precision=EXACT)]
    all_gather x1 -> x4, waiting for transfers between devices: 158 us -> 0.08 us  [shards(): lax.all_gather(jnp.concatenate(back, axis=0), 'dp', axis=0, tiled=True)]
    ppermute x0 -> x64, waiting for transfers between devices: none -> 103 us  [the longest x32 73.7 us: shards(): lax.ppermute(piece, MESH_AXES, to_column[key])]
    reduce_scatter x1 -> x4, waiting for transfers between devices: 73.2 us -> 0.05 us  [shards(): lax.psum_scatter(packed, 'dp', scatter_dimension=0, tiled=True)]
    all_to_all x3 -> x0, local copies, waits for them, and re-layouts: 59.1 us -> none  [the longest x2 36.9 us: shards(): lax.all_to_all(copied, 'fsdp', split_axis=3, concat_axis=1, tiled=True)]
  transfers between devices with their start and end apart: 2 -> 72, of which waited for: 2 -> 19; matrix products, arithmetic and copies ran while one was open for 6% -> 0% of each run, Pallas kernels for 0% -> 56%
where the time goes in v1:
time: 1560 us; the launch traced here: 1550 us
  Pallas kernels  1120 us (72%)
  starting transfers between devices  296 us (19%)
  waiting for transfers between devices  103 us (7%)
    pallas_call x4, Pallas kernels, unpack(): pl.pallas_call(functools.partial(unpack_kernel, ranks, inner, slot, per),...  514 us
    pallas_call x4, Pallas kernels, pack(): pl.pallas_call(functools.partial(pack_kernel, ranks, inner, slot, per), i...  514 us
    ppermute x32, starting transfers between devices, shards(): lax.ppermute(piece, MESH_AXES, to_column[key])  199 us
    ppermute x32, starting transfers between devices, shards(): lax.ppermute(summed[slot][at * rows:(at + 1) * rows], MESH_AXES, to_owner...  96.9 us
    ppermute x32, waiting for transfers between devices, shards(): lax.ppermute(piece, MESH_AXES, to_column[key])  73.7 us
    pallas_call x4, Pallas kernels, precondition(): pl.pallas_call(functools.partial(block_kernel, ranks, inner, col_blocks),...  65.7 us
    pallas_call x1, Pallas kernels, fourth_powers(): pl.pallas_call(fourth_kernel, grid=(slabs, col_blocks), in_specs=[spec, s...  31.3 us
  transfers between devices with their start and end apart: 72, of which 19 were waited for; matrix products, arithmetic and copies ran while one was open for 0% of the time, Pallas kernels for 56%

profile of v1, /device:TPU:0, one launch (start us, length us, event | category | flops | bytes accessed | tf_op | source)
XLA Modules:
  0.0 1553.5 jit_solution(11607839026143898939)
XLA Ops:
  6.5 128.4 %pack_slabs.5 = bf16[4096,512]{1,0:T(8,128)(2,1)} custom-call(s32[1]{0:T(128)} %bitcast.inner_ref, bf16[32,512,512]{2,1,0:T(8,128)(2,1)} %bitcast.3), custom_call_target="tpu_custom_call" | custom-call | bytes 8388608 | tf_op jit(solution)/shard_map/pack_slabs/pallas_call | solution.py:87
  135.1 128.4 %pack_slabs.7 = bf16[4096,512]{1,0:T(8,128)(2,1)} custom-call(s32[1]{0:T(128)} %bitcast.inner_ref, bf16[32,512,512]{2,1,0:T(8,128)(2,1)} %bitcast.4), custom_call_target="tpu_custom_call" | custom-call | bytes 8388608 | tf_op jit(solution)/shard_map/pack_slabs/pallas_call | solution.py:87
  263.6 128.4 %pack_slabs.6 = bf16[4096,512]{1,0:T(8,128)(2,1)} custom-call(s32[1]{0:T(128)} %bitcast.inner_ref, bf16[32,512,512]{2,1,0:T(8,128)(2,1)} %bitcast.5), custom_call_target="tpu_custom_call" | custom-call | bytes 8388608 | tf_op jit(solution)/shard_map/pack_slabs/pallas_call | solution.py:87
  392.1 128.4 %pack_slabs.4 = bf16[4096,512]{1,0:T(8,128)(2,1)} custom-call(s32[1]{0:T(128)} %bitcast.inner_ref, bf16[32,512,512]{2,1,0:T(8,128)(2,1)} %bitcast.6), custom_call_target="tpu_custom_call" | custom-call | bytes 8388608 | tf_op jit(solution)/shard_map/pack_slabs/pallas_call | solution.py:87
  520.7 31.3 %fourth_powers.1 = (f32[4,2,512,512]{3,2,1,0:T(8,128)}, f32[4,2,512,512]{3,2,1,0:T(8,128)}) custom-call(f32[4,2,512,512]{3,2,1,0:T(8,128)} %refs_10_.7, f32[4,2,512,512]{3,2,1,0:T(8,128)} %refs_11_.7), custom_call_target="tpu_custom_call" | custom-call | flops 25769803776 | bytes 33554432 | tf_op jit(solution)/shard_map/fourth_powers/pallas_call | solution.py:43
  553.3 4.5 collective-permute-start.55
  557.8 2.4 collective-permute-start.54
  562.2 12.2 collective-permute-start.50
  576.1 2.5 collective-permute-done.50.refs_2_
  579.9 16.5 %precondition.7 = (bf16[128,512]{1,0:T(8,128)(2,1)}, bf16[128,512]{1,0:T(8,128)(2,1)}, bf16[128,512]{1,0:T(8,128)(2,1)}, bf16[128,512]{1,0:T(8,128)(2,1)}, bf16[...) custom-call(s32[2]{0:T(128)} %pad_add_fusion.place_ref, ...), custom_call_target="tpu_custom_call" | custom-call | flops 10200547328 | bytes 14680064 | tf_op jit(solution)/shard_map/precondition/pallas_call | solution.py:191
  597.9 21.4 %collective-permute-start.58 = (bf16[128,512]{1,0:T(8,128)(2,1)}, bf16[128,512]{1,0:T(8,128)(2,1)S(1)}, u32[]{:S(2)}, u32[]{:S(2)}) collective-permute-start(bf16[128,512]{1,0:T(8,128)(2,1)} %get-tuple-element.73), channel_id=1, source_target_pairs={{2,0},{3,1},{10,2},{11,3},{18,4},{19,5},{26,6},{27,7},{0,8},{1,9},... | collective-permute-start | bytes 393224 | tf_op jit(solution)/shard_map/ppermute | solution.py:242
  621.1 27.8 %collective-permute-start.62 = (bf16[128,512]{1,0:T(8,128)(2,1)}, bf16[128,512]{1,0:T(8,128)(2,1)S(1)}, u32[]{:S(2)}, u32[]{:S(2)}) collective-permute-start(bf16[128,512]{1,0:T(8,128)(2,1)} %get-tuple-element.77), channel_id=1, source_target_pairs={{6,0},{7,1},{14,2},{15,3},{22,4},{23,5},{30,6},{31,7},{4,8},{5,9},... | collective-permute-start | bytes 393224 | tf_op jit(solution)/shard_map/ppermute | solution.py:242
  648.9 2.1 collective-permute-done.58
  651.0 16.7 %collective-permute-done.59 = bf16[128,512]{1,0:T(8,128)(2,1)S(1)} collective-permute-done((bf16[128,512]{1,0:T(8,128)(2,1)}, bf16[128,512]{1,0:T(8,128)(2,1)S(1)}, u32[]{:S(2)}, u32[]{:S(2)}) %collective-permute-start.59) | collective-permute-done | bytes 131104 | tf_op jit(solution)/shard_map/ppermute | solution.py:242
  670.2 7.8 collective-permute-start.39
  678.3 5.8 collective-permute-start.35
  684.1 10.1 collective-permute-start.34
  695.4 2.4 collective-permute-done.35.refs_3_
  697.8 6.4 collective-permute-done.34.refs_2_
  705.6 16.5 %precondition.6 = (bf16[128,512]{1,0:T(8,128)(2,1)}, bf16[128,512]{1,0:T(8,128)(2,1)}, bf16[128,512]{1,0:T(8,128)(2,1)}, bf16[128,512]{1,0:T(8,128)(2,1)}, bf16[...) custom-call(s32[2]{0:T(128)} %pad_add_fusion.place_ref, ...), custom_call_target="tpu_custom_call" | custom-call | flops 10200547328 | bytes 14680064 | tf_op jit(solution)/shard_map/precondition/pallas_call | solution.py:191
  723.7 15.3 collective-permute-start.42
  739.3 3.6 collective-permute-start.44
  742.9 27.8 %collective-permute-start.46 = (bf16[128,512]{1,0:T(8,128)(2,1)}, bf16[128,512]{1,0:T(8,128)(2,1)S(1)}, u32[]{:S(2)}, u32[]{:S(2)}) collective-permute-start(bf16[128,512]{1,0:T(8,128)(2,1)} %get-tuple-element.68), channel_id=1, source_target_pairs={{6,0},{7,1},{14,2},{15,3},{22,4},{23,5},{30,6},{31,7},{4,8},{5,9},... | collective-permute-start | bytes 393224 | tf_op jit(solution)/shard_map/ppermute | solution.py:242
  772.1 16.7 %collective-permute-done.43 = bf16[128,512]{1,0:T(8,128)(2,1)S(1)} collective-permute-done((bf16[128,512]{1,0:T(8,128)(2,1)}, bf16[128,512]{1,0:T(8,128)(2,1)S(1)}, u32[]{:S(2)}, u32[]{:S(2)}) %collective-permute-start.43) | collective-permute-done | bytes 131104 | tf_op jit(solution)/shard_map/ppermute | solution.py:242
  791.4 8.4 collective-permute-start.23
  800.2 5.8 collective-permute-start.19
  806.0 10.1 collective-permute-start.18
  819.1 5.9 collective-permute-done.18.refs_2_
  826.4 16.4 %precondition.5 = (bf16[128,512]{1,0:T(8,128)(2,1)}, bf16[128,512]{1,0:T(8,128)(2,1)}, bf16[128,512]{1,0:T(8,128)(2,1)}, bf16[128,512]{1,0:T(8,128)(2,1)}, bf16[...) custom-call(s32[2]{0:T(128)} %pad_add_fusion.place_ref, ...), custom_call_target="tpu_custom_call" | custom-call | flops 10200547328 | bytes 14680064 | tf_op jit(solution)/shard_map/precondition/pallas_call | solution.py:191
  844.4 16.1 %collective-permute-start.26 = (bf16[128,512]{1,0:T(8,128)(2,1)}, bf16[128,512]{1,0:T(8,128)(2,1)S(1)}, u32[]{:S(2)}, u32[]{:S(2)}) collective-permute-start(bf16[128,512]{1,0:T(8,128)(2,1)} %get-tuple-element.56), channel_id=1, source_target_pairs={{2,0},{3,1},{10,2},{11,3},{18,4},{19,5},{26,6},{27,7},{0,8},{1,9},... | collective-permute-start | bytes 393224 | tf_op jit(solution)/shard_map/ppermute | solution.py:242
  860.7 3.4 collective-permute-start.28
  864.2 27.6 %collective-permute-start.30 = (bf16[128,512]{1,0:T(8,128)(2,1)}, bf16[128,512]{1,0:T(8,128)(2,1)S(1)}, u32[]{:S(2)}, u32[]{:S(2)}) collective-permute-start(bf16[128,512]{1,0:T(8,128)(2,1)} %get-tuple-element.60), channel_id=1, source_target_pairs={{6,0},{7,1},{14,2},{15,3},{22,4},{23,5},{30,6},{31,7},{4,8},{5,9},... | collective-permute-start | bytes 393224 | tf_op jit(solution)/shard_map/ppermute | solution.py:242
  891.8 2.0 collective-permute-done.26
  893.8 16.7 %collective-permute-done.27 = bf16[128,512]{1,0:T(8,128)(2,1)S(1)} collective-permute-done((bf16[128,512]{1,0:T(8,128)(2,1)}, bf16[128,512]{1,0:T(8,128)(2,1)S(1)}, u32[]{:S(2)}, u32[]{:S(2)}) %collective-permute-start.27) | collective-permute-done | bytes 131104 | tf_op jit(solution)/shard_map/ppermute | solution.py:242
  913.1 7.9 collective-permute-start.7
  921.3 5.8 collective-permute-start.3
  927.1 10.1 collective-permute-start.2
  938.4 2.3 collective-permute-done.3.refs_3_
  940.7 6.4 collective-permute-done.2.refs_2_
  948.4 16.4 %precondition.4 = (bf16[128,512]{1,0:T(8,128)(2,1)}, bf16[128,512]{1,0:T(8,128)(2,1)}, bf16[128,512]{1,0:T(8,128)(2,1)}, bf16[128,512]{1,0:T(8,128)(2,1)}, bf16[...) custom-call(s32[2]{0:T(128)} %pad_add_fusion.place_ref, ...), custom_call_target="tpu_custom_call" | custom-call | flops 10200547328 | bytes 14680064 | tf_op jit(solution)/shard_map/precondition/pallas_call | solution.py:191
  966.3 15.6 %collective-permute-start.10 = (bf16[128,512]{1,0:T(8,128)(2,1)}, bf16[128,512]{1,0:T(8,128)(2,1)S(1)}, u32[]{:S(2)}, u32[]{:S(2)}) collective-permute-start(bf16[128,512]{1,0:T(8,128)(2,1)} %get-tuple-element.48), channel_id=1, source_target_pairs={{2,0},{3,1},{10,2},{11,3},{18,4},{19,5},{26,6},{27,7},{0,8},{1,9},... | collective-permute-start | bytes 393224 | tf_op jit(solution)/shard_map/ppermute | solution.py:242
  982.2 3.6 collective-permute-start.12
  985.8 27.6 %collective-permute-start.14 = (bf16[128,512]{1,0:T(8,128)(2,1)}, bf16[128,512]{1,0:T(8,128)(2,1)S(1)}, u32[]{:S(2)}, u32[]{:S(2)}) collective-permute-start(bf16[128,512]{1,0:T(8,128)(2,1)} %get-tuple-element.52), channel_id=1, source_target_pairs={{6,0},{7,1},{14,2},{15,3},{22,4},{23,5},{30,6},{31,7},{4,8},{5,9},... | collective-permute-start | bytes 393224 | tf_op jit(solution)/shard_map/ppermute | solution.py:242
  1014.9 16.7 %collective-permute-done.11 = bf16[128,512]{1,0:T(8,128)(2,1)S(1)} collective-permute-done((bf16[128,512]{1,0:T(8,128)(2,1)}, bf16[128,512]{1,0:T(8,128)(2,1)S(1)}, u32[]{:S(2)}, u32[]{:S(2)}) %collective-permute-start.11) | collective-permute-done | bytes 131104 | tf_op jit(solution)/shard_map/ppermute | solution.py:242
  1032.7 128.4 %unpack_slabs.4.rest_0_ = bf16[32,512,512]{2,1,0:T(8,128)(2,1)} custom-call(s32[1]{0:T(128)} %bitcast.inner_ref, bf16[4096,512]{1,0:T(8,128)(2,1)} %all-gather.11.cloned.1.call-done.got_ref), custom_call_target="tpu_custom_call" | custom-call | bytes 8388608 | tf_op jit(solution)/shard_map/unpack_slabs/pallas_call | solution.py:121
  1161.2 128.4 %unpack_slabs.5.rest_0_ = bf16[32,512,512]{2,1,0:T(8,128)(2,1)} custom-call(s32[1]{0:T(128)} %bitcast.inner_ref, bf16[4096,512]{1,0:T(8,128)(2,1)} %all-gather.9.cloned.1.call-done.got_ref, bf16[32,512,512]{2,1,0:T(8,128)(2,1)} %unpack_slabs.4.rest_0_), custom_call_target="tpu_custom_call", output_to_operand_aliasing={{}: (2, {})} | custom-call | bytes 8388608 | tf_op jit(solution)/shard_map/unpack_slabs/pallas_call | solution.py:121
  1289.7 128.4 %unpack_slabs.6.rest_0_ = bf16[32,512,512]{2,1,0:T(8,128)(2,1)} custom-call(s32[1]{0:T(128)} %bitcast.inner_ref, bf16[4096,512]{1,0:T(8,128)(2,1)} %all-gather.7.cloned.1.call-done.got_ref, bf16[32,512,512]{2,1,0:T(8,128)(2,1)} %unpack_slabs.5.rest_0_), custom_call_target="tpu_custom_call", output_to_operand_aliasing={{}: (2, {})} | custom-call | bytes 8388608 | tf_op jit(solution)/shard_map/unpack_slabs/pallas_call | solution.py:121
  1418.2 128.4 %unpack_slabs.7 = bf16[32,512,512]{2,1,0:T(8,128)(2,1)} custom-call(s32[1]{0:T(128)} %bitcast.inner_ref, bf16[4096,512]{1,0:T(8,128)(2,1)} %all-gather.5.cloned.1.call-done.got_ref, bf16[32,512,512]{2,1,0:T(8,128)(2,1)} %unpack_slabs.6.rest_0_), custom_call_target="tpu_custom_call", output_to_operand_aliasing={{}: (2, {})} | custom-call | bytes 8388608 | tf_op jit(solution)/shard_map/unpack_slabs/pallas_call | solution.py:121
  (226 shorter events, 37.2 us)
Async XLA Ops:
  6.5 545.4 %reduce-scatter.7.cloned.1.call-start = ((), (), s32[]{:S(2)}) async-start(), calls=%async_computation.5 | async-start | bytes 5242880 | tf_op jit(solution)/shard_map/reduce_scatter | solution.py:231
  135.0 533.8 %reduce-scatter.11.cloned.1.call-start = ((), (), s32[]{:S(2)}) async-start(), calls=%async_computation.9 | async-start | bytes 5242880 | tf_op jit(solution)/shard_map/reduce_scatter | solution.py:231
  263.5 526.5 %reduce-scatter.9.cloned.1.call-start = ((), (), s32[]{:S(2)}) async-start(), calls=%async_computation.7 | async-start | bytes 5242880 | tf_op jit(solution)/shard_map/reduce_scatter | solution.py:231
  392.1 519.6 %reduce-scatter.5.cloned.1.call-start = ((), (), s32[]{:S(2)}) async-start(), calls=%async_computation.4 | async-start | bytes 5242880 | tf_op jit(solution)/shard_map/reduce_scatter | solution.py:231
  520.6 512.1 %all-gather.11.cloned.1.call-start = ((), (), s32[]{:S(2)}) async-start(), calls=%async_computation.11 | async-start | bytes 5242880 | tf_op jit(solution)/shard_map/all_gather | solution.py:243
  596.3 24.7 %collective-permute-start.56 = (bf16[128,512]{1,0:T(8,128)(2,1)}, bf16[128,512]{1,0:T(8,128)(2,1)S(1)}, u32[]{:S(2)}, u32[]{:S(2)}) collective-permute-start(bf16[128,512]{1,0:T(8,128)(2,1)} %get-tuple-element.71), channel_id=1, source_target_pairs={{0,0},{1,1},{8,2},{9,3},{16,4},{17,5},{24,6},{25,7},{2,8},{3,9},{1... | collective-permute-start | bytes 393224 | tf_op jit(solution)/shard_map/ppermute | solution.py:242
  597.9 23.2 %collective-permute-start.57 = (bf16[128,512]{1,0:T(8,128)(2,1)}, bf16[128,512]{1,0:T(8,128)(2,1)S(1)}, u32[]{:S(2)}, u32[]{:S(2)}) collective-permute-start(bf16[128,512]{1,0:T(8,128)(2,1)} %get-tuple-element.72), channel_id=1, source_target_pairs={{1,0},{0,1},{9,2},{8,3},{17,4},{16,5},{25,6},{24,7},{3,8},{2,9},{1... | collective-permute-start | bytes 393224 | tf_op jit(solution)/shard_map/ppermute | solution.py:242
  597.9 53.1 %collective-permute-start.58 = (bf16[128,512]{1,0:T(8,128)(2,1)}, bf16[128,512]{1,0:T(8,128)(2,1)S(1)}, u32[]{:S(2)}, u32[]{:S(2)}) collective-permute-start(bf16[128,512]{1,0:T(8,128)(2,1)} %get-tuple-element.73), channel_id=1, source_target_pairs={{2,0},{3,1},{10,2},{11,3},{18,4},{19,5},{26,6},{27,7},{0,8},{1,9},... | collective-permute-start | bytes 393224 | tf_op jit(solution)/shard_map/ppermute | solution.py:242
  619.3 48.3 %collective-permute-start.59 = (bf16[128,512]{1,0:T(8,128)(2,1)}, bf16[128,512]{1,0:T(8,128)(2,1)S(1)}, u32[]{:S(2)}, u32[]{:S(2)}) collective-permute-start(bf16[128,512]{1,0:T(8,128)(2,1)} %get-tuple-element.74), channel_id=1, source_target_pairs={{3,0},{2,1},{11,2},{10,3},{19,4},{18,5},{27,6},{26,7},{1,8},{0,9},... | collective-permute-start | bytes 393224 | tf_op jit(solution)/shard_map/ppermute | solution.py:242
  619.7 48.0 %collective-permute-start.60 = (bf16[128,512]{1,0:T(8,128)(2,1)}, bf16[128,512]{1,0:T(8,128)(2,1)S(1)}, u32[]{:S(2)}, u32[]{:S(2)}) collective-permute-start(bf16[128,512]{1,0:T(8,128)(2,1)} %get-tuple-element.75), channel_id=1, source_target_pairs={{4,0},{5,1},{12,2},{13,3},{20,4},{21,5},{28,6},{29,7},{6,8},{7,9},... | collective-permute-start | bytes 393224 | tf_op jit(solution)/shard_map/ppermute | solution.py:242
  621.1 46.6 %collective-permute-start.61 = (bf16[128,512]{1,0:T(8,128)(2,1)}, bf16[128,512]{1,0:T(8,128)(2,1)S(1)}, u32[]{:S(2)}, u32[]{:S(2)}) collective-permute-start(bf16[128,512]{1,0:T(8,128)(2,1)} %get-tuple-element.76), channel_id=1, source_target_pairs={{5,0},{4,1},{13,2},{12,3},{21,4},{20,5},{29,6},{28,7},{7,8},{6,9},... | collective-permute-start | bytes 393224 | tf_op jit(solution)/shard_map/ppermute | solution.py:242
  621.1 46.6 %collective-permute-start.62 = (bf16[128,512]{1,0:T(8,128)(2,1)}, bf16[128,512]{1,0:T(8,128)(2,1)S(1)}, u32[]{:S(2)}, u32[]{:S(2)}) collective-permute-start(bf16[128,512]{1,0:T(8,128)(2,1)} %get-tuple-element.77), channel_id=1, source_target_pairs={{6,0},{7,1},{14,2},{15,3},{22,4},{23,5},{30,6},{31,7},{4,8},{5,9},... | collective-permute-start | bytes 393224 | tf_op jit(solution)/shard_map/ppermute | solution.py:242
  651.0 16.8 %collective-permute-start.63 = (bf16[128,512]{1,0:T(8,128)(2,1)}, bf16[128,512]{1,0:T(8,128)(2,1)S(1)}, u32[]{:S(2)}, u32[]{:S(2)}) collective-permute-start(bf16[128,512]{1,0:T(8,128)(2,1)} %get-tuple-element.78), channel_id=1, source_target_pairs={{7,0},{6,1},{15,2},{14,3},{23,4},{22,5},{31,6},{30,7},{5,8},{4,9},... | collective-permute-start | bytes 393224 | tf_op jit(solution)/shard_map/ppermute | solution.py:242
  668.8 492.4 %all-gather.9.cloned.1.call-start = ((), (), s32[]{:S(2)}) async-start(), calls=%async_computation.10 | async-start | bytes 5242880 | tf_op jit(solution)/shard_map/all_gather | solution.py:243
  678.3 17.1 %collective-permute-start.36 = (bf16[128,512]{1,0:T(8,128)(2,1)S(1)}, bf16[128,512]{1,0:T(8,128)(2,1)S(1)}, u32[]{:S(2)}, u32[]{:S(2)}) collective-permute-start(bf16[128,512]{1,0:T(8,128)(2,1)S(1)} %get-tuple-element.90), channel_id=1, source_target_pairs={{0,4},{1,5},{2,12},{3,13},{4,20},{5,21},{6,28},{7,29},{8,6},{9,7},... | collective-permute-start | bytes 393224 | tf_op jit(solution)/shard_map/ppermute | solution.py:238
  678.3 19.5 %collective-permute-start.35 = (bf16[128,512]{1,0:T(8,128)(2,1)S(1)}, bf16[128,512]{1,0:T(8,128)(2,1)S(1)}, u32[]{:S(2)}, u32[]{:S(2)}) collective-permute-start(bf16[128,512]{1,0:T(8,128)(2,1)S(1)} %get-tuple-element.91), channel_id=1, source_target_pairs={{0,3},{1,2},{2,11},{3,10},{4,19},{5,18},{6,27},{7,26},{8,1},{9,0},... | collective-permute-start | bytes 393224 | tf_op jit(solution)/shard_map/ppermute | solution.py:238
  684.1 20.1 %collective-permute-start.34 = (bf16[128,512]{1,0:T(8,128)(2,1)S(1)}, bf16[128,512]{1,0:T(8,128)(2,1)S(1)}, u32[]{:S(2)}, u32[]{:S(2)}) collective-permute-start(bf16[128,512]{1,0:T(8,128)(2,1)S(1)} %get-tuple-element.92), channel_id=1, source_target_pairs={{0,2},{1,3},{2,10},{3,11},{4,18},{5,19},{6,26},{7,27},{8,0},{9,1},... | collective-permute-start | bytes 393224 | tf_op jit(solution)/shard_map/ppermute | solution.py:238
  722.1 20.8 %collective-permute-start.40 = (bf16[128,512]{1,0:T(8,128)(2,1)}, bf16[128,512]{1,0:T(8,128)(2,1)S(1)}, u32[]{:S(2)}, u32[]{:S(2)}) collective-permute-start(bf16[128,512]{1,0:T(8,128)(2,1)} %get-tuple-element.62), channel_id=1, source_target_pairs={{0,0},{1,1},{8,2},{9,3},{16,4},{17,5},{24,6},{25,7},{2,8},{3,9},{1... | collective-permute-start | bytes 393224 | tf_op jit(solution)/shard_map/ppermute | solution.py:242
  723.7 19.2 %collective-permute-start.41 = (bf16[128,512]{1,0:T(8,128)(2,1)}, bf16[128,512]{1,0:T(8,128)(2,1)S(1)}, u32[]{:S(2)}, u32[]{:S(2)}) collective-permute-start(bf16[128,512]{1,0:T(8,128)(2,1)} %get-tuple-element.63), channel_id=1, source_target_pairs={{1,0},{0,1},{9,2},{8,3},{17,4},{16,5},{25,6},{24,7},{3,8},{2,9},{1... | collective-permute-start | bytes 393224 | tf_op jit(solution)/shard_map/ppermute | solution.py:242
  723.7 48.4 %collective-permute-start.42 = (bf16[128,512]{1,0:T(8,128)(2,1)}, bf16[128,512]{1,0:T(8,128)(2,1)S(1)}, u32[]{:S(2)}, u32[]{:S(2)}) collective-permute-start(bf16[128,512]{1,0:T(8,128)(2,1)} %get-tuple-element.64), channel_id=1, source_target_pairs={{2,0},{3,1},{10,2},{11,3},{18,4},{19,5},{26,6},{27,7},{0,8},{1,9},... | collective-permute-start | bytes 393224 | tf_op jit(solution)/shard_map/ppermute | solution.py:242
  739.0 49.8 %collective-permute-start.43 = (bf16[128,512]{1,0:T(8,128)(2,1)}, bf16[128,512]{1,0:T(8,128)(2,1)S(1)}, u32[]{:S(2)}, u32[]{:S(2)}) collective-permute-start(bf16[128,512]{1,0:T(8,128)(2,1)} %get-tuple-element.65), channel_id=1, source_target_pairs={{3,0},{2,1},{11,2},{10,3},{19,4},{18,5},{27,6},{26,7},{1,8},{0,9},... | collective-permute-start | bytes 393224 | tf_op jit(solution)/shard_map/ppermute | solution.py:242
  739.3 49.5 %collective-permute-start.44 = (bf16[128,512]{1,0:T(8,128)(2,1)}, bf16[128,512]{1,0:T(8,128)(2,1)S(1)}, u32[]{:S(2)}, u32[]{:S(2)}) collective-permute-start(bf16[128,512]{1,0:T(8,128)(2,1)} %get-tuple-element.66), channel_id=1, source_target_pairs={{4,0},{5,1},{12,2},{13,3},{20,4},{21,5},{28,6},{29,7},{6,8},{7,9},... | collective-permute-start | bytes 393224 | tf_op jit(solution)/shard_map/ppermute | solution.py:242
  742.9 45.9 %collective-permute-start.45 = (bf16[128,512]{1,0:T(8,128)(2,1)}, bf16[128,512]{1,0:T(8,128)(2,1)S(1)}, u32[]{:S(2)}, u32[]{:S(2)}) collective-permute-start(bf16[128,512]{1,0:T(8,128)(2,1)} %get-tuple-element.67), channel_id=1, source_target_pairs={{5,0},{4,1},{13,2},{12,3},{21,4},{20,5},{29,6},{28,7},{7,8},{6,9},... | collective-permute-start | bytes 393224 | tf_op jit(solution)/shard_map/ppermute | solution.py:242
  742.9 45.9 %collective-permute-start.46 = (bf16[128,512]{1,0:T(8,128)(2,1)}, bf16[128,512]{1,0:T(8,128)(2,1)S(1)}, u32[]{:S(2)}, u32[]{:S(2)}) collective-permute-start(bf16[128,512]{1,0:T(8,128)(2,1)} %get-tuple-element.68), channel_id=1, source_target_pairs={{6,0},{7,1},{14,2},{15,3},{22,4},{23,5},{30,6},{31,7},{4,8},{5,9},... | collective-permute-start | bytes 393224 | tf_op jit(solution)/shard_map/ppermute | solution.py:242
  772.1 16.8 %collective-permute-start.47 = (bf16[128,512]{1,0:T(8,128)(2,1)}, bf16[128,512]{1,0:T(8,128)(2,1)S(1)}, u32[]{:S(2)}, u32[]{:S(2)}) collective-permute-start(bf16[128,512]{1,0:T(8,128)(2,1)} %get-tuple-element.69), channel_id=1, source_target_pairs={{7,0},{6,1},{15,2},{14,3},{23,4},{22,5},{31,6},{30,7},{5,8},{4,9},... | collective-permute-start | bytes 393224 | tf_op jit(solution)/shard_map/ppermute | solution.py:242
  789.9 499.7 %all-gather.7.cloned.1.call-start = ((), (), s32[]{:S(2)}) async-start(), calls=%async_computation.8 | async-start | bytes 5242880 | tf_op jit(solution)/shard_map/all_gather | solution.py:243
  800.2 17.1 %collective-permute-start.20 = (bf16[128,512]{1,0:T(8,128)(2,1)S(1)}, bf16[128,512]{1,0:T(8,128)(2,1)S(1)}, u32[]{:S(2)}, u32[]{:S(2)}) collective-permute-start(bf16[128,512]{1,0:T(8,128)(2,1)S(1)} %get-tuple-element.98), channel_id=1, source_target_pairs={{0,4},{1,5},{2,12},{3,13},{4,20},{5,21},{6,28},{7,29},{8,6},{9,7},... | collective-permute-start | bytes 393224 | tf_op jit(solution)/shard_map/ppermute | solution.py:238
  800.2 18.9 %collective-permute-start.19 = (bf16[128,512]{1,0:T(8,128)(2,1)S(1)}, bf16[128,512]{1,0:T(8,128)(2,1)S(1)}, u32[]{:S(2)}, u32[]{:S(2)}) collective-permute-start(bf16[128,512]{1,0:T(8,128)(2,1)S(1)} %get-tuple-element.99), channel_id=1, source_target_pairs={{0,3},{1,2},{2,11},{3,10},{4,19},{5,18},{6,27},{7,26},{8,1},{9,0},... | collective-permute-start | bytes 393224 | tf_op jit(solution)/shard_map/ppermute | solution.py:238
  806.0 19.0 %collective-permute-start.18 = (bf16[128,512]{1,0:T(8,128)(2,1)S(1)}, bf16[128,512]{1,0:T(8,128)(2,1)S(1)}, u32[]{:S(2)}, u32[]{:S(2)}) collective-permute-start(bf16[128,512]{1,0:T(8,128)(2,1)S(1)} %get-tuple-element.100), channel_id=1, source_target_pairs={{0,2},{1,3},{2,10},{3,11},{4,18},{5,19},{6,26},{7,27},{8,0},{9,1},... | collective-permute-start | bytes 393224 | tf_op jit(solution)/shard_map/ppermute | solution.py:238
  842.8 21.4 %collective-permute-start.24 = (bf16[128,512]{1,0:T(8,128)(2,1)}, bf16[128,512]{1,0:T(8,128)(2,1)S(1)}, u32[]{:S(2)}, u32[]{:S(2)}) collective-permute-start(bf16[128,512]{1,0:T(8,128)(2,1)} %get-tuple-element.54), channel_id=1, source_target_pairs={{0,0},{1,1},{8,2},{9,3},{16,4},{17,5},{24,6},{25,7},{2,8},{3,9},{1... | collective-permute-start | bytes 393224 | tf_op jit(solution)/shard_map/ppermute | solution.py:242
  844.3 19.8 %collective-permute-start.25 = (bf16[128,512]{1,0:T(8,128)(2,1)}, bf16[128,512]{1,0:T(8,128)(2,1)S(1)}, u32[]{:S(2)}, u32[]{:S(2)}) collective-permute-start(bf16[128,512]{1,0:T(8,128)(2,1)} %get-tuple-element.55), channel_id=1, source_target_pairs={{1,0},{0,1},{9,2},{8,3},{17,4},{16,5},{25,6},{24,7},{3,8},{2,9},{1... | collective-permute-start | bytes 393224 | tf_op jit(solution)/shard_map/ppermute | solution.py:242
  844.4 49.4 %collective-permute-start.26 = (bf16[128,512]{1,0:T(8,128)(2,1)}, bf16[128,512]{1,0:T(8,128)(2,1)S(1)}, u32[]{:S(2)}, u32[]{:S(2)}) collective-permute-start(bf16[128,512]{1,0:T(8,128)(2,1)} %get-tuple-element.56), channel_id=1, source_target_pairs={{2,0},{3,1},{10,2},{11,3},{18,4},{19,5},{26,6},{27,7},{0,8},{1,9},... | collective-permute-start | bytes 393224 | tf_op jit(solution)/shard_map/ppermute | solution.py:242
  860.4 50.0 %collective-permute-start.27 = (bf16[128,512]{1,0:T(8,128)(2,1)}, bf16[128,512]{1,0:T(8,128)(2,1)S(1)}, u32[]{:S(2)}, u32[]{:S(2)}) collective-permute-start(bf16[128,512]{1,0:T(8,128)(2,1)} %get-tuple-element.57), channel_id=1, source_target_pairs={{3,0},{2,1},{11,2},{10,3},{19,4},{18,5},{27,6},{26,7},{1,8},{0,9},... | collective-permute-start | bytes 393224 | tf_op jit(solution)/shard_map/ppermute | solution.py:242
  860.7 49.7 %collective-permute-start.28 = (bf16[128,512]{1,0:T(8,128)(2,1)}, bf16[128,512]{1,0:T(8,128)(2,1)S(1)}, u32[]{:S(2)}, u32[]{:S(2)}) collective-permute-start(bf16[128,512]{1,0:T(8,128)(2,1)} %get-tuple-element.58), channel_id=1, source_target_pairs={{4,0},{5,1},{12,2},{13,3},{20,4},{21,5},{28,6},{29,7},{6,8},{7,9},... | collective-permute-start | bytes 393224 | tf_op jit(solution)/shard_map/ppermute | solution.py:242
  864.1 46.4 %collective-permute-start.29 = (bf16[128,512]{1,0:T(8,128)(2,1)}, bf16[128,512]{1,0:T(8,128)(2,1)S(1)}, u32[]{:S(2)}, u32[]{:S(2)}) collective-permute-start(bf16[128,512]{1,0:T(8,128)(2,1)} %get-tuple-element.59), channel_id=1, source_target_pairs={{5,0},{4,1},{13,2},{12,3},{21,4},{20,5},{29,6},{28,7},{7,8},{6,9},... | collective-permute-start | bytes 393224 | tf_op jit(solution)/shard_map/ppermute | solution.py:242
  864.2 46.4 %collective-permute-start.30 = (bf16[128,512]{1,0:T(8,128)(2,1)}, bf16[128,512]{1,0:T(8,128)(2,1)S(1)}, u32[]{:S(2)}, u32[]{:S(2)}) collective-permute-start(bf16[128,512]{1,0:T(8,128)(2,1)} %get-tuple-element.60), channel_id=1, source_target_pairs={{6,0},{7,1},{14,2},{15,3},{22,4},{23,5},{30,6},{31,7},{4,8},{5,9},... | collective-permute-start | bytes 393224 | tf_op jit(solution)/shard_map/ppermute | solution.py:242
  893.7 16.8 %collective-permute-start.31 = (bf16[128,512]{1,0:T(8,128)(2,1)}, bf16[128,512]{1,0:T(8,128)(2,1)S(1)}, u32[]{:S(2)}, u32[]{:S(2)}) collective-permute-start(bf16[128,512]{1,0:T(8,128)(2,1)} %get-tuple-element.61), channel_id=1, source_target_pairs={{7,0},{6,1},{15,2},{14,3},{23,4},{22,5},{31,6},{30,7},{5,8},{4,9},... | collective-permute-start | bytes 393224 | tf_op jit(solution)/shard_map/ppermute | solution.py:242
  911.6 506.5 %all-gather.5.cloned.1.call-start = ((), (), s32[]{:S(2)}) async-start(), calls=%async_computation.6 | async-start | bytes 5242880 | tf_op jit(solution)/shard_map/all_gather | solution.py:243
  921.3 17.1 %collective-permute-start.4 = (bf16[128,512]{1,0:T(8,128)(2,1)S(1)}, bf16[128,512]{1,0:T(8,128)(2,1)S(1)}, u32[]{:S(2)}, u32[]{:S(2)}) collective-permute-start(bf16[128,512]{1,0:T(8,128)(2,1)S(1)} %get-tuple-element.106), channel_id=1, source_target_pairs={{0,4},{1,5},{2,12},{3,13},{4,20},{5,21},{6,28},{7,29},{8,6},{9,7},... | collective-permute-start | bytes 393224 | tf_op jit(solution)/shard_map/ppermute | solution.py:238
  921.3 19.4 %collective-permute-start.3 = (bf16[128,512]{1,0:T(8,128)(2,1)S(1)}, bf16[128,512]{1,0:T(8,128)(2,1)S(1)}, u32[]{:S(2)}, u32[]{:S(2)}) collective-permute-start(bf16[128,512]{1,0:T(8,128)(2,1)S(1)} %get-tuple-element.107), channel_id=1, source_target_pairs={{0,3},{1,2},{2,11},{3,10},{4,19},{5,18},{6,27},{7,26},{8,1},{9,0},... | collective-permute-start | bytes 393224 | tf_op jit(solution)/shard_map/ppermute | solution.py:238
  927.1 19.9 %collective-permute-start.2 = (bf16[128,512]{1,0:T(8,128)(2,1)S(1)}, bf16[128,512]{1,0:T(8,128)(2,1)S(1)}, u32[]{:S(2)}, u32[]{:S(2)}) collective-permute-start(bf16[128,512]{1,0:T(8,128)(2,1)S(1)} %get-tuple-element.108), channel_id=1, source_target_pairs={{0,2},{1,3},{2,10},{3,11},{4,18},{5,19},{6,26},{7,27},{8,0},{9,1},... | collective-permute-start | bytes 393224 | tf_op jit(solution)/shard_map/ppermute | solution.py:238
  964.8 21.0 %collective-permute-start.8 = (bf16[128,512]{1,0:T(8,128)(2,1)}, bf16[128,512]{1,0:T(8,128)(2,1)S(1)}, u32[]{:S(2)}, u32[]{:S(2)}) collective-permute-start(bf16[128,512]{1,0:T(8,128)(2,1)} %get-tuple-element.46), channel_id=1, source_target_pairs={{0,0},{1,1},{8,2},{9,3},{16,4},{17,5},{24,6},{25,7},{2,8},{3,9},{1... | collective-permute-start | bytes 393224 | tf_op jit(solution)/shard_map/ppermute | solution.py:242
  966.3 19.5 %collective-permute-start.9 = (bf16[128,512]{1,0:T(8,128)(2,1)}, bf16[128,512]{1,0:T(8,128)(2,1)S(1)}, u32[]{:S(2)}, u32[]{:S(2)}) collective-permute-start(bf16[128,512]{1,0:T(8,128)(2,1)} %get-tuple-element.47), channel_id=1, source_target_pairs={{1,0},{0,1},{9,2},{8,3},{17,4},{16,5},{25,6},{24,7},{3,8},{2,9},{1... | collective-permute-start | bytes 393224 | tf_op jit(solution)/shard_map/ppermute | solution.py:242
  966.3 48.6 %collective-permute-start.10 = (bf16[128,512]{1,0:T(8,128)(2,1)}, bf16[128,512]{1,0:T(8,128)(2,1)S(1)}, u32[]{:S(2)}, u32[]{:S(2)}) collective-permute-start(bf16[128,512]{1,0:T(8,128)(2,1)} %get-tuple-element.48), channel_id=1, source_target_pairs={{2,0},{3,1},{10,2},{11,3},{18,4},{19,5},{26,6},{27,7},{0,8},{1,9},... | collective-permute-start | bytes 393224 | tf_op jit(solution)/shard_map/ppermute | solution.py:242
  981.9 49.7 %collective-permute-start.11 = (bf16[128,512]{1,0:T(8,128)(2,1)}, bf16[128,512]{1,0:T(8,128)(2,1)S(1)}, u32[]{:S(2)}, u32[]{:S(2)}) collective-permute-start(bf16[128,512]{1,0:T(8,128)(2,1)} %get-tuple-element.49), channel_id=1, source_target_pairs={{3,0},{2,1},{11,2},{10,3},{19,4},{18,5},{27,6},{26,7},{1,8},{0,9},... | collective-permute-start | bytes 393224 | tf_op jit(solution)/shard_map/ppermute | solution.py:242
  982.2 49.4 %collective-permute-start.12 = (bf16[128,512]{1,0:T(8,128)(2,1)}, bf16[128,512]{1,0:T(8,128)(2,1)S(1)}, u32[]{:S(2)}, u32[]{:S(2)}) collective-permute-start(bf16[128,512]{1,0:T(8,128)(2,1)} %get-tuple-element.50), channel_id=1, source_target_pairs={{4,0},{5,1},{12,2},{13,3},{20,4},{21,5},{28,6},{29,7},{6,8},{7,9},... | collective-permute-start | bytes 393224 | tf_op jit(solution)/shard_map/ppermute | solution.py:242
  985.8 45.8 %collective-permute-start.13 = (bf16[128,512]{1,0:T(8,128)(2,1)}, bf16[128,512]{1,0:T(8,128)(2,1)S(1)}, u32[]{:S(2)}, u32[]{:S(2)}) collective-permute-start(bf16[128,512]{1,0:T(8,128)(2,1)} %get-tuple-element.51), channel_id=1, source_target_pairs={{5,0},{4,1},{13,2},{12,3},{21,4},{20,5},{29,6},{28,7},{7,8},{6,9},... | collective-permute-start | bytes 393224 | tf_op jit(solution)/shard_map/ppermute | solution.py:242
  985.8 45.8 %collective-permute-start.14 = (bf16[128,512]{1,0:T(8,128)(2,1)}, bf16[128,512]{1,0:T(8,128)(2,1)S(1)}, u32[]{:S(2)}, u32[]{:S(2)}) collective-permute-start(bf16[128,512]{1,0:T(8,128)(2,1)} %get-tuple-element.52), channel_id=1, source_target_pairs={{6,0},{7,1},{14,2},{15,3},{22,4},{23,5},{30,6},{31,7},{4,8},{5,9},... | collective-permute-start | bytes 393224 | tf_op jit(solution)/shard_map/ppermute | solution.py:242
  (60 other events, 510.9 us)
Sparse Core Ops, SparseCore 0:
  135.1 55.3 reduce-scatter.6
  263.7 55.4 reduce-scatter.10
  392.2 55.3 reduce-scatter.8
  520.7 63.8 reduce-scatter.4
  668.9 82.6 all-gather.10
  790.1 89.7 all-gather.8
  911.8 88.5 all-gather.6
  1032.8 62.6 all-gather.4

commit v2 on v1

v2 whole, which is shorter than its diff:
```python
import functools

import jax
import jax.numpy as jnp
from jax import lax
from jax.experimental import pallas as pl
from jax.experimental.pallas import tpu as pltpu
from jax.sharding import PartitionSpec as P

ema_decay = 0.999
MESH_AXES = ("dp", "fsdp")
VMEM_LIMIT = 60 * 1024 * 1024


def split(x):
    high = x.astype(jnp.bfloat16)
    low = (x - high.astype(jnp.float32)).astype(jnp.bfloat16)
    return high, low


def mm(a, b):
    return jnp.dot(a, b, preferred_element_type=jnp.float32)


def dot3(a, b):
    a_high, a_low = split(a)
    b_high, b_low = split(b)
    return mm(a_high, b_high) + (mm(a_high, b_low) + mm(a_low, b_high))


def fourth_kernel(left_ref, right_ref, left_out, right_out):
    for ref, out in ((left_ref, left_out), (right_ref, right_out)):
        root = ref[0, 0]
        square = dot3(root, root)
        out[0, 0] = dot3(square, square)


def fourth_powers(left_root, right_root):
    slabs, col_blocks, order, _ = left_root.shape
    spec = pl.BlockSpec((1, 1, order, order), lambda i, j: (i, j, 0, 0))
    shape = jax.ShapeDtypeStruct(left_root.shape, jnp.float32)
    count = slabs * col_blocks
    return pl.pallas_call(
        fourth_kernel,
        grid=(slabs, col_blocks),
        in_specs=[spec, spec],
        out_specs=[spec, spec],
        out_shape=[shape, shape],
        compiler_params=pltpu.CompilerParams(vmem_limit_bytes=VMEM_LIMIT),
        cost_estimate=pl.CostEstimate(
            flops=count * 4 * 3 * 2 * order**3, bytes_accessed=count * 16 * order**2, transcendentals=0
        ),
        name="fourth_powers",
    )(left_root, right_root)


def slab_of(k, e, outer_place, inner_place, inner):
    return (outer_place ^ k) * inner + (inner_place ^ e)


def pack_kernel(ranks, inner, place_ref, grads_ref, out_ref):
    rows = grads_ref.shape[2]
    d = pl.program_id(0)
    for k in range(ranks):
        for e in range(inner):
            at = (k * inner + e) * rows
            out_ref[at : at + rows] = grads_ref[slab_of(k, e, d, place_ref[1], inner), 0]


def pack(ranks, inner, slot, per, place, grads):
    slabs, order, width = grads.shape
    owners, rows = slabs // per, order // ranks
    return pl.pallas_call(
        functools.partial(pack_kernel, ranks, inner),
        grid=(ranks,),
        in_specs=[
            pl.BlockSpec(memory_space=pltpu.SMEM),
            pl.BlockSpec((owners, 1, rows, width), lambda d: (0, slot, d, 0)),
        ],
        out_specs=pl.BlockSpec((owners * rows, width), lambda d: (d, 0)),
        out_shape=jax.ShapeDtypeStruct((owners * order, width), grads.dtype),
        compiler_params=pltpu.CompilerParams(vmem_limit_bytes=VMEM_LIMIT),
        cost_estimate=pl.CostEstimate(
            flops=0, bytes_accessed=4 * owners * order * width, transcendentals=0
        ),
        name="pack_slabs",
    )(place, grads.reshape(owners, per, order, width))


def unpack_kernel(ranks, inner, place_ref, got_ref, *rest):
    out_ref = rest[-1]
    rows = out_ref.shape[2]
    for k in range(ranks):
        for e in range(inner):
            at = (k * inner + e) * rows
            out_ref[slab_of(k, e, place_ref[0], place_ref[1], inner), 0] = got_ref[at : at + rows]


def unpack(ranks, inner, slot, per, place, got, so_far):
    order = got.shape[0] // (ranks * inner)
    width, owners, rows = got.shape[1], ranks * inner, order // ranks
    operands = [place, got] + ([] if so_far is None else [so_far])
    return pl.pallas_call(
        functools.partial(unpack_kernel, ranks, inner),
        grid=(ranks,),
        in_specs=[
            pl.BlockSpec(memory_space=pltpu.SMEM),
            pl.BlockSpec((owners * rows, width), lambda d: (d, 0)),
        ]
        + [pl.BlockSpec(memory_space=pl.ANY)] * (len(operands) - 2),
        out_specs=pl.BlockSpec((owners, 1, rows, width), lambda d: (0, slot, d, 0)),
        out_shape=jax.ShapeDtypeStruct((owners, per, order, width), got.dtype),
        input_output_aliases={} if so_far is None else {2: 0},
        compiler_params=pltpu.CompilerParams(vmem_limit_bytes=VMEM_LIMIT),
        cost_estimate=pl.CostEstimate(flops=0, bytes_accessed=4 * got.size, transcendentals=0),
        name="unpack_slabs",
    )(*operands)


def route_kernel(ranks, inner, place_ref, *refs):
    taken, outs, held = refs[:ranks], refs[ranks:-1], refs[-1]
    rows = outs[0].shape[0]
    turn, inner_place = place_ref[2] ^ place_ref[0], place_ref[1]
    for k in range(ranks):
        held[k] = taken[k][...]
    for m in range(ranks):
        for e in range(inner):
            start = pl.multiple_of((inner_place ^ e) * rows, rows)
            outs[m * inner + e][...] = held[turn ^ m, pl.ds(start, rows), :]


def route(ranks, inner, place, taken):
    rows, width = taken[0].shape[0] // inner, taken[0].shape[1]
    vmem = pl.BlockSpec(memory_space=pltpu.VMEM)
    return pl.pallas_call(
        functools.partial(route_kernel, ranks, inner),
        in_specs=[pl.BlockSpec(memory_space=pltpu.SMEM)] + [vmem] * ranks,
        out_specs=[vmem] * (ranks * inner),
        out_shape=[jax.ShapeDtypeStruct((rows, width), taken[0].dtype)] * (ranks * inner),
        scratch_shapes=[pltpu.VMEM((ranks, inner * rows, width), taken[0].dtype)],
        compiler_params=pltpu.CompilerParams(vmem_limit_bytes=VMEM_LIMIT // 4),
        cost_estimate=pl.CostEstimate(
            flops=0, bytes_accessed=4 * ranks * taken[0].size, transcendentals=0
        ),
        name="route",
    )(place, *taken)


def refine(root, fourth, stats):
    order = root.shape[0]
    coupled = dot3(fourth, stats)
    on_diagonal = lax.broadcasted_iota(jnp.int32, (order, order), 0) == lax.broadcasted_iota(
        jnp.int32, (order, order), 1
    )
    factor = (jnp.where(on_diagonal, 5.0, 0.0) - coupled) * 0.25
    return dot3(root, factor)


def block_kernel(ranks, inner, steps, place_ref, *refs):
    count = ranks * inner
    pieces = refs[:count]
    left_stats, right_stats, left_root, right_root, left_fourth, right_fourth = refs[count : count + 6]
    outs = refs[count + 6 : count + 6 + ranks]
    blocks, results = refs[count + 6 + ranks :]
    rows, width = pieces[0].shape
    order = blocks.shape[1]
    outer_place, inner_place = place_ref[0], place_ref[1]
    step = pl.program_id(0)
    per_block = order // width

    def spot(rank, shard):
        row = pl.multiple_of(rank * rows, rows)
        column = pl.multiple_of((shard % per_block) * width, width)
        return shard // per_block, pl.ds(row, rows), pl.ds(column, width)

    @pl.when(step == 0)
    def _():
        for k in range(ranks):
            for e in range(inner):
                blocks[spot(outer_place ^ k, inner_place ^ e)] = pieces[k * inner + e][...]

    block = blocks[step]
    turned = block.T
    left = ema_decay * left_stats[0, 0] + (1.0 - ema_decay) * mm(block, turned)
    right = ema_decay * right_stats[0, 0] + (1.0 - ema_decay) * mm(turned, block)
    new_left = refine(left_root[0, 0], left_fourth[0, 0], left)
    new_right = refine(right_root[0, 0], right_fourth[0, 0], right)
    high, low = split(new_left)
    halfway = mm(high, block) + mm(low, block)
    results[step] = dot3(halfway, new_right).astype(results.dtype)

    @pl.when(step == steps - 1)
    def _():
        for k in range(ranks):
            for b in range(inner):
                outs[k][b * rows : (b + 1) * rows] = results[spot(place_ref[2] ^ k, b)]


def precondition(ranks, inner, slot, place, pieces, stats_and_roots):
    _, col_blocks, order, _ = stats_and_roots[0].shape
    rows, width = pieces[0].shape
    count = ranks * inner
    piece = pl.BlockSpec((rows, width), lambda j: (0, 0))
    strip = pl.BlockSpec((inner * rows, width), lambda j: (0, 0))
    matrix = pl.BlockSpec((1, 1, order, order), lambda j: (slot, j, 0, 0))
    return pl.pallas_call(
        functools.partial(block_kernel, ranks, inner, col_blocks),
        grid=(col_blocks,),
        in_specs=[pl.BlockSpec(memory_space=pltpu.SMEM)] + [piece] * count + [matrix] * 6,
        out_specs=[strip] * ranks,
        out_shape=[jax.ShapeDtypeStruct((inner * rows, width), jnp.bfloat16)] * ranks,
        scratch_shapes=[pltpu.VMEM((col_blocks, order, order), jnp.bfloat16)] * 2,
        compiler_params=pltpu.CompilerParams(vmem_limit_bytes=VMEM_LIMIT),
        cost_estimate=pl.CostEstimate(
            flops=col_blocks * 19 * 2 * order**3,
            bytes_accessed=col_blocks * 28 * order**2,
            transcendentals=0,
        ),
        name="precondition",
    )(place, *pieces, *stats_and_roots)


def shards(ranks, fsdp, grads, left_stats, right_stats, left_root, right_root):
    per = left_stats.shape[0]
    inner = fsdp // ranks
    grads = grads[0]
    slabs, order, width = grads.shape
    rows = order // ranks
    f = lax.axis_index("fsdp")
    place = jnp.stack([f // inner, f % inner, lax.axis_index("dp")]).astype(jnp.int32)
    rounds = [(k, e) for k in range(ranks) for e in range(inner)]

    def number(d, a, b):
        return (d * ranks + a) * inner + b

    sources = [(d, a, b) for d in range(ranks) for a in range(ranks) for b in range(inner)]
    to_owner = {
        (k, e): [(number(d, a, b), number(a, d ^ k, b ^ e)) for d, a, b in sources] for k, e in rounds
    }
    to_row = [[(d, d ^ k) for d in range(ranks)] for k in range(ranks)]
    to_column = {
        (m, e): [(a * inner + b, (a ^ m) * inner + (b ^ e)) for a in range(ranks) for b in range(inner)]
        for m, e in rounds
    }

    summed = []
    for slot in range(per):
        packed = pack(ranks, inner, slot, per, place, grads)
        summed.append(lax.psum_scatter(packed, "dp", scatter_dimension=0, tiled=True))
    left_fourth, right_fourth = fourth_powers(left_root, right_root)
    summed[0], left_fourth, right_fourth = lax.optimization_barrier((summed[0], left_fourth, right_fourth))
    matrices = (left_stats, right_stats, left_root, right_root, left_fourth, right_fourth)
    out = None
    for slot in range(per):
        arrived = [
            lax.ppermute(summed[slot][at * rows : (at + 1) * rows], MESH_AXES, to_owner[key])
            for at, key in enumerate(rounds)
        ]
        strips = precondition(ranks, inner, slot, place, arrived, matrices)
        strips = [strips[0]] + [lax.ppermute(strips[k], "dp", to_row[k]) for k in range(1, ranks)]
        routed = route(ranks, inner, place, strips)
        back = [routed[0]] + [
            lax.ppermute(piece, "fsdp", to_column[key]) for piece, key in zip(routed[1:], rounds[1:])
        ]
        gathered = lax.all_gather(jnp.concatenate(back, axis=0), "dp", axis=0, tiled=True)
        out = unpack(ranks, inner, slot, per, place, gathered, out)
    return out.reshape(grads.shape)


def solution(mesh):
    placed = (
        P("dp", None, None, "fsdp"),
        P("fsdp", "dp", None, None),
        P("fsdp", "dp", None, None),
        P("fsdp", "dp", None, None),
        P("fsdp", "dp", None, None),
    )
    run = functools.partial(shards, mesh.shape["dp"], mesh.shape["fsdp"])
    return jax.shard_map(
        run, mesh=mesh, in_specs=placed, out_specs=P(None, None, "fsdp"), check_vma=False
    )
```

time: 1560 us -> 565 us (0.36)
  Pallas kernels: 1120 us -> 139 us
  starting transfers between devices: 296 us -> 185 us
  waiting for transfers between devices: 103 us -> 206 us
    pallas_call x8 -> x12, Pallas kernels: 1030 us -> 41.1 us  [the longest x4 19.2 us: unpack(): pl.pallas_call(functools.partial(unpack_kernel, ranks, inner), grid=(rank...]
    ppermute x32 -> x40, starting transfers between devices: 199 us -> 106 us  [the longest x12 75.2 us: shards(): lax.ppermute(strips[k], 'dp', to_row[k])]
    ppermute x32 -> x40, waiting for transfers between devices: 73.7 us -> 128 us  [the longest x12 69.4 us: shards(): lax.ppermute(strips[k], 'dp', to_row[k])]
    all_gather x4, waiting for transfers between devices: 0.08 us -> 42.9 us  [shards(): lax.all_gather(jnp.concatenate(back, axis=0), 'dp', axis=0, tiled=True)]
    ppermute x32, starting transfers between devices: 96.9 us -> 79.4 us  [shards(): lax.ppermute(summed[slot][at * rows:(at + 1) * rows], MESH_AXES, to_owner...]
  transfers between devices with their start and end apart: 72 -> 80, of which waited for: 19 -> 35; matrix products, arithmetic and copies ran while one was open for 0% -> 1% of each run, Pallas kernels for 56% -> 23%
where the time goes in v2:
time: 565 us; the launch traced here: 564 us
  waiting for transfers between devices  206 us (36%)
  starting transfers between devices  185 us (33%)
  Pallas kernels  139 us (25%)
  local copies, waits for them, and re-layouts  18.8 us (3%)
  between operations  14.4 us (3%)
    ppermute x32, starting transfers between devices, shards(): lax.ppermute(summed[slot][at * rows:(at + 1) * rows], MESH_AXES, to_owner...  79.4 us
    ppermute x12, starting transfers between devices, shards(): lax.ppermute(strips[k], 'dp', to_row[k])  75.2 us
    ppermute x12, waiting for transfers between devices, shards(): lax.ppermute(strips[k], 'dp', to_row[k])  69.4 us
    pallas_call x4, Pallas kernels, precondition(): pl.pallas_call(functools.partial(block_kernel, ranks, inner, col_blocks),...  66.2 us
    ppermute x28, waiting for transfers between devices, shards(): lax.ppermute(piece, 'fsdp', to_column[key])  58.1 us
    all_gather x4, waiting for transfers between devices, shards(): lax.all_gather(jnp.concatenate(back, axis=0), 'dp', axis=0, tiled=True)  42.9 us
    pallas_call x1, Pallas kernels, fourth_powers(): pl.pallas_call(fourth_kernel, grid=(slabs, col_blocks), in_specs=[spec, s...  31.4 us
    ppermute x28, starting transfers between devices, shards(): lax.ppermute(piece, 'fsdp', to_column[key])  30.3 us
  transfers between devices with their start and end apart: 80, of which 35 were waited for; matrix products, arithmetic and copies ran while one was open for 1% of the time, Pallas kernels for 23%

profile of v2, /device:TPU:0, one launch (start us, length us, event | category | flops | bytes accessed | tf_op | source)
XLA Modules:
  0.0 563.5 jit_solution(7983862102327902865)
XLA Ops:
  7.2 4.8 pack_slabs.5
  12.1 4.8 pack_slabs.7
  16.9 4.8 pack_slabs.6
  21.8 4.8 pack_slabs.4
  26.7 31.4 %fourth_powers.1 = (f32[4,2,512,512]{3,2,1,0:T(8,128)}, f32[4,2,512,512]{3,2,1,0:T(8,128)}) custom-call(f32[4,2,512,512]{3,2,1,0:T(8,128)} %refs_10_.7, f32[4,2,512,512]{3,2,1,0:T(8,128)} %refs_11_.7), custom_call_target="tpu_custom_call" | custom-call | flops 25769803776 | bytes 33554432 | tf_op jit(solution)/shard_map/fourth_powers/pallas_call | solution.py:43
  58.1 9.5 %reduce-scatter.7.cloned.1.call-done = bf16[1024,512]{1,0:T(8,128)(2,1)} async-done(((bf16[4096,512]{1,0:T(8,128)(2,1)}), bf16[1024,512]{1,0:T(8,128)(2,1)}) %reduce-scatter.7.cloned.1.call-update) | async-done | bytes 1048592 | tf_op jit(solution)/shard_map/reduce_scatter | solution.py:249
  76.0 12.3 %collective-permute-start.56 = (bf16[128,512]{1,0:T(8,128)(2,1)S(1)}, bf16[128,512]{1,0:T(8,128)(2,1)S(1)}, u32[]{:S(2)}, u32[]{:S(2)}) collective-permute-start(bf16[128,512]{1,0:T(8,128)(2,1)S(1)} %get-tuple-element.116), channel_id=1, source_target_pairs={{0,2},{1,3},{2,10},{3,11},{4,18},{5,19},{6,26},{7,27},{8,0},{9,1},... | collective-permute-start | bytes 393224 | tf_op jit(solution)/shard_map/ppermute | solution.py:256
  93.3 16.7 %precondition.7 = (bf16[256,512]{1,0:T(8,128)(2,1)}, bf16[256,512]{1,0:T(8,128)(2,1)}, bf16[256,512]{1,0:T(8,128)(2,1)}, bf16[256,512]{1,0:T(8,128)(2,1)}) custom-call(s32[3]{0:T(128)} %pad_add_fusion.place_ref, bf16[128,512]{1,0:T(8,128)(2,1)} %copy-done.41, bf16[128,512]{1,0:T(8,128)(2,1)} %copy-done.37, bf16[128,512]{1,0:T(8,128)(2,1)} %copy-done.33, ...), custom_call_target="tpu_custom_call" | custom-call | flops 10200547328 | bytes 14680064 | tf_op jit(solution)/shard_map/precondition/pallas_call | solution.py:206
  110.1 18.8 %collective-permute-start.62 = (bf16[256,512]{1,0:T(8,128)(2,1)}, bf16[256,512]{1,0:T(8,128)(2,1)S(1)}, u32[]{:S(2)}, u32[]{:S(2)}) collective-permute-start(bf16[256,512]{1,0:T(8,128)(2,1)} %get-tuple-element.100), channel_id=1, source_target_pairs={{0,8},{8,0},{16,24},{24,16},{1,9},{9,1},{17,25},{25,17},{2,10},{10... | collective-permute-start | bytes 786440 | tf_op jit(solution)/shard_map/ppermute | solution.py:260
  130.5 8.5 %collective-permute-done.62.refs_1_ = bf16[256,512]{1,0:T(8,128)(2,1)S(1)} collective-permute-done((bf16[256,512]{1,0:T(8,128)(2,1)}, bf16[256,512]{1,0:T(8,128)(2,1)S(1)}, u32[]{:S(2)}, u32[]{:S(2)}) %collective-permute-start.62) | collective-permute-done | bytes 262176 | tf_op jit(solution)/shard_map/ppermute | solution.py:260
  138.9 6.3 %collective-permute-done.64.refs_3_ = bf16[256,512]{1,0:T(8,128)(2,1)S(1)} collective-permute-done((bf16[256,512]{1,0:T(8,128)(2,1)}, bf16[256,512]{1,0:T(8,128)(2,1)S(1)}, u32[]{:S(2)}, u32[]{:S(2)}) %collective-permute-start.64) | collective-permute-done | bytes 262176 | tf_op jit(solution)/shard_map/ppermute | solution.py:260
  160.2 9.0 %collective-permute-done.69 = bf16[128,512]{1,0:T(8,128)(2,1)S(1)} collective-permute-done((bf16[128,512]{1,0:T(8,128)(2,1)S(1)}, bf16[128,512]{1,0:T(8,128)(2,1)S(1)}, u32[]{:S(2)}, u32[]{:S(2)}) %collective-permute-start.69) | collective-permute-done | bytes 131104 | tf_op jit(solution)/shard_map/ppermute | solution.py:263
  171.7 3.8 collective-permute-start.43
  176.0 4.5 collective-permute-start.41
  182.1 8.9 %collective-permute-start.38 = (bf16[128,512]{1,0:T(8,128)(2,1)S(1)}, bf16[128,512]{1,0:T(8,128)(2,1)S(1)}, u32[]{:S(2)}, u32[]{:S(2)}) collective-permute-start(bf16[128,512]{1,0:T(8,128)(2,1)S(1)} %get-tuple-element.124), channel_id=1, source_target_pairs={{0,2},{1,3},{2,10},{3,11},{4,18},{5,19},{6,26},{7,27},{8,0},{9,1},... | collective-permute-start | bytes 393224 | tf_op jit(solution)/shard_map/ppermute | solution.py:256
  191.9 3.9 collective-permute-done.39.refs_3_
  195.8 7.3 %collective-permute-done.38.refs_2_ = bf16[128,512]{1,0:T(8,128)(2,1)S(1)} collective-permute-done((bf16[128,512]{1,0:T(8,128)(2,1)S(1)}, bf16[128,512]{1,0:T(8,128)(2,1)S(1)}, u32[]{:S(2)}, u32[]{:S(2)}) %collective-permute-start.38) | collective-permute-done | bytes 131104 | tf_op jit(solution)/shard_map/ppermute | solution.py:256
  204.4 16.5 %precondition.6 = (bf16[256,512]{1,0:T(8,128)(2,1)}, bf16[256,512]{1,0:T(8,128)(2,1)}, bf16[256,512]{1,0:T(8,128)(2,1)}, bf16[256,512]{1,0:T(8,128)(2,1)}) custom-call(s32[3]{0:T(128)} %pad_add_fusion.place_ref, bf16[128,512]{1,0:T(8,128)(2,1)} %copy-done.42, bf16[128,512]{1,0:T(8,128)(2,1)} %copy-done.38, bf16[128,512]{1,0:T(8,128)(2,1)} %copy-done.34, ...), custom_call_target="tpu_custom_call" | custom-call | flops 10200547328 | bytes 14680064 | tf_op jit(solution)/shard_map/precondition/pallas_call | solution.py:206
  221.0 12.7 %collective-permute-start.44 = (bf16[256,512]{1,0:T(8,128)(2,1)}, bf16[256,512]{1,0:T(8,128)(2,1)S(1)}, u32[]{:S(2)}, u32[]{:S(2)}) collective-permute-start(bf16[256,512]{1,0:T(8,128)(2,1)} %get-tuple-element.87), channel_id=1, source_target_pairs={{0,8},{8,0},{16,24},{24,16},{1,9},{9,1},{17,25},{25,17},{2,10},{10... | collective-permute-start | bytes 786440 | tf_op jit(solution)/shard_map/ppermute | solution.py:260
  235.2 11.4 %collective-permute-done.44.refs_1_ = bf16[256,512]{1,0:T(8,128)(2,1)S(1)} collective-permute-done((bf16[256,512]{1,0:T(8,128)(2,1)}, bf16[256,512]{1,0:T(8,128)(2,1)S(1)}, u32[]{:S(2)}, u32[]{:S(2)}) %collective-permute-start.44) | collective-permute-done | bytes 262176 | tf_op jit(solution)/shard_map/ppermute | solution.py:260
  246.6 4.3 collective-permute-done.45.refs_2_
  250.9 4.7 collective-permute-done.46.refs_3_
  261.8 3.4 collective-permute-start.52
  270.3 9.1 %collective-permute-done.51 = bf16[128,512]{1,0:T(8,128)(2,1)S(1)} collective-permute-done((bf16[128,512]{1,0:T(8,128)(2,1)S(1)}, bf16[128,512]{1,0:T(8,128)(2,1)S(1)}, u32[]{:S(2)}, u32[]{:S(2)}) %collective-permute-start.51) | collective-permute-done | bytes 131104 | tf_op jit(solution)/shard_map/ppermute | solution.py:263
  281.8 4.0 collective-permute-start.25
  286.3 4.7 collective-permute-start.23
  292.6 8.8 %collective-permute-start.20 = (bf16[128,512]{1,0:T(8,128)(2,1)S(1)}, bf16[128,512]{1,0:T(8,128)(2,1)S(1)}, u32[]{:S(2)}, u32[]{:S(2)}) collective-permute-start(bf16[128,512]{1,0:T(8,128)(2,1)S(1)} %get-tuple-element.132), channel_id=1, source_target_pairs={{0,2},{1,3},{2,10},{3,11},{4,18},{5,19},{6,26},{7,27},{8,0},{9,1},... | collective-permute-start | bytes 393224 | tf_op jit(solution)/shard_map/ppermute | solution.py:256
  304.7 3.4 collective-permute-done.20.refs_2_
  309.5 16.4 %precondition.5 = (bf16[256,512]{1,0:T(8,128)(2,1)}, bf16[256,512]{1,0:T(8,128)(2,1)}, bf16[256,512]{1,0:T(8,128)(2,1)}, bf16[256,512]{1,0:T(8,128)(2,1)}) custom-call(s32[3]{0:T(128)} %pad_add_fusion.place_ref, bf16[128,512]{1,0:T(8,128)(2,1)} %copy-done.43, bf16[128,512]{1,0:T(8,128)(2,1)} %copy-done.39, bf16[128,512]{1,0:T(8,128)(2,1)} %copy-done.35, ...), custom_call_target="tpu_custom_call" | custom-call | flops 10200547328 | bytes 14680064 | tf_op jit(solution)/shard_map/precondition/pallas_call | solution.py:206
  325.9 18.1 %collective-permute-start.26 = (bf16[256,512]{1,0:T(8,128)(2,1)}, bf16[256,512]{1,0:T(8,128)(2,1)S(1)}, u32[]{:S(2)}, u32[]{:S(2)}) collective-permute-start(bf16[256,512]{1,0:T(8,128)(2,1)} %get-tuple-element.75), channel_id=1, source_target_pairs={{0,8},{8,0},{16,24},{24,16},{1,9},{9,1},{17,25},{25,17},{2,10},{10... | collective-permute-start | bytes 786440 | tf_op jit(solution)/shard_map/ppermute | solution.py:260
  345.5 5.8 %collective-permute-done.26.refs_1_ = bf16[256,512]{1,0:T(8,128)(2,1)S(1)} collective-permute-done((bf16[256,512]{1,0:T(8,128)(2,1)}, bf16[256,512]{1,0:T(8,128)(2,1)S(1)}, u32[]{:S(2)}, u32[]{:S(2)}) %collective-permute-start.26) | collective-permute-done | bytes 262176 | tf_op jit(solution)/shard_map/ppermute | solution.py:260
  351.3 6.5 %collective-permute-done.27.refs_2_ = bf16[256,512]{1,0:T(8,128)(2,1)S(1)} collective-permute-done((bf16[256,512]{1,0:T(8,128)(2,1)}, bf16[256,512]{1,0:T(8,128)(2,1)S(1)}, u32[]{:S(2)}, u32[]{:S(2)}) %collective-permute-start.27) | collective-permute-done | bytes 262176 | tf_op jit(solution)/shard_map/ppermute | solution.py:260
  370.9 8.9 %collective-permute-done.32 = bf16[128,512]{1,0:T(8,128)(2,1)S(1)} collective-permute-done((bf16[128,512]{1,0:T(8,128)(2,1)S(1)}, bf16[128,512]{1,0:T(8,128)(2,1)S(1)}, u32[]{:S(2)}, u32[]{:S(2)}) %collective-permute-start.32) | collective-permute-done | bytes 131104 | tf_op jit(solution)/shard_map/ppermute | solution.py:263
  388.4 4.9 collective-permute-start.5
  395.2 6.8 %collective-permute-start.2 = (bf16[128,512]{1,0:T(8,128)(2,1)S(1)}, bf16[128,512]{1,0:T(8,128)(2,1)S(1)}, u32[]{:S(2)}, u32[]{:S(2)}) collective-permute-start(bf16[128,512]{1,0:T(8,128)(2,1)S(1)} %get-tuple-element.140), channel_id=1, source_target_pairs={{0,2},{1,3},{2,10},{3,11},{4,18},{5,19},{6,26},{7,27},{8,0},{9,1},... | collective-permute-start | bytes 393224 | tf_op jit(solution)/shard_map/ppermute | solution.py:256
  403.7 4.1 collective-permute-done.4.refs_4_
  410.1 16.6 %precondition.4 = (bf16[256,512]{1,0:T(8,128)(2,1)}, bf16[256,512]{1,0:T(8,128)(2,1)}, bf16[256,512]{1,0:T(8,128)(2,1)}, bf16[256,512]{1,0:T(8,128)(2,1)}) custom-call(s32[3]{0:T(128)} %pad_add_fusion.place_ref, bf16[128,512]{1,0:T(8,128)(2,1)} %copy-done.40, bf16[128,512]{1,0:T(8,128)(2,1)} %copy-done.36, bf16[128,512]{1,0:T(8,128)(2,1)} %copy-done.32, ...), custom_call_target="tpu_custom_call" | custom-call | flops 10200547328 | bytes 14680064 | tf_op jit(solution)/shard_map/precondition/pallas_call | solution.py:206
  426.6 19.5 %collective-permute-start.8 = (bf16[256,512]{1,0:T(8,128)(2,1)}, bf16[256,512]{1,0:T(8,128)(2,1)S(1)}, u32[]{:S(2)}, u32[]{:S(2)}) collective-permute-start(bf16[256,512]{1,0:T(8,128)(2,1)} %get-tuple-element.63), channel_id=1, source_target_pairs={{0,8},{8,0},{16,24},{24,16},{1,9},{9,1},{17,25},{25,17},{2,10},{10... | collective-permute-start | bytes 786440 | tf_op jit(solution)/shard_map/ppermute | solution.py:260
  447.6 11.4 %collective-permute-done.8.refs_1_ = bf16[256,512]{1,0:T(8,128)(2,1)S(1)} collective-permute-done((bf16[256,512]{1,0:T(8,128)(2,1)}, bf16[256,512]{1,0:T(8,128)(2,1)S(1)}, u32[]{:S(2)}, u32[]{:S(2)}) %collective-permute-start.8) | collective-permute-done | bytes 262176 | tf_op jit(solution)/shard_map/ppermute | solution.py:260
  459.0 4.5 collective-permute-done.9.refs_2_
  463.5 6.1 %collective-permute-done.10.refs_3_ = bf16[256,512]{1,0:T(8,128)(2,1)S(1)} collective-permute-done((bf16[256,512]{1,0:T(8,128)(2,1)}, bf16[256,512]{1,0:T(8,128)(2,1)S(1)}, u32[]{:S(2)}, u32[]{:S(2)}) %collective-permute-start.10) | collective-permute-done | bytes 262176 | tf_op jit(solution)/shard_map/ppermute | solution.py:260
  475.8 3.5 collective-permute-start.16
  484.4 9.1 %collective-permute-done.15 = bf16[128,512]{1,0:T(8,128)(2,1)S(1)} collective-permute-done((bf16[128,512]{1,0:T(8,128)(2,1)S(1)}, bf16[128,512]{1,0:T(8,128)(2,1)S(1)}, u32[]{:S(2)}, u32[]{:S(2)}) %collective-permute-start.15) | collective-permute-done | bytes 131104 | tf_op jit(solution)/shard_map/ppermute | solution.py:263
  494.6 4.8 unpack_slabs.4.rest_0_
  499.4 4.8 unpack_slabs.5.rest_0_
  504.1 4.9 unpack_slabs.6.rest_0_
  509.0 42.9 %all-gather.5.cloned.1.call-done.got_ref = bf16[4096,512]{1,0:T(8,128)(2,1)} async-done(((bf16[1024,512]{1,0:T(8,128)(2,1)}), bf16[4096,512]{1,0:T(8,128)(2,1)}) %all-gather.5.cloned.1.call-update) | async-done | bytes 4194320 | tf_op jit(solution)/shard_map/all_gather | solution.py:265
  551.9 4.8 unpack_slabs.7
  (262 shorter events, 101.9 us)
Async XLA Ops:
  6.5 61.0 %reduce-scatter.7.cloned.1.call-start = ((), (), s32[]{:S(2)}) async-start(), calls=%async_computation.5 | async-start | bytes 5242880 | tf_op jit(solution)/shard_map/reduce_scatter | solution.py:249
  12.0 158.4 %reduce-scatter.11.cloned.1.call-start = ((), (), s32[]{:S(2)}) async-start(), calls=%async_computation.9 | async-start | bytes 5242880 | tf_op jit(solution)/shard_map/reduce_scatter | solution.py:249
  16.9 263.6 %reduce-scatter.9.cloned.1.call-start = ((), (), s32[]{:S(2)}) async-start(), calls=%async_computation.7 | async-start | bytes 5242880 | tf_op jit(solution)/shard_map/reduce_scatter | solution.py:249
  21.8 361.0 %reduce-scatter.5.cloned.1.call-start = ((), (), s32[]{:S(2)}) async-start(), calls=%async_computation.4 | async-start | bytes 5242880 | tf_op jit(solution)/shard_map/reduce_scatter | solution.py:249
  26.6 468.0 %all-gather.11.cloned.1.call-start = ((), (), s32[]{:S(2)}) async-start(), calls=%async_computation.11 | async-start | bytes 5242880 | tf_op jit(solution)/shard_map/all_gather | solution.py:265
  71.7 16.6 %collective-permute-start.60 = (bf16[128,512]{1,0:T(8,128)(2,1)S(1)}, bf16[128,512]{1,0:T(8,128)(2,1)S(1)}, u32[]{:S(2)}, u32[]{:S(2)}) collective-permute-start(bf16[128,512]{1,0:T(8,128)(2,1)S(1)} %get-tuple-element.112), channel_id=1, source_target_pairs={{0,6},{1,7},{2,14},{3,15},{4,22},{5,23},{6,30},{7,31},{8,4},{9,5},... | collective-permute-start | bytes 393224 | tf_op jit(solution)/shard_map/ppermute | solution.py:256
  73.2 15.1 %collective-permute-start.59 = (bf16[128,512]{1,0:T(8,128)(2,1)S(1)}, bf16[128,512]{1,0:T(8,128)(2,1)S(1)}, u32[]{:S(2)}, u32[]{:S(2)}) collective-permute-start(bf16[128,512]{1,0:T(8,128)(2,1)S(1)} %get-tuple-element.113), channel_id=1, source_target_pairs={{0,5},{1,4},{2,13},{3,12},{4,21},{5,20},{6,29},{7,28},{8,7},{9,6},... | collective-permute-start | bytes 393224 | tf_op jit(solution)/shard_map/ppermute | solution.py:256
  73.7 15.6 %collective-permute-start.58 = (bf16[128,512]{1,0:T(8,128)(2,1)S(1)}, bf16[128,512]{1,0:T(8,128)(2,1)S(1)}, u32[]{:S(2)}, u32[]{:S(2)}) collective-permute-start(bf16[128,512]{1,0:T(8,128)(2,1)S(1)} %get-tuple-element.114), channel_id=1, source_target_pairs={{0,4},{1,5},{2,12},{3,13},{4,20},{5,21},{6,28},{7,29},{8,6},{9,7},... | collective-permute-start | bytes 393224 | tf_op jit(solution)/shard_map/ppermute | solution.py:256
  74.2 15.1 %collective-permute-start.57 = (bf16[128,512]{1,0:T(8,128)(2,1)S(1)}, bf16[128,512]{1,0:T(8,128)(2,1)S(1)}, u32[]{:S(2)}, u32[]{:S(2)}) collective-permute-start(bf16[128,512]{1,0:T(8,128)(2,1)S(1)} %get-tuple-element.115), channel_id=1, source_target_pairs={{0,3},{1,2},{2,11},{3,10},{4,19},{5,18},{6,27},{7,26},{8,1},{9,0},... | collective-permute-start | bytes 393224 | tf_op jit(solution)/shard_map/ppermute | solution.py:256
  76.0 16.0 %collective-permute-start.56 = (bf16[128,512]{1,0:T(8,128)(2,1)S(1)}, bf16[128,512]{1,0:T(8,128)(2,1)S(1)}, u32[]{:S(2)}, u32[]{:S(2)}) collective-permute-start(bf16[128,512]{1,0:T(8,128)(2,1)S(1)} %get-tuple-element.116), channel_id=1, source_target_pairs={{0,2},{1,3},{2,10},{3,11},{4,18},{5,19},{6,26},{7,27},{8,0},{9,1},... | collective-permute-start | bytes 393224 | tf_op jit(solution)/shard_map/ppermute | solution.py:256
  110.1 28.8 %collective-permute-start.62 = (bf16[256,512]{1,0:T(8,128)(2,1)}, bf16[256,512]{1,0:T(8,128)(2,1)S(1)}, u32[]{:S(2)}, u32[]{:S(2)}) collective-permute-start(bf16[256,512]{1,0:T(8,128)(2,1)} %get-tuple-element.100), channel_id=1, source_target_pairs={{0,8},{8,0},{16,24},{24,16},{1,9},{9,1},{17,25},{25,17},{2,10},{10... | collective-permute-start | bytes 786440 | tf_op jit(solution)/shard_map/ppermute | solution.py:260
  128.9 16.3 %collective-permute-start.64 = (bf16[256,512]{1,0:T(8,128)(2,1)}, bf16[256,512]{1,0:T(8,128)(2,1)S(1)}, u32[]{:S(2)}, u32[]{:S(2)}) collective-permute-start(bf16[256,512]{1,0:T(8,128)(2,1)} %get-tuple-element.102), channel_id=1, source_target_pairs={{0,24},{8,16},{16,8},{24,0},{1,25},{9,17},{17,9},{25,1},{2,26},{10... | collective-permute-start | bytes 786440 | tf_op jit(solution)/shard_map/ppermute | solution.py:260
  151.2 18.0 %collective-permute-start.69 = (bf16[128,512]{1,0:T(8,128)(2,1)S(1)}, bf16[128,512]{1,0:T(8,128)(2,1)S(1)}, u32[]{:S(2)}, u32[]{:S(2)}) collective-permute-start(bf16[128,512]{1,0:T(8,128)(2,1)S(1)} %get-tuple-element.108), channel_id=1, source_target_pairs={{0,5},{1,4},{2,7},{3,6},{4,1},{5,0},{6,3},{7,2},{8,13},{9,12},{10,... | collective-permute-start | bytes 393224 | tf_op jit(solution)/shard_map/ppermute | solution.py:263
  151.4 17.8 %collective-permute-start.70 = (bf16[128,512]{1,0:T(8,128)(2,1)S(1)}, bf16[128,512]{1,0:T(8,128)(2,1)S(1)}, u32[]{:S(2)}, u32[]{:S(2)}) collective-permute-start(bf16[128,512]{1,0:T(8,128)(2,1)S(1)} %get-tuple-element.109), channel_id=1, source_target_pairs={{0,6},{1,7},{2,4},{3,5},{4,2},{5,3},{6,0},{7,1},{8,14},{9,15},{10,... | collective-permute-start | bytes 393224 | tf_op jit(solution)/shard_map/ppermute | solution.py:263
  170.3 329.1 %all-gather.9.cloned.1.call-start = ((), (), s32[]{:S(2)}) async-start(), calls=%async_computation.10 | async-start | bytes 5242880 | tf_op jit(solution)/shard_map/all_gather | solution.py:265
  175.5 15.5 %collective-permute-start.42 = (bf16[128,512]{1,0:T(8,128)(2,1)S(1)}, bf16[128,512]{1,0:T(8,128)(2,1)S(1)}, u32[]{:S(2)}, u32[]{:S(2)}) collective-permute-start(bf16[128,512]{1,0:T(8,128)(2,1)S(1)} %get-tuple-element.120), channel_id=1, source_target_pairs={{0,6},{1,7},{2,14},{3,15},{4,22},{5,23},{6,30},{7,31},{8,4},{9,5},... | collective-permute-start | bytes 393224 | tf_op jit(solution)/shard_map/ppermute | solution.py:256
  176.0 15.0 %collective-permute-start.41 = (bf16[128,512]{1,0:T(8,128)(2,1)S(1)}, bf16[128,512]{1,0:T(8,128)(2,1)S(1)}, u32[]{:S(2)}, u32[]{:S(2)}) collective-permute-start(bf16[128,512]{1,0:T(8,128)(2,1)S(1)} %get-tuple-element.121), channel_id=1, source_target_pairs={{0,5},{1,4},{2,13},{3,12},{4,21},{5,20},{6,29},{7,28},{8,7},{9,6},... | collective-permute-start | bytes 393224 | tf_op jit(solution)/shard_map/ppermute | solution.py:256
  181.1 14.7 %collective-permute-start.39 = (bf16[128,512]{1,0:T(8,128)(2,1)S(1)}, bf16[128,512]{1,0:T(8,128)(2,1)S(1)}, u32[]{:S(2)}, u32[]{:S(2)}) collective-permute-start(bf16[128,512]{1,0:T(8,128)(2,1)S(1)} %get-tuple-element.123), channel_id=1, source_target_pairs={{0,3},{1,2},{2,11},{3,10},{4,19},{5,18},{6,27},{7,26},{8,1},{9,0},... | collective-permute-start | bytes 393224 | tf_op jit(solution)/shard_map/ppermute | solution.py:256
  182.1 21.0 %collective-permute-start.38 = (bf16[128,512]{1,0:T(8,128)(2,1)S(1)}, bf16[128,512]{1,0:T(8,128)(2,1)S(1)}, u32[]{:S(2)}, u32[]{:S(2)}) collective-permute-start(bf16[128,512]{1,0:T(8,128)(2,1)S(1)} %get-tuple-element.124), channel_id=1, source_target_pairs={{0,2},{1,3},{2,10},{3,11},{4,18},{5,19},{6,26},{7,27},{8,0},{9,1},... | collective-permute-start | bytes 393224 | tf_op jit(solution)/shard_map/ppermute | solution.py:256
  221.0 25.6 %collective-permute-start.44 = (bf16[256,512]{1,0:T(8,128)(2,1)}, bf16[256,512]{1,0:T(8,128)(2,1)S(1)}, u32[]{:S(2)}, u32[]{:S(2)}) collective-permute-start(bf16[256,512]{1,0:T(8,128)(2,1)} %get-tuple-element.87), channel_id=1, source_target_pairs={{0,8},{8,0},{16,24},{24,16},{1,9},{9,1},{17,25},{25,17},{2,10},{10... | collective-permute-start | bytes 786440 | tf_op jit(solution)/shard_map/ppermute | solution.py:260
  233.6 17.3 %collective-permute-start.45 = (bf16[256,512]{1,0:T(8,128)(2,1)}, bf16[256,512]{1,0:T(8,128)(2,1)S(1)}, u32[]{:S(2)}, u32[]{:S(2)}) collective-permute-start(bf16[256,512]{1,0:T(8,128)(2,1)} %get-tuple-element.88), channel_id=1, source_target_pairs={{0,16},{8,24},{16,0},{24,8},{1,17},{9,25},{17,1},{25,9},{2,18},{10... | collective-permute-start | bytes 786440 | tf_op jit(solution)/shard_map/ppermute | solution.py:260
  233.6 21.9 %collective-permute-start.46 = (bf16[256,512]{1,0:T(8,128)(2,1)}, bf16[256,512]{1,0:T(8,128)(2,1)S(1)}, u32[]{:S(2)}, u32[]{:S(2)}) collective-permute-start(bf16[256,512]{1,0:T(8,128)(2,1)} %get-tuple-element.89), channel_id=1, source_target_pairs={{0,24},{8,16},{16,8},{24,0},{1,25},{9,17},{17,9},{25,1},{2,26},{10... | collective-permute-start | bytes 786440 | tf_op jit(solution)/shard_map/ppermute | solution.py:260
  261.3 18.0 %collective-permute-start.51 = (bf16[128,512]{1,0:T(8,128)(2,1)S(1)}, bf16[128,512]{1,0:T(8,128)(2,1)S(1)}, u32[]{:S(2)}, u32[]{:S(2)}) collective-permute-start(bf16[128,512]{1,0:T(8,128)(2,1)S(1)} %get-tuple-element.95), channel_id=1, source_target_pairs={{0,5},{1,4},{2,7},{3,6},{4,1},{5,0},{6,3},{7,2},{8,13},{9,12},{10,... | collective-permute-start | bytes 393224 | tf_op jit(solution)/shard_map/ppermute | solution.py:263
  261.8 17.6 %collective-permute-start.52 = (bf16[128,512]{1,0:T(8,128)(2,1)S(1)}, bf16[128,512]{1,0:T(8,128)(2,1)S(1)}, u32[]{:S(2)}, u32[]{:S(2)}) collective-permute-start(bf16[128,512]{1,0:T(8,128)(2,1)S(1)} %get-tuple-element.96), channel_id=1, source_target_pairs={{0,6},{1,7},{2,4},{3,5},{4,2},{5,3},{6,0},{7,1},{8,14},{9,15},{10,... | collective-permute-start | bytes 393224 | tf_op jit(solution)/shard_map/ppermute | solution.py:263
  280.4 223.7 %all-gather.7.cloned.1.call-start = ((), (), s32[]{:S(2)}) async-start(), calls=%async_computation.8 | async-start | bytes 5242880 | tf_op jit(solution)/shard_map/all_gather | solution.py:265
  285.8 15.5 %collective-permute-start.24 = (bf16[128,512]{1,0:T(8,128)(2,1)S(1)}, bf16[128,512]{1,0:T(8,128)(2,1)S(1)}, u32[]{:S(2)}, u32[]{:S(2)}) collective-permute-start(bf16[128,512]{1,0:T(8,128)(2,1)S(1)} %get-tuple-element.128), channel_id=1, source_target_pairs={{0,6},{1,7},{2,14},{3,15},{4,22},{5,23},{6,30},{7,31},{8,4},{9,5},... | collective-permute-start | bytes 393224 | tf_op jit(solution)/shard_map/ppermute | solution.py:256
  286.3 15.0 %collective-permute-start.23 = (bf16[128,512]{1,0:T(8,128)(2,1)S(1)}, bf16[128,512]{1,0:T(8,128)(2,1)S(1)}, u32[]{:S(2)}, u32[]{:S(2)}) collective-permute-start(bf16[128,512]{1,0:T(8,128)(2,1)S(1)} %get-tuple-element.129), channel_id=1, source_target_pairs={{0,5},{1,4},{2,13},{3,12},{4,21},{5,20},{6,29},{7,28},{8,7},{9,6},... | collective-permute-start | bytes 393224 | tf_op jit(solution)/shard_map/ppermute | solution.py:256
  291.0 13.0 %collective-permute-start.22 = (bf16[128,512]{1,0:T(8,128)(2,1)S(1)}, bf16[128,512]{1,0:T(8,128)(2,1)S(1)}, u32[]{:S(2)}, u32[]{:S(2)}) collective-permute-start(bf16[128,512]{1,0:T(8,128)(2,1)S(1)} %get-tuple-element.130), channel_id=1, source_target_pairs={{0,4},{1,5},{2,12},{3,13},{4,20},{5,21},{6,28},{7,29},{8,6},{9,7},... | collective-permute-start | bytes 393224 | tf_op jit(solution)/shard_map/ppermute | solution.py:256
  291.7 13.0 %collective-permute-start.21 = (bf16[128,512]{1,0:T(8,128)(2,1)S(1)}, bf16[128,512]{1,0:T(8,128)(2,1)S(1)}, u32[]{:S(2)}, u32[]{:S(2)}) collective-permute-start(bf16[128,512]{1,0:T(8,128)(2,1)S(1)} %get-tuple-element.131), channel_id=1, source_target_pairs={{0,3},{1,2},{2,11},{3,10},{4,19},{5,18},{6,27},{7,26},{8,1},{9,0},... | collective-permute-start | bytes 393224 | tf_op jit(solution)/shard_map/ppermute | solution.py:256
  292.6 15.5 %collective-permute-start.20 = (bf16[128,512]{1,0:T(8,128)(2,1)S(1)}, bf16[128,512]{1,0:T(8,128)(2,1)S(1)}, u32[]{:S(2)}, u32[]{:S(2)}) collective-permute-start(bf16[128,512]{1,0:T(8,128)(2,1)S(1)} %get-tuple-element.132), channel_id=1, source_target_pairs={{0,2},{1,3},{2,10},{3,11},{4,18},{5,19},{6,26},{7,27},{8,0},{9,1},... | collective-permute-start | bytes 393224 | tf_op jit(solution)/shard_map/ppermute | solution.py:256
  325.9 25.4 %collective-permute-start.26 = (bf16[256,512]{1,0:T(8,128)(2,1)}, bf16[256,512]{1,0:T(8,128)(2,1)S(1)}, u32[]{:S(2)}, u32[]{:S(2)}) collective-permute-start(bf16[256,512]{1,0:T(8,128)(2,1)} %get-tuple-element.75), channel_id=1, source_target_pairs={{0,8},{8,0},{16,24},{24,16},{1,9},{9,1},{17,25},{25,17},{2,10},{10... | collective-permute-start | bytes 786440 | tf_op jit(solution)/shard_map/ppermute | solution.py:260
  344.0 13.8 %collective-permute-start.27 = (bf16[256,512]{1,0:T(8,128)(2,1)}, bf16[256,512]{1,0:T(8,128)(2,1)S(1)}, u32[]{:S(2)}, u32[]{:S(2)}) collective-permute-start(bf16[256,512]{1,0:T(8,128)(2,1)} %get-tuple-element.76), channel_id=1, source_target_pairs={{0,16},{8,24},{16,0},{24,8},{1,17},{9,25},{17,1},{25,9},{2,18},{10... | collective-permute-start | bytes 786440 | tf_op jit(solution)/shard_map/ppermute | solution.py:260
  344.0 13.8 %collective-permute-start.28 = (bf16[256,512]{1,0:T(8,128)(2,1)}, bf16[256,512]{1,0:T(8,128)(2,1)S(1)}, u32[]{:S(2)}, u32[]{:S(2)}) collective-permute-start(bf16[256,512]{1,0:T(8,128)(2,1)} %get-tuple-element.77), channel_id=1, source_target_pairs={{0,24},{8,16},{16,8},{24,0},{1,25},{9,17},{17,9},{25,1},{2,26},{10... | collective-permute-start | bytes 786440 | tf_op jit(solution)/shard_map/ppermute | solution.py:260
  361.4 18.5 %collective-permute-start.32 = (bf16[128,512]{1,0:T(8,128)(2,1)S(1)}, bf16[128,512]{1,0:T(8,128)(2,1)S(1)}, u32[]{:S(2)}, u32[]{:S(2)}) collective-permute-start(bf16[128,512]{1,0:T(8,128)(2,1)S(1)} %get-tuple-element.82), channel_id=1, source_target_pairs={{0,4},{1,5},{2,6},{3,7},{4,0},{5,1},{6,2},{7,3},{8,12},{9,13},{10,... | collective-permute-start | bytes 393224 | tf_op jit(solution)/shard_map/ppermute | solution.py:263
  362.1 19.5 %collective-permute-start.33 = (bf16[128,512]{1,0:T(8,128)(2,1)S(1)}, bf16[128,512]{1,0:T(8,128)(2,1)S(1)}, u32[]{:S(2)}, u32[]{:S(2)}) collective-permute-start(bf16[128,512]{1,0:T(8,128)(2,1)S(1)} %get-tuple-element.83), channel_id=1, source_target_pairs={{0,5},{1,4},{2,7},{3,6},{4,1},{5,0},{6,3},{7,2},{8,13},{9,12},{10,... | collective-permute-start | bytes 393224 | tf_op jit(solution)/shard_map/ppermute | solution.py:263
  364.0 17.6 %collective-permute-start.34 = (bf16[128,512]{1,0:T(8,128)(2,1)S(1)}, bf16[128,512]{1,0:T(8,128)(2,1)S(1)}, u32[]{:S(2)}, u32[]{:S(2)}) collective-permute-start(bf16[128,512]{1,0:T(8,128)(2,1)S(1)} %get-tuple-element.84), channel_id=1, source_target_pairs={{0,6},{1,7},{2,4},{3,5},{4,2},{5,3},{6,0},{7,1},{8,14},{9,15},{10,... | collective-permute-start | bytes 393224 | tf_op jit(solution)/shard_map/ppermute | solution.py:263
  382.7 169.2 %all-gather.5.cloned.1.call-start = ((), (), s32[]{:S(2)}) async-start(), calls=%async_computation.6 | async-start | bytes 5242880 | tf_op jit(solution)/shard_map/all_gather | solution.py:265
  386.6 16.1 %collective-permute-start.6 = (bf16[128,512]{1,0:T(8,128)(2,1)S(1)}, bf16[128,512]{1,0:T(8,128)(2,1)S(1)}, u32[]{:S(2)}, u32[]{:S(2)}) collective-permute-start(bf16[128,512]{1,0:T(8,128)(2,1)S(1)} %get-tuple-element.136), channel_id=1, source_target_pairs={{0,6},{1,7},{2,14},{3,15},{4,22},{5,23},{6,30},{7,31},{8,4},{9,5},... | collective-permute-start | bytes 393224 | tf_op jit(solution)/shard_map/ppermute | solution.py:256
  388.4 14.3 %collective-permute-start.5 = (bf16[128,512]{1,0:T(8,128)(2,1)S(1)}, bf16[128,512]{1,0:T(8,128)(2,1)S(1)}, u32[]{:S(2)}, u32[]{:S(2)}) collective-permute-start(bf16[128,512]{1,0:T(8,128)(2,1)S(1)} %get-tuple-element.137), channel_id=1, source_target_pairs={{0,5},{1,4},{2,13},{3,12},{4,21},{5,20},{6,29},{7,28},{8,7},{9,6},... | collective-permute-start | bytes 393224 | tf_op jit(solution)/shard_map/ppermute | solution.py:256
  393.3 14.5 %collective-permute-start.4 = (bf16[128,512]{1,0:T(8,128)(2,1)S(1)}, bf16[128,512]{1,0:T(8,128)(2,1)S(1)}, u32[]{:S(2)}, u32[]{:S(2)}) collective-permute-start(bf16[128,512]{1,0:T(8,128)(2,1)S(1)} %get-tuple-element.138), channel_id=1, source_target_pairs={{0,4},{1,5},{2,12},{3,13},{4,20},{5,21},{6,28},{7,29},{8,6},{9,7},... | collective-permute-start | bytes 393224 | tf_op jit(solution)/shard_map/ppermute | solution.py:256
  394.3 13.5 %collective-permute-start.3 = (bf16[128,512]{1,0:T(8,128)(2,1)S(1)}, bf16[128,512]{1,0:T(8,128)(2,1)S(1)}, u32[]{:S(2)}, u32[]{:S(2)}) collective-permute-start(bf16[128,512]{1,0:T(8,128)(2,1)S(1)} %get-tuple-element.139), channel_id=1, source_target_pairs={{0,3},{1,2},{2,11},{3,10},{4,19},{5,18},{6,27},{7,26},{8,1},{9,0},... | collective-permute-start | bytes 393224 | tf_op jit(solution)/shard_map/ppermute | solution.py:256
  395.2 13.6 %collective-permute-start.2 = (bf16[128,512]{1,0:T(8,128)(2,1)S(1)}, bf16[128,512]{1,0:T(8,128)(2,1)S(1)}, u32[]{:S(2)}, u32[]{:S(2)}) collective-permute-start(bf16[128,512]{1,0:T(8,128)(2,1)S(1)} %get-tuple-element.140), channel_id=1, source_target_pairs={{0,2},{1,3},{2,10},{3,11},{4,18},{5,19},{6,26},{7,27},{8,0},{9,1},... | collective-permute-start | bytes 393224 | tf_op jit(solution)/shard_map/ppermute | solution.py:256
  426.6 32.4 %collective-permute-start.8 = (bf16[256,512]{1,0:T(8,128)(2,1)}, bf16[256,512]{1,0:T(8,128)(2,1)S(1)}, u32[]{:S(2)}, u32[]{:S(2)}) collective-permute-start(bf16[256,512]{1,0:T(8,128)(2,1)} %get-tuple-element.63), channel_id=1, source_target_pairs={{0,8},{8,0},{16,24},{24,16},{1,9},{9,1},{17,25},{25,17},{2,10},{10... | collective-permute-start | bytes 786440 | tf_op jit(solution)/shard_map/ppermute | solution.py:260
  446.1 17.4 %collective-permute-start.9 = (bf16[256,512]{1,0:T(8,128)(2,1)}, bf16[256,512]{1,0:T(8,128)(2,1)S(1)}, u32[]{:S(2)}, u32[]{:S(2)}) collective-permute-start(bf16[256,512]{1,0:T(8,128)(2,1)} %get-tuple-element.64), channel_id=1, source_target_pairs={{0,16},{8,24},{16,0},{24,8},{1,17},{9,25},{17,1},{25,9},{2,18},{10... | collective-permute-start | bytes 786440 | tf_op jit(solution)/shard_map/ppermute | solution.py:260
  446.1 23.5 %collective-permute-start.10 = (bf16[256,512]{1,0:T(8,128)(2,1)}, bf16[256,512]{1,0:T(8,128)(2,1)S(1)}, u32[]{:S(2)}, u32[]{:S(2)}) collective-permute-start(bf16[256,512]{1,0:T(8,128)(2,1)} %get-tuple-element.65), channel_id=1, source_target_pairs={{0,24},{8,16},{16,8},{24,0},{1,25},{9,17},{17,9},{25,1},{2,26},{10... | collective-permute-start | bytes 786440 | tf_op jit(solution)/shard_map/ppermute | solution.py:260
  471.4 13.0 %collective-permute-start.13 = (bf16[128,512]{1,0:T(8,128)(2,1)S(1)}, bf16[128,512]{1,0:T(8,128)(2,1)S(1)}, u32[]{:S(2)}, u32[]{:S(2)}) collective-permute-start(bf16[128,512]{1,0:T(8,128)(2,1)S(1)} %get-tuple-element.69), channel_id=1, source_target_pairs={{0,3},{1,2},{2,1},{3,0},{4,7},{5,6},{6,5},{7,4},{8,11},{9,10},{10,... | collective-permute-start | bytes 393224 | tf_op jit(solution)/shard_map/ppermute | solution.py:263
  475.5 18.0 %collective-permute-start.15 = (bf16[128,512]{1,0:T(8,128)(2,1)S(1)}, bf16[128,512]{1,0:T(8,128)(2,1)S(1)}, u32[]{:S(2)}, u32[]{:S(2)}) collective-permute-start(bf16[128,512]{1,0:T(8,128)(2,1)S(1)} %get-tuple-element.71), channel_id=1, source_target_pairs={{0,5},{1,4},{2,7},{3,6},{4,1},{5,0},{6,3},{7,2},{8,13},{9,12},{10,... | collective-permute-start | bytes 393224 | tf_op jit(solution)/shard_map/ppermute | solution.py:263
  475.8 17.7 %collective-permute-start.16 = (bf16[128,512]{1,0:T(8,128)(2,1)S(1)}, bf16[128,512]{1,0:T(8,128)(2,1)S(1)}, u32[]{:S(2)}, u32[]{:S(2)}) collective-permute-start(bf16[128,512]{1,0:T(8,128)(2,1)S(1)} %get-tuple-element.72), channel_id=1, source_target_pairs={{0,6},{1,7},{2,4},{3,5},{4,2},{5,3},{6,0},{7,1},{8,14},{9,15},{10,... | collective-permute-start | bytes 393224 | tf_op jit(solution)/shard_map/ppermute | solution.py:263
  (76 other events, 710.8 us)
Sparse Core Ops, SparseCore 0:
  12.1 55.3 reduce-scatter.6
  70.8 66.7 reduce-scatter.10
  140.6 69.1 reduce-scatter.8
  212.9 63.3 reduce-scatter.4
  277.9 66.2 all-gather.10
  345.9 65.8 all-gather.8
  413.7 64.7 all-gather.6
  494.7 57.1 all-gather.4

commit v3 on v2

--- a/solution.py
+++ b/solution.py
@@ -25,7 +25,9 @@
 def dot3(a, b):
     a_high, a_low = split(a)
     b_high, b_low = split(b)
-    return mm(a_high, b_high) + (mm(a_high, b_low) + mm(a_low, b_high))
+    return mm(
+        jnp.concatenate([a_high, a_high, a_low], axis=1), jnp.concatenate([b_high, b_low, b_high], axis=0)
+    )
 
 
 def fourth_kernel(left_ref, right_ref, left_out, right_out):
@@ -59,57 +61,58 @@
 
 
 def pack_kernel(ranks, inner, place_ref, grads_ref, out_ref):
-    rows = grads_ref.shape[2]
     d = pl.program_id(0)
     for k in range(ranks):
         for e in range(inner):
-            at = (k * inner + e) * rows
-            out_ref[at : at + rows] = grads_ref[slab_of(k, e, d, place_ref[1], inner), 0]
-
-
-def pack(ranks, inner, slot, per, place, grads):
+            out_ref[0, k * inner + e, 0] = grads_ref[slab_of(k, e, d, place_ref[1], inner), 0]
+
+
+def pack(ranks, inner, slots, per, place, grads):
+    first, count = slots
     slabs, order, width = grads.shape
     owners, rows = slabs // per, order // ranks
-    return pl.pallas_call(
+    packed = pl.pallas_call(
         functools.partial(pack_kernel, ranks, inner),
-        grid=(ranks,),
+        grid=(ranks, count),
         in_specs=[
             pl.BlockSpec(memory_space=pltpu.SMEM),
-            pl.BlockSpec((owners, 1, rows, width), lambda d: (0, slot, d, 0)),
+            pl.BlockSpec((owners, 1, rows, width), lambda d, s: (0, first + s, d, 0)),
         ],
-        out_specs=pl.BlockSpec((owners * rows, width), lambda d: (d, 0)),
-        out_shape=jax.ShapeDtypeStruct((owners * order, width), grads.dtype),
+        out_specs=pl.BlockSpec((1, owners, 1, rows, width), lambda d, s: (d, 0, s, 0, 0)),
+        out_shape=jax.ShapeDtypeStruct((ranks, owners, count, rows, width), grads.dtype),
         compiler_params=pltpu.CompilerParams(vmem_limit_bytes=VMEM_LIMIT),
         cost_estimate=pl.CostEstimate(
-            flops=0, bytes_accessed=4 * owners * order * width, transcendentals=0
+            flops=0, bytes_accessed=4 * owners * count * order * width, transcendentals=0
         ),
         name="pack_slabs",
     )(place, grads.reshape(owners, per, order, width))
+    return packed.reshape(-1, width)
 
 
 def unpack_kernel(ranks, inner, place_ref, got_ref, *rest):
     out_ref = rest[-1]
-    rows = out_ref.shape[2]
     for k in range(ranks):
         for e in range(inner):
-            at = (k * inner + e) * rows
-            out_ref[slab_of(k, e, place_ref[0], place_ref[1], inner), 0] = got_ref[at : at + rows]
-
-
-def unpack(ranks, inner, slot, per, place, got, so_far):
-    order = got.shape[0] // (ranks * inner)
-    width, owners, rows = got.shape[1], ranks * inner, order // ranks
-    operands = [place, got] + ([] if so_far is None else [so_far])
+            slab = slab_of(k, e, place_ref[0], place_ref[1], inner)
+            out_ref[slab, 0] = got_ref[0, k * inner + e, 0]
+
+
+def unpack(ranks, inner, slots, per, place, got, so_far):
+    first, count = slots
+    width, owners = got.shape[1], ranks * inner
+    rows = got.shape[0] // (ranks * owners * count)
+    operands = [place, got.reshape(ranks, owners, count, rows, width)]
+    operands += [] if so_far is None else [so_far]
     return pl.pallas_call(
         functools.partial(unpack_kernel, ranks, inner),
-        grid=(ranks,),
+        grid=(ranks, count),
         in_specs=[
             pl.BlockSpec(memory_space=pltpu.SMEM),
-            pl.BlockSpec((owners * rows, width), lambda d: (d, 0)),
+            pl.BlockSpec((1, owners, 1, rows, width), lambda d, s: (d, 0, s, 0, 0)),
         ]
         + [pl.BlockSpec(memory_space=pl.ANY)] * (len(operands) - 2),
-        out_specs=pl.BlockSpec((owners, 1, rows, width), lambda d: (0, slot, d, 0)),
-        out_shape=jax.ShapeDtypeStruct((owners, per, order, width), got.dtype),
+        out_specs=pl.BlockSpec((owners, 1, rows, width), lambda d, s: (0, first + s, d, 0)),
+        out_shape=jax.ShapeDtypeStruct((owners, per, ranks * rows, width), got.dtype),
         input_output_aliases={} if so_far is None else {2: 0},
         compiler_params=pltpu.CompilerParams(vmem_limit_bytes=VMEM_LIMIT),
         cost_estimate=pl.CostEstimate(flops=0, bytes_accessed=4 * got.size, transcendentals=0),
@@ -117,23 +120,24 @@
     )(*operands)
 
 
-def route_kernel(ranks, inner, place_ref, *refs):
+def route_kernel(ranks, inner, count, place_ref, *refs):
     taken, outs, held = refs[:ranks], refs[ranks:-1], refs[-1]
-    rows = outs[0].shape[0]
+    rows = outs[0].shape[0] // count
     turn, inner_place = place_ref[2] ^ place_ref[0], place_ref[1]
     for k in range(ranks):
         held[k] = taken[k][...]
     for m in range(ranks):
         for e in range(inner):
-            start = pl.multiple_of((inner_place ^ e) * rows, rows)
-            outs[m * inner + e][...] = held[turn ^ m, pl.ds(start, rows), :]
-
-
-def route(ranks, inner, place, taken):
+            for s in range(count):
+                start = pl.multiple_of((s * inner + (inner_place ^ e)) * rows, rows)
+                outs[m * inner + e][s * rows : (s + 1) * rows] = held[turn ^ m, pl.ds(start, rows), :]
+
+
+def route(ranks, inner, count, place, taken):
     rows, width = taken[0].shape[0] // inner, taken[0].shape[1]
     vmem = pl.BlockSpec(memory_space=pltpu.VMEM)
     return pl.pallas_call(
-        functools.partial(route_kernel, ranks, inner),
+        functools.partial(route_kernel, ranks, inner, count),
         in_specs=[pl.BlockSpec(memory_space=pltpu.SMEM)] + [vmem] * ranks,
         out_specs=[vmem] * (ranks * inner),
         out_shape=[jax.ShapeDtypeStruct((rows, width), taken[0].dtype)] * (ranks * inner),
@@ -165,7 +169,7 @@
     rows, width = pieces[0].shape
     order = blocks.shape[1]
     outer_place, inner_place = place_ref[0], place_ref[1]
-    step = pl.program_id(0)
+    step = pl.program_id(1)
     per_block = order // width
 
     def spot(rank, shard):
@@ -196,24 +200,25 @@
                 outs[k][b * rows : (b + 1) * rows] = results[spot(place_ref[2] ^ k, b)]
 
 
-def precondition(ranks, inner, slot, place, pieces, stats_and_roots):
+def precondition(ranks, inner, slots, place, pieces, stats_and_roots):
+    first, count = slots
     _, col_blocks, order, _ = stats_and_roots[0].shape
-    rows, width = pieces[0].shape
-    count = ranks * inner
-    piece = pl.BlockSpec((rows, width), lambda j: (0, 0))
-    strip = pl.BlockSpec((inner * rows, width), lambda j: (0, 0))
-    matrix = pl.BlockSpec((1, 1, order, order), lambda j: (slot, j, 0, 0))
+    rows, width = pieces[0].shape[0] // count, pieces[0].shape[1]
+    owners = ranks * inner
+    piece = pl.BlockSpec((rows, width), lambda s, j: (s, 0))
+    strip = pl.BlockSpec((inner * rows, width), lambda s, j: (s, 0))
+    matrix = pl.BlockSpec((1, 1, order, order), lambda s, j: (first + s, j, 0, 0))
     return pl.pallas_call(
         functools.partial(block_kernel, ranks, inner, col_blocks),
-        grid=(col_blocks,),
-        in_specs=[pl.BlockSpec(memory_space=pltpu.SMEM)] + [piece] * count + [matrix] * 6,
+        grid=(count, col_blocks),
+        in_specs=[pl.BlockSpec(memory_space=pltpu.SMEM)] + [piece] * owners + [matrix] * 6,
         out_specs=[strip] * ranks,
-        out_shape=[jax.ShapeDtypeStruct((inner * rows, width), jnp.bfloat16)] * ranks,
+        out_shape=[jax.ShapeDtypeStruct((count * inner * rows, width), jnp.bfloat16)] * ranks,
         scratch_shapes=[pltpu.VMEM((col_blocks, order, order), jnp.bfloat16)] * 2,
-        compiler_params=pltpu.CompilerParams(vmem_limit_bytes=VMEM_LIMIT),
+        compiler_params=pltpu.CompilerParams(vmem_limit_bytes=VMEM_LIMIT * 2 // 3),
         cost_estimate=pl.CostEstimate(
-            flops=col_blocks * 19 * 2 * order**3,
-            bytes_accessed=col_blocks * 28 * order**2,
+            flops=count * col_blocks * 19 * 2 * order**3,
+            bytes_accessed=count * col_blocks * 28 * order**2,
             transcendentals=0,
         ),
         name="precondition",
@@ -243,27 +248,44 @@
         for m, e in rounds
     }
 
+    half = max(per // 2, 1)
+    groups = [(first, min(half, per - first)) for first in range(0, per, half)]
     summed = []
-    for slot in range(per):
-        packed = pack(ranks, inner, slot, per, place, grads)
+    for slots in groups:
+        packed = pack(ranks, inner, slots, per, place, grads)
         summed.append(lax.psum_scatter(packed, "dp", scatter_dimension=0, tiled=True))
     left_fourth, right_fourth = fourth_powers(left_root, right_root)
     summed[0], left_fourth, right_fourth = lax.optimization_barrier((summed[0], left_fourth, right_fourth))
     matrices = (left_stats, right_stats, left_root, right_root, left_fourth, right_fourth)
-    out = None
-    for slot in range(per):
-        arrived = [
-            lax.ppermute(summed[slot][at * rows : (at + 1) * rows], MESH_AXES, to_owner[key])
+
+    def send_in(g):
+        size = groups[g][1] * rows
+        return [
+            lax.ppermute(summed[g][at * size : (at + 1) * size], MESH_AXES, to_owner[key])
             for at, key in enumerate(rounds)
         ]
-        strips = precondition(ranks, inner, slot, place, arrived, matrices)
-        strips = [strips[0]] + [lax.ppermute(strips[k], "dp", to_row[k]) for k in range(1, ranks)]
-        routed = route(ranks, inner, place, strips)
+
+    def work(g, arrived):
+        return precondition(ranks, inner, groups[g], place, arrived, matrices)
+
+    strips = work(0, send_in(0))
+    out = None
+    for g, slots in enumerate(groups):
+        last = g + 1 == len(groups)
+        if not last:
+            summed[g + 1], held = lax.optimization_barrier((summed[g + 1], strips[0]))
+            strips = [held] + list(strips[1:])
+        moved = [strips[0]] + [lax.ppermute(strips[k], "dp", to_row[k]) for k in range(1, ranks)]
+        if not last:
+            moved, arrived = lax.optimization_barrier((moved, send_in(g + 1)))
+        routed = route(ranks, inner, slots[1], place, moved)
         back = [routed[0]] + [
             lax.ppermute(piece, "fsdp", to_column[key]) for piece, key in zip(routed[1:], rounds[1:])
         ]
+        if not last:
+            back, strips = lax.optimization_barrier((back, work(g + 1, arrived)))
         gathered = lax.all_gather(jnp.concatenate(back, axis=0), "dp", axis=0, tiled=True)
-        out = unpack(ranks, inner, slot, per, place, gathered, out)
+        out = unpack(ranks, inner, slots, per, place, gathered, out)
     return out.reshape(grads.shape)
 
 

time: 565 us -> 581 us (1.028)
  waiting for transfers between devices: 206 us -> 320 us
  starting transfers between devices: 185 us -> 107 us
  Pallas kernels: 139 us -> 121 us
    reduce_scatter x4 -> x2, waiting for transfers between devices: 9.53 us -> 98.9 us  [shards(): lax.psum_scatter(packed, 'dp', scatter_dimension=0, tiled=True)]
    ppermute x12 -> x6, starting transfers between devices: 75.2 us -> 15.6 us  [shards(): lax.ppermute(strips[k], 'dp', to_row[k])]
    all_gather x4 -> x2, waiting for transfers between devices: 42.9 us -> 98.5 us  [shards(): lax.all_gather(jnp.concatenate(back, axis=0), 'dp', axis=0, tiled=True)]
    ppermute x28 -> x14, waiting for transfers between devices: 58.1 us -> 37.8 us  [shards(): lax.ppermute(piece, 'fsdp', to_column[key])]
    ppermute x32 -> x16, waiting for transfers between devices: 25.7 us -> 9.94 us  [send_in(): lax.ppermute(summed[g][at * size:(at + 1) * size], MESH_AXES, to_owner[key])]
    pallas_call x4 -> x2, Pallas kernels: 66.2 us -> 52.3 us  [precondition(): pl.pallas_call(functools.partial(block_kernel, ranks, inner, col_blocks),...]
    ppermute x32 -> x16, starting transfers between devices: 79.4 us -> 66.5 us  [send_in(): lax.ppermute(summed[g][at * size:(at + 1) * size], MESH_AXES, to_owner[key])]
    ppermute x28 -> x14, starting transfers between devices: 30.3 us -> 24.6 us  [shards(): lax.ppermute(piece, 'fsdp', to_column[key])]
  transfers between devices with their start and end apart: 80 -> 40, of which waited for: 35 -> 18; matrix products, arithmetic and copies ran while one was open for 1% -> 0% of each run, Pallas kernels for 23% -> 18%
where the time goes in v3:
time: 581 us; the launch traced here: 580 us
  waiting for transfers between devices  320 us (55%)
  Pallas kernels  121 us (21%)
  starting transfers between devices  107 us (18%)
  local copies, waits for them, and re-layouts  17.5 us (3%)
  between operations  13.4 us (2%)
    reduce_scatter x2, waiting for transfers between devices, shards(): lax.psum_scatter(packed, 'dp', scatter_dimension=0, tiled=True)  98.9 us
    all_gather x2, waiting for transfers between devices, shards(): lax.all_gather(jnp.concatenate(back, axis=0), 'dp', axis=0, tiled=True)  98.5 us
    ppermute x6, waiting for transfers between devices, shards(): lax.ppermute(strips[k], 'dp', to_row[k])  75 us
    ppermute x16, starting transfers between devices, send_in(): lax.ppermute(summed[g][at * size:(at + 1) * size], MESH_AXES, to_owner[key])  66.5 us
    pallas_call x2, Pallas kernels, precondition(): pl.pallas_call(functools.partial(block_kernel, ranks, inner, col_blocks),...  52.3 us
    ppermute x14, waiting for transfers between devices, shards(): lax.ppermute(piece, 'fsdp', to_column[key])  37.8 us
    pallas_call x1, Pallas kernels, fourth_powers(): pl.pallas_call(fourth_kernel, grid=(slabs, col_blocks), in_specs=[spec, s...  31.3 us
    ppermute x14, starting transfers between devices, shards(): lax.ppermute(piece, 'fsdp', to_column[key])  24.6 us
  transfers between devices with their start and end apart: 40, of which 18 were waited for; matrix products, arithmetic and copies ran while one was open for 0% of the time, Pallas kernels for 18%

profile of v3, /device:TPU:0, one launch (start us, length us, event | category | flops | bytes accessed | tf_op | source)
XLA Modules:
  0.0 579.9 jit_solution(18018938191519334097)
XLA Ops:
  7.1 9.1 %pack_slabs.3 = bf16[4,8,2,128,512]{4,3,2,1,0:T(8,128)(2,1)} custom-call(s32[3]{0:T(128)} %pad_add_fusion.place_ref, bf16[8,4,512,512]{3,2,1,0:T(8,128)(2,1)} %bitcast.9), custom_call_target="tpu_custom_call" | custom-call | bytes 16777216 | tf_op jit(solution)/shard_map/pack_slabs/pallas_call | solution.py:74
  16.3 9.1 %pack_slabs.2 = bf16[4,8,2,128,512]{4,3,2,1,0:T(8,128)(2,1)} custom-call(s32[3]{0:T(128)} %pad_add_fusion.place_ref, bf16[8,4,512,512]{3,2,1,0:T(8,128)(2,1)} %bitcast.10), custom_call_target="tpu_custom_call" | custom-call | bytes 16777216 | tf_op jit(solution)/shard_map/pack_slabs/pallas_call | solution.py:74
  25.4 31.3 %fourth_powers.1 = (f32[4,2,512,512]{3,2,1,0:T(8,128)}, f32[4,2,512,512]{3,2,1,0:T(8,128)}) custom-call(f32[4,2,512,512]{3,2,1,0:T(8,128)} %refs_10_.3, f32[4,2,512,512]{3,2,1,0:T(8,128)} %refs_11_.3), custom_call_target="tpu_custom_call" | custom-call | flops 25769803776 | bytes 33554432 | tf_op jit(solution)/shard_map/fourth_powers/pallas_call | solution.py:45
  56.7 48.8 %reduce-scatter.5.cloned.1.call-done = bf16[2048,512]{1,0:T(8,128)(2,1)} async-done(((bf16[8192,512]{1,0:T(8,128)(2,1)}), bf16[2048,512]{1,0:T(8,128)(2,1)}) %reduce-scatter.5.cloned.1.call-update) | async-done | bytes 2097168 | tf_op jit(solution)/shard_map/reduce_scatter | solution.py:256
  105.5 1.6 fusion.1
  107.1 2.8 collective-permute-start.7
  109.9 1.4 collective-permute-start.6
  112.4 1.7 collective-permute-start.3
  114.1 2.9 collective-permute-done.7.refs_7_
  117.0 23.5 %collective-permute-start.2 = (bf16[256,512]{1,0:T(8,128)(2,1)S(1)}, bf16[256,512]{1,0:T(8,128)(2,1)S(1)}, u32[]{:S(2)}, u32[]{:S(2)}) collective-permute-start(bf16[256,512]{1,0:T(8,128)(2,1)S(1)} %get-tuple-element.128), channel_id=1, source_target_pairs={{0,2},{1,3},{2,10},{3,11},{4,18},{5,19},{6,26},{7,27},{8,0},{9,1},... | collective-permute-start | bytes 786440 | tf_op jit(solution)/shard_map/ppermute | solution.py:264
  141.2 3.7 collective-permute-done.4.refs_4_
  144.9 1.5 collective-permute-done.2.refs_2_
  146.4 3.6 copy-done.1
  150.0 26.2 %precondition.2 = (bf16[512,512]{1,0:T(8,128)(2,1)S(1)}, bf16[512,512]{1,0:T(8,128)(2,1)S(1)}, bf16[512,512]{1,0:T(8,128)(2,1)S(1)}, bf16[512,512]{1,0:T(8,128)(2,1)S(1)}) custom-call(s32[3]{0:T(128)S(1)} %copy-done, bf16[256,512]{1,0:T(8,128)(2,1)S(1)} %collective-permute-done.refs_0_, bf16[256,512]{1,0:T(8,128)(2,1)S(1)} %collective-permute-done.1.refs_1_, ...), custom_call_target="tpu_custom_call" | custom-call | flops 20401094656 | bytes 29360128 | tf_op jit(solution)/shard_map/precondition/pallas_call | solution.py:211
  176.2 50.1 %reduce-scatter.3.cloned.1.call-done = bf16[2048,512]{1,0:T(8,128)(2,1)} async-done(((bf16[8192,512]{1,0:T(8,128)(2,1)}), bf16[2048,512]{1,0:T(8,128)(2,1)}) %reduce-scatter.3.cloned.1.call-update) | async-done | bytes 2097168 | tf_op jit(solution)/shard_map/reduce_scatter | solution.py:256
  226.3 1.6 fusion
  228.0 2.8 collective-permute-start.18
  230.7 1.5 collective-permute-start.17
  233.3 3.3 collective-permute-start.8
  236.6 1.2 collective-permute-done.18.refs_7_
  237.8 23.3 %collective-permute-start.14 = (bf16[256,512]{1,0:T(8,128)(2,1)S(1)}, bf16[256,512]{1,0:T(8,128)(2,1)S(1)}, u32[]{:S(2)}, u32[]{:S(2)}) collective-permute-start(bf16[256,512]{1,0:T(8,128)(2,1)S(1)} %get-tuple-element.119), channel_id=1, source_target_pairs={{0,3},{1,2},{2,11},{3,10},{4,19},{5,18},{6,27},{7,26},{8,1},{9,0},... | collective-permute-start | bytes 786440 | tf_op jit(solution)/shard_map/ppermute | solution.py:264
  261.1 5.9 %collective-permute-start.13 = (bf16[256,512]{1,0:T(8,128)(2,1)S(1)}, bf16[256,512]{1,0:T(8,128)(2,1)S(1)}, u32[]{:S(2)}, u32[]{:S(2)}) collective-permute-start(bf16[256,512]{1,0:T(8,128)(2,1)S(1)} %get-tuple-element.120), channel_id=1, source_target_pairs={{0,2},{1,3},{2,10},{3,11},{4,18},{5,19},{6,26},{7,27},{8,0},{9,1},... | collective-permute-start | bytes 786440 | tf_op jit(solution)/shard_map/ppermute | solution.py:264
  266.9 5.6 collective-permute-start.9
  274.2 43.6 %collective-permute-done.9.refs_2_ = bf16[512,512]{1,0:T(8,128)(2,1)S(1)} collective-permute-done((bf16[512,512]{1,0:T(8,128)(2,1)S(1)}, bf16[512,512]{1,0:T(8,128)(2,1)S(1)}, u32[]{:S(2)}, u32[]{:S(2)}) %collective-permute-start.9) | collective-permute-done | bytes 524320 | tf_op jit(solution)/shard_map/ppermute | solution.py:278
  318.7 1.8 collective-permute-start.21
  320.5 2.6 collective-permute-start.23
  323.2 7.0 %collective-permute-done.20 = bf16[256,512]{1,0:T(8,128)(2,1)S(1)} collective-permute-done((bf16[256,512]{1,0:T(8,128)(2,1)S(1)}, bf16[256,512]{1,0:T(8,128)(2,1)S(1)}, u32[]{:S(2)}, u32[]{:S(2)}) %collective-permute-start.20) | collective-permute-done | bytes 262176 | tf_op jit(solution)/shard_map/ppermute | solution.py:283
  330.2 3.4 copy-done.2
  333.6 26.1 %precondition.3 = (bf16[512,512]{1,0:T(8,128)(2,1)S(1)}, bf16[512,512]{1,0:T(8,128)(2,1)S(1)}, bf16[512,512]{1,0:T(8,128)(2,1)S(1)}, bf16[512,512]{1,0:T(8,128)(2,1)S(1)}) custom-call(s32[3]{0:T(128)S(1)} %copy-done, bf16[256,512]{1,0:T(8,128)(2,1)S(1)} %collective-permute-done.11.refs_0_, bf16[256,512]{1,0:T(8,128)(2,1)S(1)} %collective-permute-done.12.refs_1_, ...), custom_call_target="tpu_custom_call" | custom-call | flops 20401094656 | bytes 29360128 | tf_op jit(solution)/shard_map/precondition/pallas_call | solution.py:211
  365.5 4.8 collective-permute-start.26
  370.7 1.4 collective-permute-start.28
  372.1 10.4 %collective-permute-done.26.refs_1_ = bf16[512,512]{1,0:T(8,128)(2,1)S(1)} collective-permute-done((bf16[512,512]{1,0:T(8,128)(2,1)S(1)}, bf16[512,512]{1,0:T(8,128)(2,1)S(1)}, u32[]{:S(2)}, u32[]{:S(2)}) %collective-permute-start.26) | collective-permute-done | bytes 524320 | tf_op jit(solution)/shard_map/ppermute | solution.py:278
  382.5 3.6 collective-permute-done.27.refs_2_
  386.1 17.4 %collective-permute-done.28.refs_3_ = bf16[512,512]{1,0:T(8,128)(2,1)S(1)} collective-permute-done((bf16[512,512]{1,0:T(8,128)(2,1)S(1)}, bf16[512,512]{1,0:T(8,128)(2,1)S(1)}, u32[]{:S(2)}, u32[]{:S(2)}) %collective-permute-start.28) | collective-permute-done | bytes 524320 | tf_op jit(solution)/shard_map/ppermute | solution.py:278
  404.4 4.1 collective-permute-start.29
  408.5 10.2 %collective-permute-start.30 = (bf16[256,512]{1,0:T(8,128)(2,1)S(1)}, bf16[256,512]{1,0:T(8,128)(2,1)S(1)}, u32[]{:S(2)}, u32[]{:S(2)}) collective-permute-start(bf16[256,512]{1,0:T(8,128)(2,1)S(1)} %get-tuple-element.101), channel_id=1, source_target_pairs={{0,2},{1,3},{2,0},{3,1},{4,6},{5,7},{6,4},{7,5},{8,10},{9,11},{10,... | collective-permute-start | bytes 786440 | tf_op jit(solution)/shard_map/ppermute | solution.py:283
  418.7 1.4 collective-permute-start.32
  420.1 1.0 collective-permute-start.33
  421.2 1.8 collective-permute-start.34
  423.0 12.6 %collective-permute-done.30 = bf16[256,512]{1,0:T(8,128)(2,1)S(1)} collective-permute-done((bf16[256,512]{1,0:T(8,128)(2,1)S(1)}, bf16[256,512]{1,0:T(8,128)(2,1)S(1)}, u32[]{:S(2)}, u32[]{:S(2)}) %collective-permute-start.30) | collective-permute-done | bytes 262176 | tf_op jit(solution)/shard_map/ppermute | solution.py:283
  435.6 1.5 collective-permute-start.35
  437.1 3.6 collective-permute-done.31
  440.7 14.6 %collective-permute-done.33 = bf16[256,512]{1,0:T(8,128)(2,1)S(1)} collective-permute-done((bf16[256,512]{1,0:T(8,128)(2,1)S(1)}, bf16[256,512]{1,0:T(8,128)(2,1)S(1)}, u32[]{:S(2)}, u32[]{:S(2)}) %collective-permute-start.33) | collective-permute-done | bytes 262176 | tf_op jit(solution)/shard_map/ppermute | solution.py:283
  455.4 1.3 copy-done.3
  456.8 18.2 %all-gather.5.cloned.1.call-done = bf16[8192,512]{1,0:T(8,128)(2,1)} async-done(((bf16[2048,512]{1,0:T(8,128)(2,1)}), bf16[8192,512]{1,0:T(8,128)(2,1)}) %all-gather.5.cloned.1.call-update) | async-done | bytes 8388624 | tf_op jit(solution)/shard_map/all_gather | solution.py:287
  475.0 9.0 %unpack_slabs.2.rest_0_ = bf16[8,4,512,512]{3,2,1,0:T(8,128)(2,1)} custom-call(s32[3]{0:T(128)} %pad_add_fusion.place_ref, bf16[4,8,2,128,512]{4,3,2,1,0:T(8,128)(2,1)} %bitcast.13), custom_call_target="tpu_custom_call" | custom-call | bytes 16777216 | tf_op jit(solution)/shard_map/unpack_slabs/pallas_call | solution.py:106
  484.0 80.3 %all-gather.3.cloned.1.call-done = bf16[8192,512]{1,0:T(8,128)(2,1)} async-done(((bf16[2048,512]{1,0:T(8,128)(2,1)}), bf16[8192,512]{1,0:T(8,128)(2,1)}) %all-gather.3.cloned.1.call-update) | async-done | bytes 8388624 | tf_op jit(solution)/shard_map/all_gather | solution.py:287
  564.3 9.0 %unpack_slabs.3 = bf16[8,4,512,512]{3,2,1,0:T(8,128)(2,1)} custom-call(s32[3]{0:T(128)} %pad_add_fusion.place_ref, bf16[4,8,2,128,512]{4,3,2,1,0:T(8,128)(2,1)} %bitcast.14, bf16[8,4,512,512]{3,2,1,0:T(8,128)(2,1)} %unpack_slabs.2.rest_0_), custom_call_target="tpu_custom_call", output_to_operand_aliasing={{}: (2, {})} | custom-call | bytes 16777216 | tf_op jit(solution)/shard_map/unpack_slabs/pallas_call | solution.py:106
  (72 shorter events, 13.4 us)
Async XLA Ops:
  6.5 99.0 %reduce-scatter.5.cloned.1.call-start = ((), (), s32[]{:S(2)}) async-start(), calls=%async_computation.3 | async-start | bytes 10485760 | tf_op jit(solution)/shard_map/reduce_scatter | solution.py:256
  16.2 210.1 %reduce-scatter.3.cloned.1.call-start = ((), (), s32[]{:S(2)}) async-start(), calls=%async_computation.2 | async-start | bytes 10485760 | tf_op jit(solution)/shard_map/reduce_scatter | solution.py:256
  25.4 449.6 %all-gather.5.cloned.1.call-start = ((), (), s32[]{:S(2)}) async-start(), calls=%async_computation.5 | async-start | bytes 10485760 | tf_op jit(solution)/shard_map/all_gather | solution.py:287
  105.5 40.9 %copy-start = (s32[3]{0:T(128)S(1)}, s32[3]{0:T(128)}, u32[]{:S(2)}) copy-start(s32[3]{0:T(128)} %pad_add_fusion.place_ref) | copy-start | bytes 40
  107.1 9.9 %collective-permute-start.7 = (bf16[256,512]{1,0:T(8,128)(2,1)S(1)}, bf16[256,512]{1,0:T(8,128)(2,1)S(1)}, u32[]{:S(2)}, u32[]{:S(2)}) collective-permute-start(bf16[256,512]{1,0:T(8,128)(2,1)S(1)} %get-tuple-element.123), channel_id=1, source_target_pairs={{0,7},{1,6},{2,15},{3,14},{4,23},{5,22},{6,31},{7,30},{8,5},{9,4},... | collective-permute-start | bytes 786440 | tf_op jit(solution)/shard_map/ppermute | solution.py:264
  109.9 30.6 %collective-permute-start.6 = (bf16[256,512]{1,0:T(8,128)(2,1)S(1)}, bf16[256,512]{1,0:T(8,128)(2,1)S(1)}, u32[]{:S(2)}, u32[]{:S(2)}) collective-permute-start(bf16[256,512]{1,0:T(8,128)(2,1)S(1)} %get-tuple-element.124), channel_id=1, source_target_pairs={{0,6},{1,7},{2,14},{3,15},{4,22},{5,23},{6,30},{7,31},{8,4},{9,5},... | collective-permute-start | bytes 786440 | tf_op jit(solution)/shard_map/ppermute | solution.py:264
  111.3 29.1 %collective-permute-start.5 = (bf16[256,512]{1,0:T(8,128)(2,1)S(1)}, bf16[256,512]{1,0:T(8,128)(2,1)S(1)}, u32[]{:S(2)}, u32[]{:S(2)}) collective-permute-start(bf16[256,512]{1,0:T(8,128)(2,1)S(1)} %get-tuple-element.125), channel_id=1, source_target_pairs={{0,5},{1,4},{2,13},{3,12},{4,21},{5,20},{6,29},{7,28},{8,7},{9,6},... | collective-permute-start | bytes 786440 | tf_op jit(solution)/shard_map/ppermute | solution.py:264
  111.9 33.0 %collective-permute-start.4 = (bf16[256,512]{1,0:T(8,128)(2,1)S(1)}, bf16[256,512]{1,0:T(8,128)(2,1)S(1)}, u32[]{:S(2)}, u32[]{:S(2)}) collective-permute-start(bf16[256,512]{1,0:T(8,128)(2,1)S(1)} %get-tuple-element.126), channel_id=1, source_target_pairs={{0,4},{1,5},{2,12},{3,13},{4,20},{5,21},{6,28},{7,29},{8,6},{9,7},... | collective-permute-start | bytes 786440 | tf_op jit(solution)/shard_map/ppermute | solution.py:264
  112.4 32.5 %collective-permute-start.3 = (bf16[256,512]{1,0:T(8,128)(2,1)S(1)}, bf16[256,512]{1,0:T(8,128)(2,1)S(1)}, u32[]{:S(2)}, u32[]{:S(2)}) collective-permute-start(bf16[256,512]{1,0:T(8,128)(2,1)S(1)} %get-tuple-element.127), channel_id=1, source_target_pairs={{0,3},{1,2},{2,11},{3,10},{4,19},{5,18},{6,27},{7,26},{8,1},{9,0},... | collective-permute-start | bytes 786440 | tf_op jit(solution)/shard_map/ppermute | solution.py:264
  117.0 29.4 %collective-permute-start.2 = (bf16[256,512]{1,0:T(8,128)(2,1)S(1)}, bf16[256,512]{1,0:T(8,128)(2,1)S(1)}, u32[]{:S(2)}, u32[]{:S(2)}) collective-permute-start(bf16[256,512]{1,0:T(8,128)(2,1)S(1)} %get-tuple-element.128), channel_id=1, source_target_pairs={{0,2},{1,3},{2,10},{3,11},{4,18},{5,19},{6,26},{7,27},{8,0},{9,1},... | collective-permute-start | bytes 786440 | tf_op jit(solution)/shard_map/ppermute | solution.py:264
  140.5 5.9 %collective-permute-start.1 = (bf16[256,512]{1,0:T(8,128)(2,1)S(1)}, bf16[256,512]{1,0:T(8,128)(2,1)S(1)}, u32[]{:S(2)}, u32[]{:S(2)}) collective-permute-start(bf16[256,512]{1,0:T(8,128)(2,1)S(1)} %get-tuple-element.129), channel_id=1, source_target_pairs={{0,1},{1,0},{2,9},{3,8},{4,17},{5,16},{6,25},{7,24},{8,3},{9,2},{1... | collective-permute-start | bytes 786440 | tf_op jit(solution)/shard_map/ppermute | solution.py:264
  140.5 5.9 %collective-permute-start = (bf16[256,512]{1,0:T(8,128)(2,1)S(1)}, bf16[256,512]{1,0:T(8,128)(2,1)S(1)}, u32[]{:S(2)}, u32[]{:S(2)}) collective-permute-start(bf16[256,512]{1,0:T(8,128)(2,1)S(1)} %get-tuple-element.130), channel_id=1, source_target_pairs={{0,0},{1,1},{2,8},{3,9},{4,16},{5,17},{6,24},{7,25},{8,2},{9,3},{1... | collective-permute-start | bytes 786440 | tf_op jit(solution)/shard_map/ppermute | solution.py:264
  146.4 3.6 copy-start.1
  228.0 9.8 %collective-permute-start.18 = (bf16[256,512]{1,0:T(8,128)(2,1)S(1)}, bf16[256,512]{1,0:T(8,128)(2,1)S(1)}, u32[]{:S(2)}, u32[]{:S(2)}) collective-permute-start(bf16[256,512]{1,0:T(8,128)(2,1)S(1)} %get-tuple-element.115), channel_id=1, source_target_pairs={{0,7},{1,6},{2,15},{3,14},{4,23},{5,22},{6,31},{7,30},{8,5},{9,4},... | collective-permute-start | bytes 786440 | tf_op jit(solution)/shard_map/ppermute | solution.py:264
  230.7 30.3 %collective-permute-start.17 = (bf16[256,512]{1,0:T(8,128)(2,1)S(1)}, bf16[256,512]{1,0:T(8,128)(2,1)S(1)}, u32[]{:S(2)}, u32[]{:S(2)}) collective-permute-start(bf16[256,512]{1,0:T(8,128)(2,1)S(1)} %get-tuple-element.116), channel_id=1, source_target_pairs={{0,6},{1,7},{2,14},{3,15},{4,22},{5,23},{6,30},{7,31},{8,4},{9,5},... | collective-permute-start | bytes 786440 | tf_op jit(solution)/shard_map/ppermute | solution.py:264
  232.2 34.7 %collective-permute-start.16 = (bf16[256,512]{1,0:T(8,128)(2,1)S(1)}, bf16[256,512]{1,0:T(8,128)(2,1)S(1)}, u32[]{:S(2)}, u32[]{:S(2)}) collective-permute-start(bf16[256,512]{1,0:T(8,128)(2,1)S(1)} %get-tuple-element.117), channel_id=1, source_target_pairs={{0,5},{1,4},{2,13},{3,12},{4,21},{5,20},{6,29},{7,28},{8,7},{9,6},... | collective-permute-start | bytes 786440 | tf_op jit(solution)/shard_map/ppermute | solution.py:264
  232.8 39.8 %collective-permute-start.15 = (bf16[256,512]{1,0:T(8,128)(2,1)S(1)}, bf16[256,512]{1,0:T(8,128)(2,1)S(1)}, u32[]{:S(2)}, u32[]{:S(2)}) collective-permute-start(bf16[256,512]{1,0:T(8,128)(2,1)S(1)} %get-tuple-element.118), channel_id=1, source_target_pairs={{0,4},{1,5},{2,12},{3,13},{4,20},{5,21},{6,28},{7,29},{8,6},{9,7},... | collective-permute-start | bytes 786440 | tf_op jit(solution)/shard_map/ppermute | solution.py:264
  233.3 40.9 %collective-permute-start.8 = (bf16[512,512]{1,0:T(8,128)(2,1)S(1)}, bf16[512,512]{1,0:T(8,128)(2,1)S(1)}, u32[]{:S(2)}, u32[]{:S(2)}) collective-permute-start(bf16[512,512]{1,0:T(8,128)(2,1)S(1)} %get-tuple-element.67), channel_id=1, source_target_pairs={{0,8},{8,0},{16,24},{24,16},{1,9},{9,1},{17,25},{25,17},{2,10},{10... | collective-permute-start | bytes 1572872 | tf_op jit(solution)/shard_map/ppermute | solution.py:278
  237.8 34.8 %collective-permute-start.14 = (bf16[256,512]{1,0:T(8,128)(2,1)S(1)}, bf16[256,512]{1,0:T(8,128)(2,1)S(1)}, u32[]{:S(2)}, u32[]{:S(2)}) collective-permute-start(bf16[256,512]{1,0:T(8,128)(2,1)S(1)} %get-tuple-element.119), channel_id=1, source_target_pairs={{0,3},{1,2},{2,11},{3,10},{4,19},{5,18},{6,27},{7,26},{8,1},{9,0},... | collective-permute-start | bytes 786440 | tf_op jit(solution)/shard_map/ppermute | solution.py:264
  261.1 12.0 %collective-permute-start.13 = (bf16[256,512]{1,0:T(8,128)(2,1)S(1)}, bf16[256,512]{1,0:T(8,128)(2,1)S(1)}, u32[]{:S(2)}, u32[]{:S(2)}) collective-permute-start(bf16[256,512]{1,0:T(8,128)(2,1)S(1)} %get-tuple-element.120), channel_id=1, source_target_pairs={{0,2},{1,3},{2,10},{3,11},{4,18},{5,19},{6,26},{7,27},{8,0},{9,1},... | collective-permute-start | bytes 786440 | tf_op jit(solution)/shard_map/ppermute | solution.py:264
  266.9 50.8 %collective-permute-start.9 = (bf16[512,512]{1,0:T(8,128)(2,1)S(1)}, bf16[512,512]{1,0:T(8,128)(2,1)S(1)}, u32[]{:S(2)}, u32[]{:S(2)}) collective-permute-start(bf16[512,512]{1,0:T(8,128)(2,1)S(1)} %get-tuple-element.68), channel_id=1, source_target_pairs={{0,16},{8,24},{16,0},{24,8},{1,17},{9,25},{17,1},{25,9},{2,18},{10... | collective-permute-start | bytes 1572872 | tf_op jit(solution)/shard_map/ppermute | solution.py:278
  272.6 45.2 %collective-permute-start.10 = (bf16[512,512]{1,0:T(8,128)(2,1)S(1)}, bf16[512,512]{1,0:T(8,128)(2,1)S(1)}, u32[]{:S(2)}, u32[]{:S(2)}) collective-permute-start(bf16[512,512]{1,0:T(8,128)(2,1)S(1)} %get-tuple-element.69), channel_id=1, source_target_pairs={{0,24},{8,16},{16,8},{24,0},{1,25},{9,17},{17,9},{25,1},{2,26},{10... | collective-permute-start | bytes 1572872 | tf_op jit(solution)/shard_map/ppermute | solution.py:278
  272.6 1.6 collective-permute-start.12
  273.1 1.1 collective-permute-start.11
  318.6 4.5 collective-permute-start.19
  318.7 11.5 %collective-permute-start.20 = (bf16[256,512]{1,0:T(8,128)(2,1)S(1)}, bf16[256,512]{1,0:T(8,128)(2,1)S(1)}, u32[]{:S(2)}, u32[]{:S(2)}) collective-permute-start(bf16[256,512]{1,0:T(8,128)(2,1)S(1)} %get-tuple-element.77), channel_id=1, source_target_pairs={{0,2},{1,3},{2,0},{3,1},{4,6},{5,7},{6,4},{7,5},{8,10},{9,11},{10,... | collective-permute-start | bytes 786440 | tf_op jit(solution)/shard_map/ppermute | solution.py:283
  318.7 40.9 %collective-permute-start.21 = (bf16[256,512]{1,0:T(8,128)(2,1)S(1)}, bf16[256,512]{1,0:T(8,128)(2,1)S(1)}, u32[]{:S(2)}, u32[]{:S(2)}) collective-permute-start(bf16[256,512]{1,0:T(8,128)(2,1)S(1)} %get-tuple-element.78), channel_id=1, source_target_pairs={{0,3},{1,2},{2,1},{3,0},{4,7},{5,6},{6,5},{7,4},{8,11},{9,10},{10,... | collective-permute-start | bytes 786440 | tf_op jit(solution)/shard_map/ppermute | solution.py:283
  320.5 39.1 %collective-permute-start.22 = (bf16[256,512]{1,0:T(8,128)(2,1)S(1)}, bf16[256,512]{1,0:T(8,128)(2,1)S(1)}, u32[]{:S(2)}, u32[]{:S(2)}) collective-permute-start(bf16[256,512]{1,0:T(8,128)(2,1)S(1)} %get-tuple-element.79), channel_id=1, source_target_pairs={{0,4},{1,5},{2,6},{3,7},{4,0},{5,1},{6,2},{7,3},{8,12},{9,13},{10,... | collective-permute-start | bytes 786440 | tf_op jit(solution)/shard_map/ppermute | solution.py:283
  320.5 39.1 %collective-permute-start.23 = (bf16[256,512]{1,0:T(8,128)(2,1)S(1)}, bf16[256,512]{1,0:T(8,128)(2,1)S(1)}, u32[]{:S(2)}, u32[]{:S(2)}) collective-permute-start(bf16[256,512]{1,0:T(8,128)(2,1)S(1)} %get-tuple-element.80), channel_id=1, source_target_pairs={{0,5},{1,4},{2,7},{3,6},{4,1},{5,0},{6,3},{7,2},{8,13},{9,12},{10,... | collective-permute-start | bytes 786440 | tf_op jit(solution)/shard_map/ppermute | solution.py:283
  323.1 36.5 %collective-permute-start.24 = (bf16[256,512]{1,0:T(8,128)(2,1)S(1)}, bf16[256,512]{1,0:T(8,128)(2,1)S(1)}, u32[]{:S(2)}, u32[]{:S(2)}) collective-permute-start(bf16[256,512]{1,0:T(8,128)(2,1)S(1)} %get-tuple-element.81), channel_id=1, source_target_pairs={{0,6},{1,7},{2,4},{3,5},{4,2},{5,3},{6,0},{7,1},{8,14},{9,15},{10,... | collective-permute-start | bytes 786440 | tf_op jit(solution)/shard_map/ppermute | solution.py:283
  330.2 29.5 %collective-permute-start.25 = (bf16[256,512]{1,0:T(8,128)(2,1)S(1)}, bf16[256,512]{1,0:T(8,128)(2,1)S(1)}, u32[]{:S(2)}, u32[]{:S(2)}) collective-permute-start(bf16[256,512]{1,0:T(8,128)(2,1)S(1)} %get-tuple-element.82), channel_id=1, source_target_pairs={{0,7},{1,6},{2,5},{3,4},{4,3},{5,2},{6,1},{7,0},{8,15},{9,14},{10,... | collective-permute-start | bytes 786440 | tf_op jit(solution)/shard_map/ppermute | solution.py:283
  330.2 3.4 copy-start.2
  365.5 198.8 %all-gather.3.cloned.1.call-start = ((), (), s32[]{:S(2)}) async-start(), calls=%async_computation.4 | async-start | bytes 10485760 | tf_op jit(solution)/shard_map/all_gather | solution.py:287
  365.5 17.0 %collective-permute-start.26 = (bf16[512,512]{1,0:T(8,128)(2,1)S(1)}, bf16[512,512]{1,0:T(8,128)(2,1)S(1)}, u32[]{:S(2)}, u32[]{:S(2)}) collective-permute-start(bf16[512,512]{1,0:T(8,128)(2,1)S(1)} %get-tuple-element.96), channel_id=1, source_target_pairs={{0,8},{8,0},{16,24},{24,16},{1,9},{9,1},{17,25},{25,17},{2,10},{10... | collective-permute-start | bytes 1572872 | tf_op jit(solution)/shard_map/ppermute | solution.py:278
  370.3 15.8 %collective-permute-start.27 = (bf16[512,512]{1,0:T(8,128)(2,1)S(1)}, bf16[512,512]{1,0:T(8,128)(2,1)S(1)}, u32[]{:S(2)}, u32[]{:S(2)}) collective-permute-start(bf16[512,512]{1,0:T(8,128)(2,1)S(1)} %get-tuple-element.97), channel_id=1, source_target_pairs={{0,16},{8,24},{16,0},{24,8},{1,17},{9,25},{17,1},{25,9},{2,18},{10... | collective-permute-start | bytes 1572872 | tf_op jit(solution)/shard_map/ppermute | solution.py:278
  370.7 32.8 %collective-permute-start.28 = (bf16[512,512]{1,0:T(8,128)(2,1)S(1)}, bf16[512,512]{1,0:T(8,128)(2,1)S(1)}, u32[]{:S(2)}, u32[]{:S(2)}) collective-permute-start(bf16[512,512]{1,0:T(8,128)(2,1)S(1)} %get-tuple-element.98), channel_id=1, source_target_pairs={{0,24},{8,16},{16,8},{24,0},{1,25},{9,17},{17,9},{25,1},{2,26},{10... | collective-permute-start | bytes 1572872 | tf_op jit(solution)/shard_map/ppermute | solution.py:278
  404.4 16.8 %collective-permute-start.29 = (bf16[256,512]{1,0:T(8,128)(2,1)S(1)}, bf16[256,512]{1,0:T(8,128)(2,1)S(1)}, u32[]{:S(2)}, u32[]{:S(2)}) collective-permute-start(bf16[256,512]{1,0:T(8,128)(2,1)S(1)} %get-tuple-element.100), channel_id=1, source_target_pairs={{0,1},{1,0},{2,3},{3,2},{4,5},{5,4},{6,7},{7,6},{8,9},{9,8},{10,11... | collective-permute-start | bytes 786440 | tf_op jit(solution)/shard_map/ppermute | solution.py:283
  408.5 27.1 %collective-permute-start.30 = (bf16[256,512]{1,0:T(8,128)(2,1)S(1)}, bf16[256,512]{1,0:T(8,128)(2,1)S(1)}, u32[]{:S(2)}, u32[]{:S(2)}) collective-permute-start(bf16[256,512]{1,0:T(8,128)(2,1)S(1)} %get-tuple-element.101), channel_id=1, source_target_pairs={{0,2},{1,3},{2,0},{3,1},{4,6},{5,7},{6,4},{7,5},{8,10},{9,11},{10,... | collective-permute-start | bytes 786440 | tf_op jit(solution)/shard_map/ppermute | solution.py:283
  418.7 22.0 %collective-permute-start.31 = (bf16[256,512]{1,0:T(8,128)(2,1)S(1)}, bf16[256,512]{1,0:T(8,128)(2,1)S(1)}, u32[]{:S(2)}, u32[]{:S(2)}) collective-permute-start(bf16[256,512]{1,0:T(8,128)(2,1)S(1)} %get-tuple-element.102), channel_id=1, source_target_pairs={{0,3},{1,2},{2,1},{3,0},{4,7},{5,6},{6,5},{7,4},{8,11},{9,10},{10,... | collective-permute-start | bytes 786440 | tf_op jit(solution)/shard_map/ppermute | solution.py:283
  418.7 21.9 %collective-permute-start.32 = (bf16[256,512]{1,0:T(8,128)(2,1)S(1)}, bf16[256,512]{1,0:T(8,128)(2,1)S(1)}, u32[]{:S(2)}, u32[]{:S(2)}) collective-permute-start(bf16[256,512]{1,0:T(8,128)(2,1)S(1)} %get-tuple-element.103), channel_id=1, source_target_pairs={{0,4},{1,5},{2,6},{3,7},{4,0},{5,1},{6,2},{7,3},{8,12},{9,13},{10,... | collective-permute-start | bytes 786440 | tf_op jit(solution)/shard_map/ppermute | solution.py:283
  420.1 35.2 %collective-permute-start.33 = (bf16[256,512]{1,0:T(8,128)(2,1)S(1)}, bf16[256,512]{1,0:T(8,128)(2,1)S(1)}, u32[]{:S(2)}, u32[]{:S(2)}) collective-permute-start(bf16[256,512]{1,0:T(8,128)(2,1)S(1)} %get-tuple-element.104), channel_id=1, source_target_pairs={{0,5},{1,4},{2,7},{3,6},{4,1},{5,0},{6,3},{7,2},{8,13},{9,12},{10,... | collective-permute-start | bytes 786440 | tf_op jit(solution)/shard_map/ppermute | solution.py:283
  421.2 34.2 %collective-permute-start.34 = (bf16[256,512]{1,0:T(8,128)(2,1)S(1)}, bf16[256,512]{1,0:T(8,128)(2,1)S(1)}, u32[]{:S(2)}, u32[]{:S(2)}) collective-permute-start(bf16[256,512]{1,0:T(8,128)(2,1)S(1)} %get-tuple-element.105), channel_id=1, source_target_pairs={{0,6},{1,7},{2,4},{3,5},{4,2},{5,3},{6,0},{7,1},{8,14},{9,15},{10,... | collective-permute-start | bytes 786440 | tf_op jit(solution)/shard_map/ppermute | solution.py:283
  435.6 19.8 %collective-permute-start.35 = (bf16[256,512]{1,0:T(8,128)(2,1)S(1)}, bf16[256,512]{1,0:T(8,128)(2,1)S(1)}, u32[]{:S(2)}, u32[]{:S(2)}) collective-permute-start(bf16[256,512]{1,0:T(8,128)(2,1)S(1)} %get-tuple-element.106), channel_id=1, source_target_pairs={{0,7},{1,6},{2,5},{3,4},{4,3},{5,2},{6,1},{7,0},{8,15},{9,14},{10,... | collective-permute-start | bytes 786440 | tf_op jit(solution)/shard_map/ppermute | solution.py:283
  455.4 1.3 copy-start.3
Sparse Core Ops, SparseCore 0:
  16.3 89.0 reduce-scatter.4
  108.8 117.4 reduce-scatter.2
  365.6 109.3 all-gather.4
  476.7 87.5 all-gather.2

commit v4 on v2

--- a/solution.py
+++ b/solution.py
@@ -25,7 +25,9 @@
 def dot3(a, b):
     a_high, a_low = split(a)
     b_high, b_low = split(b)
-    return mm(a_high, b_high) + (mm(a_high, b_low) + mm(a_low, b_high))
+    return mm(
+        jnp.concatenate([a_high, a_high, a_low], axis=1), jnp.concatenate([b_high, b_low, b_high], axis=0)
+    )
 
 
 def fourth_kernel(left_ref, right_ref, left_out, right_out):
@@ -59,57 +61,59 @@
 
 
 def pack_kernel(ranks, inner, place_ref, grads_ref, out_ref):
-    rows = grads_ref.shape[2]
     d = pl.program_id(0)
     for k in range(ranks):
         for e in range(inner):
-            at = (k * inner + e) * rows
-            out_ref[at : at + rows] = grads_ref[slab_of(k, e, d, place_ref[1], inner), 0]
-
-
-def pack(ranks, inner, slot, per, place, grads):
+            slab = slab_of(k, e, d ^ place_ref[0], place_ref[1], inner)
+            out_ref[0, 0, k * inner + e] = grads_ref[slab, 0]
+
+
+def pack(ranks, inner, slots, per, place, grads):
+    first, count = slots
     slabs, order, width = grads.shape
     owners, rows = slabs // per, order // ranks
-    return pl.pallas_call(
+    packed = pl.pallas_call(
         functools.partial(pack_kernel, ranks, inner),
-        grid=(ranks,),
+        grid=(ranks, count),
         in_specs=[
             pl.BlockSpec(memory_space=pltpu.SMEM),
-            pl.BlockSpec((owners, 1, rows, width), lambda d: (0, slot, d, 0)),
+            pl.BlockSpec((owners, 1, rows, width), lambda d, s: (0, first + s, d, 0)),
         ],
-        out_specs=pl.BlockSpec((owners * rows, width), lambda d: (d, 0)),
-        out_shape=jax.ShapeDtypeStruct((owners * order, width), grads.dtype),
+        out_specs=pl.BlockSpec((1, 1, owners, rows, width), lambda d, s: (d, s, 0, 0, 0)),
+        out_shape=jax.ShapeDtypeStruct((ranks, count, owners, rows, width), grads.dtype),
         compiler_params=pltpu.CompilerParams(vmem_limit_bytes=VMEM_LIMIT),
         cost_estimate=pl.CostEstimate(
-            flops=0, bytes_accessed=4 * owners * order * width, transcendentals=0
+            flops=0, bytes_accessed=4 * owners * count * order * width, transcendentals=0
         ),
         name="pack_slabs",
     )(place, grads.reshape(owners, per, order, width))
+    return packed.reshape(-1, width)
 
 
 def unpack_kernel(ranks, inner, place_ref, got_ref, *rest):
     out_ref = rest[-1]
-    rows = out_ref.shape[2]
     for k in range(ranks):
         for e in range(inner):
-            at = (k * inner + e) * rows
-            out_ref[slab_of(k, e, place_ref[0], place_ref[1], inner), 0] = got_ref[at : at + rows]
-
-
-def unpack(ranks, inner, slot, per, place, got, so_far):
-    order = got.shape[0] // (ranks * inner)
-    width, owners, rows = got.shape[1], ranks * inner, order // ranks
-    operands = [place, got] + ([] if so_far is None else [so_far])
+            slab = slab_of(k, e, place_ref[0], place_ref[1], inner)
+            out_ref[slab, 0] = got_ref[0, 0, k * inner + e]
+
+
+def unpack(ranks, inner, slots, per, place, got, so_far):
+    first, count = slots
+    width, owners = got.shape[1], ranks * inner
+    rows = got.shape[0] // (ranks * owners * count)
+    operands = [place, got.reshape(ranks, count, owners, rows, width)]
+    operands += [] if so_far is None else [so_far]
     return pl.pallas_call(
         functools.partial(unpack_kernel, ranks, inner),
-        grid=(ranks,),
+        grid=(ranks, count),
         in_specs=[
             pl.BlockSpec(memory_space=pltpu.SMEM),
-            pl.BlockSpec((owners * rows, width), lambda d: (d, 0)),
+            pl.BlockSpec((1, 1, owners, rows, width), lambda d, s: (d, s, 0, 0, 0)),
         ]
         + [pl.BlockSpec(memory_space=pl.ANY)] * (len(operands) - 2),
-        out_specs=pl.BlockSpec((owners, 1, rows, width), lambda d: (0, slot, d, 0)),
-        out_shape=jax.ShapeDtypeStruct((owners, per, order, width), got.dtype),
+        out_specs=pl.BlockSpec((owners, 1, rows, width), lambda d, s: (0, first + s, d, 0)),
+        out_shape=jax.ShapeDtypeStruct((owners, per, ranks * rows, width), got.dtype),
         input_output_aliases={} if so_far is None else {2: 0},
         compiler_params=pltpu.CompilerParams(vmem_limit_bytes=VMEM_LIMIT),
         cost_estimate=pl.CostEstimate(flops=0, bytes_accessed=4 * got.size, transcendentals=0),
@@ -177,7 +181,7 @@
     def _():
         for k in range(ranks):
             for e in range(inner):
-                blocks[spot(outer_place ^ k, inner_place ^ e)] = pieces[k * inner + e][...]
+                blocks[spot(place_ref[2] ^ outer_place ^ k, inner_place ^ e)] = pieces[k * inner + e][...]
 
     block = blocks[step]
     turned = block.T
@@ -199,18 +203,18 @@
 def precondition(ranks, inner, slot, place, pieces, stats_and_roots):
     _, col_blocks, order, _ = stats_and_roots[0].shape
     rows, width = pieces[0].shape
-    count = ranks * inner
+    owners = ranks * inner
     piece = pl.BlockSpec((rows, width), lambda j: (0, 0))
     strip = pl.BlockSpec((inner * rows, width), lambda j: (0, 0))
     matrix = pl.BlockSpec((1, 1, order, order), lambda j: (slot, j, 0, 0))
     return pl.pallas_call(
         functools.partial(block_kernel, ranks, inner, col_blocks),
         grid=(col_blocks,),
-        in_specs=[pl.BlockSpec(memory_space=pltpu.SMEM)] + [piece] * count + [matrix] * 6,
+        in_specs=[pl.BlockSpec(memory_space=pltpu.SMEM)] + [piece] * owners + [matrix] * 6,
         out_specs=[strip] * ranks,
         out_shape=[jax.ShapeDtypeStruct((inner * rows, width), jnp.bfloat16)] * ranks,
         scratch_shapes=[pltpu.VMEM((col_blocks, order, order), jnp.bfloat16)] * 2,
-        compiler_params=pltpu.CompilerParams(vmem_limit_bytes=VMEM_LIMIT),
+        compiler_params=pltpu.CompilerParams(vmem_limit_bytes=VMEM_LIMIT * 9 // 10),
         cost_estimate=pl.CostEstimate(
             flops=col_blocks * 19 * 2 * order**3,
             bytes_accessed=col_blocks * 28 * order**2,
@@ -235,7 +239,7 @@
 
     sources = [(d, a, b) for d in range(ranks) for a in range(ranks) for b in range(inner)]
     to_owner = {
-        (k, e): [(number(d, a, b), number(a, d ^ k, b ^ e)) for d, a, b in sources] for k, e in rounds
+        (k, e): [(number(d, a, b), number(a, d ^ a ^ k, b ^ e)) for d, a, b in sources] for k, e in rounds
     }
     to_row = [[(d, d ^ k) for d in range(ranks)] for k in range(ranks)]
     to_column = {
@@ -243,27 +247,57 @@
         for m, e in rounds
     }
 
+    half = max(per // 2, 1)
+    groups = [(first, min(half, per - first)) for first in range(0, per, half)]
     summed = []
-    for slot in range(per):
-        packed = pack(ranks, inner, slot, per, place, grads)
+    for slots in groups:
+        packed = pack(ranks, inner, slots, per, place, grads)
         summed.append(lax.psum_scatter(packed, "dp", scatter_dimension=0, tiled=True))
     left_fourth, right_fourth = fourth_powers(left_root, right_root)
     summed[0], left_fourth, right_fourth = lax.optimization_barrier((summed[0], left_fourth, right_fourth))
     matrices = (left_stats, right_stats, left_root, right_root, left_fourth, right_fourth)
-    out = None
-    for slot in range(per):
-        arrived = [
-            lax.ppermute(summed[slot][at * rows : (at + 1) * rows], MESH_AXES, to_owner[key])
-            for at, key in enumerate(rounds)
-        ]
-        strips = precondition(ranks, inner, slot, place, arrived, matrices)
-        strips = [strips[0]] + [lax.ppermute(strips[k], "dp", to_row[k]) for k in range(1, ranks)]
-        routed = route(ranks, inner, place, strips)
-        back = [routed[0]] + [
+
+    piece_count = len(rounds)
+
+    def send_in(slot):
+        g, s = divmod(slot, half)
+        pieces = summed[g].reshape(-1, rows, width)[s * piece_count : (s + 1) * piece_count]
+        return [lax.ppermute(pieces[at], MESH_AXES, to_owner[key]) for at, key in enumerate(rounds)]
+
+    def work(slot, arrived):
+        return precondition(ranks, inner, slot, place, arrived, matrices)
+
+    def send_rows(slot, strips):
+        return [strips[0]] + [lax.ppermute(strips[k], "dp", to_row[k]) for k in range(1, ranks)]
+
+    def send_columns(slot, moved):
+        routed = route(ranks, inner, place, moved)
+        return [routed[0]] + [
             lax.ppermute(piece, "fsdp", to_column[key]) for piece, key in zip(routed[1:], rounds[1:])
         ]
-        gathered = lax.all_gather(jnp.concatenate(back, axis=0), "dp", axis=0, tiled=True)
-        out = unpack(ranks, inner, slot, per, place, gathered, out)
+
+    stages = (send_in, work, send_rows, send_columns)
+    begins = [slot + (slot // half) * (len(stages) - 1) for slot in range(per)]
+    held = {}
+    out = None
+    for tick in range(begins[-1] + len(stages)):
+        now = {}
+        for slot, begin in enumerate(begins):
+            stage = tick - begin
+            if stage == 0:
+                now[slot] = send_in(slot)
+            elif 0 < stage < len(stages):
+                now[slot] = stages[stage](slot, held[slot])
+        wanted = [begins.index(tick + 1) // half] if tick + 1 in begins else []
+        now, ahead = lax.optimization_barrier((now, [summed[g] for g in wanted]))
+        for g, value in zip(wanted, ahead):
+            summed[g] = value
+        held.update(now)
+        for g, (first, count) in enumerate(groups):
+            if begins[first + count - 1] + len(stages) - 1 == tick:
+                back = [piece for slot in range(first, first + count) for piece in held[slot]]
+                gathered = lax.all_gather(jnp.concatenate(back, axis=0), "dp", axis=0, tiled=True)
+                out = unpack(ranks, inner, (first, count), per, place, gathered, out)
     return out.reshape(grads.shape)
 
 

time: 565 us -> 552 us (0.977)
  starting transfers between devices: 185 us -> 160 us
  waiting for transfers between devices: 206 us -> 229 us
  local copies, waits for them, and re-layouts: 18.8 us -> 9.95 us
    ppermute x72, waiting for transfers between devices: 153 us -> 98.8 us  [the longest x28 61.2 us: send_columns(): lax.ppermute(piece, 'fsdp', to_column[key])]
    reduce_scatter x4 -> x2, waiting for transfers between devices: 9.53 us -> 48.8 us  [shards(): lax.psum_scatter(packed, 'dp', scatter_dimension=0, tiled=True)]
    all_gather x4 -> x2, waiting for transfers between devices: 42.9 us -> 81.2 us  [shards(): lax.all_gather(jnp.concatenate(back, axis=0), 'dp', axis=0, tiled=True)]
    ppermute x72, starting transfers between devices: 185 us -> 160 us  [the longest x32 95.3 us: send_in(): lax.ppermute(pieces[at], MESH_AXES, to_owner[key])]
    unnamed x116 -> x114, local copies, waits for them, and re-layouts: 13.3 us -> 5.9 us
    pallas_call x4 -> x2, Pallas kernels: 19.2 us -> 18.1 us  [unpack(): pl.pallas_call(functools.partial(unpack_kernel, ranks, inner), grid=(rank...]
    pallas_call x4 -> x2, Pallas kernels: 19.2 us -> 18.1 us  [pack(): pl.pallas_call(functools.partial(pack_kernel, ranks, inner), grid=(ranks,...]
  transfers between devices with their start and end apart: 80 -> 76, of which waited for: 35 -> 28; matrix products, arithmetic and copies ran while one was open for 1% -> 1% of each run, Pallas kernels for 23% -> 21%
where the time goes in v4:
time: 552 us; the launch traced here: 550 us
  waiting for transfers between devices  229 us (41%)
  starting transfers between devices  160 us (29%)
  Pallas kernels  136 us (25%)
  between operations  14.3 us (3%)
  local copies, waits for them, and re-layouts  9.95 us (2%)
    ppermute x32, starting transfers between devices, send_in(): lax.ppermute(pieces[at], MESH_AXES, to_owner[key])  95.3 us
    all_gather x2, waiting for transfers between devices, shards(): lax.all_gather(jnp.concatenate(back, axis=0), 'dp', axis=0, tiled=True)  81.2 us
    pallas_call x4, Pallas kernels, precondition(): pl.pallas_call(functools.partial(block_kernel, ranks, inner, col_blocks),...  66 us
    ppermute x28, waiting for transfers between devices, send_columns(): lax.ppermute(piece, 'fsdp', to_column[key])  61.2 us
    reduce_scatter x2, waiting for transfers between devices, shards(): lax.psum_scatter(packed, 'dp', scatter_dimension=0, tiled=True)  48.8 us
    ppermute x28, starting transfers between devices, send_columns(): lax.ppermute(piece, 'fsdp', to_column[key])  40.3 us
    pallas_call x1, Pallas kernels, fourth_powers(): pl.pallas_call(fourth_kernel, grid=(slabs, col_blocks), in_specs=[spec, s...  31.3 us
    ppermute x12, starting transfers between devices, send_rows(): lax.ppermute(strips[k], 'dp', to_row[k])  24.5 us
  transfers between devices with their start and end apart: 76, of which 28 were waited for; matrix products, arithmetic and copies ran while one was open for 1% of the time, Pallas kernels for 21%

profile of v4, /device:TPU:0, one launch (start us, length us, event | category | flops | bytes accessed | tf_op | source)
XLA Modules:
  0.0 550.4 jit_solution(7740225207890171324)
XLA Ops:
  7.2 9.1 %pack_slabs.2 = bf16[4,2,8,128,512]{4,3,2,1,0:T(8,128)(2,1)} custom-call(s32[3]{0:T(128)} %pad_add_fusion.place_ref, bf16[8,4,512,512]{3,2,1,0:T(8,128)(2,1)} %bitcast.9), custom_call_target="tpu_custom_call" | custom-call | bytes 16777216 | tf_op jit(solution)/shard_map/pack_slabs/pallas_call | solution.py:75
  16.3 9.0 %pack_slabs.3 = bf16[4,2,8,128,512]{4,3,2,1,0:T(8,128)(2,1)} custom-call(s32[3]{0:T(128)} %pad_add_fusion.place_ref, bf16[8,4,512,512]{3,2,1,0:T(8,128)(2,1)} %bitcast.10), custom_call_target="tpu_custom_call" | custom-call | bytes 16777216 | tf_op jit(solution)/shard_map/pack_slabs/pallas_call | solution.py:75
  25.4 31.3 %fourth_powers.1 = (f32[4,2,512,512]{3,2,1,0:T(8,128)}, f32[4,2,512,512]{3,2,1,0:T(8,128)}) custom-call(f32[4,2,512,512]{3,2,1,0:T(8,128)} %refs_10_.7, f32[4,2,512,512]{3,2,1,0:T(8,128)} %refs_11_.7), custom_call_target="tpu_custom_call" | custom-call | flops 25769803776 | bytes 33554432 | tf_op jit(solution)/shard_map/fourth_powers/pallas_call | solution.py:45
  56.8 48.8 %reduce-scatter.3.cloned.1.call-done = bf16[2048,512]{1,0:T(8,128)(2,1)} async-done(((bf16[8192,512]{1,0:T(8,128)(2,1)}), bf16[2048,512]{1,0:T(8,128)(2,1)}) %reduce-scatter.3.cloned.1.call-update) | async-done | bytes 2097168 | tf_op jit(solution)/shard_map/reduce_scatter | solution.py:255
  107.0 2.8 collective-permute-start.7
  109.8 3.3 collective-permute-start.6
  113.7 4.3 collective-permute-start.4
  119.9 7.9 %collective-permute-start.2 = (bf16[128,512]{1,0:T(8,128)(2,1)S(1)}, bf16[128,512]{1,0:T(8,128)(2,1)S(1)}, u32[]{:S(2)}, u32[]{:S(2)}) collective-permute-start(bf16[128,512]{1,0:T(8,128)(2,1)S(1)} %get-tuple-element.338), channel_id=1, source_target_pairs={{0,2},{1,3},{2,8},{3,9},{4,22},{5,23},{6,28},{7,29},{8,0},{9,1},{1... | collective-permute-start | bytes 393224 | tf_op jit(solution)/shard_map/ppermute | solution.py:265
  131.4 6.5 %collective-permute-done.2.refs_2_ = bf16[128,512]{1,0:T(8,128)(2,1)S(1)} collective-permute-done((bf16[128,512]{1,0:T(8,128)(2,1)S(1)}, bf16[128,512]{1,0:T(8,128)(2,1)S(1)}, u32[]{:S(2)}, u32[]{:S(2)}) %collective-permute-start.2) | collective-permute-done | bytes 131104 | tf_op jit(solution)/shard_map/ppermute | solution.py:265
  138.0 6.6 %collective-permute-start.15 = (bf16[128,512]{1,0:T(8,128)(2,1)S(1)}, bf16[128,512]{1,0:T(8,128)(2,1)S(1)}, u32[]{:S(2)}, u32[]{:S(2)}) collective-permute-start(bf16[128,512]{1,0:T(8,128)(2,1)S(1)} %get-tuple-element.325), channel_id=1, source_target_pairs={{0,7},{1,6},{2,13},{3,12},{4,19},{5,18},{6,25},{7,24},{8,5},{9,4},... | collective-permute-start | bytes 393224 | tf_op jit(solution)/shard_map/ppermute | solution.py:265
  146.9 5.6 %collective-permute-start.13 = (bf16[128,512]{1,0:T(8,128)(2,1)S(1)}, bf16[128,512]{1,0:T(8,128)(2,1)S(1)}, u32[]{:S(2)}, u32[]{:S(2)}) collective-permute-start(bf16[128,512]{1,0:T(8,128)(2,1)S(1)} %get-tuple-element.327), channel_id=1, source_target_pairs={{0,5},{1,4},{2,15},{3,14},{4,17},{5,16},{6,27},{7,26},{8,7},{9,6},... | collective-permute-start | bytes 393224 | tf_op jit(solution)/shard_map/ppermute | solution.py:265
  152.5 7.4 %collective-permute-start.12 = (bf16[128,512]{1,0:T(8,128)(2,1)S(1)}, bf16[128,512]{1,0:T(8,128)(2,1)S(1)}, u32[]{:S(2)}, u32[]{:S(2)}) collective-permute-start(bf16[128,512]{1,0:T(8,128)(2,1)S(1)} %get-tuple-element.328), channel_id=1, source_target_pairs={{0,4},{1,5},{2,14},{3,15},{4,16},{5,17},{6,26},{7,27},{8,6},{9,7},... | collective-permute-start | bytes 393224 | tf_op jit(solution)/shard_map/ppermute | solution.py:265
  159.9 5.3 collective-permute-start.10
  166.7 16.4 %precondition.4 = (bf16[256,512]{1,0:T(8,128)(2,1)}, bf16[256,512]{1,0:T(8,128)(2,1)}, bf16[256,512]{1,0:T(8,128)(2,1)}, bf16[256,512]{1,0:T(8,128)(2,1)}) custom-call(s32[3]{0:T(128)} %pad_add_fusion.place_ref, bf16[128,512]{1,0:T(8,128)(2,1)} %copy-done.29, bf16[128,512]{1,0:T(8,128)(2,1)} %copy-done.22, bf16[128,512]{1,0:T(8,128)(2,1)} %copy-done.20, ...), custom_call_target="tpu_custom_call" | custom-call | flops 10200547328 | bytes 14680064 | tf_op jit(solution)/shard_map/precondition/pallas_call | solution.py:210
  183.2 5.8 %collective-permute-start.16 = (bf16[256,512]{1,0:T(8,128)(2,1)}, bf16[256,512]{1,0:T(8,128)(2,1)S(1)}, u32[]{:S(2)}, u32[]{:S(2)}) collective-permute-start(bf16[256,512]{1,0:T(8,128)(2,1)} %get-tuple-element.176), channel_id=1, source_target_pairs={{0,8},{8,0},{16,24},{24,16},{1,9},{9,1},{17,25},{25,17},{2,10},{10... | collective-permute-start | bytes 786440 | tf_op jit(solution)/shard_map/ppermute | solution.py:271
  189.0 4.9 collective-permute-start.17
  195.4 16.6 %precondition.5 = (bf16[256,512]{1,0:T(8,128)(2,1)}, bf16[256,512]{1,0:T(8,128)(2,1)}, bf16[256,512]{1,0:T(8,128)(2,1)}, bf16[256,512]{1,0:T(8,128)(2,1)}) custom-call(s32[3]{0:T(128)} %pad_add_fusion.place_ref, bf16[128,512]{1,0:T(8,128)(2,1)} %copy-done.41, bf16[128,512]{1,0:T(8,128)(2,1)} %copy-done.39, bf16[128,512]{1,0:T(8,128)(2,1)} %copy-done.37, ...), custom_call_target="tpu_custom_call" | custom-call | flops 10200547328 | bytes 14680064 | tf_op jit(solution)/shard_map/precondition/pallas_call | solution.py:210
  212.0 6.7 %collective-permute-done.18.refs_3_ = bf16[256,512]{1,0:T(8,128)(2,1)S(1)} collective-permute-done((bf16[256,512]{1,0:T(8,128)(2,1)}, bf16[256,512]{1,0:T(8,128)(2,1)S(1)}, u32[]{:S(2)}, u32[]{:S(2)}) %collective-permute-start.18) | collective-permute-done | bytes 262176 | tf_op jit(solution)/shard_map/ppermute | solution.py:271
  219.4 4.3 collective-permute-start.20
  226.7 4.9 collective-permute-done.20
  246.3 4.2 collective-permute-start.29
  256.4 4.4 collective-permute-done.30
  262.0 10.7 %collective-permute-done.33 = bf16[128,512]{1,0:T(8,128)(2,1)S(1)} collective-permute-done((bf16[128,512]{1,0:T(8,128)(2,1)S(1)}, bf16[128,512]{1,0:T(8,128)(2,1)S(1)}, u32[]{:S(2)}, u32[]{:S(2)}) %collective-permute-start.33) | collective-permute-done | bytes 131104 | tf_op jit(solution)/shard_map/ppermute | solution.py:276
  279.1 3.5 collective-permute-start.42
  282.6 3.1 collective-permute-start.41
  285.7 6.6 %collective-permute-start.40 = (bf16[128,512]{1,0:T(8,128)(2,1)S(1)}, bf16[128,512]{1,0:T(8,128)(2,1)S(1)}, u32[]{:S(2)}, u32[]{:S(2)}) collective-permute-start(bf16[128,512]{1,0:T(8,128)(2,1)S(1)} %get-tuple-element.320), channel_id=1, source_target_pairs={{0,4},{1,5},{2,14},{3,15},{4,16},{5,17},{6,26},{7,27},{8,6},{9,7},... | collective-permute-start | bytes 393224 | tf_op jit(solution)/shard_map/ppermute | solution.py:265
  292.3 3.1 collective-permute-start.38
  296.3 3.1 collective-permute-done.40.refs_4_
  299.4 5.5 collective-permute-done.39.refs_3_
  304.9 5.9 %collective-permute-done.38.refs_2_ = bf16[128,512]{1,0:T(8,128)(2,1)S(1)} collective-permute-done((bf16[128,512]{1,0:T(8,128)(2,1)S(1)}, bf16[128,512]{1,0:T(8,128)(2,1)S(1)}, u32[]{:S(2)}, u32[]{:S(2)}) %collective-permute-start.38) | collective-permute-done | bytes 131104 | tf_op jit(solution)/shard_map/ppermute | solution.py:265
  310.9 5.6 %collective-permute-start.51 = (bf16[128,512]{1,0:T(8,128)(2,1)S(1)}, bf16[128,512]{1,0:T(8,128)(2,1)S(1)}, u32[]{:S(2)}, u32[]{:S(2)}) collective-permute-start(bf16[128,512]{1,0:T(8,128)(2,1)S(1)} %get-tuple-element.309), channel_id=1, source_target_pairs={{0,7},{1,6},{2,13},{3,12},{4,19},{5,18},{6,25},{7,24},{8,5},{9,4},... | collective-permute-start | bytes 393224 | tf_op jit(solution)/shard_map/ppermute | solution.py:265
  318.8 5.0 collective-permute-start.49
  323.8 7.5 %collective-permute-start.48 = (bf16[128,512]{1,0:T(8,128)(2,1)S(1)}, bf16[128,512]{1,0:T(8,128)(2,1)S(1)}, u32[]{:S(2)}, u32[]{:S(2)}) collective-permute-start(bf16[128,512]{1,0:T(8,128)(2,1)S(1)} %get-tuple-element.312), channel_id=1, source_target_pairs={{0,4},{1,5},{2,14},{3,15},{4,16},{5,17},{6,26},{7,27},{8,6},{9,7},... | collective-permute-start | bytes 393224 | tf_op jit(solution)/shard_map/ppermute | solution.py:265
  331.3 5.0 collective-permute-start.46
  337.7 16.4 %precondition.6 = (bf16[256,512]{1,0:T(8,128)(2,1)}, bf16[256,512]{1,0:T(8,128)(2,1)}, bf16[256,512]{1,0:T(8,128)(2,1)}, bf16[256,512]{1,0:T(8,128)(2,1)}) custom-call(s32[3]{0:T(128)} %pad_add_fusion.place_ref, bf16[128,512]{1,0:T(8,128)(2,1)} %copy-done.30, bf16[128,512]{1,0:T(8,128)(2,1)} %copy-done.23, bf16[128,512]{1,0:T(8,128)(2,1)} %copy-done.21, ...), custom_call_target="tpu_custom_call" | custom-call | flops 10200547328 | bytes 14680064 | tf_op jit(solution)/shard_map/precondition/pallas_call | solution.py:210
  354.3 5.7 %collective-permute-start.52 = (bf16[256,512]{1,0:T(8,128)(2,1)}, bf16[256,512]{1,0:T(8,128)(2,1)S(1)}, u32[]{:S(2)}, u32[]{:S(2)}) collective-permute-start(bf16[256,512]{1,0:T(8,128)(2,1)} %get-tuple-element.234), channel_id=1, source_target_pairs={{0,8},{8,0},{16,24},{24,16},{1,9},{9,1},{17,25},{25,17},{2,10},{10... | collective-permute-start | bytes 786440 | tf_op jit(solution)/shard_map/ppermute | solution.py:271
  360.0 4.7 collective-permute-start.53
  366.1 16.6 %precondition.7 = (bf16[256,512]{1,0:T(8,128)(2,1)}, bf16[256,512]{1,0:T(8,128)(2,1)}, bf16[256,512]{1,0:T(8,128)(2,1)}, bf16[256,512]{1,0:T(8,128)(2,1)}) custom-call(s32[3]{0:T(128)} %pad_add_fusion.place_ref, bf16[128,512]{1,0:T(8,128)(2,1)} %copy-done.40, bf16[128,512]{1,0:T(8,128)(2,1)} %copy-done.38, bf16[128,512]{1,0:T(8,128)(2,1)} %copy-done.36, ...), custom_call_target="tpu_custom_call" | custom-call | flops 10200547328 | bytes 14680064 | tf_op jit(solution)/shard_map/precondition/pallas_call | solution.py:210
  382.7 6.7 %collective-permute-done.54.refs_3_ = bf16[256,512]{1,0:T(8,128)(2,1)S(1)} collective-permute-done((bf16[256,512]{1,0:T(8,128)(2,1)}, bf16[256,512]{1,0:T(8,128)(2,1)S(1)}, u32[]{:S(2)}, u32[]{:S(2)}) %collective-permute-start.54) | collective-permute-done | bytes 262176 | tf_op jit(solution)/shard_map/ppermute | solution.py:271
  390.1 4.8 collective-permute-start.56
  397.6 4.9 collective-permute-done.56
  411.2 4.4 collective-permute-done.60
  420.3 3.0 collective-permute-start.66
  427.6 3.9 collective-permute-done.66
  433.6 9.4 %collective-permute-done.69 = bf16[128,512]{1,0:T(8,128)(2,1)S(1)} collective-permute-done((bf16[128,512]{1,0:T(8,128)(2,1)S(1)}, bf16[128,512]{1,0:T(8,128)(2,1)S(1)}, u32[]{:S(2)}, u32[]{:S(2)}) %collective-permute-start.69) | collective-permute-done | bytes 131104 | tf_op jit(solution)/shard_map/ppermute | solution.py:276
  444.6 9.0 %unpack_slabs.2.rest_0_ = bf16[8,4,512,512]{3,2,1,0:T(8,128)(2,1)} custom-call(s32[3]{0:T(128)} %pad_add_fusion.place_ref, bf16[4,2,8,128,512]{4,3,2,1,0:T(8,128)(2,1)} %bitcast.13), custom_call_target="tpu_custom_call" | custom-call | bytes 16777216 | tf_op jit(solution)/shard_map/unpack_slabs/pallas_call | solution.py:107
  453.6 81.2 %all-gather.3.cloned.1.call-done = bf16[8192,512]{1,0:T(8,128)(2,1)} async-done(((bf16[2048,512]{1,0:T(8,128)(2,1)}), bf16[8192,512]{1,0:T(8,128)(2,1)}) %all-gather.3.cloned.1.call-update) | async-done | bytes 8388624 | tf_op jit(solution)/shard_map/all_gather | solution.py:299
  534.8 9.0 %unpack_slabs.3 = bf16[8,4,512,512]{3,2,1,0:T(8,128)(2,1)} custom-call(s32[3]{0:T(128)} %pad_add_fusion.place_ref, bf16[4,2,8,128,512]{4,3,2,1,0:T(8,128)(2,1)} %bitcast.14, bf16[8,4,512,512]{3,2,1,0:T(8,128)(2,1)} %unpack_slabs.2.rest_0_), custom_call_target="tpu_custom_call", output_to_operand_aliasing={{}: (2, {})} | custom-call | bytes 16777216 | tf_op jit(solution)/shard_map/unpack_slabs/pallas_call | solution.py:107
  (242 shorter events, 75.7 us)
Async XLA Ops:
  6.5 99.0 %reduce-scatter.3.cloned.1.call-start = ((), (), s32[]{:S(2)}) async-start(), calls=%async_computation.2 | async-start | bytes 10485760 | tf_op jit(solution)/shard_map/reduce_scatter | solution.py:255
  16.3 244.6 %reduce-scatter.5.cloned.1.call-start = ((), (), s32[]{:S(2)}) async-start(), calls=%async_computation.3 | async-start | bytes 10485760 | tf_op jit(solution)/shard_map/reduce_scatter | solution.py:255
  25.4 419.2 %all-gather.5.cloned.1.call-start = ((), (), s32[]{:S(2)}) async-start(), calls=%async_computation.5 | async-start | bytes 10485760 | tf_op jit(solution)/shard_map/all_gather | solution.py:299
  109.8 18.1 %collective-permute-start.6 = (bf16[128,512]{1,0:T(8,128)(2,1)S(1)}, bf16[128,512]{1,0:T(8,128)(2,1)S(1)}, u32[]{:S(2)}, u32[]{:S(2)}) collective-permute-start(bf16[128,512]{1,0:T(8,128)(2,1)S(1)} %get-tuple-element.334), channel_id=1, source_target_pairs={{0,6},{1,7},{2,12},{3,13},{4,18},{5,19},{6,24},{7,25},{8,4},{9,5},... | collective-permute-start | bytes 393224 | tf_op jit(solution)/shard_map/ppermute | solution.py:265
  113.1 14.9 %collective-permute-start.5 = (bf16[128,512]{1,0:T(8,128)(2,1)S(1)}, bf16[128,512]{1,0:T(8,128)(2,1)S(1)}, u32[]{:S(2)}, u32[]{:S(2)}) collective-permute-start(bf16[128,512]{1,0:T(8,128)(2,1)S(1)} %get-tuple-element.335), channel_id=1, source_target_pairs={{0,5},{1,4},{2,15},{3,14},{4,17},{5,16},{6,27},{7,26},{8,7},{9,6},... | collective-permute-start | bytes 393224 | tf_op jit(solution)/shard_map/ppermute | solution.py:265
  113.7 16.2 %collective-permute-start.4 = (bf16[128,512]{1,0:T(8,128)(2,1)S(1)}, bf16[128,512]{1,0:T(8,128)(2,1)S(1)}, u32[]{:S(2)}, u32[]{:S(2)}) collective-permute-start(bf16[128,512]{1,0:T(8,128)(2,1)S(1)} %get-tuple-element.336), channel_id=1, source_target_pairs={{0,4},{1,5},{2,14},{3,15},{4,16},{5,17},{6,26},{7,27},{8,6},{9,7},... | collective-permute-start | bytes 393224 | tf_op jit(solution)/shard_map/ppermute | solution.py:265
  118.0 13.4 %collective-permute-start.3 = (bf16[128,512]{1,0:T(8,128)(2,1)S(1)}, bf16[128,512]{1,0:T(8,128)(2,1)S(1)}, u32[]{:S(2)}, u32[]{:S(2)}) collective-permute-start(bf16[128,512]{1,0:T(8,128)(2,1)S(1)} %get-tuple-element.337), channel_id=1, source_target_pairs={{0,3},{1,2},{2,9},{3,8},{4,23},{5,22},{6,29},{7,28},{8,1},{9,0},{1... | collective-permute-start | bytes 393224 | tf_op jit(solution)/shard_map/ppermute | solution.py:265
  119.9 18.0 %collective-permute-start.2 = (bf16[128,512]{1,0:T(8,128)(2,1)S(1)}, bf16[128,512]{1,0:T(8,128)(2,1)S(1)}, u32[]{:S(2)}, u32[]{:S(2)}) collective-permute-start(bf16[128,512]{1,0:T(8,128)(2,1)S(1)} %get-tuple-element.338), channel_id=1, source_target_pairs={{0,2},{1,3},{2,8},{3,9},{4,22},{5,23},{6,28},{7,29},{8,0},{9,1},{1... | collective-permute-start | bytes 393224 | tf_op jit(solution)/shard_map/ppermute | solution.py:265
  138.0 21.9 %collective-permute-start.15 = (bf16[128,512]{1,0:T(8,128)(2,1)S(1)}, bf16[128,512]{1,0:T(8,128)(2,1)S(1)}, u32[]{:S(2)}, u32[]{:S(2)}) collective-permute-start(bf16[128,512]{1,0:T(8,128)(2,1)S(1)} %get-tuple-element.325), channel_id=1, source_target_pairs={{0,7},{1,6},{2,13},{3,12},{4,19},{5,18},{6,25},{7,24},{8,5},{9,4},... | collective-permute-start | bytes 393224 | tf_op jit(solution)/shard_map/ppermute | solution.py:265
  144.6 20.6 %collective-permute-start.14 = (bf16[128,512]{1,0:T(8,128)(2,1)S(1)}, bf16[128,512]{1,0:T(8,128)(2,1)S(1)}, u32[]{:S(2)}, u32[]{:S(2)}) collective-permute-start(bf16[128,512]{1,0:T(8,128)(2,1)S(1)} %get-tuple-element.326), channel_id=1, source_target_pairs={{0,6},{1,7},{2,12},{3,13},{4,18},{5,19},{6,24},{7,25},{8,4},{9,5},... | collective-permute-start | bytes 393224 | tf_op jit(solution)/shard_map/ppermute | solution.py:265
  146.9 18.9 %collective-permute-start.13 = (bf16[128,512]{1,0:T(8,128)(2,1)S(1)}, bf16[128,512]{1,0:T(8,128)(2,1)S(1)}, u32[]{:S(2)}, u32[]{:S(2)}) collective-permute-start(bf16[128,512]{1,0:T(8,128)(2,1)S(1)} %get-tuple-element.327), channel_id=1, source_target_pairs={{0,5},{1,4},{2,15},{3,14},{4,17},{5,16},{6,27},{7,26},{8,7},{9,6},... | collective-permute-start | bytes 393224 | tf_op jit(solution)/shard_map/ppermute | solution.py:265
  152.5 30.7 %collective-permute-start.12 = (bf16[128,512]{1,0:T(8,128)(2,1)S(1)}, bf16[128,512]{1,0:T(8,128)(2,1)S(1)}, u32[]{:S(2)}, u32[]{:S(2)}) collective-permute-start(bf16[128,512]{1,0:T(8,128)(2,1)S(1)} %get-tuple-element.328), channel_id=1, source_target_pairs={{0,4},{1,5},{2,14},{3,15},{4,16},{5,17},{6,26},{7,27},{8,6},{9,7},... | collective-permute-start | bytes 393224 | tf_op jit(solution)/shard_map/ppermute | solution.py:265
  159.8 23.3 %collective-permute-start.11 = (bf16[128,512]{1,0:T(8,128)(2,1)S(1)}, bf16[128,512]{1,0:T(8,128)(2,1)S(1)}, u32[]{:S(2)}, u32[]{:S(2)}) collective-permute-start(bf16[128,512]{1,0:T(8,128)(2,1)S(1)} %get-tuple-element.329), channel_id=1, source_target_pairs={{0,3},{1,2},{2,9},{3,8},{4,23},{5,22},{6,29},{7,28},{8,1},{9,0},{1... | collective-permute-start | bytes 393224 | tf_op jit(solution)/shard_map/ppermute | solution.py:265
  159.9 23.2 %collective-permute-start.10 = (bf16[128,512]{1,0:T(8,128)(2,1)S(1)}, bf16[128,512]{1,0:T(8,128)(2,1)S(1)}, u32[]{:S(2)}, u32[]{:S(2)}) collective-permute-start(bf16[128,512]{1,0:T(8,128)(2,1)S(1)} %get-tuple-element.330), channel_id=1, source_target_pairs={{0,2},{1,3},{2,8},{3,9},{4,22},{5,23},{6,28},{7,29},{8,0},{9,1},{1... | collective-permute-start | bytes 393224 | tf_op jit(solution)/shard_map/ppermute | solution.py:265
  165.2 17.9 %collective-permute-start.9 = (bf16[128,512]{1,0:T(8,128)(2,1)S(1)}, bf16[128,512]{1,0:T(8,128)(2,1)S(1)}, u32[]{:S(2)}, u32[]{:S(2)}) collective-permute-start(bf16[128,512]{1,0:T(8,128)(2,1)S(1)} %get-tuple-element.331), channel_id=1, source_target_pairs={{0,1},{1,0},{2,11},{3,10},{4,21},{5,20},{6,31},{7,30},{8,3},{9,2},... | collective-permute-start | bytes 393224 | tf_op jit(solution)/shard_map/ppermute | solution.py:265
  165.7 17.5 %collective-permute-start.8 = (bf16[128,512]{1,0:T(8,128)(2,1)S(1)}, bf16[128,512]{1,0:T(8,128)(2,1)S(1)}, u32[]{:S(2)}, u32[]{:S(2)}) collective-permute-start(bf16[128,512]{1,0:T(8,128)(2,1)S(1)} %get-tuple-element.332), channel_id=1, source_target_pairs={{0,0},{1,1},{2,10},{3,11},{4,20},{5,21},{6,30},{7,31},{8,2},{9,3},... | collective-permute-start | bytes 393224 | tf_op jit(solution)/shard_map/ppermute | solution.py:265
  183.2 28.7 %collective-permute-start.16 = (bf16[256,512]{1,0:T(8,128)(2,1)}, bf16[256,512]{1,0:T(8,128)(2,1)S(1)}, u32[]{:S(2)}, u32[]{:S(2)}) collective-permute-start(bf16[256,512]{1,0:T(8,128)(2,1)} %get-tuple-element.176), channel_id=1, source_target_pairs={{0,8},{8,0},{16,24},{24,16},{1,9},{9,1},{17,25},{25,17},{2,10},{10... | collective-permute-start | bytes 786440 | tf_op jit(solution)/shard_map/ppermute | solution.py:271
  189.0 23.0 %collective-permute-start.17 = (bf16[256,512]{1,0:T(8,128)(2,1)}, bf16[256,512]{1,0:T(8,128)(2,1)S(1)}, u32[]{:S(2)}, u32[]{:S(2)}) collective-permute-start(bf16[256,512]{1,0:T(8,128)(2,1)} %get-tuple-element.177), channel_id=1, source_target_pairs={{0,16},{8,24},{16,0},{24,8},{1,17},{9,25},{17,1},{25,9},{2,18},{10... | collective-permute-start | bytes 786440 | tf_op jit(solution)/shard_map/ppermute | solution.py:271
  193.9 24.7 %collective-permute-start.18 = (bf16[256,512]{1,0:T(8,128)(2,1)}, bf16[256,512]{1,0:T(8,128)(2,1)S(1)}, u32[]{:S(2)}, u32[]{:S(2)}) collective-permute-start(bf16[256,512]{1,0:T(8,128)(2,1)} %get-tuple-element.178), channel_id=1, source_target_pairs={{0,24},{8,16},{16,8},{24,0},{1,25},{9,17},{17,9},{25,1},{2,26},{10... | collective-permute-start | bytes 786440 | tf_op jit(solution)/shard_map/ppermute | solution.py:271
  224.9 13.1 %collective-permute-start.23 = (bf16[128,512]{1,0:T(8,128)(2,1)S(1)}, bf16[128,512]{1,0:T(8,128)(2,1)S(1)}, u32[]{:S(2)}, u32[]{:S(2)}) collective-permute-start(bf16[128,512]{1,0:T(8,128)(2,1)S(1)} %get-tuple-element.200), channel_id=1, source_target_pairs={{0,5},{1,4},{2,7},{3,6},{4,1},{5,0},{6,3},{7,2},{8,13},{9,12},{10,... | collective-permute-start | bytes 393224 | tf_op jit(solution)/shard_map/ppermute | solution.py:276
  226.2 18.0 %collective-permute-start.26 = (bf16[256,512]{1,0:T(8,128)(2,1)}, bf16[256,512]{1,0:T(8,128)(2,1)S(1)}, u32[]{:S(2)}, u32[]{:S(2)}) collective-permute-start(bf16[256,512]{1,0:T(8,128)(2,1)} %get-tuple-element.204), channel_id=1, source_target_pairs={{0,8},{8,0},{16,24},{24,16},{1,9},{9,1},{17,25},{25,17},{2,10},{10... | collective-permute-start | bytes 786440 | tf_op jit(solution)/shard_map/ppermute | solution.py:271
  231.6 13.1 %collective-permute-start.27 = (bf16[256,512]{1,0:T(8,128)(2,1)}, bf16[256,512]{1,0:T(8,128)(2,1)S(1)}, u32[]{:S(2)}, u32[]{:S(2)}) collective-permute-start(bf16[256,512]{1,0:T(8,128)(2,1)} %get-tuple-element.205), channel_id=1, source_target_pairs={{0,16},{8,24},{16,0},{24,8},{1,17},{9,25},{17,1},{25,9},{2,18},{10... | collective-permute-start | bytes 786440 | tf_op jit(solution)/shard_map/ppermute | solution.py:271
  253.9 18.8 %collective-permute-start.33 = (bf16[128,512]{1,0:T(8,128)(2,1)S(1)}, bf16[128,512]{1,0:T(8,128)(2,1)S(1)}, u32[]{:S(2)}, u32[]{:S(2)}) collective-permute-start(bf16[128,512]{1,0:T(8,128)(2,1)S(1)} %get-tuple-element.216), channel_id=1, source_target_pairs={{0,5},{1,4},{2,7},{3,6},{4,1},{5,0},{6,3},{7,2},{8,13},{9,12},{10,... | collective-permute-start | bytes 393224 | tf_op jit(solution)/shard_map/ppermute | solution.py:276
  255.0 17.7 %collective-permute-start.34 = (bf16[128,512]{1,0:T(8,128)(2,1)S(1)}, bf16[128,512]{1,0:T(8,128)(2,1)}, u32[]{:S(2)}, u32[]{:S(2)}) collective-permute-start(bf16[128,512]{1,0:T(8,128)(2,1)S(1)} %get-tuple-element.217), channel_id=1, source_target_pairs={{0,6},{1,7},{2,4},{3,5},{4,2},{5,3},{6,0},{7,1},{8,14},{9,15},{10,... | collective-permute-start | bytes 393224 | tf_op jit(solution)/shard_map/ppermute | solution.py:276
  276.0 258.8 %all-gather.3.cloned.1.call-start = ((), (), s32[]{:S(2)}) async-start(), calls=%async_computation.4 | async-start | bytes 10485760 | tf_op jit(solution)/shard_map/all_gather | solution.py:299
  277.5 14.8 %collective-permute-start.43 = (bf16[128,512]{1,0:T(8,128)(2,1)S(1)}, bf16[128,512]{1,0:T(8,128)(2,1)S(1)}, u32[]{:S(2)}, u32[]{:S(2)}) collective-permute-start(bf16[128,512]{1,0:T(8,128)(2,1)S(1)} %get-tuple-element.317), channel_id=1, source_target_pairs={{0,7},{1,6},{2,13},{3,12},{4,19},{5,18},{6,25},{7,24},{8,5},{9,4},... | collective-permute-start | bytes 393224 | tf_op jit(solution)/shard_map/ppermute | solution.py:265
  279.1 16.4 %collective-permute-start.42 = (bf16[128,512]{1,0:T(8,128)(2,1)S(1)}, bf16[128,512]{1,0:T(8,128)(2,1)S(1)}, u32[]{:S(2)}, u32[]{:S(2)}) collective-permute-start(bf16[128,512]{1,0:T(8,128)(2,1)S(1)} %get-tuple-element.318), channel_id=1, source_target_pairs={{0,6},{1,7},{2,12},{3,13},{4,18},{5,19},{6,24},{7,25},{8,4},{9,5},... | collective-permute-start | bytes 393224 | tf_op jit(solution)/shard_map/ppermute | solution.py:265
  282.6 13.0 %collective-permute-start.41 = (bf16[128,512]{1,0:T(8,128)(2,1)S(1)}, bf16[128,512]{1,0:T(8,128)(2,1)S(1)}, u32[]{:S(2)}, u32[]{:S(2)}) collective-permute-start(bf16[128,512]{1,0:T(8,128)(2,1)S(1)} %get-tuple-element.319), channel_id=1, source_target_pairs={{0,5},{1,4},{2,15},{3,14},{4,17},{5,16},{6,27},{7,26},{8,7},{9,6},... | collective-permute-start | bytes 393224 | tf_op jit(solution)/shard_map/ppermute | solution.py:265
  285.7 13.7 %collective-permute-start.40 = (bf16[128,512]{1,0:T(8,128)(2,1)S(1)}, bf16[128,512]{1,0:T(8,128)(2,1)S(1)}, u32[]{:S(2)}, u32[]{:S(2)}) collective-permute-start(bf16[128,512]{1,0:T(8,128)(2,1)S(1)} %get-tuple-element.320), channel_id=1, source_target_pairs={{0,4},{1,5},{2,14},{3,15},{4,16},{5,17},{6,26},{7,27},{8,6},{9,7},... | collective-permute-start | bytes 393224 | tf_op jit(solution)/shard_map/ppermute | solution.py:265
  292.3 18.5 %collective-permute-start.38 = (bf16[128,512]{1,0:T(8,128)(2,1)S(1)}, bf16[128,512]{1,0:T(8,128)(2,1)S(1)}, u32[]{:S(2)}, u32[]{:S(2)}) collective-permute-start(bf16[128,512]{1,0:T(8,128)(2,1)S(1)} %get-tuple-element.322), channel_id=1, source_target_pairs={{0,2},{1,3},{2,8},{3,9},{4,22},{5,23},{6,28},{7,29},{8,0},{9,1},{1... | collective-permute-start | bytes 393224 | tf_op jit(solution)/shard_map/ppermute | solution.py:265
  295.5 15.3 %collective-permute-start.37 = (bf16[128,512]{1,0:T(8,128)(2,1)S(1)}, bf16[128,512]{1,0:T(8,128)(2,1)S(1)}, u32[]{:S(2)}, u32[]{:S(2)}) collective-permute-start(bf16[128,512]{1,0:T(8,128)(2,1)S(1)} %get-tuple-element.323), channel_id=1, source_target_pairs={{0,1},{1,0},{2,11},{3,10},{4,21},{5,20},{6,31},{7,30},{8,3},{9,2},... | collective-permute-start | bytes 393224 | tf_op jit(solution)/shard_map/ppermute | solution.py:265
  295.6 15.2 %collective-permute-start.36 = (bf16[128,512]{1,0:T(8,128)(2,1)S(1)}, bf16[128,512]{1,0:T(8,128)(2,1)S(1)}, u32[]{:S(2)}, u32[]{:S(2)}) collective-permute-start(bf16[128,512]{1,0:T(8,128)(2,1)S(1)} %get-tuple-element.324), channel_id=1, source_target_pairs={{0,0},{1,1},{2,10},{3,11},{4,20},{5,21},{6,30},{7,31},{8,2},{9,3},... | collective-permute-start | bytes 393224 | tf_op jit(solution)/shard_map/ppermute | solution.py:265
  310.9 20.3 %collective-permute-start.51 = (bf16[128,512]{1,0:T(8,128)(2,1)S(1)}, bf16[128,512]{1,0:T(8,128)(2,1)S(1)}, u32[]{:S(2)}, u32[]{:S(2)}) collective-permute-start(bf16[128,512]{1,0:T(8,128)(2,1)S(1)} %get-tuple-element.309), channel_id=1, source_target_pairs={{0,7},{1,6},{2,13},{3,12},{4,19},{5,18},{6,25},{7,24},{8,5},{9,4},... | collective-permute-start | bytes 393224 | tf_op jit(solution)/shard_map/ppermute | solution.py:265
  316.6 19.7 %collective-permute-start.50 = (bf16[128,512]{1,0:T(8,128)(2,1)S(1)}, bf16[128,512]{1,0:T(8,128)(2,1)S(1)}, u32[]{:S(2)}, u32[]{:S(2)}) collective-permute-start(bf16[128,512]{1,0:T(8,128)(2,1)S(1)} %get-tuple-element.310), channel_id=1, source_target_pairs={{0,6},{1,7},{2,12},{3,13},{4,18},{5,19},{6,24},{7,25},{8,4},{9,5},... | collective-permute-start | bytes 393224 | tf_op jit(solution)/shard_map/ppermute | solution.py:265
  318.8 18.2 %collective-permute-start.49 = (bf16[128,512]{1,0:T(8,128)(2,1)S(1)}, bf16[128,512]{1,0:T(8,128)(2,1)S(1)}, u32[]{:S(2)}, u32[]{:S(2)}) collective-permute-start(bf16[128,512]{1,0:T(8,128)(2,1)S(1)} %get-tuple-element.311), channel_id=1, source_target_pairs={{0,5},{1,4},{2,15},{3,14},{4,17},{5,16},{6,27},{7,26},{8,7},{9,6},... | collective-permute-start | bytes 393224 | tf_op jit(solution)/shard_map/ppermute | solution.py:265
  323.8 30.4 %collective-permute-start.48 = (bf16[128,512]{1,0:T(8,128)(2,1)S(1)}, bf16[128,512]{1,0:T(8,128)(2,1)S(1)}, u32[]{:S(2)}, u32[]{:S(2)}) collective-permute-start(bf16[128,512]{1,0:T(8,128)(2,1)S(1)} %get-tuple-element.312), channel_id=1, source_target_pairs={{0,4},{1,5},{2,14},{3,15},{4,16},{5,17},{6,26},{7,27},{8,6},{9,7},... | collective-permute-start | bytes 393224 | tf_op jit(solution)/shard_map/ppermute | solution.py:265
  331.2 23.0 %collective-permute-start.47 = (bf16[128,512]{1,0:T(8,128)(2,1)S(1)}, bf16[128,512]{1,0:T(8,128)(2,1)S(1)}, u32[]{:S(2)}, u32[]{:S(2)}) collective-permute-start(bf16[128,512]{1,0:T(8,128)(2,1)S(1)} %get-tuple-element.313), channel_id=1, source_target_pairs={{0,3},{1,2},{2,9},{3,8},{4,23},{5,22},{6,29},{7,28},{8,1},{9,0},{1... | collective-permute-start | bytes 393224 | tf_op jit(solution)/shard_map/ppermute | solution.py:265
  331.3 22.9 %collective-permute-start.46 = (bf16[128,512]{1,0:T(8,128)(2,1)S(1)}, bf16[128,512]{1,0:T(8,128)(2,1)S(1)}, u32[]{:S(2)}, u32[]{:S(2)}) collective-permute-start(bf16[128,512]{1,0:T(8,128)(2,1)S(1)} %get-tuple-element.314), channel_id=1, source_target_pairs={{0,2},{1,3},{2,8},{3,9},{4,22},{5,23},{6,28},{7,29},{8,0},{9,1},{1... | collective-permute-start | bytes 393224 | tf_op jit(solution)/shard_map/ppermute | solution.py:265
  336.3 18.0 %collective-permute-start.45 = (bf16[128,512]{1,0:T(8,128)(2,1)S(1)}, bf16[128,512]{1,0:T(8,128)(2,1)S(1)}, u32[]{:S(2)}, u32[]{:S(2)}) collective-permute-start(bf16[128,512]{1,0:T(8,128)(2,1)S(1)} %get-tuple-element.315), channel_id=1, source_target_pairs={{0,1},{1,0},{2,11},{3,10},{4,21},{5,20},{6,31},{7,30},{8,3},{9,2},... | collective-permute-start | bytes 393224 | tf_op jit(solution)/shard_map/ppermute | solution.py:265
  337.0 17.3 %collective-permute-start.44 = (bf16[128,512]{1,0:T(8,128)(2,1)S(1)}, bf16[128,512]{1,0:T(8,128)(2,1)S(1)}, u32[]{:S(2)}, u32[]{:S(2)}) collective-permute-start(bf16[128,512]{1,0:T(8,128)(2,1)S(1)} %get-tuple-element.316), channel_id=1, source_target_pairs={{0,0},{1,1},{2,10},{3,11},{4,20},{5,21},{6,30},{7,31},{8,2},{9,3},... | collective-permute-start | bytes 393224 | tf_op jit(solution)/shard_map/ppermute | solution.py:265
  354.3 28.4 %collective-permute-start.52 = (bf16[256,512]{1,0:T(8,128)(2,1)}, bf16[256,512]{1,0:T(8,128)(2,1)S(1)}, u32[]{:S(2)}, u32[]{:S(2)}) collective-permute-start(bf16[256,512]{1,0:T(8,128)(2,1)} %get-tuple-element.234), channel_id=1, source_target_pairs={{0,8},{8,0},{16,24},{24,16},{1,9},{9,1},{17,25},{25,17},{2,10},{10... | collective-permute-start | bytes 786440 | tf_op jit(solution)/shard_map/ppermute | solution.py:271
  360.0 22.7 %collective-permute-start.53 = (bf16[256,512]{1,0:T(8,128)(2,1)}, bf16[256,512]{1,0:T(8,128)(2,1)S(1)}, u32[]{:S(2)}, u32[]{:S(2)}) collective-permute-start(bf16[256,512]{1,0:T(8,128)(2,1)} %get-tuple-element.235), channel_id=1, source_target_pairs={{0,16},{8,24},{16,0},{24,8},{1,17},{9,25},{17,1},{25,9},{2,18},{10... | collective-permute-start | bytes 786440 | tf_op jit(solution)/shard_map/ppermute | solution.py:271
  364.7 24.7 %collective-permute-start.54 = (bf16[256,512]{1,0:T(8,128)(2,1)}, bf16[256,512]{1,0:T(8,128)(2,1)S(1)}, u32[]{:S(2)}, u32[]{:S(2)}) collective-permute-start(bf16[256,512]{1,0:T(8,128)(2,1)} %get-tuple-element.236), channel_id=1, source_target_pairs={{0,24},{8,16},{16,8},{24,0},{1,25},{9,17},{17,9},{25,1},{2,26},{10... | collective-permute-start | bytes 786440 | tf_op jit(solution)/shard_map/ppermute | solution.py:271
  395.9 13.3 %collective-permute-start.59 = (bf16[128,512]{1,0:T(8,128)(2,1)S(1)}, bf16[128,512]{1,0:T(8,128)(2,1)S(1)}, u32[]{:S(2)}, u32[]{:S(2)}) collective-permute-start(bf16[128,512]{1,0:T(8,128)(2,1)S(1)} %get-tuple-element.258), channel_id=1, source_target_pairs={{0,5},{1,4},{2,7},{3,6},{4,1},{5,0},{6,3},{7,2},{8,13},{9,12},{10,... | collective-permute-start | bytes 393224 | tf_op jit(solution)/shard_map/ppermute | solution.py:276
  397.4 18.8 %collective-permute-start.62 = (bf16[256,512]{1,0:T(8,128)(2,1)}, bf16[256,512]{1,0:T(8,128)(2,1)S(1)}, u32[]{:S(2)}, u32[]{:S(2)}) collective-permute-start(bf16[256,512]{1,0:T(8,128)(2,1)} %get-tuple-element.262), channel_id=1, source_target_pairs={{0,8},{8,0},{16,24},{24,16},{1,9},{9,1},{17,25},{25,17},{2,10},{10... | collective-permute-start | bytes 786440 | tf_op jit(solution)/shard_map/ppermute | solution.py:271
  402.5 13.7 %collective-permute-start.63 = (bf16[256,512]{1,0:T(8,128)(2,1)}, bf16[256,512]{1,0:T(8,128)(2,1)S(1)}, u32[]{:S(2)}, u32[]{:S(2)}) collective-permute-start(bf16[256,512]{1,0:T(8,128)(2,1)} %get-tuple-element.263), channel_id=1, source_target_pairs={{0,16},{8,24},{16,0},{24,8},{1,17},{9,25},{17,1},{25,9},{2,18},{10... | collective-permute-start | bytes 786440 | tf_op jit(solution)/shard_map/ppermute | solution.py:271
  424.9 18.1 %collective-permute-start.69 = (bf16[128,512]{1,0:T(8,128)(2,1)S(1)}, bf16[128,512]{1,0:T(8,128)(2,1)S(1)}, u32[]{:S(2)}, u32[]{:S(2)}) collective-permute-start(bf16[128,512]{1,0:T(8,128)(2,1)S(1)} %get-tuple-element.282), channel_id=1, source_target_pairs={{0,5},{1,4},{2,7},{3,6},{4,1},{5,0},{6,3},{7,2},{8,13},{9,12},{10,... | collective-permute-start | bytes 393224 | tf_op jit(solution)/shard_map/ppermute | solution.py:276
  425.8 17.2 %collective-permute-start.70 = (bf16[128,512]{1,0:T(8,128)(2,1)S(1)}, bf16[128,512]{1,0:T(8,128)(2,1)S(1)}, u32[]{:S(2)}, u32[]{:S(2)}) collective-permute-start(bf16[128,512]{1,0:T(8,128)(2,1)S(1)} %get-tuple-element.283), channel_id=1, source_target_pairs={{0,6},{1,7},{2,4},{3,5},{4,2},{5,3},{6,0},{7,1},{8,14},{9,15},{10,... | collective-permute-start | bytes 393224 | tf_op jit(solution)/shard_map/ppermute | solution.py:276
  (70 other events, 1292.9 us)
Sparse Core Ops, SparseCore 0:
  16.4 89.0 reduce-scatter.2
  108.9 119.7 reduce-scatter.4
  276.1 122.8 all-gather.4
  444.7 90.1 all-gather.2

commit v5 on v4

--- a/solution.py
+++ b/solution.py
@@ -65,7 +65,7 @@
     for k in range(ranks):
         for e in range(inner):
             slab = slab_of(k, e, d ^ place_ref[0], place_ref[1], inner)
-            out_ref[0, 0, k * inner + e] = grads_ref[slab, 0]
+            out_ref[0, e, 0, k] = grads_ref[slab, 0]
 
 
 def pack(ranks, inner, slots, per, place, grads):
@@ -79,8 +79,8 @@
             pl.BlockSpec(memory_space=pltpu.SMEM),
             pl.BlockSpec((owners, 1, rows, width), lambda d, s: (0, first + s, d, 0)),
         ],
-        out_specs=pl.BlockSpec((1, 1, owners, rows, width), lambda d, s: (d, s, 0, 0, 0)),
-        out_shape=jax.ShapeDtypeStruct((ranks, count, owners, rows, width), grads.dtype),
+        out_specs=pl.BlockSpec((1, inner, 1, ranks, rows, width), lambda d, s: (d, 0, s, 0, 0, 0)),
+        out_shape=jax.ShapeDtypeStruct((ranks, inner, count, ranks, rows, width), grads.dtype),
         compiler_params=pltpu.CompilerParams(vmem_limit_bytes=VMEM_LIMIT),
         cost_estimate=pl.CostEstimate(
             flops=0, bytes_accessed=4 * owners * count * order * width, transcendentals=0
@@ -161,12 +161,11 @@
 
 
 def block_kernel(ranks, inner, steps, place_ref, *refs):
-    count = ranks * inner
-    pieces = refs[:count]
-    left_stats, right_stats, left_root, right_root, left_fourth, right_fourth = refs[count : count + 6]
-    outs = refs[count + 6 : count + 6 + ranks]
-    blocks, results = refs[count + 6 + ranks :]
-    rows, width = pieces[0].shape
+    pieces = refs[:ranks]
+    left_stats, right_stats, left_root, right_root, left_fourth, right_fourth = refs[ranks : ranks + 6]
+    outs = refs[ranks + 6 : 2 * ranks + 6]
+    blocks, results = refs[2 * ranks + 6 :]
+    rows, width = pieces[0].shape[0] // inner, pieces[0].shape[1]
     order = blocks.shape[1]
     outer_place, inner_place = place_ref[0], place_ref[1]
     step = pl.program_id(0)
@@ -181,7 +180,7 @@
     def _():
         for k in range(ranks):
             for e in range(inner):
-                blocks[spot(place_ref[2] ^ outer_place ^ k, inner_place ^ e)] = pieces[k * inner + e][...]
+                blocks[spot(place_ref[2] ^ outer_place ^ k, inner_place ^ e)] = pieces[k][e * rows : (e + 1) * rows]
 
     block = blocks[step]
     turned = block.T
@@ -189,9 +188,8 @@
     right = ema_decay * right_stats[0, 0] + (1.0 - ema_decay) * mm(turned, block)
     new_left = refine(left_root[0, 0], left_fourth[0, 0], left)
     new_right = refine(right_root[0, 0], right_fourth[0, 0], right)
-    high, low = split(new_left)
-    halfway = mm(high, block) + mm(low, block)
-    results[step] = dot3(halfway, new_right).astype(results.dtype)
+    halfway = mm(new_left.astype(jnp.bfloat16), block)
+    results[step] = mm(halfway.astype(jnp.bfloat16), new_right.astype(jnp.bfloat16)).astype(results.dtype)
 
     @pl.when(step == steps - 1)
     def _():
@@ -202,21 +200,18 @@
 
 def precondition(ranks, inner, slot, place, pieces, stats_and_roots):
     _, col_blocks, order, _ = stats_and_roots[0].shape
-    rows, width = pieces[0].shape
-    owners = ranks * inner
-    piece = pl.BlockSpec((rows, width), lambda j: (0, 0))
-    strip = pl.BlockSpec((inner * rows, width), lambda j: (0, 0))
+    strip = pl.BlockSpec(pieces[0].shape, lambda j: (0, 0))
     matrix = pl.BlockSpec((1, 1, order, order), lambda j: (slot, j, 0, 0))
     return pl.pallas_call(
         functools.partial(block_kernel, ranks, inner, col_blocks),
         grid=(col_blocks,),
-        in_specs=[pl.BlockSpec(memory_space=pltpu.SMEM)] + [piece] * owners + [matrix] * 6,
+        in_specs=[pl.BlockSpec(memory_space=pltpu.SMEM)] + [strip] * ranks + [matrix] * 6,
         out_specs=[strip] * ranks,
-        out_shape=[jax.ShapeDtypeStruct((inner * rows, width), jnp.bfloat16)] * ranks,
+        out_shape=[jax.ShapeDtypeStruct(pieces[0].shape, jnp.bfloat16)] * ranks,
         scratch_shapes=[pltpu.VMEM((col_blocks, order, order), jnp.bfloat16)] * 2,
         compiler_params=pltpu.CompilerParams(vmem_limit_bytes=VMEM_LIMIT * 9 // 10),
         cost_estimate=pl.CostEstimate(
-            flops=col_blocks * 19 * 2 * order**3,
+            flops=col_blocks * 16 * 2 * order**3,
             bytes_accessed=col_blocks * 28 * order**2,
             transcendentals=0,
         ),
@@ -238,9 +233,12 @@
         return (d * ranks + a) * inner + b
 
     sources = [(d, a, b) for d in range(ranks) for a in range(ranks) for b in range(inner)]
-    to_owner = {
-        (k, e): [(number(d, a, b), number(a, d ^ a ^ k, b ^ e)) for d, a, b in sources] for k, e in rounds
-    }
+    to_core = [
+        [(a * inner + b, a * inner + (b ^ e)) for a in range(ranks) for b in range(inner)] for e in range(inner)
+    ]
+    to_owner = [
+        [(number(d, a, b), number(a, d ^ a ^ k, b)) for d, a, b in sources] for k in range(ranks)
+    ]
     to_row = [[(d, d ^ k) for d in range(ranks)] for k in range(ranks)]
     to_column = {
         (m, e): [(a * inner + b, (a ^ m) * inner + (b ^ e)) for a in range(ranks) for b in range(inner)]
@@ -248,21 +246,32 @@
     }
 
     half = max(per // 2, 1)
-    groups = [(first, min(half, per - first)) for first in range(0, per, half)]
-    summed = []
-    for slots in groups:
+    sums = [(0, half)] + [(slot, 1) for slot in range(half, per)]
+    gathers = [(first, min(half, per - first)) for first in range(0, per, half)]
+    begins = [slot if slot < half else half + 1 + 2 * (slot - half) for slot in range(per)]
+    group_of = [max(g for g, (first, _) in enumerate(sums) if first <= slot) for slot in range(per)]
+    ready = []
+    for slots in sums:
         packed = pack(ranks, inner, slots, per, place, grads)
-        summed.append(lax.psum_scatter(packed, "dp", scatter_dimension=0, tiled=True))
+        ready.append([lax.psum_scatter(packed, "dp", scatter_dimension=0, tiled=True)])
     left_fourth, right_fourth = fourth_powers(left_root, right_root)
-    summed[0], left_fourth, right_fourth = lax.optimization_barrier((summed[0], left_fourth, right_fourth))
+    ready[0], left_fourth, right_fourth = lax.optimization_barrier((ready[0], left_fourth, right_fourth))
     matrices = (left_stats, right_stats, left_root, right_root, left_fourth, right_fourth)
 
-    piece_count = len(rounds)
+    def between_cores(g):
+        parts = ready[g][0].reshape(inner, -1, width)
+        ready[g] = [parts[0]] + [lax.ppermute(parts[e], "fsdp", to_core[e]) for e in range(1, inner)]
 
     def send_in(slot):
-        g, s = divmod(slot, half)
-        pieces = summed[g].reshape(-1, rows, width)[s * piece_count : (s + 1) * piece_count]
-        return [lax.ppermute(pieces[at], MESH_AXES, to_owner[key]) for at, key in enumerate(rounds)]
+        g = group_of[slot]
+        if slot == sums[g][0]:
+            between_cores(g)
+        at = (slot - sums[g][0]) * ranks
+        strips = [
+            jnp.concatenate([part[(at + k) * rows : (at + k + 1) * rows] for part in ready[g]], axis=0)
+            for k in range(ranks)
+        ]
+        return [lax.ppermute(strips[k], MESH_AXES, to_owner[k]) for k in range(ranks)]
 
     def work(slot, arrived):
         return precondition(ranks, inner, slot, place, arrived, matrices)
@@ -277,8 +286,7 @@
         ]
 
     stages = (send_in, work, send_rows, send_columns)
-    begins = [slot + (slot // half) * (len(stages) - 1) for slot in range(per)]
-    held = {}
+    held, finished = {}, {}
     out = None
     for tick in range(begins[-1] + len(stages)):
         now = {}
@@ -288,16 +296,19 @@
                 now[slot] = send_in(slot)
             elif 0 < stage < len(stages):
                 now[slot] = stages[stage](slot, held[slot])
-        wanted = [begins.index(tick + 1) // half] if tick + 1 in begins else []
-        now, ahead = lax.optimization_barrier((now, [summed[g] for g in wanted]))
-        for g, value in zip(wanted, ahead):
-            summed[g] = value
-        held.update(now)
-        for g, (first, count) in enumerate(groups):
+            if stage == len(stages) - 1:
+                finished[slot] = now.pop(slot)
+                now[slot] = finished[slot][-1:]
+        for first, count in gathers:
             if begins[first + count - 1] + len(stages) - 1 == tick:
-                back = [piece for slot in range(first, first + count) for piece in held[slot]]
+                back = [piece for slot in range(first, first + count) for piece in finished[slot]]
                 gathered = lax.all_gather(jnp.concatenate(back, axis=0), "dp", axis=0, tiled=True)
                 out = unpack(ranks, inner, (first, count), per, place, gathered, out)
+        wanted = [group_of[begins.index(tick + 1)]] if tick + 1 in begins else []
+        now, ahead = lax.optimization_barrier((now, [ready[g] for g in wanted]))
+        for g, value in zip(wanted, ahead):
+            ready[g] = value
+        held.update(now)
     return out.reshape(grads.shape)
 
 

time: 552 us -> 537 us (0.973)
  starting transfers between devices: 160 us -> 145 us
  Pallas kernels: 136 us -> 130 us
  waiting for transfers between devices: 229 us -> 235 us
    ppermute x28, waiting for transfers between devices: 61.2 us -> 46.1 us  [send_columns(): lax.ppermute(piece, 'fsdp', to_column[key])]
    ppermute x32 -> x19, waiting for transfers between devices: 23.8 us -> 38.4 us  [the longest x16 36.9 us: send_in(): lax.ppermute(strips[k], MESH_AXES, to_owner[k])]
    ppermute x32 -> x19, starting transfers between devices: 95.3 us -> 82.9 us  [the longest x16 82.1 us: send_in(): lax.ppermute(strips[k], MESH_AXES, to_owner[k])]
    pallas_call x4, Pallas kernels: 66 us -> 59 us  [precondition(): pl.pallas_call(functools.partial(block_kernel, ranks, inner, col_blocks),...]
    ppermute x12, waiting for transfers between devices: 13.8 us -> 20.6 us  [send_rows(): lax.ppermute(strips[k], 'dp', to_row[k])]
    pallas_call x2 -> x3, Pallas kernels: 18.1 us -> 18.7 us  [pack(): pl.pallas_call(functools.partial(pack_kernel, ranks, inner), grid=(ranks,...]
    reduce_scatter x2 -> x3, waiting for transfers between devices: 48.8 us -> 48.3 us  [shards(): lax.psum_scatter(packed, 'dp', scatter_dimension=0, tiled=True)]
  transfers between devices with their start and end apart: 76 -> 64, of which waited for: 28 -> 27; matrix products, arithmetic and copies ran while one was open for 1% -> 1% of each run, Pallas kernels for 21% -> 21%
where the time goes in v5:
time: 537 us; the launch traced here: 535 us
  waiting for transfers between devices  235 us (44%)
  starting transfers between devices  145 us (27%)
  Pallas kernels  130 us (24%)
  between operations  14.2 us (3%)
  local copies, waits for them, and re-layouts  10.4 us (2%)
    ppermute x16, starting transfers between devices, send_in(): lax.ppermute(strips[k], MESH_AXES, to_owner[k])  82.1 us
    all_gather x2, waiting for transfers between devices, shards(): lax.all_gather(jnp.concatenate(back, axis=0), 'dp', axis=0, tiled=True)  81.6 us
    pallas_call x4, Pallas kernels, precondition(): pl.pallas_call(functools.partial(block_kernel, ranks, inner, col_blocks),...  59 us
    reduce_scatter x3, waiting for transfers between devices, shards(): lax.psum_scatter(packed, 'dp', scatter_dimension=0, tiled=True)  48.3 us
    ppermute x28, waiting for transfers between devices, send_columns(): lax.ppermute(piece, 'fsdp', to_column[key])  46.1 us
    ppermute x16, waiting for transfers between devices, send_in(): lax.ppermute(strips[k], MESH_AXES, to_owner[k])  36.9 us
    ppermute x28, starting transfers between devices, send_columns(): lax.ppermute(piece, 'fsdp', to_column[key])  35.8 us
    pallas_call x1, Pallas kernels, fourth_powers(): pl.pallas_call(fourth_kernel, grid=(slabs, col_blocks), in_specs=[spec, s...  31.1 us
  transfers between devices with their start and end apart: 64, of which 27 were waited for; matrix products, arithmetic and copies ran while one was open for 1% of the time, Pallas kernels for 21%

profile of v5, /device:TPU:0, one launch (start us, length us, event | category | flops | bytes accessed | tf_op | source)
XLA Modules:
  0.0 535.3 jit_solution(14439110629300059105)
XLA Ops:
  7.2 9.1 %pack_slabs.3 = bf16[4,2,2,4,128,512]{5,4,3,2,1,0:T(8,128)(2,1)} custom-call(s32[3]{0:T(128)} %pad_add_fusion.place_ref, bf16[8,4,512,512]{3,2,1,0:T(8,128)(2,1)} %bitcast.10), custom_call_target="tpu_custom_call" | custom-call | bytes 16777216 | tf_op jit(solution)/shard_map/pack_slabs/pallas_call | solution.py:75
  16.3 4.9 pack_slabs.4
  21.3 4.8 pack_slabs.5
  26.2 31.1 %fourth_powers.1 = (f32[4,2,512,512]{3,2,1,0:T(8,128)}, f32[4,2,512,512]{3,2,1,0:T(8,128)}) custom-call(f32[4,2,512,512]{3,2,1,0:T(8,128)} %refs_6_.7, f32[4,2,512,512]{3,2,1,0:T(8,128)} %refs_7_.7), custom_call_target="tpu_custom_call" | custom-call | flops 25769803776 | bytes 33554432 | tf_op jit(solution)/shard_map/fourth_powers/pallas_call | solution.py:45
  57.3 48.3 %reduce-scatter.4.cloned.1.call-done = bf16[2048,512]{1,0:T(8,128)(2,1)} async-done(((bf16[8192,512]{1,0:T(8,128)(2,1)}), bf16[2048,512]{1,0:T(8,128)(2,1)}) %reduce-scatter.4.cloned.1.call-update) | async-done | bytes 2097168 | tf_op jit(solution)/shard_map/reduce_scatter | solution.py:256
  110.7 6.0 %collective-permute-start.2 = (bf16[256,512]{1,0:T(8,128)(2,1)S(1)}, bf16[256,512]{1,0:T(8,128)(2,1)S(1)}, u32[]{:S(2)}, u32[]{:S(2)}) collective-permute-start(bf16[256,512]{1,0:T(8,128)(2,1)S(1)} %pad_maximum_fusion.1), channel_id=1, source_target_pairs={{0,2},{1,3},{2,8},{3,9},{4,22},{5,23},{6,28},{7,29},{8,0},{9,1},{1... | collective-permute-start | bytes 786440 | tf_op jit(solution)/shard_map/ppermute | solution.py:274
  116.7 4.4 collective-permute-start.3
  121.1 5.2 collective-permute-start.4
  126.4 2.6 collective-permute-done.2.refs_1_
  128.9 10.7 %collective-permute-done.3.refs_2_ = bf16[256,512]{1,0:T(8,128)(2,1)S(1)} collective-permute-done((bf16[256,512]{1,0:T(8,128)(2,1)S(1)}, bf16[256,512]{1,0:T(8,128)(2,1)S(1)}, u32[]{:S(2)}, u32[]{:S(2)}) %collective-permute-start.3) | collective-permute-done | bytes 262176 | tf_op jit(solution)/shard_map/ppermute | solution.py:274
  139.7 4.1 collective-permute-done.4.refs_3_
  144.6 4.4 collective-permute-start.6
  149.0 4.4 collective-permute-start.7
  153.4 7.9 %collective-permute-start.8 = (bf16[256,512]{1,0:T(8,128)(2,1)S(1)}, bf16[256,512]{1,0:T(8,128)(2,1)S(1)}, u32[]{:S(2)}, u32[]{:S(2)}) collective-permute-start(bf16[256,512]{1,0:T(8,128)(2,1)S(1)} %pad_maximum_fusion.7), channel_id=1, source_target_pairs={{0,6},{1,7},{2,12},{3,13},{4,18},{5,19},{6,24},{7,25},{8,4},{9,5},... | collective-permute-start | bytes 786440 | tf_op jit(solution)/shard_map/ppermute | solution.py:274
  161.3 14.7 %precondition.4 = (bf16[256,512]{1,0:T(8,128)(2,1)}, bf16[256,512]{1,0:T(8,128)(2,1)}, bf16[256,512]{1,0:T(8,128)(2,1)}, bf16[256,512]{1,0:T(8,128)(2,1)}) custom-call(s32[3]{0:T(128)} %pad_add_fusion.place_ref, bf16[256,512]{1,0:T(8,128)(2,1)} %copy-done.15, bf16[256,512]{1,0:T(8,128)(2,1)} %copy-done.17, bf16[256,512]{1,0:T(8,128)(2,1)} %copy-done.18, ...), custom_call_target="tpu_custom_call" | custom-call | flops 8589934592 | bytes 14680064 | tf_op jit(solution)/shard_map/precondition/pallas_call | solution.py:205
  177.6 5.0 collective-permute-start.10
  184.0 14.8 %precondition.5 = (bf16[256,512]{1,0:T(8,128)(2,1)}, bf16[256,512]{1,0:T(8,128)(2,1)}, bf16[256,512]{1,0:T(8,128)(2,1)}, bf16[256,512]{1,0:T(8,128)(2,1)}) custom-call(s32[3]{0:T(128)} %pad_add_fusion.place_ref, bf16[256,512]{1,0:T(8,128)(2,1)} %copy-done.21, bf16[256,512]{1,0:T(8,128)(2,1)} %copy-done.23, bf16[256,512]{1,0:T(8,128)(2,1)} %copy-done.24, ...), custom_call_target="tpu_custom_call" | custom-call | flops 8589934592 | bytes 14680064 | tf_op jit(solution)/shard_map/precondition/pallas_call | solution.py:205
  201.4 2.5 collective-permute-start.12
  208.0 3.9 collective-permute-done.48
  212.5 4.9 collective-permute-done.49
  224.4 2.8 collective-permute-done.52
  227.2 4.0 collective-permute-start.18
  232.2 3.7 collective-permute-start.19
  235.9 13.1 %collective-permute-start.20 = (bf16[256,512]{1,0:T(8,128)(2,1)S(1)}, bf16[256,512]{1,0:T(8,128)(2,1)S(1)}, u32[]{:S(2)}, u32[]{:S(2)}) collective-permute-start(bf16[256,512]{1,0:T(8,128)(2,1)S(1)} %pad_maximum_fusion.11), channel_id=1, source_target_pairs={{0,6},{1,7},{2,12},{3,13},{4,18},{5,19},{6,24},{7,25},{8,4},{9,5},... | collective-permute-start | bytes 786440 | tf_op jit(solution)/shard_map/ppermute | solution.py:274
  249.1 3.1 collective-permute-done.18.refs_1_
  253.6 5.1 collective-permute-done.20.refs_3_
  260.2 5.4 %collective-permute-start.54 = (bf16[128,512]{1,0:T(8,128)(2,1)S(1)}, bf16[128,512]{1,0:T(8,128)(2,1)S(1)}, u32[]{:S(2)}, u32[]{:S(2)}) collective-permute-start(bf16[128,512]{1,0:T(8,128)(2,1)S(1)} %get-tuple-element.210), channel_id=1, source_target_pairs={{0,2},{1,3},{2,0},{3,1},{4,6},{5,7},{6,4},{7,5},{8,10},{9,11},{10,... | collective-permute-start | bytes 393224 | tf_op jit(solution)/shard_map/ppermute | solution.py:285
  270.9 5.1 collective-permute-done.55
  276.0 8.2 %collective-permute-done.57 = bf16[128,512]{1,0:T(8,128)(2,1)S(1)} collective-permute-done((bf16[128,512]{1,0:T(8,128)(2,1)S(1)}, bf16[128,512]{1,0:T(8,128)(2,1)S(1)}, u32[]{:S(2)}, u32[]{:S(2)}) %collective-permute-start.57) | collective-permute-done | bytes 131104 | tf_op jit(solution)/shard_map/ppermute | solution.py:285
  285.9 14.7 %precondition.6 = (bf16[256,512]{1,0:T(8,128)(2,1)}, bf16[256,512]{1,0:T(8,128)(2,1)}, bf16[256,512]{1,0:T(8,128)(2,1)}, bf16[256,512]{1,0:T(8,128)(2,1)}) custom-call(s32[3]{0:T(128)} %pad_add_fusion.place_ref, bf16[256,512]{1,0:T(8,128)(2,1)} %copy-done.10, bf16[256,512]{1,0:T(8,128)(2,1)} %copy-done.11, bf16[256,512]{1,0:T(8,128)(2,1)} %copy-done.12, ...), custom_call_target="tpu_custom_call" | custom-call | flops 8589934592 | bytes 14680064 | tf_op jit(solution)/shard_map/precondition/pallas_call | solution.py:205
  302.0 5.2 collective-permute-start.22
  307.2 2.4 collective-permute-start.23
  313.0 7.0 %collective-permute-start.27 = (bf16[256,512]{1,0:T(8,128)(2,1)S(1)}, bf16[256,512]{1,0:T(8,128)(2,1)S(1)}, u32[]{:S(2)}, u32[]{:S(2)}) collective-permute-start(bf16[256,512]{1,0:T(8,128)(2,1)S(1)} %pad_maximum_fusion.13), channel_id=1, source_target_pairs={{0,2},{1,3},{2,8},{3,9},{4,22},{5,23},{6,28},{7,29},{8,0},{9,1},{1... | collective-permute-start | bytes 786440 | tf_op jit(solution)/shard_map/ppermute | solution.py:274
  320.1 5.7 %collective-permute-start.28 = (bf16[256,512]{1,0:T(8,128)(2,1)S(1)}, bf16[256,512]{1,0:T(8,128)(2,1)S(1)}, u32[]{:S(2)}, u32[]{:S(2)}) collective-permute-start(bf16[256,512]{1,0:T(8,128)(2,1)S(1)} %pad_maximum_fusion.14), channel_id=1, source_target_pairs={{0,4},{1,5},{2,14},{3,15},{4,16},{5,17},{6,26},{7,27},{8,6},{9,7},... | collective-permute-start | bytes 786440 | tf_op jit(solution)/shard_map/ppermute | solution.py:274
  325.9 13.8 %collective-permute-start.29 = (bf16[256,512]{1,0:T(8,128)(2,1)S(1)}, bf16[256,512]{1,0:T(8,128)(2,1)S(1)}, u32[]{:S(2)}, u32[]{:S(2)}) collective-permute-start(bf16[256,512]{1,0:T(8,128)(2,1)S(1)} %pad_maximum_fusion.15), channel_id=1, source_target_pairs={{0,6},{1,7},{2,12},{3,13},{4,18},{5,19},{6,24},{7,25},{8,4},{9,5},... | collective-permute-start | bytes 786440 | tf_op jit(solution)/shard_map/ppermute | solution.py:274
  339.7 2.8 collective-permute-done.27.refs_1_
  343.1 6.4 %collective-permute-done.29.refs_3_ = bf16[256,512]{1,0:T(8,128)(2,1)S(1)} collective-permute-done((bf16[256,512]{1,0:T(8,128)(2,1)S(1)}, bf16[256,512]{1,0:T(8,128)(2,1)S(1)}, u32[]{:S(2)}, u32[]{:S(2)}) %collective-permute-start.29) | collective-permute-done | bytes 262176 | tf_op jit(solution)/shard_map/ppermute | solution.py:274
  350.3 3.1 collective-permute-start.31
  353.5 4.0 collective-permute-start.33
  357.6 14.8 %precondition.7 = (bf16[256,512]{1,0:T(8,128)(2,1)}, bf16[256,512]{1,0:T(8,128)(2,1)}, bf16[256,512]{1,0:T(8,128)(2,1)}, bf16[256,512]{1,0:T(8,128)(2,1)}) custom-call(s32[3]{0:T(128)} %pad_add_fusion.place_ref, bf16[256,512]{1,0:T(8,128)(2,1)} %copy-done.14, bf16[256,512]{1,0:T(8,128)(2,1)} %copy-done.16, bf16[256,512]{1,0:T(8,128)(2,1)} %copy-done.19, ...), custom_call_target="tpu_custom_call" | custom-call | flops 8589934592 | bytes 14680064 | tf_op jit(solution)/shard_map/precondition/pallas_call | solution.py:205
  380.6 4.0 collective-permute-done.34
  384.6 6.5 %collective-permute-done.37.refs_1_ = bf16[256,512]{1,0:T(8,128)(2,1)S(1)} collective-permute-done((bf16[256,512]{1,0:T(8,128)(2,1)}, bf16[256,512]{1,0:T(8,128)(2,1)S(1)}, u32[]{:S(2)}, u32[]{:S(2)}) %collective-permute-start.37) | collective-permute-done | bytes 262176 | tf_op jit(solution)/shard_map/ppermute | solution.py:280
  391.7 12.3 %collective-permute-done.39.refs_3_ = bf16[256,512]{1,0:T(8,128)(2,1)S(1)} collective-permute-done((bf16[256,512]{1,0:T(8,128)(2,1)}, bf16[256,512]{1,0:T(8,128)(2,1)S(1)}, u32[]{:S(2)}, u32[]{:S(2)}) %collective-permute-start.39) | collective-permute-done | bytes 262176 | tf_op jit(solution)/shard_map/ppermute | solution.py:280
  412.6 3.5 collective-permute-done.41
  418.3 9.3 %collective-permute-done.44 = bf16[128,512]{1,0:T(8,128)(2,1)S(1)} collective-permute-done((bf16[128,512]{1,0:T(8,128)(2,1)S(1)}, bf16[128,512]{1,0:T(8,128)(2,1)S(1)}, u32[]{:S(2)}, u32[]{:S(2)}) %collective-permute-start.44) | collective-permute-done | bytes 131104 | tf_op jit(solution)/shard_map/ppermute | solution.py:285
  429.1 9.0 %unpack_slabs.2.rest_0_ = bf16[8,4,512,512]{3,2,1,0:T(8,128)(2,1)} custom-call(s32[3]{0:T(128)} %pad_add_fusion.place_ref, bf16[4,2,8,128,512]{4,3,2,1,0:T(8,128)(2,1)} %bitcast.16), custom_call_target="tpu_custom_call" | custom-call | bytes 16777216 | tf_op jit(solution)/shard_map/unpack_slabs/pallas_call | solution.py:107
  438.1 81.6 %all-gather.3.cloned.1.call-done = bf16[8192,512]{1,0:T(8,128)(2,1)} async-done(((bf16[2048,512]{1,0:T(8,128)(2,1)}), bf16[8192,512]{1,0:T(8,128)(2,1)}) %all-gather.3.cloned.1.call-update) | async-done | bytes 8388624 | tf_op jit(solution)/shard_map/all_gather | solution.py:305
  519.7 9.0 %unpack_slabs.3 = bf16[8,4,512,512]{3,2,1,0:T(8,128)(2,1)} custom-call(s32[3]{0:T(128)} %pad_add_fusion.place_ref, bf16[4,2,8,128,512]{4,3,2,1,0:T(8,128)(2,1)} %bitcast.17, bf16[8,4,512,512]{3,2,1,0:T(8,128)(2,1)} %unpack_slabs.2.rest_0_), custom_call_target="tpu_custom_call", output_to_operand_aliasing={{}: (2, {})} | custom-call | bytes 16777216 | tf_op jit(solution)/shard_map/unpack_slabs/pallas_call | solution.py:107
  (216 shorter events, 61.8 us)
Async XLA Ops:
  6.5 99.0 %reduce-scatter.4.cloned.1.call-start = ((), (), s32[]{:S(2)}) async-start(), calls=%async_computation.3 | async-start | bytes 10485760 | tf_op jit(solution)/shard_map/reduce_scatter | solution.py:256
  16.3 182.6 %reduce-scatter.6.cloned.1.call-start = ((), (), s32[]{:S(2)}) async-start(), calls=%async_computation.4 | async-start | bytes 5242880 | tf_op jit(solution)/shard_map/reduce_scatter | solution.py:256
  21.2 279.5 %reduce-scatter.8.cloned.1.call-start = ((), (), s32[]{:S(2)}) async-start(), calls=%async_computation.5 | async-start | bytes 5242880 | tf_op jit(solution)/shard_map/reduce_scatter | solution.py:256
  26.1 403.0 %all-gather.5.cloned.1.call-start = ((), (), s32[]{:S(2)}) async-start(), calls=%async_computation.7 | async-start | bytes 10485760 | tf_op jit(solution)/shard_map/all_gather | solution.py:305
  110.0 16.3 %collective-permute-start.1 = (bf16[256,512]{1,0:T(8,128)(2,1)S(1)}, bf16[256,512]{1,0:T(8,128)(2,1)S(1)}, u32[]{:S(2)}, u32[]{:S(2)}) collective-permute-start(bf16[256,512]{1,0:T(8,128)(2,1)S(1)} %pad_maximum_fusion), channel_id=1, source_target_pairs={{0,0},{1,1},{2,10},{3,11},{4,20},{5,21},{6,30},{7,31},{8,2},{9,3},... | collective-permute-start | bytes 786440 | tf_op jit(solution)/shard_map/ppermute | solution.py:274
  110.7 18.2 %collective-permute-start.2 = (bf16[256,512]{1,0:T(8,128)(2,1)S(1)}, bf16[256,512]{1,0:T(8,128)(2,1)S(1)}, u32[]{:S(2)}, u32[]{:S(2)}) collective-permute-start(bf16[256,512]{1,0:T(8,128)(2,1)S(1)} %pad_maximum_fusion.1), channel_id=1, source_target_pairs={{0,2},{1,3},{2,8},{3,9},{4,22},{5,23},{6,28},{7,29},{8,0},{9,1},{1... | collective-permute-start | bytes 786440 | tf_op jit(solution)/shard_map/ppermute | solution.py:274
  116.7 22.9 %collective-permute-start.3 = (bf16[256,512]{1,0:T(8,128)(2,1)S(1)}, bf16[256,512]{1,0:T(8,128)(2,1)S(1)}, u32[]{:S(2)}, u32[]{:S(2)}) collective-permute-start(bf16[256,512]{1,0:T(8,128)(2,1)S(1)} %pad_maximum_fusion.2), channel_id=1, source_target_pairs={{0,4},{1,5},{2,14},{3,15},{4,16},{5,17},{6,26},{7,27},{8,6},{9,7},... | collective-permute-start | bytes 786440 | tf_op jit(solution)/shard_map/ppermute | solution.py:274
  121.1 22.6 %collective-permute-start.4 = (bf16[256,512]{1,0:T(8,128)(2,1)S(1)}, bf16[256,512]{1,0:T(8,128)(2,1)S(1)}, u32[]{:S(2)}, u32[]{:S(2)}) collective-permute-start(bf16[256,512]{1,0:T(8,128)(2,1)S(1)} %pad_maximum_fusion.3), channel_id=1, source_target_pairs={{0,6},{1,7},{2,12},{3,13},{4,18},{5,19},{6,24},{7,25},{8,4},{9,5},... | collective-permute-start | bytes 786440 | tf_op jit(solution)/shard_map/ppermute | solution.py:274
  143.9 32.1 %collective-permute-start.5 = (bf16[256,512]{1,0:T(8,128)(2,1)S(1)}, bf16[256,512]{1,0:T(8,128)(2,1)S(1)}, u32[]{:S(2)}, u32[]{:S(2)}) collective-permute-start(bf16[256,512]{1,0:T(8,128)(2,1)S(1)} %pad_maximum_fusion.4), channel_id=1, source_target_pairs={{0,0},{1,1},{2,10},{3,11},{4,20},{5,21},{6,30},{7,31},{8,2},{9,3},... | collective-permute-start | bytes 786440 | tf_op jit(solution)/shard_map/ppermute | solution.py:274
  144.6 31.4 %collective-permute-start.6 = (bf16[256,512]{1,0:T(8,128)(2,1)S(1)}, bf16[256,512]{1,0:T(8,128)(2,1)S(1)}, u32[]{:S(2)}, u32[]{:S(2)}) collective-permute-start(bf16[256,512]{1,0:T(8,128)(2,1)S(1)} %pad_maximum_fusion.5), channel_id=1, source_target_pairs={{0,2},{1,3},{2,8},{3,9},{4,22},{5,23},{6,28},{7,29},{8,0},{9,1},{1... | collective-permute-start | bytes 786440 | tf_op jit(solution)/shard_map/ppermute | solution.py:274
  149.0 27.1 %collective-permute-start.7 = (bf16[256,512]{1,0:T(8,128)(2,1)S(1)}, bf16[256,512]{1,0:T(8,128)(2,1)S(1)}, u32[]{:S(2)}, u32[]{:S(2)}) collective-permute-start(bf16[256,512]{1,0:T(8,128)(2,1)S(1)} %pad_maximum_fusion.6), channel_id=1, source_target_pairs={{0,4},{1,5},{2,14},{3,15},{4,16},{5,17},{6,26},{7,27},{8,6},{9,7},... | collective-permute-start | bytes 786440 | tf_op jit(solution)/shard_map/ppermute | solution.py:274
  153.4 22.6 %collective-permute-start.8 = (bf16[256,512]{1,0:T(8,128)(2,1)S(1)}, bf16[256,512]{1,0:T(8,128)(2,1)S(1)}, u32[]{:S(2)}, u32[]{:S(2)}) collective-permute-start(bf16[256,512]{1,0:T(8,128)(2,1)S(1)} %pad_maximum_fusion.7), channel_id=1, source_target_pairs={{0,6},{1,7},{2,12},{3,13},{4,18},{5,19},{6,24},{7,25},{8,4},{9,5},... | collective-permute-start | bytes 786440 | tf_op jit(solution)/shard_map/ppermute | solution.py:274
  176.1 22.8 %collective-permute-start.9 = (bf16[256,512]{1,0:T(8,128)(2,1)}, bf16[256,512]{1,0:T(8,128)(2,1)S(1)}, u32[]{:S(2)}, u32[]{:S(2)}) collective-permute-start(bf16[256,512]{1,0:T(8,128)(2,1)} %get-tuple-element.126), channel_id=1, source_target_pairs={{0,8},{8,0},{16,24},{24,16},{1,9},{9,1},{17,25},{25,17},{2,10},{10... | collective-permute-start | bytes 786440 | tf_op jit(solution)/shard_map/ppermute | solution.py:280
  177.6 21.3 %collective-permute-start.10 = (bf16[256,512]{1,0:T(8,128)(2,1)}, bf16[256,512]{1,0:T(8,128)(2,1)S(1)}, u32[]{:S(2)}, u32[]{:S(2)}) collective-permute-start(bf16[256,512]{1,0:T(8,128)(2,1)} %get-tuple-element.127), channel_id=1, source_target_pairs={{0,16},{8,24},{16,0},{24,8},{1,17},{9,25},{17,1},{25,9},{2,18},{10... | collective-permute-start | bytes 786440 | tf_op jit(solution)/shard_map/ppermute | solution.py:280
  182.6 16.3 %collective-permute-start.11 = (bf16[256,512]{1,0:T(8,128)(2,1)}, bf16[256,512]{1,0:T(8,128)(2,1)S(1)}, u32[]{:S(2)}, u32[]{:S(2)}) collective-permute-start(bf16[256,512]{1,0:T(8,128)(2,1)} %get-tuple-element.128), channel_id=1, source_target_pairs={{0,24},{8,16},{16,8},{24,0},{1,25},{9,17},{17,9},{25,1},{2,26},{10... | collective-permute-start | bytes 786440 | tf_op jit(solution)/shard_map/ppermute | solution.py:280
  200.8 17.6 %collective-permute-start.16 = (bf16[512,512]{1,0:T(8,128)(2,1)S(1)}, bf16[512,512]{1,0:T(8,128)(2,1)S(1)}, u32[]{:S(2)}, u32[]{:S(2)}) collective-permute-start(bf16[512,512]{1,0:T(8,128)(2,1)S(1)} %slice.150), channel_id=1, source_target_pairs={{0,1},{1,0},{2,3},{3,2},{4,5},{5,4},{6,7},{7,6},{8,9},{9,8},{10,11... | collective-permute-start | bytes 1572872 | tf_op jit(solution)/shard_map/ppermute | solution.py:263
  201.4 18.5 %collective-permute-start.12 = (bf16[128,512]{1,0:T(8,128)(2,1)S(1)}, bf16[128,512]{1,0:T(8,128)(2,1)S(1)}, u32[]{:S(2)}, u32[]{:S(2)}) collective-permute-start(bf16[128,512]{1,0:T(8,128)(2,1)S(1)} %get-tuple-element.141), channel_id=1, source_target_pairs={{0,7},{1,6},{2,5},{3,4},{4,3},{5,2},{6,1},{7,0},{8,15},{9,14},{10,... | collective-permute-start | bytes 393224 | tf_op jit(solution)/shard_map/ppermute | solution.py:285
  205.0 12.5 %collective-permute-start.49 = (bf16[128,512]{1,0:T(8,128)(2,1)S(1)}, bf16[128,512]{1,0:T(8,128)(2,1)S(1)}, u32[]{:S(2)}, u32[]{:S(2)}) collective-permute-start(bf16[128,512]{1,0:T(8,128)(2,1)S(1)} %get-tuple-element.204), channel_id=1, source_target_pairs={{0,3},{1,2},{2,1},{3,0},{4,7},{5,6},{6,5},{7,4},{8,11},{9,10},{10,... | collective-permute-start | bytes 393224 | tf_op jit(solution)/shard_map/ppermute | solution.py:285
  205.7 15.6 %collective-permute-start.50 = (bf16[128,512]{1,0:T(8,128)(2,1)S(1)}, bf16[128,512]{1,0:T(8,128)(2,1)S(1)}, u32[]{:S(2)}, u32[]{:S(2)}) collective-permute-start(bf16[128,512]{1,0:T(8,128)(2,1)S(1)} %get-tuple-element.205), channel_id=1, source_target_pairs={{0,4},{1,5},{2,6},{3,7},{4,0},{5,1},{6,2},{7,3},{8,12},{9,13},{10,... | collective-permute-start | bytes 393224 | tf_op jit(solution)/shard_map/ppermute | solution.py:285
  217.5 14.8 %collective-permute-start.13 = (bf16[256,512]{1,0:T(8,128)(2,1)S(1)}, bf16[256,512]{1,0:T(8,128)(2,1)S(1)}, u32[]{:S(2)}, u32[]{:S(2)}) collective-permute-start(bf16[256,512]{1,0:T(8,128)(2,1)S(1)} %copy-done.28), channel_id=1, source_target_pairs={{0,8},{8,0},{16,24},{24,16},{1,9},{9,1},{17,25},{25,17},{2,10},{10... | collective-permute-start | bytes 786440 | tf_op jit(solution)/shard_map/ppermute | solution.py:280
  218.4 17.5 %collective-permute-start.14 = (bf16[256,512]{1,0:T(8,128)(2,1)S(1)}, bf16[256,512]{1,0:T(8,128)(2,1)S(1)}, u32[]{:S(2)}, u32[]{:S(2)}) collective-permute-start(bf16[256,512]{1,0:T(8,128)(2,1)S(1)} %copy-done.27), channel_id=1, source_target_pairs={{0,16},{8,24},{16,0},{24,8},{1,17},{9,25},{17,1},{25,9},{2,18},{10... | collective-permute-start | bytes 786440 | tf_op jit(solution)/shard_map/ppermute | solution.py:280
  221.4 27.7 %collective-permute-start.15 = (bf16[256,512]{1,0:T(8,128)(2,1)S(1)}, bf16[256,512]{1,0:T(8,128)(2,1)S(1)}, u32[]{:S(2)}, u32[]{:S(2)}) collective-permute-start(bf16[256,512]{1,0:T(8,128)(2,1)S(1)} %copy-done.26), channel_id=1, source_target_pairs={{0,24},{8,16},{16,8},{24,0},{1,25},{9,17},{17,9},{25,1},{2,26},{10... | collective-permute-start | bytes 786440 | tf_op jit(solution)/shard_map/ppermute | solution.py:280
  223.7 25.3 %collective-permute-start.17 = (bf16[256,512]{1,0:T(8,128)(2,1)S(1)}, bf16[256,512]{1,0:T(8,128)(2,1)S(1)}, u32[]{:S(2)}, u32[]{:S(2)}) collective-permute-start(bf16[256,512]{1,0:T(8,128)(2,1)S(1)} %pad_maximum_fusion.8), channel_id=1, source_target_pairs={{0,0},{1,1},{2,10},{3,11},{4,20},{5,21},{6,30},{7,31},{8,2},{9,3},... | collective-permute-start | bytes 786440 | tf_op jit(solution)/shard_map/ppermute | solution.py:274
  227.2 24.9 %collective-permute-start.18 = (bf16[256,512]{1,0:T(8,128)(2,1)S(1)}, bf16[256,512]{1,0:T(8,128)(2,1)S(1)}, u32[]{:S(2)}, u32[]{:S(2)}) collective-permute-start(bf16[256,512]{1,0:T(8,128)(2,1)S(1)} %pad_maximum_fusion.9), channel_id=1, source_target_pairs={{0,2},{1,3},{2,8},{3,9},{4,22},{5,23},{6,28},{7,29},{8,0},{9,1},{1... | collective-permute-start | bytes 786440 | tf_op jit(solution)/shard_map/ppermute | solution.py:274
  232.2 21.4 %collective-permute-start.19 = (bf16[256,512]{1,0:T(8,128)(2,1)S(1)}, bf16[256,512]{1,0:T(8,128)(2,1)S(1)}, u32[]{:S(2)}, u32[]{:S(2)}) collective-permute-start(bf16[256,512]{1,0:T(8,128)(2,1)S(1)} %pad_maximum_fusion.10), channel_id=1, source_target_pairs={{0,4},{1,5},{2,14},{3,15},{4,16},{5,17},{6,26},{7,27},{8,6},{9,7},... | collective-permute-start | bytes 786440 | tf_op jit(solution)/shard_map/ppermute | solution.py:274
  235.9 22.8 %collective-permute-start.20 = (bf16[256,512]{1,0:T(8,128)(2,1)S(1)}, bf16[256,512]{1,0:T(8,128)(2,1)S(1)}, u32[]{:S(2)}, u32[]{:S(2)}) collective-permute-start(bf16[256,512]{1,0:T(8,128)(2,1)S(1)} %pad_maximum_fusion.11), channel_id=1, source_target_pairs={{0,6},{1,7},{2,12},{3,13},{4,18},{5,19},{6,24},{7,25},{8,4},{9,5},... | collective-permute-start | bytes 786440 | tf_op jit(solution)/shard_map/ppermute | solution.py:274
  259.5 24.8 %collective-permute-start.21 = (bf16[128,512]{1,0:T(8,128)(2,1)S(1)}, bf16[128,512]{1,0:T(8,128)(2,1)S(1)}, u32[]{:S(2)}, u32[]{:S(2)}) collective-permute-start(bf16[128,512]{1,0:T(8,128)(2,1)S(1)} %get-tuple-element.151), channel_id=1, source_target_pairs={{0,7},{1,6},{2,5},{3,4},{4,3},{5,2},{6,1},{7,0},{8,15},{9,14},{10,... | collective-permute-start | bytes 393224 | tf_op jit(solution)/shard_map/ppermute | solution.py:285
  266.9 17.3 %collective-permute-start.57 = (bf16[128,512]{1,0:T(8,128)(2,1)S(1)}, bf16[128,512]{1,0:T(8,128)(2,1)S(1)}, u32[]{:S(2)}, u32[]{:S(2)}) collective-permute-start(bf16[128,512]{1,0:T(8,128)(2,1)S(1)} %get-tuple-element.213), channel_id=1, source_target_pairs={{0,5},{1,4},{2,7},{3,6},{4,1},{5,0},{6,3},{7,2},{8,13},{9,12},{10,... | collective-permute-start | bytes 393224 | tf_op jit(solution)/shard_map/ppermute | solution.py:285
  270.2 14.1 %collective-permute-start.58 = (bf16[128,512]{1,0:T(8,128)(2,1)S(1)}, bf16[128,512]{1,0:T(8,128)(2,1)S(1)}, u32[]{:S(2)}, u32[]{:S(2)}) collective-permute-start(bf16[128,512]{1,0:T(8,128)(2,1)S(1)} %get-tuple-element.214), channel_id=1, source_target_pairs={{0,6},{1,7},{2,4},{3,5},{4,2},{5,3},{6,0},{7,1},{8,14},{9,15},{10,... | collective-permute-start | bytes 393224 | tf_op jit(solution)/shard_map/ppermute | solution.py:285
  285.7 234.0 %all-gather.3.cloned.1.call-start = ((), (), s32[]{:S(2)}) async-start(), calls=%async_computation.6 | async-start | bytes 10485760 | tf_op jit(solution)/shard_map/all_gather | solution.py:305
  302.0 18.1 %collective-permute-start.22 = (bf16[256,512]{1,0:T(8,128)(2,1)}, bf16[256,512]{1,0:T(8,128)(2,1)S(1)}, u32[]{:S(2)}, u32[]{:S(2)}) collective-permute-start(bf16[256,512]{1,0:T(8,128)(2,1)} %get-tuple-element.161), channel_id=1, source_target_pairs={{0,8},{8,0},{16,24},{24,16},{1,9},{9,1},{17,25},{25,17},{2,10},{10... | collective-permute-start | bytes 786440 | tf_op jit(solution)/shard_map/ppermute | solution.py:280
  307.2 18.7 %collective-permute-start.23 = (bf16[256,512]{1,0:T(8,128)(2,1)}, bf16[256,512]{1,0:T(8,128)(2,1)S(1)}, u32[]{:S(2)}, u32[]{:S(2)}) collective-permute-start(bf16[256,512]{1,0:T(8,128)(2,1)} %get-tuple-element.162), channel_id=1, source_target_pairs={{0,16},{8,24},{16,0},{24,8},{1,17},{9,25},{17,1},{25,9},{2,18},{10... | collective-permute-start | bytes 786440 | tf_op jit(solution)/shard_map/ppermute | solution.py:280
  309.6 30.1 %collective-permute-start.24 = (bf16[256,512]{1,0:T(8,128)(2,1)}, bf16[256,512]{1,0:T(8,128)(2,1)S(1)}, u32[]{:S(2)}, u32[]{:S(2)}) collective-permute-start(bf16[256,512]{1,0:T(8,128)(2,1)} %get-tuple-element.163), channel_id=1, source_target_pairs={{0,24},{8,16},{16,8},{24,0},{1,25},{9,17},{17,9},{25,1},{2,26},{10... | collective-permute-start | bytes 786440 | tf_op jit(solution)/shard_map/ppermute | solution.py:280
  312.2 27.5 %collective-permute-start.26 = (bf16[256,512]{1,0:T(8,128)(2,1)S(1)}, bf16[256,512]{1,0:T(8,128)(2,1)S(1)}, u32[]{:S(2)}, u32[]{:S(2)}) collective-permute-start(bf16[256,512]{1,0:T(8,128)(2,1)S(1)} %pad_maximum_fusion.12), channel_id=1, source_target_pairs={{0,0},{1,1},{2,10},{3,11},{4,20},{5,21},{6,30},{7,31},{8,2},{9,3},... | collective-permute-start | bytes 786440 | tf_op jit(solution)/shard_map/ppermute | solution.py:274
  313.0 29.5 %collective-permute-start.27 = (bf16[256,512]{1,0:T(8,128)(2,1)S(1)}, bf16[256,512]{1,0:T(8,128)(2,1)S(1)}, u32[]{:S(2)}, u32[]{:S(2)}) collective-permute-start(bf16[256,512]{1,0:T(8,128)(2,1)S(1)} %pad_maximum_fusion.13), channel_id=1, source_target_pairs={{0,2},{1,3},{2,8},{3,9},{4,22},{5,23},{6,28},{7,29},{8,0},{9,1},{1... | collective-permute-start | bytes 786440 | tf_op jit(solution)/shard_map/ppermute | solution.py:274
  320.1 23.0 %collective-permute-start.28 = (bf16[256,512]{1,0:T(8,128)(2,1)S(1)}, bf16[256,512]{1,0:T(8,128)(2,1)S(1)}, u32[]{:S(2)}, u32[]{:S(2)}) collective-permute-start(bf16[256,512]{1,0:T(8,128)(2,1)S(1)} %pad_maximum_fusion.14), channel_id=1, source_target_pairs={{0,4},{1,5},{2,14},{3,15},{4,16},{5,17},{6,26},{7,27},{8,6},{9,7},... | collective-permute-start | bytes 786440 | tf_op jit(solution)/shard_map/ppermute | solution.py:274
  325.9 23.7 %collective-permute-start.29 = (bf16[256,512]{1,0:T(8,128)(2,1)S(1)}, bf16[256,512]{1,0:T(8,128)(2,1)S(1)}, u32[]{:S(2)}, u32[]{:S(2)}) collective-permute-start(bf16[256,512]{1,0:T(8,128)(2,1)S(1)} %pad_maximum_fusion.15), channel_id=1, source_target_pairs={{0,6},{1,7},{2,12},{3,13},{4,18},{5,19},{6,24},{7,25},{8,4},{9,5},... | collective-permute-start | bytes 786440 | tf_op jit(solution)/shard_map/ppermute | solution.py:274
  350.2 22.2 %collective-permute-start.30 = (bf16[128,512]{1,0:T(8,128)(2,1)S(1)}, bf16[128,512]{1,0:T(8,128)(2,1)S(1)}, u32[]{:S(2)}, u32[]{:S(2)}) collective-permute-start(bf16[128,512]{1,0:T(8,128)(2,1)S(1)} %get-tuple-element.170), channel_id=1, source_target_pairs={{0,1},{1,0},{2,3},{3,2},{4,5},{5,4},{6,7},{7,6},{8,9},{9,8},{10,11... | collective-permute-start | bytes 393224 | tf_op jit(solution)/shard_map/ppermute | solution.py:285
  350.3 25.8 %collective-permute-start.31 = (bf16[128,512]{1,0:T(8,128)(2,1)S(1)}, bf16[128,512]{1,0:T(8,128)(2,1)S(1)}, u32[]{:S(2)}, u32[]{:S(2)}) collective-permute-start(bf16[128,512]{1,0:T(8,128)(2,1)S(1)} %get-tuple-element.171), channel_id=1, source_target_pairs={{0,2},{1,3},{2,0},{3,1},{4,6},{5,7},{6,4},{7,5},{8,10},{9,11},{10,... | collective-permute-start | bytes 393224 | tf_op jit(solution)/shard_map/ppermute | solution.py:285
  353.4 23.6 %collective-permute-start.32 = (bf16[128,512]{1,0:T(8,128)(2,1)S(1)}, bf16[128,512]{1,0:T(8,128)(2,1)S(1)}, u32[]{:S(2)}, u32[]{:S(2)}) collective-permute-start(bf16[128,512]{1,0:T(8,128)(2,1)S(1)} %get-tuple-element.172), channel_id=1, source_target_pairs={{0,3},{1,2},{2,1},{3,0},{4,7},{5,6},{6,5},{7,4},{8,11},{9,10},{10,... | collective-permute-start | bytes 393224 | tf_op jit(solution)/shard_map/ppermute | solution.py:285
  353.5 25.5 %collective-permute-start.33 = (bf16[128,512]{1,0:T(8,128)(2,1)S(1)}, bf16[128,512]{1,0:T(8,128)(2,1)S(1)}, u32[]{:S(2)}, u32[]{:S(2)}) collective-permute-start(bf16[128,512]{1,0:T(8,128)(2,1)S(1)} %get-tuple-element.173), channel_id=1, source_target_pairs={{0,4},{1,5},{2,6},{3,7},{4,0},{5,1},{6,2},{7,3},{8,12},{9,13},{10,... | collective-permute-start | bytes 393224 | tf_op jit(solution)/shard_map/ppermute | solution.py:285
  357.5 16.7 %collective-permute-start.36 = (bf16[128,512]{1,0:T(8,128)(2,1)S(1)}, bf16[128,512]{1,0:T(8,128)(2,1)S(1)}, u32[]{:S(2)}, u32[]{:S(2)}) collective-permute-start(bf16[128,512]{1,0:T(8,128)(2,1)S(1)} %get-tuple-element.176), channel_id=1, source_target_pairs={{0,7},{1,6},{2,5},{3,4},{4,3},{5,2},{6,1},{7,0},{8,15},{9,14},{10,... | collective-permute-start | bytes 393224 | tf_op jit(solution)/shard_map/ppermute | solution.py:285
  372.4 12.1 %collective-permute-start.34 = (bf16[128,512]{1,0:T(8,128)(2,1)S(1)}, bf16[128,512]{1,0:T(8,128)(2,1)S(1)}, u32[]{:S(2)}, u32[]{:S(2)}) collective-permute-start(bf16[128,512]{1,0:T(8,128)(2,1)S(1)} %get-tuple-element.174), channel_id=1, source_target_pairs={{0,5},{1,4},{2,7},{3,6},{4,1},{5,0},{6,3},{7,2},{8,13},{9,12},{10,... | collective-permute-start | bytes 393224 | tf_op jit(solution)/shard_map/ppermute | solution.py:285
  376.1 15.0 %collective-permute-start.37 = (bf16[256,512]{1,0:T(8,128)(2,1)}, bf16[256,512]{1,0:T(8,128)(2,1)S(1)}, u32[]{:S(2)}, u32[]{:S(2)}) collective-permute-start(bf16[256,512]{1,0:T(8,128)(2,1)} %get-tuple-element.186), channel_id=1, source_target_pairs={{0,8},{8,0},{16,24},{24,16},{1,9},{9,1},{17,25},{25,17},{2,10},{10... | collective-permute-start | bytes 786440 | tf_op jit(solution)/shard_map/ppermute | solution.py:280
  377.0 14.7 %collective-permute-start.38 = (bf16[256,512]{1,0:T(8,128)(2,1)}, bf16[256,512]{1,0:T(8,128)(2,1)S(1)}, u32[]{:S(2)}, u32[]{:S(2)}) collective-permute-start(bf16[256,512]{1,0:T(8,128)(2,1)} %get-tuple-element.187), channel_id=1, source_target_pairs={{0,16},{8,24},{16,0},{24,8},{1,17},{9,25},{17,1},{25,9},{2,18},{10... | collective-permute-start | bytes 786440 | tf_op jit(solution)/shard_map/ppermute | solution.py:280
  379.0 25.1 %collective-permute-start.39 = (bf16[256,512]{1,0:T(8,128)(2,1)}, bf16[256,512]{1,0:T(8,128)(2,1)S(1)}, u32[]{:S(2)}, u32[]{:S(2)}) collective-permute-start(bf16[256,512]{1,0:T(8,128)(2,1)} %get-tuple-element.188), channel_id=1, source_target_pairs={{0,24},{8,16},{16,8},{24,0},{1,25},{9,17},{17,9},{25,1},{2,26},{10... | collective-permute-start | bytes 786440 | tf_op jit(solution)/shard_map/ppermute | solution.py:280
  409.1 18.5 %collective-permute-start.44 = (bf16[128,512]{1,0:T(8,128)(2,1)S(1)}, bf16[128,512]{1,0:T(8,128)(2,1)S(1)}, u32[]{:S(2)}, u32[]{:S(2)}) collective-permute-start(bf16[128,512]{1,0:T(8,128)(2,1)S(1)} %get-tuple-element.198), channel_id=1, source_target_pairs={{0,5},{1,4},{2,7},{3,6},{4,1},{5,0},{6,3},{7,2},{8,13},{9,12},{10,... | collective-permute-start | bytes 393224 | tf_op jit(solution)/shard_map/ppermute | solution.py:285
  410.3 17.4 %collective-permute-start.45 = (bf16[128,512]{1,0:T(8,128)(2,1)S(1)}, bf16[128,512]{1,0:T(8,128)(2,1)S(1)}, u32[]{:S(2)}, u32[]{:S(2)}) collective-permute-start(bf16[128,512]{1,0:T(8,128)(2,1)S(1)} %get-tuple-element.199), channel_id=1, source_target_pairs={{0,6},{1,7},{2,4},{3,5},{4,2},{5,3},{6,0},{7,1},{8,14},{9,15},{10,... | collective-permute-start | bytes 393224 | tf_op jit(solution)/shard_map/ppermute | solution.py:285
  (45 other events, 727.1 us)
Sparse Core Ops, SparseCore 0:
  16.4 89.0 reduce-scatter.3
  108.8 85.8 reduce-scatter.5
  197.7 83.8 reduce-scatter.7
  285.8 128.0 all-gather.4
  429.2 90.4 all-gather.2

commit v6 on v5

--- a/solution.py
+++ b/solution.py
@@ -246,10 +246,9 @@
     }
 
     half = max(per // 2, 1)
-    sums = [(0, half)] + [(slot, 1) for slot in range(half, per)]
-    gathers = [(first, min(half, per - first)) for first in range(0, per, half)]
-    begins = [slot if slot < half else half + 1 + 2 * (slot - half) for slot in range(per)]
-    group_of = [max(g for g, (first, _) in enumerate(sums) if first <= slot) for slot in range(per)]
+    sums = gathers = [(first, min(half, per - first)) for first in range(0, per, half)]
+    begins = [slot + 2 * (slot // half) for slot in range(per)]
+    group_of = [slot // half for slot in range(per)]
     ready = []
     for slots in sums:
         packed = pack(ranks, inner, slots, per, place, grads)

time: 537 us -> 530 us (0.987)
  starting transfers between devices: 145 us -> 122 us
  waiting for transfers between devices: 235 us -> 252 us
    reduce_scatter x3 -> x2, waiting for transfers between devices: 48.3 us -> 64.9 us  [shards(): lax.psum_scatter(packed, 'dp', scatter_dimension=0, tiled=True)]
    ppermute x16, starting transfers between devices: 82.1 us -> 66.1 us  [send_in(): lax.ppermute(strips[k], MESH_AXES, to_owner[k])]
    ppermute x28, waiting for transfers between devices: 46.1 us -> 52 us  [send_columns(): lax.ppermute(piece, 'fsdp', to_column[key])]
    pallas_call x3 -> x2, Pallas kernels: 18.7 us -> 18.2 us  [pack(): pl.pallas_call(functools.partial(pack_kernel, ranks, inner), grid=(ranks,...]
  transfers between devices with their start and end apart: 64 -> 62, of which waited for: 27 -> 27; matrix products, arithmetic and copies ran while one was open for 1% -> 2% of each run, Pallas kernels for 21% -> 21%
where the time goes in v6:
time: 530 us; the launch traced here: 529 us
  waiting for transfers between devices  252 us (48%)
  Pallas kernels  130 us (25%)
  starting transfers between devices  122 us (23%)
  between operations  14.1 us (3%)
  local copies, waits for them, and re-layouts  10.2 us (2%)
    all_gather x2, waiting for transfers between devices, shards(): lax.all_gather(jnp.concatenate(back, axis=0), 'dp', axis=0, tiled=True)  81.2 us
    ppermute x16, starting transfers between devices, send_in(): lax.ppermute(strips[k], MESH_AXES, to_owner[k])  66.1 us
    reduce_scatter x2, waiting for transfers between devices, shards(): lax.psum_scatter(packed, 'dp', scatter_dimension=0, tiled=True)  64.9 us
    pallas_call x4, Pallas kernels, precondition(): pl.pallas_call(functools.partial(block_kernel, ranks, inner, col_blocks),...  59.4 us
    ppermute x28, waiting for transfers between devices, send_columns(): lax.ppermute(piece, 'fsdp', to_column[key])  52 us
    ppermute x16, waiting for transfers between devices, send_in(): lax.ppermute(strips[k], MESH_AXES, to_owner[k])  34.8 us
    ppermute x28, starting transfers between devices, send_columns(): lax.ppermute(piece, 'fsdp', to_column[key])  31.8 us
    pallas_call x1, Pallas kernels, fourth_powers(): pl.pallas_call(fourth_kernel, grid=(slabs, col_blocks), in_specs=[spec, s...  31.3 us
  transfers between devices with their start and end apart: 62, of which 27 were waited for; matrix products, arithmetic and copies ran while one was open for 2% of the time, Pallas kernels for 21%

profile of v6, /device:TPU:0, one launch (start us, length us, event | category | flops | bytes accessed | tf_op | source)
XLA Modules:
  0.0 528.7 jit_solution(13830964728203681008)
XLA Ops:
  7.1 9.1 %pack_slabs.2 = bf16[4,2,2,4,128,512]{5,4,3,2,1,0:T(8,128)(2,1)} custom-call(s32[3]{0:T(128)} %pad_add_fusion.place_ref, bf16[8,4,512,512]{3,2,1,0:T(8,128)(2,1)} %bitcast.9), custom_call_target="tpu_custom_call" | custom-call | bytes 16777216 | tf_op jit(solution)/shard_map/pack_slabs/pallas_call | solution.py:75
  16.3 9.1 %pack_slabs.3 = bf16[4,2,2,4,128,512]{5,4,3,2,1,0:T(8,128)(2,1)} custom-call(s32[3]{0:T(128)} %pad_add_fusion.place_ref, bf16[8,4,512,512]{3,2,1,0:T(8,128)(2,1)} %bitcast.10), custom_call_target="tpu_custom_call" | custom-call | bytes 16777216 | tf_op jit(solution)/shard_map/pack_slabs/pallas_call | solution.py:75
  25.4 31.3 %fourth_powers.1 = (f32[4,2,512,512]{3,2,1,0:T(8,128)}, f32[4,2,512,512]{3,2,1,0:T(8,128)}) custom-call(f32[4,2,512,512]{3,2,1,0:T(8,128)} %refs_6_.7, f32[4,2,512,512]{3,2,1,0:T(8,128)} %refs_7_.7), custom_call_target="tpu_custom_call" | custom-call | flops 25769803776 | bytes 33554432 | tf_op jit(solution)/shard_map/fourth_powers/pallas_call | solution.py:45
  56.7 48.8 %reduce-scatter.3.cloned.1.call-done = bf16[2048,512]{1,0:T(8,128)(2,1)} async-done(((bf16[8192,512]{1,0:T(8,128)(2,1)}), bf16[2048,512]{1,0:T(8,128)(2,1)}) %reduce-scatter.3.cloned.1.call-update) | async-done | bytes 2097168 | tf_op jit(solution)/shard_map/reduce_scatter | solution.py:255
  110.7 6.0 %collective-permute-start.2 = (bf16[256,512]{1,0:T(8,128)(2,1)S(1)}, bf16[256,512]{1,0:T(8,128)(2,1)S(1)}, u32[]{:S(2)}, u32[]{:S(2)}) collective-permute-start(bf16[256,512]{1,0:T(8,128)(2,1)S(1)} %pad_maximum_fusion.1), channel_id=1, source_target_pairs={{0,2},{1,3},{2,8},{3,9},{4,22},{5,23},{6,28},{7,29},{8,0},{9,1},{1... | collective-permute-start | bytes 786440 | tf_op jit(solution)/shard_map/ppermute | solution.py:273
  116.7 4.4 collective-permute-start.3
  121.1 5.2 collective-permute-start.4
  126.3 2.6 collective-permute-done.2.refs_1_
  128.9 10.7 %collective-permute-done.3.refs_2_ = bf16[256,512]{1,0:T(8,128)(2,1)S(1)} collective-permute-done((bf16[256,512]{1,0:T(8,128)(2,1)S(1)}, bf16[256,512]{1,0:T(8,128)(2,1)S(1)}, u32[]{:S(2)}, u32[]{:S(2)}) %collective-permute-start.3) | collective-permute-done | bytes 262176 | tf_op jit(solution)/shard_map/ppermute | solution.py:273
  139.6 4.1 collective-permute-done.4.refs_3_
  144.5 4.4 collective-permute-start.6
  148.9 4.4 collective-permute-start.7
  153.3 7.9 %collective-permute-start.8 = (bf16[256,512]{1,0:T(8,128)(2,1)S(1)}, bf16[256,512]{1,0:T(8,128)(2,1)S(1)}, u32[]{:S(2)}, u32[]{:S(2)}) collective-permute-start(bf16[256,512]{1,0:T(8,128)(2,1)S(1)} %pad_maximum_fusion.7), channel_id=1, source_target_pairs={{0,6},{1,7},{2,12},{3,13},{4,18},{5,19},{6,24},{7,25},{8,4},{9,5},... | collective-permute-start | bytes 786440 | tf_op jit(solution)/shard_map/ppermute | solution.py:273
  161.2 14.9 %precondition.4 = (bf16[256,512]{1,0:T(8,128)(2,1)}, bf16[256,512]{1,0:T(8,128)(2,1)}, bf16[256,512]{1,0:T(8,128)(2,1)}, bf16[256,512]{1,0:T(8,128)(2,1)}) custom-call(s32[3]{0:T(128)} %pad_add_fusion.place_ref, bf16[256,512]{1,0:T(8,128)(2,1)} %copy-done.10, bf16[256,512]{1,0:T(8,128)(2,1)} %copy-done.12, bf16[256,512]{1,0:T(8,128)(2,1)} %copy-done.14, ...), custom_call_target="tpu_custom_call" | custom-call | flops 8589934592 | bytes 14680064 | tf_op jit(solution)/shard_map/precondition/pallas_call | solution.py:205
  177.8 4.8 collective-permute-start.10
  184.0 14.9 %precondition.5 = (bf16[256,512]{1,0:T(8,128)(2,1)}, bf16[256,512]{1,0:T(8,128)(2,1)}, bf16[256,512]{1,0:T(8,128)(2,1)}, bf16[256,512]{1,0:T(8,128)(2,1)}) custom-call(s32[3]{0:T(128)} %pad_add_fusion.place_ref, bf16[256,512]{1,0:T(8,128)(2,1)} %copy-done.18, bf16[256,512]{1,0:T(8,128)(2,1)} %copy-done.20, bf16[256,512]{1,0:T(8,128)(2,1)} %copy-done.22, ...), custom_call_target="tpu_custom_call" | custom-call | flops 8589934592 | bytes 14680064 | tf_op jit(solution)/shard_map/precondition/pallas_call | solution.py:205
  204.2 2.9 collective-permute-start.51
  207.0 3.1 collective-permute-done.47
  212.6 2.8 collective-permute-start.15
  215.4 3.5 collective-permute-done.50
  218.9 3.4 collective-permute-start.12
  222.4 16.1 %reduce-scatter.5.cloned.1.call-done = bf16[2048,512]{1,0:T(8,128)(2,1)} async-done(((bf16[8192,512]{1,0:T(8,128)(2,1)}), bf16[2048,512]{1,0:T(8,128)(2,1)}) %reduce-scatter.5.cloned.1.call-update) | async-done | bytes 2097168 | tf_op jit(solution)/shard_map/reduce_scatter | solution.py:255
  239.3 3.5 collective-permute-start.16
  244.8 3.0 collective-permute-start.56
  248.5 5.2 collective-permute-done.53
  253.7 3.5 collective-permute-start.57
  259.2 3.3 collective-permute-done.56
  268.5 7.4 %collective-permute-start.19 = (bf16[256,512]{1,0:T(8,128)(2,1)S(1)}, bf16[256,512]{1,0:T(8,128)(2,1)S(1)}, u32[]{:S(2)}, u32[]{:S(2)}) collective-permute-start(bf16[256,512]{1,0:T(8,128)(2,1)S(1)} %pad_maximum_fusion.9), channel_id=1, source_target_pairs={{0,2},{1,3},{2,8},{3,9},{4,22},{5,23},{6,28},{7,29},{8,0},{9,1},{1... | collective-permute-start | bytes 786440 | tf_op jit(solution)/shard_map/ppermute | solution.py:273
  275.9 4.4 collective-permute-start.20
  280.3 5.2 collective-permute-start.21
  288.0 9.3 %collective-permute-done.20.refs_2_ = bf16[256,512]{1,0:T(8,128)(2,1)S(1)} collective-permute-done((bf16[256,512]{1,0:T(8,128)(2,1)S(1)}, bf16[256,512]{1,0:T(8,128)(2,1)S(1)}, u32[]{:S(2)}, u32[]{:S(2)}) %collective-permute-start.20) | collective-permute-done | bytes 262176 | tf_op jit(solution)/shard_map/ppermute | solution.py:273
  297.3 5.7 %collective-permute-done.21.refs_3_ = bf16[256,512]{1,0:T(8,128)(2,1)S(1)} collective-permute-done((bf16[256,512]{1,0:T(8,128)(2,1)S(1)}, bf16[256,512]{1,0:T(8,128)(2,1)S(1)}, u32[]{:S(2)}, u32[]{:S(2)}) %collective-permute-start.21) | collective-permute-done | bytes 262176 | tf_op jit(solution)/shard_map/ppermute | solution.py:273
  303.8 3.4 collective-permute-start.23
  307.2 3.1 collective-permute-start.24
  310.4 7.9 %collective-permute-start.25 = (bf16[256,512]{1,0:T(8,128)(2,1)S(1)}, bf16[256,512]{1,0:T(8,128)(2,1)S(1)}, u32[]{:S(2)}, u32[]{:S(2)}) collective-permute-start(bf16[256,512]{1,0:T(8,128)(2,1)S(1)} %pad_maximum_fusion.15), channel_id=1, source_target_pairs={{0,6},{1,7},{2,12},{3,13},{4,18},{5,19},{6,24},{7,25},{8,4},{9,5},... | collective-permute-start | bytes 786440 | tf_op jit(solution)/shard_map/ppermute | solution.py:273
  318.3 14.7 %precondition.6 = (bf16[256,512]{1,0:T(8,128)(2,1)}, bf16[256,512]{1,0:T(8,128)(2,1)}, bf16[256,512]{1,0:T(8,128)(2,1)}, bf16[256,512]{1,0:T(8,128)(2,1)}) custom-call(s32[3]{0:T(128)} %pad_add_fusion.place_ref, bf16[256,512]{1,0:T(8,128)(2,1)} %copy-done.9, bf16[256,512]{1,0:T(8,128)(2,1)} %copy-done.11, bf16[256,512]{1,0:T(8,128)(2,1)} %copy-done.13, ...), custom_call_target="tpu_custom_call" | custom-call | flops 8589934592 | bytes 14680064 | tf_op jit(solution)/shard_map/precondition/pallas_call | solution.py:205
  334.6 5.3 %collective-permute-start.27 = (bf16[256,512]{1,0:T(8,128)(2,1)}, bf16[256,512]{1,0:T(8,128)(2,1)S(1)}, u32[]{:S(2)}, u32[]{:S(2)}) collective-permute-start(bf16[256,512]{1,0:T(8,128)(2,1)} %get-tuple-element.165), channel_id=1, source_target_pairs={{0,16},{8,24},{16,0},{24,8},{1,17},{9,25},{17,1},{25,9},{2,18},{10... | collective-permute-start | bytes 786440 | tf_op jit(solution)/shard_map/ppermute | solution.py:279
  341.4 14.9 %precondition.7 = (bf16[256,512]{1,0:T(8,128)(2,1)}, bf16[256,512]{1,0:T(8,128)(2,1)}, bf16[256,512]{1,0:T(8,128)(2,1)}, bf16[256,512]{1,0:T(8,128)(2,1)}) custom-call(s32[3]{0:T(128)} %pad_add_fusion.place_ref, bf16[256,512]{1,0:T(8,128)(2,1)} %copy-done.15, bf16[256,512]{1,0:T(8,128)(2,1)} %copy-done.19, bf16[256,512]{1,0:T(8,128)(2,1)} %copy-done.21, ...), custom_call_target="tpu_custom_call" | custom-call | flops 8589934592 | bytes 14680064 | tf_op jit(solution)/shard_map/precondition/pallas_call | solution.py:205
  356.3 8.9 %collective-permute-done.28.refs_3_ = bf16[256,512]{1,0:T(8,128)(2,1)S(1)} collective-permute-done((bf16[256,512]{1,0:T(8,128)(2,1)}, bf16[256,512]{1,0:T(8,128)(2,1)S(1)}, u32[]{:S(2)}, u32[]{:S(2)}) %collective-permute-start.28) | collective-permute-done | bytes 262176 | tf_op jit(solution)/shard_map/ppermute | solution.py:279
  367.8 2.6 collective-permute-start.33
  376.7 6.5 %collective-permute-done.32 = bf16[128,512]{1,0:T(8,128)(2,1)S(1)} collective-permute-done((bf16[128,512]{1,0:T(8,128)(2,1)S(1)}, bf16[128,512]{1,0:T(8,128)(2,1)S(1)}, u32[]{:S(2)}, u32[]{:S(2)}) %collective-permute-start.32) | collective-permute-done | bytes 131104 | tf_op jit(solution)/shard_map/ppermute | solution.py:284
  385.4 6.9 %collective-permute-done.35 = bf16[128,512]{1,0:T(8,128)(2,1)S(1)} collective-permute-done((bf16[128,512]{1,0:T(8,128)(2,1)S(1)}, bf16[128,512]{1,0:T(8,128)(2,1)S(1)}, u32[]{:S(2)}, u32[]{:S(2)}) %collective-permute-start.35) | collective-permute-done | bytes 131104 | tf_op jit(solution)/shard_map/ppermute | solution.py:284
  392.3 6.5 %collective-permute-done.38.refs_3_ = bf16[256,512]{1,0:T(8,128)(2,1)S(1)} collective-permute-done((bf16[256,512]{1,0:T(8,128)(2,1)S(1)}, bf16[256,512]{1,0:T(8,128)(2,1)S(1)}, u32[]{:S(2)}, u32[]{:S(2)}) %collective-permute-start.38) | collective-permute-done | bytes 262176 | tf_op jit(solution)/shard_map/ppermute | solution.py:279
  404.3 3.4 collective-permute-done.40
  409.8 10.2 %collective-permute-done.42 = bf16[128,512]{1,0:T(8,128)(2,1)S(1)} collective-permute-done((bf16[128,512]{1,0:T(8,128)(2,1)S(1)}, bf16[128,512]{1,0:T(8,128)(2,1)S(1)}, u32[]{:S(2)}, u32[]{:S(2)}) %collective-permute-start.42) | collective-permute-done | bytes 131104 | tf_op jit(solution)/shard_map/ppermute | solution.py:284
  422.9 9.0 %unpack_slabs.2.rest_0_ = bf16[8,4,512,512]{3,2,1,0:T(8,128)(2,1)} custom-call(s32[3]{0:T(128)} %pad_add_fusion.place_ref, bf16[4,2,8,128,512]{4,3,2,1,0:T(8,128)(2,1)} %bitcast.13), custom_call_target="tpu_custom_call" | custom-call | bytes 16777216 | tf_op jit(solution)/shard_map/unpack_slabs/pallas_call | solution.py:107
  432.0 81.1 %all-gather.3.cloned.1.call-done = bf16[8192,512]{1,0:T(8,128)(2,1)} async-done(((bf16[2048,512]{1,0:T(8,128)(2,1)}), bf16[8192,512]{1,0:T(8,128)(2,1)}) %all-gather.3.cloned.1.call-update) | async-done | bytes 8388624 | tf_op jit(solution)/shard_map/all_gather | solution.py:304
  513.1 9.0 %unpack_slabs.3 = bf16[8,4,512,512]{3,2,1,0:T(8,128)(2,1)} custom-call(s32[3]{0:T(128)} %pad_add_fusion.place_ref, bf16[4,2,8,128,512]{4,3,2,1,0:T(8,128)(2,1)} %bitcast.14, bf16[8,4,512,512]{3,2,1,0:T(8,128)(2,1)} %unpack_slabs.2.rest_0_), custom_call_target="tpu_custom_call", output_to_operand_aliasing={{}: (2, {})} | custom-call | bytes 16777216 | tf_op jit(solution)/shard_map/unpack_slabs/pallas_call | solution.py:107
  (203 shorter events, 56.6 us)
Async XLA Ops:
  6.5 99.0 %reduce-scatter.3.cloned.1.call-start = ((), (), s32[]{:S(2)}) async-start(), calls=%async_computation.2 | async-start | bytes 10485760 | tf_op jit(solution)/shard_map/reduce_scatter | solution.py:255
  16.2 222.2 %reduce-scatter.5.cloned.1.call-start = ((), (), s32[]{:S(2)}) async-start(), calls=%async_computation.3 | async-start | bytes 10485760 | tf_op jit(solution)/shard_map/reduce_scatter | solution.py:255
  25.4 397.6 %all-gather.5.cloned.1.call-start = ((), (), s32[]{:S(2)}) async-start(), calls=%async_computation.5 | async-start | bytes 10485760 | tf_op jit(solution)/shard_map/all_gather | solution.py:304
  110.0 16.3 %collective-permute-start.1 = (bf16[256,512]{1,0:T(8,128)(2,1)S(1)}, bf16[256,512]{1,0:T(8,128)(2,1)S(1)}, u32[]{:S(2)}, u32[]{:S(2)}) collective-permute-start(bf16[256,512]{1,0:T(8,128)(2,1)S(1)} %pad_maximum_fusion), channel_id=1, source_target_pairs={{0,0},{1,1},{2,10},{3,11},{4,20},{5,21},{6,30},{7,31},{8,2},{9,3},... | collective-permute-start | bytes 786440 | tf_op jit(solution)/shard_map/ppermute | solution.py:273
  110.7 18.2 %collective-permute-start.2 = (bf16[256,512]{1,0:T(8,128)(2,1)S(1)}, bf16[256,512]{1,0:T(8,128)(2,1)S(1)}, u32[]{:S(2)}, u32[]{:S(2)}) collective-permute-start(bf16[256,512]{1,0:T(8,128)(2,1)S(1)} %pad_maximum_fusion.1), channel_id=1, source_target_pairs={{0,2},{1,3},{2,8},{3,9},{4,22},{5,23},{6,28},{7,29},{8,0},{9,1},{1... | collective-permute-start | bytes 786440 | tf_op jit(solution)/shard_map/ppermute | solution.py:273
  116.7 22.9 %collective-permute-start.3 = (bf16[256,512]{1,0:T(8,128)(2,1)S(1)}, bf16[256,512]{1,0:T(8,128)(2,1)S(1)}, u32[]{:S(2)}, u32[]{:S(2)}) collective-permute-start(bf16[256,512]{1,0:T(8,128)(2,1)S(1)} %pad_maximum_fusion.2), channel_id=1, source_target_pairs={{0,4},{1,5},{2,14},{3,15},{4,16},{5,17},{6,26},{7,27},{8,6},{9,7},... | collective-permute-start | bytes 786440 | tf_op jit(solution)/shard_map/ppermute | solution.py:273
  121.1 22.6 %collective-permute-start.4 = (bf16[256,512]{1,0:T(8,128)(2,1)S(1)}, bf16[256,512]{1,0:T(8,128)(2,1)S(1)}, u32[]{:S(2)}, u32[]{:S(2)}) collective-permute-start(bf16[256,512]{1,0:T(8,128)(2,1)S(1)} %pad_maximum_fusion.3), channel_id=1, source_target_pairs={{0,6},{1,7},{2,12},{3,13},{4,18},{5,19},{6,24},{7,25},{8,4},{9,5},... | collective-permute-start | bytes 786440 | tf_op jit(solution)/shard_map/ppermute | solution.py:273
  143.8 32.4 %collective-permute-start.5 = (bf16[256,512]{1,0:T(8,128)(2,1)S(1)}, bf16[256,512]{1,0:T(8,128)(2,1)S(1)}, u32[]{:S(2)}, u32[]{:S(2)}) collective-permute-start(bf16[256,512]{1,0:T(8,128)(2,1)S(1)} %pad_maximum_fusion.4), channel_id=1, source_target_pairs={{0,0},{1,1},{2,10},{3,11},{4,20},{5,21},{6,30},{7,31},{8,2},{9,3},... | collective-permute-start | bytes 786440 | tf_op jit(solution)/shard_map/ppermute | solution.py:273
  144.5 31.7 %collective-permute-start.6 = (bf16[256,512]{1,0:T(8,128)(2,1)S(1)}, bf16[256,512]{1,0:T(8,128)(2,1)S(1)}, u32[]{:S(2)}, u32[]{:S(2)}) collective-permute-start(bf16[256,512]{1,0:T(8,128)(2,1)S(1)} %pad_maximum_fusion.5), channel_id=1, source_target_pairs={{0,2},{1,3},{2,8},{3,9},{4,22},{5,23},{6,28},{7,29},{8,0},{9,1},{1... | collective-permute-start | bytes 786440 | tf_op jit(solution)/shard_map/ppermute | solution.py:273
  148.9 27.3 %collective-permute-start.7 = (bf16[256,512]{1,0:T(8,128)(2,1)S(1)}, bf16[256,512]{1,0:T(8,128)(2,1)S(1)}, u32[]{:S(2)}, u32[]{:S(2)}) collective-permute-start(bf16[256,512]{1,0:T(8,128)(2,1)S(1)} %pad_maximum_fusion.6), channel_id=1, source_target_pairs={{0,4},{1,5},{2,14},{3,15},{4,16},{5,17},{6,26},{7,27},{8,6},{9,7},... | collective-permute-start | bytes 786440 | tf_op jit(solution)/shard_map/ppermute | solution.py:273
  153.3 22.9 %collective-permute-start.8 = (bf16[256,512]{1,0:T(8,128)(2,1)S(1)}, bf16[256,512]{1,0:T(8,128)(2,1)S(1)}, u32[]{:S(2)}, u32[]{:S(2)}) collective-permute-start(bf16[256,512]{1,0:T(8,128)(2,1)S(1)} %pad_maximum_fusion.7), channel_id=1, source_target_pairs={{0,6},{1,7},{2,12},{3,13},{4,18},{5,19},{6,24},{7,25},{8,4},{9,5},... | collective-permute-start | bytes 786440 | tf_op jit(solution)/shard_map/ppermute | solution.py:273
  176.3 22.6 %collective-permute-start.9 = (bf16[256,512]{1,0:T(8,128)(2,1)}, bf16[256,512]{1,0:T(8,128)(2,1)S(1)}, u32[]{:S(2)}, u32[]{:S(2)}) collective-permute-start(bf16[256,512]{1,0:T(8,128)(2,1)} %get-tuple-element.127), channel_id=1, source_target_pairs={{0,8},{8,0},{16,24},{24,16},{1,9},{9,1},{17,25},{25,17},{2,10},{10... | collective-permute-start | bytes 786440 | tf_op jit(solution)/shard_map/ppermute | solution.py:279
  177.8 21.1 %collective-permute-start.10 = (bf16[256,512]{1,0:T(8,128)(2,1)}, bf16[256,512]{1,0:T(8,128)(2,1)S(1)}, u32[]{:S(2)}, u32[]{:S(2)}) collective-permute-start(bf16[256,512]{1,0:T(8,128)(2,1)} %get-tuple-element.128), channel_id=1, source_target_pairs={{0,16},{8,24},{16,0},{24,8},{1,17},{9,25},{17,1},{25,9},{2,18},{10... | collective-permute-start | bytes 786440 | tf_op jit(solution)/shard_map/ppermute | solution.py:279
  182.6 16.3 %collective-permute-start.11 = (bf16[256,512]{1,0:T(8,128)(2,1)}, bf16[256,512]{1,0:T(8,128)(2,1)S(1)}, u32[]{:S(2)}, u32[]{:S(2)}) collective-permute-start(bf16[256,512]{1,0:T(8,128)(2,1)} %get-tuple-element.129), channel_id=1, source_target_pairs={{0,24},{8,16},{16,8},{24,0},{1,25},{9,17},{17,9},{25,1},{2,26},{10... | collective-permute-start | bytes 786440 | tf_op jit(solution)/shard_map/ppermute | solution.py:279
  200.2 11.9 %collective-permute-start.48 = (bf16[128,512]{1,0:T(8,128)(2,1)S(1)}, bf16[128,512]{1,0:T(8,128)(2,1)S(1)}, u32[]{:S(2)}, u32[]{:S(2)}) collective-permute-start(bf16[128,512]{1,0:T(8,128)(2,1)S(1)} %get-tuple-element.206), channel_id=1, source_target_pairs={{0,3},{1,2},{2,1},{3,0},{4,7},{5,6},{6,5},{7,4},{8,11},{9,10},{10,... | collective-permute-start | bytes 393224 | tf_op jit(solution)/shard_map/ppermute | solution.py:284
  201.6 11.0 %collective-permute-start.49 = (bf16[128,512]{1,0:T(8,128)(2,1)S(1)}, bf16[128,512]{1,0:T(8,128)(2,1)S(1)}, u32[]{:S(2)}, u32[]{:S(2)}) collective-permute-start(bf16[128,512]{1,0:T(8,128)(2,1)S(1)} %get-tuple-element.207), channel_id=1, source_target_pairs={{0,4},{1,5},{2,6},{3,7},{4,0},{5,1},{6,2},{7,3},{8,12},{9,13},{10,... | collective-permute-start | bytes 393224 | tf_op jit(solution)/shard_map/ppermute | solution.py:284
  203.2 15.7 %collective-permute-start.50 = (bf16[128,512]{1,0:T(8,128)(2,1)S(1)}, bf16[128,512]{1,0:T(8,128)(2,1)S(1)}, u32[]{:S(2)}, u32[]{:S(2)}) collective-permute-start(bf16[128,512]{1,0:T(8,128)(2,1)S(1)} %get-tuple-element.208), channel_id=1, source_target_pairs={{0,5},{1,4},{2,7},{3,6},{4,1},{5,0},{6,3},{7,2},{8,13},{9,12},{10,... | collective-permute-start | bytes 393224 | tf_op jit(solution)/shard_map/ppermute | solution.py:284
  204.2 18.2 %collective-permute-start.51 = (bf16[128,512]{1,0:T(8,128)(2,1)S(1)}, bf16[128,512]{1,0:T(8,128)(2,1)S(1)}, u32[]{:S(2)}, u32[]{:S(2)}) collective-permute-start(bf16[128,512]{1,0:T(8,128)(2,1)S(1)} %get-tuple-element.209), channel_id=1, source_target_pairs={{0,6},{1,7},{2,4},{3,5},{4,2},{5,3},{6,0},{7,1},{8,14},{9,15},{10,... | collective-permute-start | bytes 393224 | tf_op jit(solution)/shard_map/ppermute | solution.py:284
  210.2 28.3 %collective-permute-start.13 = (bf16[256,512]{1,0:T(8,128)(2,1)}, bf16[256,512]{1,0:T(8,128)(2,1)S(1)}, u32[]{:S(2)}, u32[]{:S(2)}) collective-permute-start(bf16[256,512]{1,0:T(8,128)(2,1)} %get-tuple-element.144), channel_id=1, source_target_pairs={{0,8},{8,0},{16,24},{24,16},{1,9},{9,1},{17,25},{25,17},{2,10},{10... | collective-permute-start | bytes 786440 | tf_op jit(solution)/shard_map/ppermute | solution.py:279
  212.1 26.4 %collective-permute-start.14 = (bf16[256,512]{1,0:T(8,128)(2,1)}, bf16[256,512]{1,0:T(8,128)(2,1)S(1)}, u32[]{:S(2)}, u32[]{:S(2)}) collective-permute-start(bf16[256,512]{1,0:T(8,128)(2,1)} %get-tuple-element.145), channel_id=1, source_target_pairs={{0,16},{8,24},{16,0},{24,8},{1,17},{9,25},{17,1},{25,9},{2,18},{10... | collective-permute-start | bytes 786440 | tf_op jit(solution)/shard_map/ppermute | solution.py:279
  212.6 25.9 %collective-permute-start.15 = (bf16[256,512]{1,0:T(8,128)(2,1)}, bf16[256,512]{1,0:T(8,128)(2,1)S(1)}, u32[]{:S(2)}, u32[]{:S(2)}) collective-permute-start(bf16[256,512]{1,0:T(8,128)(2,1)} %get-tuple-element.146), channel_id=1, source_target_pairs={{0,24},{8,16},{16,8},{24,0},{1,25},{9,17},{17,9},{25,1},{2,26},{10... | collective-permute-start | bytes 786440 | tf_op jit(solution)/shard_map/ppermute | solution.py:279
  218.9 19.5 %collective-permute-start.12 = (bf16[128,512]{1,0:T(8,128)(2,1)S(1)}, bf16[128,512]{1,0:T(8,128)(2,1)S(1)}, u32[]{:S(2)}, u32[]{:S(2)}) collective-permute-start(bf16[128,512]{1,0:T(8,128)(2,1)S(1)} %get-tuple-element.142), channel_id=1, source_target_pairs={{0,7},{1,6},{2,5},{3,4},{4,3},{5,2},{6,1},{7,0},{8,15},{9,14},{10,... | collective-permute-start | bytes 393224 | tf_op jit(solution)/shard_map/ppermute | solution.py:284
  239.3 24.6 %collective-permute-start.16 = (bf16[128,512]{1,0:T(8,128)(2,1)S(1)}, bf16[128,512]{1,0:T(8,128)(2,1)S(1)}, u32[]{:S(2)}, u32[]{:S(2)}) collective-permute-start(bf16[128,512]{1,0:T(8,128)(2,1)S(1)} %get-tuple-element.151), channel_id=1, source_target_pairs={{0,7},{1,6},{2,5},{3,4},{4,3},{5,2},{6,1},{7,0},{8,15},{9,14},{10,... | collective-permute-start | bytes 393224 | tf_op jit(solution)/shard_map/ppermute | solution.py:284
  242.8 15.1 %collective-permute-start.54 = (bf16[128,512]{1,0:T(8,128)(2,1)S(1)}, bf16[128,512]{1,0:T(8,128)(2,1)S(1)}, u32[]{:S(2)}, u32[]{:S(2)}) collective-permute-start(bf16[128,512]{1,0:T(8,128)(2,1)S(1)} %get-tuple-element.213), channel_id=1, source_target_pairs={{0,3},{1,2},{2,1},{3,0},{4,7},{5,6},{6,5},{7,4},{8,11},{9,10},{10,... | collective-permute-start | bytes 393224 | tf_op jit(solution)/shard_map/ppermute | solution.py:284
  244.1 14.4 %collective-permute-start.55 = (bf16[128,512]{1,0:T(8,128)(2,1)S(1)}, bf16[128,512]{1,0:T(8,128)(2,1)S(1)}, u32[]{:S(2)}, u32[]{:S(2)}) collective-permute-start(bf16[128,512]{1,0:T(8,128)(2,1)S(1)} %get-tuple-element.214), channel_id=1, source_target_pairs={{0,4},{1,5},{2,6},{3,7},{4,0},{5,1},{6,2},{7,3},{8,12},{9,13},{10,... | collective-permute-start | bytes 393224 | tf_op jit(solution)/shard_map/ppermute | solution.py:284
  244.8 17.7 %collective-permute-start.56 = (bf16[128,512]{1,0:T(8,128)(2,1)S(1)}, bf16[128,512]{1,0:T(8,128)(2,1)S(1)}, u32[]{:S(2)}, u32[]{:S(2)}) collective-permute-start(bf16[128,512]{1,0:T(8,128)(2,1)S(1)} %get-tuple-element.215), channel_id=1, source_target_pairs={{0,5},{1,4},{2,7},{3,6},{4,1},{5,0},{6,3},{7,2},{8,13},{9,12},{10,... | collective-permute-start | bytes 393224 | tf_op jit(solution)/shard_map/ppermute | solution.py:284
  264.6 248.5 %all-gather.3.cloned.1.call-start = ((), (), s32[]{:S(2)}) async-start(), calls=%async_computation.4 | async-start | bytes 10485760 | tf_op jit(solution)/shard_map/all_gather | solution.py:304
  267.8 17.7 %collective-permute-start.18 = (bf16[256,512]{1,0:T(8,128)(2,1)S(1)}, bf16[256,512]{1,0:T(8,128)(2,1)S(1)}, u32[]{:S(2)}, u32[]{:S(2)}) collective-permute-start(bf16[256,512]{1,0:T(8,128)(2,1)S(1)} %pad_maximum_fusion.8), channel_id=1, source_target_pairs={{0,0},{1,1},{2,10},{3,11},{4,20},{5,21},{6,30},{7,31},{8,2},{9,3},... | collective-permute-start | bytes 786440 | tf_op jit(solution)/shard_map/ppermute | solution.py:273
  268.5 19.5 %collective-permute-start.19 = (bf16[256,512]{1,0:T(8,128)(2,1)S(1)}, bf16[256,512]{1,0:T(8,128)(2,1)S(1)}, u32[]{:S(2)}, u32[]{:S(2)}) collective-permute-start(bf16[256,512]{1,0:T(8,128)(2,1)S(1)} %pad_maximum_fusion.9), channel_id=1, source_target_pairs={{0,2},{1,3},{2,8},{3,9},{4,22},{5,23},{6,28},{7,29},{8,0},{9,1},{1... | collective-permute-start | bytes 786440 | tf_op jit(solution)/shard_map/ppermute | solution.py:273
  275.9 21.3 %collective-permute-start.20 = (bf16[256,512]{1,0:T(8,128)(2,1)S(1)}, bf16[256,512]{1,0:T(8,128)(2,1)S(1)}, u32[]{:S(2)}, u32[]{:S(2)}) collective-permute-start(bf16[256,512]{1,0:T(8,128)(2,1)S(1)} %pad_maximum_fusion.10), channel_id=1, source_target_pairs={{0,4},{1,5},{2,14},{3,15},{4,16},{5,17},{6,26},{7,27},{8,6},{9,7},... | collective-permute-start | bytes 786440 | tf_op jit(solution)/shard_map/ppermute | solution.py:273
  280.3 22.6 %collective-permute-start.21 = (bf16[256,512]{1,0:T(8,128)(2,1)S(1)}, bf16[256,512]{1,0:T(8,128)(2,1)S(1)}, u32[]{:S(2)}, u32[]{:S(2)}) collective-permute-start(bf16[256,512]{1,0:T(8,128)(2,1)S(1)} %pad_maximum_fusion.11), channel_id=1, source_target_pairs={{0,6},{1,7},{2,12},{3,13},{4,18},{5,19},{6,24},{7,25},{8,4},{9,5},... | collective-permute-start | bytes 786440 | tf_op jit(solution)/shard_map/ppermute | solution.py:273
  303.1 29.9 %collective-permute-start.22 = (bf16[256,512]{1,0:T(8,128)(2,1)S(1)}, bf16[256,512]{1,0:T(8,128)(2,1)S(1)}, u32[]{:S(2)}, u32[]{:S(2)}) collective-permute-start(bf16[256,512]{1,0:T(8,128)(2,1)S(1)} %pad_maximum_fusion.12), channel_id=1, source_target_pairs={{0,0},{1,1},{2,10},{3,11},{4,20},{5,21},{6,30},{7,31},{8,2},{9,3},... | collective-permute-start | bytes 786440 | tf_op jit(solution)/shard_map/ppermute | solution.py:273
  303.8 29.2 %collective-permute-start.23 = (bf16[256,512]{1,0:T(8,128)(2,1)S(1)}, bf16[256,512]{1,0:T(8,128)(2,1)S(1)}, u32[]{:S(2)}, u32[]{:S(2)}) collective-permute-start(bf16[256,512]{1,0:T(8,128)(2,1)S(1)} %pad_maximum_fusion.13), channel_id=1, source_target_pairs={{0,2},{1,3},{2,8},{3,9},{4,22},{5,23},{6,28},{7,29},{8,0},{9,1},{1... | collective-permute-start | bytes 786440 | tf_op jit(solution)/shard_map/ppermute | solution.py:273
  307.2 25.8 %collective-permute-start.24 = (bf16[256,512]{1,0:T(8,128)(2,1)S(1)}, bf16[256,512]{1,0:T(8,128)(2,1)S(1)}, u32[]{:S(2)}, u32[]{:S(2)}) collective-permute-start(bf16[256,512]{1,0:T(8,128)(2,1)S(1)} %pad_maximum_fusion.14), channel_id=1, source_target_pairs={{0,4},{1,5},{2,14},{3,15},{4,16},{5,17},{6,26},{7,27},{8,6},{9,7},... | collective-permute-start | bytes 786440 | tf_op jit(solution)/shard_map/ppermute | solution.py:273
  310.4 22.7 %collective-permute-start.25 = (bf16[256,512]{1,0:T(8,128)(2,1)S(1)}, bf16[256,512]{1,0:T(8,128)(2,1)S(1)}, u32[]{:S(2)}, u32[]{:S(2)}) collective-permute-start(bf16[256,512]{1,0:T(8,128)(2,1)S(1)} %pad_maximum_fusion.15), channel_id=1, source_target_pairs={{0,6},{1,7},{2,12},{3,13},{4,18},{5,19},{6,24},{7,25},{8,4},{9,5},... | collective-permute-start | bytes 786440 | tf_op jit(solution)/shard_map/ppermute | solution.py:273
  333.1 23.2 %collective-permute-start.26 = (bf16[256,512]{1,0:T(8,128)(2,1)}, bf16[256,512]{1,0:T(8,128)(2,1)S(1)}, u32[]{:S(2)}, u32[]{:S(2)}) collective-permute-start(bf16[256,512]{1,0:T(8,128)(2,1)} %get-tuple-element.164), channel_id=1, source_target_pairs={{0,8},{8,0},{16,24},{24,16},{1,9},{9,1},{17,25},{25,17},{2,10},{10... | collective-permute-start | bytes 786440 | tf_op jit(solution)/shard_map/ppermute | solution.py:279
  334.6 21.6 %collective-permute-start.27 = (bf16[256,512]{1,0:T(8,128)(2,1)}, bf16[256,512]{1,0:T(8,128)(2,1)S(1)}, u32[]{:S(2)}, u32[]{:S(2)}) collective-permute-start(bf16[256,512]{1,0:T(8,128)(2,1)} %get-tuple-element.165), channel_id=1, source_target_pairs={{0,16},{8,24},{16,0},{24,8},{1,17},{9,25},{17,1},{25,9},{2,18},{10... | collective-permute-start | bytes 786440 | tf_op jit(solution)/shard_map/ppermute | solution.py:279
  340.0 25.2 %collective-permute-start.28 = (bf16[256,512]{1,0:T(8,128)(2,1)}, bf16[256,512]{1,0:T(8,128)(2,1)S(1)}, u32[]{:S(2)}, u32[]{:S(2)}) collective-permute-start(bf16[256,512]{1,0:T(8,128)(2,1)} %get-tuple-element.166), channel_id=1, source_target_pairs={{0,24},{8,16},{16,8},{24,0},{1,25},{9,17},{17,9},{25,1},{2,26},{10... | collective-permute-start | bytes 786440 | tf_op jit(solution)/shard_map/ppermute | solution.py:279
  367.8 15.4 %collective-permute-start.32 = (bf16[128,512]{1,0:T(8,128)(2,1)S(1)}, bf16[128,512]{1,0:T(8,128)(2,1)S(1)}, u32[]{:S(2)}, u32[]{:S(2)}) collective-permute-start(bf16[128,512]{1,0:T(8,128)(2,1)S(1)} %get-tuple-element.183), channel_id=1, source_target_pairs={{0,4},{1,5},{2,6},{3,7},{4,0},{5,1},{6,2},{7,3},{8,12},{9,13},{10,... | collective-permute-start | bytes 393224 | tf_op jit(solution)/shard_map/ppermute | solution.py:284
  367.8 17.5 %collective-permute-start.33 = (bf16[128,512]{1,0:T(8,128)(2,1)S(1)}, bf16[128,512]{1,0:T(8,128)(2,1)S(1)}, u32[]{:S(2)}, u32[]{:S(2)}) collective-permute-start(bf16[128,512]{1,0:T(8,128)(2,1)S(1)} %get-tuple-element.184), channel_id=1, source_target_pairs={{0,5},{1,4},{2,7},{3,6},{4,1},{5,0},{6,3},{7,2},{8,13},{9,12},{10,... | collective-permute-start | bytes 393224 | tf_op jit(solution)/shard_map/ppermute | solution.py:284
  370.4 14.9 %collective-permute-start.34 = (bf16[128,512]{1,0:T(8,128)(2,1)S(1)}, bf16[128,512]{1,0:T(8,128)(2,1)S(1)}, u32[]{:S(2)}, u32[]{:S(2)}) collective-permute-start(bf16[128,512]{1,0:T(8,128)(2,1)S(1)} %get-tuple-element.185), channel_id=1, source_target_pairs={{0,6},{1,7},{2,4},{3,5},{4,2},{5,3},{6,0},{7,1},{8,14},{9,15},{10,... | collective-permute-start | bytes 393224 | tf_op jit(solution)/shard_map/ppermute | solution.py:284
  372.8 19.4 %collective-permute-start.36 = (bf16[256,512]{1,0:T(8,128)(2,1)}, bf16[256,512]{1,0:T(8,128)(2,1)S(1)}, u32[]{:S(2)}, u32[]{:S(2)}) collective-permute-start(bf16[256,512]{1,0:T(8,128)(2,1)} %get-tuple-element.188), channel_id=1, source_target_pairs={{0,8},{8,0},{16,24},{24,16},{1,9},{9,1},{17,25},{25,17},{2,10},{10... | collective-permute-start | bytes 786440 | tf_op jit(solution)/shard_map/ppermute | solution.py:279
  374.7 17.5 %collective-permute-start.37 = (bf16[256,512]{1,0:T(8,128)(2,1)}, bf16[256,512]{1,0:T(8,128)(2,1)S(1)}, u32[]{:S(2)}, u32[]{:S(2)}) collective-permute-start(bf16[256,512]{1,0:T(8,128)(2,1)} %get-tuple-element.189), channel_id=1, source_target_pairs={{0,16},{8,24},{16,0},{24,8},{1,17},{9,25},{17,1},{25,9},{2,18},{10... | collective-permute-start | bytes 786440 | tf_op jit(solution)/shard_map/ppermute | solution.py:279
  383.2 15.5 %collective-permute-start.38 = (bf16[256,512]{1,0:T(8,128)(2,1)S(1)}, bf16[256,512]{1,0:T(8,128)(2,1)S(1)}, u32[]{:S(2)}, u32[]{:S(2)}) collective-permute-start(bf16[256,512]{1,0:T(8,128)(2,1)S(1)} %copy-done.25), channel_id=1, source_target_pairs={{0,24},{8,16},{16,8},{24,0},{1,25},{9,17},{17,9},{25,1},{2,26},{10... | collective-permute-start | bytes 786440 | tf_op jit(solution)/shard_map/ppermute | solution.py:279
  401.5 18.5 %collective-permute-start.42 = (bf16[128,512]{1,0:T(8,128)(2,1)S(1)}, bf16[128,512]{1,0:T(8,128)(2,1)S(1)}, u32[]{:S(2)}, u32[]{:S(2)}) collective-permute-start(bf16[128,512]{1,0:T(8,128)(2,1)S(1)} %get-tuple-element.199), channel_id=1, source_target_pairs={{0,4},{1,5},{2,6},{3,7},{4,0},{5,1},{6,2},{7,3},{8,12},{9,13},{10,... | collective-permute-start | bytes 393224 | tf_op jit(solution)/shard_map/ppermute | solution.py:284
  401.5 20.0 %collective-permute-start.43 = (bf16[128,512]{1,0:T(8,128)(2,1)S(1)}, bf16[128,512]{1,0:T(8,128)(2,1)S(1)}, u32[]{:S(2)}, u32[]{:S(2)}) collective-permute-start(bf16[128,512]{1,0:T(8,128)(2,1)S(1)} %get-tuple-element.200), channel_id=1, source_target_pairs={{0,5},{1,4},{2,7},{3,6},{4,1},{5,0},{6,3},{7,2},{8,13},{9,12},{10,... | collective-permute-start | bytes 393224 | tf_op jit(solution)/shard_map/ppermute | solution.py:284
  404.0 17.5 %collective-permute-start.44 = (bf16[128,512]{1,0:T(8,128)(2,1)S(1)}, bf16[128,512]{1,0:T(8,128)(2,1)S(1)}, u32[]{:S(2)}, u32[]{:S(2)}) collective-permute-start(bf16[128,512]{1,0:T(8,128)(2,1)S(1)} %get-tuple-element.201), channel_id=1, source_target_pairs={{0,6},{1,7},{2,4},{3,5},{4,2},{5,3},{6,0},{7,1},{8,14},{9,15},{10,... | collective-permute-start | bytes 393224 | tf_op jit(solution)/shard_map/ppermute | solution.py:284
  407.8 13.8 %collective-permute-start.45 = (bf16[128,512]{1,0:T(8,128)(2,1)S(1)}, bf16[128,512]{1,0:T(8,128)(2,1)S(1)}, u32[]{:S(2)}, u32[]{:S(2)}) collective-permute-start(bf16[128,512]{1,0:T(8,128)(2,1)S(1)} %get-tuple-element.202), channel_id=1, source_target_pairs={{0,7},{1,6},{2,5},{3,4},{4,3},{5,2},{6,1},{7,0},{8,15},{9,14},{10,... | collective-permute-start | bytes 393224 | tf_op jit(solution)/shard_map/ppermute | solution.py:284
  (40 other events, 549.2 us)
Sparse Core Ops, SparseCore 0:
  16.4 89.0 reduce-scatter.2
  108.9 129.5 reduce-scatter.4
  264.7 135.9 all-gather.4
  423.0 90.0 all-gather.2

commit v7 on v6

--- a/solution.py
+++ b/solution.py
@@ -280,9 +280,14 @@
 
     def send_columns(slot, moved):
         routed = route(ranks, inner, place, moved)
-        return [routed[0]] + [
+        back = [routed[0]] + [
             lax.ppermute(piece, "fsdp", to_column[key]) for piece, key in zip(routed[1:], rounds[1:])
         ]
+        g = group_of[slot] + 1
+        if slot + 1 < per and group_of[slot + 1] == g:
+            at = len(back) // 2
+            back[at], ready[g][0] = lax.optimization_barrier((back[at], ready[g][0]))
+        return back
 
     stages = (send_in, work, send_rows, send_columns)
     held, finished = {}, {}
@@ -303,7 +308,8 @@
                 back = [piece for slot in range(first, first + count) for piece in finished[slot]]
                 gathered = lax.all_gather(jnp.concatenate(back, axis=0), "dp", axis=0, tiled=True)
                 out = unpack(ranks, inner, (first, count), per, place, gathered, out)
-        wanted = [group_of[begins.index(tick + 1)]] if tick + 1 in begins else []
+        after = begins.index(tick + 1) if tick + 1 in begins else None
+        wanted = [] if after is None or after % half == 0 else [group_of[after]]
         now, ahead = lax.optimization_barrier((now, [ready[g] for g in wanted]))
         for g, value in zip(wanted, ahead):
             ready[g] = value

time: 530 us -> 525 us (level)
    reduce_scatter x2, waiting for transfers between devices: 64.9 us -> 48.8 us  [shards(): lax.psum_scatter(packed, 'dp', scatter_dimension=0, tiled=True)]
    ppermute x12, waiting for transfers between devices: 15.4 us -> 25.1 us  [send_rows(): lax.ppermute(strips[k], 'dp', to_row[k])]
  transfers between devices with their start and end apart: 62 -> 62, of which waited for: 27 -> 29; matrix products, arithmetic and copies ran while one was open for 2% -> 3% of each run, Pallas kernels for 21% -> 21%
where the time goes in v7:
time: 525 us; the launch traced here: 524 us
  waiting for transfers between devices  247 us (47%)
  Pallas kernels  130 us (25%)
  starting transfers between devices  117 us (22%)
  local copies, waits for them, and re-layouts  15.4 us (3%)
  between operations  14 us (3%)
    all_gather x2, waiting for transfers between devices, shards(): lax.all_gather(jnp.concatenate(back, axis=0), 'dp', axis=0, tiled=True)  81.3 us
    ppermute x16, starting transfers between devices, send_in(): lax.ppermute(strips[k], MESH_AXES, to_owner[k])  65 us
    pallas_call x4, Pallas kernels, precondition(): pl.pallas_call(functools.partial(block_kernel, ranks, inner, col_blocks),...  59.4 us
    ppermute x28, waiting for transfers between devices, send_columns(): lax.ppermute(piece, 'fsdp', to_column[key])  51.4 us
    reduce_scatter x2, waiting for transfers between devices, shards(): lax.psum_scatter(packed, 'dp', scatter_dimension=0, tiled=True)  48.8 us
    ppermute x16, waiting for transfers between devices, send_in(): lax.ppermute(strips[k], MESH_AXES, to_owner[k])  35.9 us
    pallas_call x1, Pallas kernels, fourth_powers(): pl.pallas_call(fourth_kernel, grid=(slabs, col_blocks), in_specs=[spec, s...  31.3 us
    ppermute x28, starting transfers between devices, send_columns(): lax.ppermute(piece, 'fsdp', to_column[key])  29.6 us
  transfers between devices with their start and end apart: 62, of which 29 were waited for; matrix products, arithmetic and copies ran while one was open for 3% of the time, Pallas kernels for 21%

profile of v7, /device:TPU:0, one launch (start us, length us, event | category | flops | bytes accessed | tf_op | source)
XLA Modules:
  0.0 523.6 jit_solution(3855820646139180588)
XLA Ops:
  7.2 9.1 %pack_slabs.2 = bf16[4,2,2,4,128,512]{5,4,3,2,1,0:T(8,128)(2,1)} custom-call(s32[3]{0:T(128)} %pad_add_fusion.place_ref, bf16[8,4,512,512]{3,2,1,0:T(8,128)(2,1)} %bitcast.9), custom_call_target="tpu_custom_call" | custom-call | bytes 16777216 | tf_op jit(solution)/shard_map/pack_slabs/pallas_call | solution.py:75
  16.4 9.1 %pack_slabs.3 = bf16[4,2,2,4,128,512]{5,4,3,2,1,0:T(8,128)(2,1)} custom-call(s32[3]{0:T(128)} %pad_add_fusion.place_ref, bf16[8,4,512,512]{3,2,1,0:T(8,128)(2,1)} %bitcast.10), custom_call_target="tpu_custom_call" | custom-call | bytes 16777216 | tf_op jit(solution)/shard_map/pack_slabs/pallas_call | solution.py:75
  25.5 31.3 %fourth_powers.1 = (f32[4,2,512,512]{3,2,1,0:T(8,128)}, f32[4,2,512,512]{3,2,1,0:T(8,128)}) custom-call(f32[4,2,512,512]{3,2,1,0:T(8,128)} %refs_6_.7, f32[4,2,512,512]{3,2,1,0:T(8,128)} %refs_7_.7), custom_call_target="tpu_custom_call" | custom-call | flops 25769803776 | bytes 33554432 | tf_op jit(solution)/shard_map/fourth_powers/pallas_call | solution.py:45
  56.8 48.8 %reduce-scatter.3.cloned.1.call-done = bf16[2048,512]{1,0:T(8,128)(2,1)} async-done(((bf16[8192,512]{1,0:T(8,128)(2,1)}), bf16[2048,512]{1,0:T(8,128)(2,1)}) %reduce-scatter.3.cloned.1.call-update) | async-done | bytes 2097168 | tf_op jit(solution)/shard_map/reduce_scatter | solution.py:255
  110.8 6.0 %collective-permute-start.2 = (bf16[256,512]{1,0:T(8,128)(2,1)S(1)}, bf16[256,512]{1,0:T(8,128)(2,1)S(1)}, u32[]{:S(2)}, u32[]{:S(2)}) collective-permute-start(bf16[256,512]{1,0:T(8,128)(2,1)S(1)} %pad_maximum_fusion.1), channel_id=1, source_target_pairs={{0,2},{1,3},{2,8},{3,9},{4,22},{5,23},{6,28},{7,29},{8,0},{9,1},{1... | collective-permute-start | bytes 786440 | tf_op jit(solution)/shard_map/ppermute | solution.py:273
  116.8 4.3 collective-permute-start.3
  121.2 5.2 collective-permute-start.4
  126.4 2.6 collective-permute-done.2.refs_1_
  129.0 10.7 %collective-permute-done.3.refs_2_ = bf16[256,512]{1,0:T(8,128)(2,1)S(1)} collective-permute-done((bf16[256,512]{1,0:T(8,128)(2,1)S(1)}, bf16[256,512]{1,0:T(8,128)(2,1)S(1)}, u32[]{:S(2)}, u32[]{:S(2)}) %collective-permute-start.3) | collective-permute-done | bytes 262176 | tf_op jit(solution)/shard_map/ppermute | solution.py:273
  139.7 4.1 collective-permute-done.4.refs_3_
  144.6 4.4 collective-permute-start.6
  149.0 4.4 collective-permute-start.7
  153.4 7.9 %collective-permute-start.8 = (bf16[256,512]{1,0:T(8,128)(2,1)S(1)}, bf16[256,512]{1,0:T(8,128)(2,1)S(1)}, u32[]{:S(2)}, u32[]{:S(2)}) collective-permute-start(bf16[256,512]{1,0:T(8,128)(2,1)S(1)} %pad_maximum_fusion.7), channel_id=1, source_target_pairs={{0,6},{1,7},{2,12},{3,13},{4,18},{5,19},{6,24},{7,25},{8,4},{9,5},... | collective-permute-start | bytes 786440 | tf_op jit(solution)/shard_map/ppermute | solution.py:273
  161.3 14.9 %precondition.4 = (bf16[256,512]{1,0:T(8,128)(2,1)}, bf16[256,512]{1,0:T(8,128)(2,1)}, bf16[256,512]{1,0:T(8,128)(2,1)}, bf16[256,512]{1,0:T(8,128)(2,1)}) custom-call(s32[3]{0:T(128)} %pad_add_fusion.place_ref, bf16[256,512]{1,0:T(8,128)(2,1)} %copy-done.9, bf16[256,512]{1,0:T(8,128)(2,1)} %copy-done.11, bf16[256,512]{1,0:T(8,128)(2,1)} %copy-done.13, ...), custom_call_target="tpu_custom_call" | custom-call | flops 8589934592 | bytes 14680064 | tf_op jit(solution)/shard_map/precondition/pallas_call | solution.py:205
  177.9 4.8 collective-permute-start.10
  184.1 14.8 %precondition.5 = (bf16[256,512]{1,0:T(8,128)(2,1)}, bf16[256,512]{1,0:T(8,128)(2,1)}, bf16[256,512]{1,0:T(8,128)(2,1)}, bf16[256,512]{1,0:T(8,128)(2,1)}) custom-call(s32[3]{0:T(128)} %pad_add_fusion.place_ref, bf16[256,512]{1,0:T(8,128)(2,1)} %copy-done.17, bf16[256,512]{1,0:T(8,128)(2,1)} %copy-done.19, bf16[256,512]{1,0:T(8,128)(2,1)} %copy-done.21, ...), custom_call_target="tpu_custom_call" | custom-call | flops 8589934592 | bytes 14680064 | tf_op jit(solution)/shard_map/precondition/pallas_call | solution.py:205
  204.9 2.8 collective-permute-start.52
  213.5 2.5 collective-permute-start.15
  219.0 3.4 collective-permute-start.12
  225.5 5.8 %collective-permute-done.14.refs_2_ = bf16[256,512]{1,0:T(8,128)(2,1)S(1)} collective-permute-done((bf16[256,512]{1,0:T(8,128)(2,1)}, bf16[256,512]{1,0:T(8,128)(2,1)S(1)}, u32[]{:S(2)}, u32[]{:S(2)}) %collective-permute-start.14) | collective-permute-done | bytes 262176 | tf_op jit(solution)/shard_map/ppermute | solution.py:279
  231.3 4.2 collective-permute-done.15.refs_3_
  236.9 2.8 collective-permute-start.16
  242.1 2.9 collective-permute-start.56
  245.7 3.5 collective-permute-done.54
  251.4 4.6 collective-permute-done.55
  260.4 2.6 collective-permute-done.18
  263.8 7.9 %collective-permute-start.20 = (bf16[256,512]{1,0:T(8,128)(2,1)S(1)}, bf16[256,512]{1,0:T(8,128)(2,1)S(1)}, u32[]{:S(2)}, u32[]{:S(2)}) collective-permute-start(bf16[256,512]{1,0:T(8,128)(2,1)S(1)} %pad_maximum_fusion.9), channel_id=1, source_target_pairs={{0,2},{1,3},{2,8},{3,9},{4,22},{5,23},{6,28},{7,29},{8,0},{9,1},{1... | collective-permute-start | bytes 786440 | tf_op jit(solution)/shard_map/ppermute | solution.py:273
  271.7 5.2 collective-permute-start.21
  277.0 4.0 collective-permute-start.22
  281.0 2.5 collective-permute-done.20.refs_1_
  283.6 9.2 %collective-permute-done.21.refs_2_ = bf16[256,512]{1,0:T(8,128)(2,1)S(1)} collective-permute-done((bf16[256,512]{1,0:T(8,128)(2,1)S(1)}, bf16[256,512]{1,0:T(8,128)(2,1)S(1)}, u32[]{:S(2)}, u32[]{:S(2)}) %collective-permute-start.21) | collective-permute-done | bytes 262176 | tf_op jit(solution)/shard_map/ppermute | solution.py:273
  292.8 6.8 %collective-permute-done.22.refs_3_ = bf16[256,512]{1,0:T(8,128)(2,1)S(1)} collective-permute-done((bf16[256,512]{1,0:T(8,128)(2,1)S(1)}, bf16[256,512]{1,0:T(8,128)(2,1)S(1)}, u32[]{:S(2)}, u32[]{:S(2)}) %collective-permute-start.22) | collective-permute-done | bytes 262176 | tf_op jit(solution)/shard_map/ppermute | solution.py:273
  302.4 3.2 collective-permute-start.25
  305.6 7.9 %collective-permute-start.26 = (bf16[256,512]{1,0:T(8,128)(2,1)S(1)}, bf16[256,512]{1,0:T(8,128)(2,1)S(1)}, u32[]{:S(2)}, u32[]{:S(2)}) collective-permute-start(bf16[256,512]{1,0:T(8,128)(2,1)S(1)} %pad_maximum_fusion.15), channel_id=1, source_target_pairs={{0,6},{1,7},{2,12},{3,13},{4,18},{5,19},{6,24},{7,25},{8,4},{9,5},... | collective-permute-start | bytes 786440 | tf_op jit(solution)/shard_map/ppermute | solution.py:273
  313.6 14.7 %precondition.6 = (bf16[256,512]{1,0:T(8,128)(2,1)}, bf16[256,512]{1,0:T(8,128)(2,1)}, bf16[256,512]{1,0:T(8,128)(2,1)}, bf16[256,512]{1,0:T(8,128)(2,1)}) custom-call(s32[3]{0:T(128)} %pad_add_fusion.place_ref, bf16[256,512]{1,0:T(8,128)(2,1)} %copy-done.8, bf16[256,512]{1,0:T(8,128)(2,1)} %copy-done.10, bf16[256,512]{1,0:T(8,128)(2,1)} %copy-done.12, ...), custom_call_target="tpu_custom_call" | custom-call | flops 8589934592 | bytes 14680064 | tf_op jit(solution)/shard_map/precondition/pallas_call | solution.py:205
  329.9 4.9 collective-permute-start.28
  336.2 14.9 %precondition.7 = (bf16[256,512]{1,0:T(8,128)(2,1)}, bf16[256,512]{1,0:T(8,128)(2,1)}, bf16[256,512]{1,0:T(8,128)(2,1)}, bf16[256,512]{1,0:T(8,128)(2,1)}) custom-call(s32[3]{0:T(128)} %pad_add_fusion.place_ref, bf16[256,512]{1,0:T(8,128)(2,1)} %copy-done.14, bf16[256,512]{1,0:T(8,128)(2,1)} %copy-done.18, bf16[256,512]{1,0:T(8,128)(2,1)} %copy-done.20, ...), custom_call_target="tpu_custom_call" | custom-call | flops 8589934592 | bytes 14680064 | tf_op jit(solution)/shard_map/precondition/pallas_call | solution.py:205
  351.1 8.8 %collective-permute-done.29.refs_3_ = bf16[256,512]{1,0:T(8,128)(2,1)S(1)} collective-permute-done((bf16[256,512]{1,0:T(8,128)(2,1)}, bf16[256,512]{1,0:T(8,128)(2,1)S(1)}, u32[]{:S(2)}, u32[]{:S(2)}) %collective-permute-start.29) | collective-permute-done | bytes 262176 | tf_op jit(solution)/shard_map/ppermute | solution.py:279
  362.5 2.6 collective-permute-start.34
  371.1 6.7 %collective-permute-done.33 = bf16[128,512]{1,0:T(8,128)(2,1)S(1)} collective-permute-done((bf16[128,512]{1,0:T(8,128)(2,1)S(1)}, bf16[128,512]{1,0:T(8,128)(2,1)S(1)}, u32[]{:S(2)}, u32[]{:S(2)}) %collective-permute-start.33) | collective-permute-done | bytes 131104 | tf_op jit(solution)/shard_map/ppermute | solution.py:284
  380.1 7.1 %collective-permute-done.36 = bf16[128,512]{1,0:T(8,128)(2,1)S(1)} collective-permute-done((bf16[128,512]{1,0:T(8,128)(2,1)S(1)}, bf16[128,512]{1,0:T(8,128)(2,1)S(1)}, u32[]{:S(2)}, u32[]{:S(2)}) %collective-permute-start.36) | collective-permute-done | bytes 131104 | tf_op jit(solution)/shard_map/ppermute | solution.py:284
  387.2 6.3 %collective-permute-done.39.refs_3_ = bf16[256,512]{1,0:T(8,128)(2,1)S(1)} collective-permute-done((bf16[256,512]{1,0:T(8,128)(2,1)S(1)}, bf16[256,512]{1,0:T(8,128)(2,1)S(1)}, u32[]{:S(2)}, u32[]{:S(2)}) %collective-permute-start.39) | collective-permute-done | bytes 262176 | tf_op jit(solution)/shard_map/ppermute | solution.py:279
  396.2 2.5 collective-permute-start.44
  399.5 3.2 collective-permute-done.41
  404.7 10.0 %collective-permute-done.43 = bf16[128,512]{1,0:T(8,128)(2,1)S(1)} collective-permute-done((bf16[128,512]{1,0:T(8,128)(2,1)S(1)}, bf16[128,512]{1,0:T(8,128)(2,1)S(1)}, u32[]{:S(2)}, u32[]{:S(2)}) %collective-permute-start.43) | collective-permute-done | bytes 131104 | tf_op jit(solution)/shard_map/ppermute | solution.py:284
  417.7 9.0 %unpack_slabs.2.rest_0_ = bf16[8,4,512,512]{3,2,1,0:T(8,128)(2,1)} custom-call(s32[3]{0:T(128)} %pad_add_fusion.place_ref, bf16[4,2,8,128,512]{4,3,2,1,0:T(8,128)(2,1)} %bitcast.13), custom_call_target="tpu_custom_call" | custom-call | bytes 16777216 | tf_op jit(solution)/shard_map/unpack_slabs/pallas_call | solution.py:107
  426.7 81.3 %all-gather.3.cloned.1.call-done = bf16[8192,512]{1,0:T(8,128)(2,1)} async-done(((bf16[2048,512]{1,0:T(8,128)(2,1)}), bf16[8192,512]{1,0:T(8,128)(2,1)}) %all-gather.3.cloned.1.call-update) | async-done | bytes 8388624 | tf_op jit(solution)/shard_map/all_gather | solution.py:309
  508.0 9.0 %unpack_slabs.3 = bf16[8,4,512,512]{3,2,1,0:T(8,128)(2,1)} custom-call(s32[3]{0:T(128)} %pad_add_fusion.place_ref, bf16[4,2,8,128,512]{4,3,2,1,0:T(8,128)(2,1)} %bitcast.14, bf16[8,4,512,512]{3,2,1,0:T(8,128)(2,1)} %unpack_slabs.2.rest_0_), custom_call_target="tpu_custom_call", output_to_operand_aliasing={{}: (2, {})} | custom-call | bytes 16777216 | tf_op jit(solution)/shard_map/unpack_slabs/pallas_call | solution.py:107
  (203 shorter events, 64.3 us)
Async XLA Ops:
  6.5 99.0 %reduce-scatter.3.cloned.1.call-start = ((), (), s32[]{:S(2)}) async-start(), calls=%async_computation.2 | async-start | bytes 10485760 | tf_op jit(solution)/shard_map/reduce_scatter | solution.py:255
  16.3 240.4 %reduce-scatter.5.cloned.1.call-start = ((), (), s32[]{:S(2)}) async-start(), calls=%async_computation.3 | async-start | bytes 10485760 | tf_op jit(solution)/shard_map/reduce_scatter | solution.py:255
  25.5 392.2 %all-gather.5.cloned.1.call-start = ((), (), s32[]{:S(2)}) async-start(), calls=%async_computation.5 | async-start | bytes 10485760 | tf_op jit(solution)/shard_map/all_gather | solution.py:309
  110.1 16.3 %collective-permute-start.1 = (bf16[256,512]{1,0:T(8,128)(2,1)S(1)}, bf16[256,512]{1,0:T(8,128)(2,1)S(1)}, u32[]{:S(2)}, u32[]{:S(2)}) collective-permute-start(bf16[256,512]{1,0:T(8,128)(2,1)S(1)} %pad_maximum_fusion), channel_id=1, source_target_pairs={{0,0},{1,1},{2,10},{3,11},{4,20},{5,21},{6,30},{7,31},{8,2},{9,3},... | collective-permute-start | bytes 786440 | tf_op jit(solution)/shard_map/ppermute | solution.py:273
  110.8 18.2 %collective-permute-start.2 = (bf16[256,512]{1,0:T(8,128)(2,1)S(1)}, bf16[256,512]{1,0:T(8,128)(2,1)S(1)}, u32[]{:S(2)}, u32[]{:S(2)}) collective-permute-start(bf16[256,512]{1,0:T(8,128)(2,1)S(1)} %pad_maximum_fusion.1), channel_id=1, source_target_pairs={{0,2},{1,3},{2,8},{3,9},{4,22},{5,23},{6,28},{7,29},{8,0},{9,1},{1... | collective-permute-start | bytes 786440 | tf_op jit(solution)/shard_map/ppermute | solution.py:273
  116.8 22.9 %collective-permute-start.3 = (bf16[256,512]{1,0:T(8,128)(2,1)S(1)}, bf16[256,512]{1,0:T(8,128)(2,1)S(1)}, u32[]{:S(2)}, u32[]{:S(2)}) collective-permute-start(bf16[256,512]{1,0:T(8,128)(2,1)S(1)} %pad_maximum_fusion.2), channel_id=1, source_target_pairs={{0,4},{1,5},{2,14},{3,15},{4,16},{5,17},{6,26},{7,27},{8,6},{9,7},... | collective-permute-start | bytes 786440 | tf_op jit(solution)/shard_map/ppermute | solution.py:273
  121.2 22.6 %collective-permute-start.4 = (bf16[256,512]{1,0:T(8,128)(2,1)S(1)}, bf16[256,512]{1,0:T(8,128)(2,1)S(1)}, u32[]{:S(2)}, u32[]{:S(2)}) collective-permute-start(bf16[256,512]{1,0:T(8,128)(2,1)S(1)} %pad_maximum_fusion.3), channel_id=1, source_target_pairs={{0,6},{1,7},{2,12},{3,13},{4,18},{5,19},{6,24},{7,25},{8,4},{9,5},... | collective-permute-start | bytes 786440 | tf_op jit(solution)/shard_map/ppermute | solution.py:273
  143.9 32.4 %collective-permute-start.5 = (bf16[256,512]{1,0:T(8,128)(2,1)S(1)}, bf16[256,512]{1,0:T(8,128)(2,1)S(1)}, u32[]{:S(2)}, u32[]{:S(2)}) collective-permute-start(bf16[256,512]{1,0:T(8,128)(2,1)S(1)} %pad_maximum_fusion.4), channel_id=1, source_target_pairs={{0,0},{1,1},{2,10},{3,11},{4,20},{5,21},{6,30},{7,31},{8,2},{9,3},... | collective-permute-start | bytes 786440 | tf_op jit(solution)/shard_map/ppermute | solution.py:273
  144.6 31.7 %collective-permute-start.6 = (bf16[256,512]{1,0:T(8,128)(2,1)S(1)}, bf16[256,512]{1,0:T(8,128)(2,1)S(1)}, u32[]{:S(2)}, u32[]{:S(2)}) collective-permute-start(bf16[256,512]{1,0:T(8,128)(2,1)S(1)} %pad_maximum_fusion.5), channel_id=1, source_target_pairs={{0,2},{1,3},{2,8},{3,9},{4,22},{5,23},{6,28},{7,29},{8,0},{9,1},{1... | collective-permute-start | bytes 786440 | tf_op jit(solution)/shard_map/ppermute | solution.py:273
  149.0 27.3 %collective-permute-start.7 = (bf16[256,512]{1,0:T(8,128)(2,1)S(1)}, bf16[256,512]{1,0:T(8,128)(2,1)S(1)}, u32[]{:S(2)}, u32[]{:S(2)}) collective-permute-start(bf16[256,512]{1,0:T(8,128)(2,1)S(1)} %pad_maximum_fusion.6), channel_id=1, source_target_pairs={{0,4},{1,5},{2,14},{3,15},{4,16},{5,17},{6,26},{7,27},{8,6},{9,7},... | collective-permute-start | bytes 786440 | tf_op jit(solution)/shard_map/ppermute | solution.py:273
  153.4 22.9 %collective-permute-start.8 = (bf16[256,512]{1,0:T(8,128)(2,1)S(1)}, bf16[256,512]{1,0:T(8,128)(2,1)S(1)}, u32[]{:S(2)}, u32[]{:S(2)}) collective-permute-start(bf16[256,512]{1,0:T(8,128)(2,1)S(1)} %pad_maximum_fusion.7), channel_id=1, source_target_pairs={{0,6},{1,7},{2,12},{3,13},{4,18},{5,19},{6,24},{7,25},{8,4},{9,5},... | collective-permute-start | bytes 786440 | tf_op jit(solution)/shard_map/ppermute | solution.py:273
  176.4 22.6 %collective-permute-start.9 = (bf16[256,512]{1,0:T(8,128)(2,1)}, bf16[256,512]{1,0:T(8,128)(2,1)S(1)}, u32[]{:S(2)}, u32[]{:S(2)}) collective-permute-start(bf16[256,512]{1,0:T(8,128)(2,1)} %get-tuple-element.128), channel_id=1, source_target_pairs={{0,8},{8,0},{16,24},{24,16},{1,9},{9,1},{17,25},{25,17},{2,10},{10... | collective-permute-start | bytes 786440 | tf_op jit(solution)/shard_map/ppermute | solution.py:279
  177.9 21.1 %collective-permute-start.10 = (bf16[256,512]{1,0:T(8,128)(2,1)}, bf16[256,512]{1,0:T(8,128)(2,1)S(1)}, u32[]{:S(2)}, u32[]{:S(2)}) collective-permute-start(bf16[256,512]{1,0:T(8,128)(2,1)} %get-tuple-element.129), channel_id=1, source_target_pairs={{0,16},{8,24},{16,0},{24,8},{1,17},{9,25},{17,1},{25,9},{2,18},{10... | collective-permute-start | bytes 786440 | tf_op jit(solution)/shard_map/ppermute | solution.py:279
  182.7 16.3 %collective-permute-start.11 = (bf16[256,512]{1,0:T(8,128)(2,1)}, bf16[256,512]{1,0:T(8,128)(2,1)S(1)}, u32[]{:S(2)}, u32[]{:S(2)}) collective-permute-start(bf16[256,512]{1,0:T(8,128)(2,1)} %get-tuple-element.130), channel_id=1, source_target_pairs={{0,24},{8,16},{16,8},{24,0},{1,25},{9,17},{17,9},{25,1},{2,26},{10... | collective-permute-start | bytes 786440 | tf_op jit(solution)/shard_map/ppermute | solution.py:279
  199.8 10.5 %collective-permute-start.48 = (bf16[128,512]{1,0:T(8,128)(2,1)S(1)}, bf16[128,512]{1,0:T(8,128)(2,1)S(1)}, u32[]{:S(2)}, u32[]{:S(2)}) collective-permute-start(bf16[128,512]{1,0:T(8,128)(2,1)S(1)} %get-tuple-element.207), channel_id=1, source_target_pairs={{0,2},{1,3},{2,0},{3,1},{4,6},{5,7},{6,4},{7,5},{8,10},{9,11},{10,... | collective-permute-start | bytes 393224 | tf_op jit(solution)/shard_map/ppermute | solution.py:284
  200.3 12.4 %collective-permute-start.49 = (bf16[128,512]{1,0:T(8,128)(2,1)S(1)}, bf16[128,512]{1,0:T(8,128)(2,1)S(1)}, u32[]{:S(2)}, u32[]{:S(2)}) collective-permute-start(bf16[128,512]{1,0:T(8,128)(2,1)S(1)} %get-tuple-element.208), channel_id=1, source_target_pairs={{0,3},{1,2},{2,1},{3,0},{4,7},{5,6},{6,5},{7,4},{8,11},{9,10},{10,... | collective-permute-start | bytes 393224 | tf_op jit(solution)/shard_map/ppermute | solution.py:284
  201.6 11.9 %collective-permute-start.50 = (bf16[128,512]{1,0:T(8,128)(2,1)S(1)}, bf16[128,512]{1,0:T(8,128)(2,1)S(1)}, u32[]{:S(2)}, u32[]{:S(2)}) collective-permute-start(bf16[128,512]{1,0:T(8,128)(2,1)S(1)} %get-tuple-element.209), channel_id=1, source_target_pairs={{0,4},{1,5},{2,6},{3,7},{4,0},{5,1},{6,2},{7,3},{8,12},{9,13},{10,... | collective-permute-start | bytes 393224 | tf_op jit(solution)/shard_map/ppermute | solution.py:284
  203.2 15.7 %collective-permute-start.51 = (bf16[128,512]{1,0:T(8,128)(2,1)S(1)}, bf16[128,512]{1,0:T(8,128)(2,1)S(1)}, u32[]{:S(2)}, u32[]{:S(2)}) collective-permute-start(bf16[128,512]{1,0:T(8,128)(2,1)S(1)} %get-tuple-element.210), channel_id=1, source_target_pairs={{0,5},{1,4},{2,7},{3,6},{4,1},{5,0},{6,3},{7,2},{8,13},{9,12},{10,... | collective-permute-start | bytes 393224 | tf_op jit(solution)/shard_map/ppermute | solution.py:284
  204.9 18.2 %collective-permute-start.52 = (bf16[128,512]{1,0:T(8,128)(2,1)S(1)}, bf16[128,512]{1,0:T(8,128)(2,1)S(1)}, u32[]{:S(2)}, u32[]{:S(2)}) collective-permute-start(bf16[128,512]{1,0:T(8,128)(2,1)S(1)} %get-tuple-element.211), channel_id=1, source_target_pairs={{0,6},{1,7},{2,4},{3,5},{4,2},{5,3},{6,0},{7,1},{8,14},{9,15},{10,... | collective-permute-start | bytes 393224 | tf_op jit(solution)/shard_map/ppermute | solution.py:284
  210.2 15.3 %collective-permute-start.13 = (bf16[256,512]{1,0:T(8,128)(2,1)}, bf16[256,512]{1,0:T(8,128)(2,1)S(1)}, u32[]{:S(2)}, u32[]{:S(2)}) collective-permute-start(bf16[256,512]{1,0:T(8,128)(2,1)} %get-tuple-element.145), channel_id=1, source_target_pairs={{0,8},{8,0},{16,24},{24,16},{1,9},{9,1},{17,25},{25,17},{2,10},{10... | collective-permute-start | bytes 786440 | tf_op jit(solution)/shard_map/ppermute | solution.py:279
  212.7 18.7 %collective-permute-start.14 = (bf16[256,512]{1,0:T(8,128)(2,1)}, bf16[256,512]{1,0:T(8,128)(2,1)S(1)}, u32[]{:S(2)}, u32[]{:S(2)}) collective-permute-start(bf16[256,512]{1,0:T(8,128)(2,1)} %get-tuple-element.146), channel_id=1, source_target_pairs={{0,16},{8,24},{16,0},{24,8},{1,17},{9,25},{17,1},{25,9},{2,18},{10... | collective-permute-start | bytes 786440 | tf_op jit(solution)/shard_map/ppermute | solution.py:279
  213.5 22.0 %collective-permute-start.15 = (bf16[256,512]{1,0:T(8,128)(2,1)S(1)}, bf16[256,512]{1,0:T(8,128)(2,1)S(1)}, u32[]{:S(2)}, u32[]{:S(2)}) collective-permute-start(bf16[256,512]{1,0:T(8,128)(2,1)S(1)} %copy-done.25), channel_id=1, source_target_pairs={{0,24},{8,16},{16,8},{24,0},{1,25},{9,17},{17,9},{25,1},{2,26},{10... | collective-permute-start | bytes 786440 | tf_op jit(solution)/shard_map/ppermute | solution.py:279
  236.9 22.5 %collective-permute-start.16 = (bf16[128,512]{1,0:T(8,128)(2,1)S(1)}, bf16[128,512]{1,0:T(8,128)(2,1)S(1)}, u32[]{:S(2)}, u32[]{:S(2)}) collective-permute-start(bf16[128,512]{1,0:T(8,128)(2,1)S(1)} %get-tuple-element.152), channel_id=1, source_target_pairs={{0,7},{1,6},{2,5},{3,4},{4,3},{5,2},{6,1},{7,0},{8,15},{9,14},{10,... | collective-permute-start | bytes 393224 | tf_op jit(solution)/shard_map/ppermute | solution.py:284
  239.7 17.0 %collective-permute-start.17 = (bf16[128,512]{1,0:T(8,128)(2,1)S(1)}, bf16[128,512]{1,0:T(8,128)(2,1)S(1)}, u32[]{:S(2)}, u32[]{:S(2)}) collective-permute-start(bf16[128,512]{1,0:T(8,128)(2,1)S(1)} %get-tuple-element.153), channel_id=1, source_target_pairs={{0,4},{1,5},{2,6},{3,7},{4,0},{5,1},{6,2},{7,3},{8,12},{9,13},{10,... | collective-permute-start | bytes 393224 | tf_op jit(solution)/shard_map/ppermute | solution.py:284
  241.4 14.6 %collective-permute-start.55 = (bf16[128,512]{1,0:T(8,128)(2,1)S(1)}, bf16[128,512]{1,0:T(8,128)(2,1)S(1)}, u32[]{:S(2)}, u32[]{:S(2)}) collective-permute-start(bf16[128,512]{1,0:T(8,128)(2,1)S(1)} %get-tuple-element.215), channel_id=1, source_target_pairs={{0,3},{1,2},{2,1},{3,0},{4,7},{5,6},{6,5},{7,4},{8,11},{9,10},{10,... | collective-permute-start | bytes 393224 | tf_op jit(solution)/shard_map/ppermute | solution.py:284
  242.1 15.3 %collective-permute-start.56 = (bf16[128,512]{1,0:T(8,128)(2,1)S(1)}, bf16[128,512]{1,0:T(8,128)(2,1)S(1)}, u32[]{:S(2)}, u32[]{:S(2)}) collective-permute-start(bf16[128,512]{1,0:T(8,128)(2,1)S(1)} %get-tuple-element.217), channel_id=1, source_target_pairs={{0,5},{1,4},{2,7},{3,6},{4,1},{5,0},{6,3},{7,2},{8,13},{9,12},{10,... | collective-permute-start | bytes 393224 | tf_op jit(solution)/shard_map/ppermute | solution.py:284
  260.1 247.9 %all-gather.3.cloned.1.call-start = ((), (), s32[]{:S(2)}) async-start(), calls=%async_computation.4 | async-start | bytes 10485760 | tf_op jit(solution)/shard_map/all_gather | solution.py:309
  263.1 17.9 %collective-permute-start.19 = (bf16[256,512]{1,0:T(8,128)(2,1)S(1)}, bf16[256,512]{1,0:T(8,128)(2,1)S(1)}, u32[]{:S(2)}, u32[]{:S(2)}) collective-permute-start(bf16[256,512]{1,0:T(8,128)(2,1)S(1)} %pad_maximum_fusion.8), channel_id=1, source_target_pairs={{0,0},{1,1},{2,10},{3,11},{4,20},{5,21},{6,30},{7,31},{8,2},{9,3},... | collective-permute-start | bytes 786440 | tf_op jit(solution)/shard_map/ppermute | solution.py:273
  263.8 19.8 %collective-permute-start.20 = (bf16[256,512]{1,0:T(8,128)(2,1)S(1)}, bf16[256,512]{1,0:T(8,128)(2,1)S(1)}, u32[]{:S(2)}, u32[]{:S(2)}) collective-permute-start(bf16[256,512]{1,0:T(8,128)(2,1)S(1)} %pad_maximum_fusion.9), channel_id=1, source_target_pairs={{0,2},{1,3},{2,8},{3,9},{4,22},{5,23},{6,28},{7,29},{8,0},{9,1},{1... | collective-permute-start | bytes 786440 | tf_op jit(solution)/shard_map/ppermute | solution.py:273
  271.7 21.1 %collective-permute-start.21 = (bf16[256,512]{1,0:T(8,128)(2,1)S(1)}, bf16[256,512]{1,0:T(8,128)(2,1)S(1)}, u32[]{:S(2)}, u32[]{:S(2)}) collective-permute-start(bf16[256,512]{1,0:T(8,128)(2,1)S(1)} %pad_maximum_fusion.10), channel_id=1, source_target_pairs={{0,4},{1,5},{2,14},{3,15},{4,16},{5,17},{6,26},{7,27},{8,6},{9,7},... | collective-permute-start | bytes 786440 | tf_op jit(solution)/shard_map/ppermute | solution.py:273
  277.0 22.6 %collective-permute-start.22 = (bf16[256,512]{1,0:T(8,128)(2,1)S(1)}, bf16[256,512]{1,0:T(8,128)(2,1)S(1)}, u32[]{:S(2)}, u32[]{:S(2)}) collective-permute-start(bf16[256,512]{1,0:T(8,128)(2,1)S(1)} %pad_maximum_fusion.11), channel_id=1, source_target_pairs={{0,6},{1,7},{2,12},{3,13},{4,18},{5,19},{6,24},{7,25},{8,4},{9,5},... | collective-permute-start | bytes 786440 | tf_op jit(solution)/shard_map/ppermute | solution.py:273
  299.7 28.6 %collective-permute-start.23 = (bf16[256,512]{1,0:T(8,128)(2,1)S(1)}, bf16[256,512]{1,0:T(8,128)(2,1)S(1)}, u32[]{:S(2)}, u32[]{:S(2)}) collective-permute-start(bf16[256,512]{1,0:T(8,128)(2,1)S(1)} %pad_maximum_fusion.12), channel_id=1, source_target_pairs={{0,0},{1,1},{2,10},{3,11},{4,20},{5,21},{6,30},{7,31},{8,2},{9,3},... | collective-permute-start | bytes 786440 | tf_op jit(solution)/shard_map/ppermute | solution.py:273
  300.4 27.9 %collective-permute-start.24 = (bf16[256,512]{1,0:T(8,128)(2,1)S(1)}, bf16[256,512]{1,0:T(8,128)(2,1)S(1)}, u32[]{:S(2)}, u32[]{:S(2)}) collective-permute-start(bf16[256,512]{1,0:T(8,128)(2,1)S(1)} %pad_maximum_fusion.13), channel_id=1, source_target_pairs={{0,2},{1,3},{2,8},{3,9},{4,22},{5,23},{6,28},{7,29},{8,0},{9,1},{1... | collective-permute-start | bytes 786440 | tf_op jit(solution)/shard_map/ppermute | solution.py:273
  302.4 26.0 %collective-permute-start.25 = (bf16[256,512]{1,0:T(8,128)(2,1)S(1)}, bf16[256,512]{1,0:T(8,128)(2,1)S(1)}, u32[]{:S(2)}, u32[]{:S(2)}) collective-permute-start(bf16[256,512]{1,0:T(8,128)(2,1)S(1)} %pad_maximum_fusion.14), channel_id=1, source_target_pairs={{0,4},{1,5},{2,14},{3,15},{4,16},{5,17},{6,26},{7,27},{8,6},{9,7},... | collective-permute-start | bytes 786440 | tf_op jit(solution)/shard_map/ppermute | solution.py:273
  305.6 22.7 %collective-permute-start.26 = (bf16[256,512]{1,0:T(8,128)(2,1)S(1)}, bf16[256,512]{1,0:T(8,128)(2,1)S(1)}, u32[]{:S(2)}, u32[]{:S(2)}) collective-permute-start(bf16[256,512]{1,0:T(8,128)(2,1)S(1)} %pad_maximum_fusion.15), channel_id=1, source_target_pairs={{0,6},{1,7},{2,12},{3,13},{4,18},{5,19},{6,24},{7,25},{8,4},{9,5},... | collective-permute-start | bytes 786440 | tf_op jit(solution)/shard_map/ppermute | solution.py:273
  328.4 22.7 %collective-permute-start.27 = (bf16[256,512]{1,0:T(8,128)(2,1)}, bf16[256,512]{1,0:T(8,128)(2,1)S(1)}, u32[]{:S(2)}, u32[]{:S(2)}) collective-permute-start(bf16[256,512]{1,0:T(8,128)(2,1)} %get-tuple-element.166), channel_id=1, source_target_pairs={{0,8},{8,0},{16,24},{24,16},{1,9},{9,1},{17,25},{25,17},{2,10},{10... | collective-permute-start | bytes 786440 | tf_op jit(solution)/shard_map/ppermute | solution.py:279
  329.9 21.2 %collective-permute-start.28 = (bf16[256,512]{1,0:T(8,128)(2,1)}, bf16[256,512]{1,0:T(8,128)(2,1)S(1)}, u32[]{:S(2)}, u32[]{:S(2)}) collective-permute-start(bf16[256,512]{1,0:T(8,128)(2,1)} %get-tuple-element.167), channel_id=1, source_target_pairs={{0,16},{8,24},{16,0},{24,8},{1,17},{9,25},{17,1},{25,9},{2,18},{10... | collective-permute-start | bytes 786440 | tf_op jit(solution)/shard_map/ppermute | solution.py:279
  334.8 25.1 %collective-permute-start.29 = (bf16[256,512]{1,0:T(8,128)(2,1)}, bf16[256,512]{1,0:T(8,128)(2,1)S(1)}, u32[]{:S(2)}, u32[]{:S(2)}) collective-permute-start(bf16[256,512]{1,0:T(8,128)(2,1)} %get-tuple-element.168), channel_id=1, source_target_pairs={{0,24},{8,16},{16,8},{24,0},{1,25},{9,17},{17,9},{25,1},{2,26},{10... | collective-permute-start | bytes 786440 | tf_op jit(solution)/shard_map/ppermute | solution.py:279
  362.5 15.3 %collective-permute-start.33 = (bf16[128,512]{1,0:T(8,128)(2,1)S(1)}, bf16[128,512]{1,0:T(8,128)(2,1)S(1)}, u32[]{:S(2)}, u32[]{:S(2)}) collective-permute-start(bf16[128,512]{1,0:T(8,128)(2,1)S(1)} %get-tuple-element.185), channel_id=1, source_target_pairs={{0,4},{1,5},{2,6},{3,7},{4,0},{5,1},{6,2},{7,3},{8,12},{9,13},{10,... | collective-permute-start | bytes 393224 | tf_op jit(solution)/shard_map/ppermute | solution.py:284
  362.5 17.5 %collective-permute-start.34 = (bf16[128,512]{1,0:T(8,128)(2,1)S(1)}, bf16[128,512]{1,0:T(8,128)(2,1)S(1)}, u32[]{:S(2)}, u32[]{:S(2)}) collective-permute-start(bf16[128,512]{1,0:T(8,128)(2,1)S(1)} %get-tuple-element.186), channel_id=1, source_target_pairs={{0,5},{1,4},{2,7},{3,6},{4,1},{5,0},{6,3},{7,2},{8,13},{9,12},{10,... | collective-permute-start | bytes 393224 | tf_op jit(solution)/shard_map/ppermute | solution.py:284
  365.1 14.9 %collective-permute-start.35 = (bf16[128,512]{1,0:T(8,128)(2,1)S(1)}, bf16[128,512]{1,0:T(8,128)(2,1)S(1)}, u32[]{:S(2)}, u32[]{:S(2)}) collective-permute-start(bf16[128,512]{1,0:T(8,128)(2,1)S(1)} %get-tuple-element.187), channel_id=1, source_target_pairs={{0,6},{1,7},{2,4},{3,5},{4,2},{5,3},{6,0},{7,1},{8,14},{9,15},{10,... | collective-permute-start | bytes 393224 | tf_op jit(solution)/shard_map/ppermute | solution.py:284
  367.3 19.9 %collective-permute-start.37 = (bf16[256,512]{1,0:T(8,128)(2,1)}, bf16[256,512]{1,0:T(8,128)(2,1)S(1)}, u32[]{:S(2)}, u32[]{:S(2)}) collective-permute-start(bf16[256,512]{1,0:T(8,128)(2,1)} %get-tuple-element.190), channel_id=1, source_target_pairs={{0,8},{8,0},{16,24},{24,16},{1,9},{9,1},{17,25},{25,17},{2,10},{10... | collective-permute-start | bytes 786440 | tf_op jit(solution)/shard_map/ppermute | solution.py:279
  369.2 18.0 %collective-permute-start.38 = (bf16[256,512]{1,0:T(8,128)(2,1)}, bf16[256,512]{1,0:T(8,128)(2,1)S(1)}, u32[]{:S(2)}, u32[]{:S(2)}) collective-permute-start(bf16[256,512]{1,0:T(8,128)(2,1)} %get-tuple-element.191), channel_id=1, source_target_pairs={{0,16},{8,24},{16,0},{24,8},{1,17},{9,25},{17,1},{25,9},{2,18},{10... | collective-permute-start | bytes 786440 | tf_op jit(solution)/shard_map/ppermute | solution.py:279
  377.8 15.7 %collective-permute-start.39 = (bf16[256,512]{1,0:T(8,128)(2,1)S(1)}, bf16[256,512]{1,0:T(8,128)(2,1)S(1)}, u32[]{:S(2)}, u32[]{:S(2)}) collective-permute-start(bf16[256,512]{1,0:T(8,128)(2,1)S(1)} %copy-done.24), channel_id=1, source_target_pairs={{0,24},{8,16},{16,8},{24,0},{1,25},{9,17},{17,9},{25,1},{2,26},{10... | collective-permute-start | bytes 786440 | tf_op jit(solution)/shard_map/ppermute | solution.py:279
  396.2 18.5 %collective-permute-start.43 = (bf16[128,512]{1,0:T(8,128)(2,1)S(1)}, bf16[128,512]{1,0:T(8,128)(2,1)S(1)}, u32[]{:S(2)}, u32[]{:S(2)}) collective-permute-start(bf16[128,512]{1,0:T(8,128)(2,1)S(1)} %get-tuple-element.201), channel_id=1, source_target_pairs={{0,4},{1,5},{2,6},{3,7},{4,0},{5,1},{6,2},{7,3},{8,12},{9,13},{10,... | collective-permute-start | bytes 393224 | tf_op jit(solution)/shard_map/ppermute | solution.py:284
  396.2 20.0 %collective-permute-start.44 = (bf16[128,512]{1,0:T(8,128)(2,1)S(1)}, bf16[128,512]{1,0:T(8,128)(2,1)S(1)}, u32[]{:S(2)}, u32[]{:S(2)}) collective-permute-start(bf16[128,512]{1,0:T(8,128)(2,1)S(1)} %get-tuple-element.202), channel_id=1, source_target_pairs={{0,5},{1,4},{2,7},{3,6},{4,1},{5,0},{6,3},{7,2},{8,13},{9,12},{10,... | collective-permute-start | bytes 393224 | tf_op jit(solution)/shard_map/ppermute | solution.py:284
  398.8 17.5 %collective-permute-start.45 = (bf16[128,512]{1,0:T(8,128)(2,1)S(1)}, bf16[128,512]{1,0:T(8,128)(2,1)S(1)}, u32[]{:S(2)}, u32[]{:S(2)}) collective-permute-start(bf16[128,512]{1,0:T(8,128)(2,1)S(1)} %get-tuple-element.203), channel_id=1, source_target_pairs={{0,6},{1,7},{2,4},{3,5},{4,2},{5,3},{6,0},{7,1},{8,14},{9,15},{10,... | collective-permute-start | bytes 393224 | tf_op jit(solution)/shard_map/ppermute | solution.py:284
  402.6 13.7 %collective-permute-start.46 = (bf16[128,512]{1,0:T(8,128)(2,1)S(1)}, bf16[128,512]{1,0:T(8,128)(2,1)S(1)}, u32[]{:S(2)}, u32[]{:S(2)}) collective-permute-start(bf16[128,512]{1,0:T(8,128)(2,1)S(1)} %get-tuple-element.204), channel_id=1, source_target_pairs={{0,7},{1,6},{2,5},{3,4},{4,3},{5,2},{6,1},{7,0},{8,15},{9,14},{10,... | collective-permute-start | bytes 393224 | tf_op jit(solution)/shard_map/ppermute | solution.py:284
  (40 other events, 528.4 us)
Sparse Core Ops, SparseCore 0:
  16.4 89.0 reduce-scatter.2
  108.9 129.4 reduce-scatter.4
  260.2 135.5 all-gather.4
  417.8 90.1 all-gather.2

commit v8 on v7

--- a/solution.py
+++ b/solution.py
@@ -278,8 +278,11 @@
     def send_rows(slot, strips):
         return [strips[0]] + [lax.ppermute(strips[k], "dp", to_row[k]) for k in range(1, ranks)]
 
-    def send_columns(slot, moved):
-        routed = route(ranks, inner, place, moved)
+    def send_columns(slot, moved, now):
+        routed = list(route(ranks, inner, place, moved))
+        if slot + 1 in now:
+            middle = len(routed) // 2
+            routed[middle:], now[slot + 1][-1] = lax.optimization_barrier((routed[middle:], now[slot + 1][-1]))
         back = [routed[0]] + [
             lax.ppermute(piece, "fsdp", to_column[key]) for piece, key in zip(routed[1:], rounds[1:])
         ]
@@ -289,22 +292,27 @@
             back[at], ready[g][0] = lax.optimization_barrier((back[at], ready[g][0]))
         return back
 
-    stages = (send_in, work, send_rows, send_columns)
+    stages = 4
     held, finished = {}, {}
     out = None
-    for tick in range(begins[-1] + len(stages)):
+    for tick in range(begins[-1] + stages):
         now = {}
-        for slot, begin in enumerate(begins):
-            stage = tick - begin
+        at_stage = {tick - begin: slot for slot, begin in enumerate(begins)}
+        for stage in (2, 3, 0, 1):
+            if stage not in at_stage:
+                continue
+            slot = at_stage[stage]
             if stage == 0:
                 now[slot] = send_in(slot)
-            elif 0 < stage < len(stages):
-                now[slot] = stages[stage](slot, held[slot])
-            if stage == len(stages) - 1:
-                finished[slot] = now.pop(slot)
+            elif stage == 1:
+                now[slot] = work(slot, held[slot])
+            elif stage == 2:
+                now[slot] = send_rows(slot, held[slot])
+            else:
+                finished[slot] = send_columns(slot, held[slot], now)
                 now[slot] = finished[slot][-1:]
         for first, count in gathers:
-            if begins[first + count - 1] + len(stages) - 1 == tick:
+            if begins[first + count - 1] + stages - 1 == tick:
                 back = [piece for slot in range(first, first + count) for piece in finished[slot]]
                 gathered = lax.all_gather(jnp.concatenate(back, axis=0), "dp", axis=0, tiled=True)
                 out = unpack(ranks, inner, (first, count), per, place, gathered, out)

time: 525 us -> 526 us (level)
    ppermute x28, waiting for transfers between devices: 51.4 us -> 34.9 us  [send_columns(): lax.ppermute(piece, 'fsdp', to_column[key])]
    ppermute x12, waiting for transfers between devices: 25.1 us -> 37.6 us  [send_rows(): lax.ppermute(strips[k], 'dp', to_row[k])]
    unnamed x82 -> x78, local copies, waits for them, and re-layouts: 11.5 us -> 11.5 us
  transfers between devices with their start and end apart: 62 -> 62, of which waited for: 29 -> 22; matrix products, arithmetic and copies ran while one was open for 3% -> 3% of each run, Pallas kernels for 21% -> 21%
where the time goes in v8:
time: 526 us; the launch traced here: 524 us
  waiting for transfers between devices  242 us (46%)
  Pallas kernels  130 us (25%)
  starting transfers between devices  122 us (23%)
  local copies, waits for them, and re-layouts  15.4 us (3%)
  between operations  14 us (3%)
    all_gather x2, waiting for transfers between devices, shards(): lax.all_gather(jnp.concatenate(back, axis=0), 'dp', axis=0, tiled=True)  81.2 us
    ppermute x16, starting transfers between devices, send_in(): lax.ppermute(strips[k], MESH_AXES, to_owner[k])  65 us
    pallas_call x4, Pallas kernels, precondition(): pl.pallas_call(functools.partial(block_kernel, ranks, inner, col_blocks),...  59.5 us
    reduce_scatter x2, waiting for transfers between devices, shards(): lax.psum_scatter(packed, 'dp', scatter_dimension=0, tiled=True)  48.8 us
    ppermute x12, waiting for transfers between devices, send_rows(): lax.ppermute(strips[k], 'dp', to_row[k])  37.6 us
    ppermute x16, waiting for transfers between devices, send_in(): lax.ppermute(strips[k], MESH_AXES, to_owner[k])  35.8 us
    ppermute x28, waiting for transfers between devices, send_columns(): lax.ppermute(piece, 'fsdp', to_column[key])  34.9 us
    ppermute x28, starting transfers between devices, send_columns(): lax.ppermute(piece, 'fsdp', to_column[key])  33.3 us
  transfers between devices with their start and end apart: 62, of which 22 were waited for; matrix products, arithmetic and copies ran while one was open for 3% of the time, Pallas kernels for 21%

profile of v8, /device:TPU:0, one launch (start us, length us, event | category | flops | bytes accessed | tf_op | source)
XLA Modules:
  0.0 524.2 jit_solution(14662666748843381416)
XLA Ops:
  7.1 9.1 %pack_slabs.2 = bf16[4,2,2,4,128,512]{5,4,3,2,1,0:T(8,128)(2,1)} custom-call(s32[3]{0:T(128)} %pad_add_fusion.place_ref, bf16[8,4,512,512]{3,2,1,0:T(8,128)(2,1)} %bitcast.9), custom_call_target="tpu_custom_call" | custom-call | bytes 16777216 | tf_op jit(solution)/shard_map/pack_slabs/pallas_call | solution.py:75
  16.3 9.1 %pack_slabs.3 = bf16[4,2,2,4,128,512]{5,4,3,2,1,0:T(8,128)(2,1)} custom-call(s32[3]{0:T(128)} %pad_add_fusion.place_ref, bf16[8,4,512,512]{3,2,1,0:T(8,128)(2,1)} %bitcast.10), custom_call_target="tpu_custom_call" | custom-call | bytes 16777216 | tf_op jit(solution)/shard_map/pack_slabs/pallas_call | solution.py:75
  25.4 31.3 %fourth_powers.1 = (f32[4,2,512,512]{3,2,1,0:T(8,128)}, f32[4,2,512,512]{3,2,1,0:T(8,128)}) custom-call(f32[4,2,512,512]{3,2,1,0:T(8,128)} %refs_6_.7, f32[4,2,512,512]{3,2,1,0:T(8,128)} %refs_7_.7), custom_call_target="tpu_custom_call" | custom-call | flops 25769803776 | bytes 33554432 | tf_op jit(solution)/shard_map/fourth_powers/pallas_call | solution.py:45
  56.7 48.8 %reduce-scatter.3.cloned.1.call-done = bf16[2048,512]{1,0:T(8,128)(2,1)} async-done(((bf16[8192,512]{1,0:T(8,128)(2,1)}), bf16[2048,512]{1,0:T(8,128)(2,1)}) %reduce-scatter.3.cloned.1.call-update) | async-done | bytes 2097168 | tf_op jit(solution)/shard_map/reduce_scatter | solution.py:255
  110.7 6.0 %collective-permute-start.2 = (bf16[256,512]{1,0:T(8,128)(2,1)S(1)}, bf16[256,512]{1,0:T(8,128)(2,1)S(1)}, u32[]{:S(2)}, u32[]{:S(2)}) collective-permute-start(bf16[256,512]{1,0:T(8,128)(2,1)S(1)} %pad_maximum_fusion.1), channel_id=1, source_target_pairs={{0,2},{1,3},{2,8},{3,9},{4,22},{5,23},{6,28},{7,29},{8,0},{9,1},{1... | collective-permute-start | bytes 786440 | tf_op jit(solution)/shard_map/ppermute | solution.py:273
  116.7 4.3 collective-permute-start.3
  121.1 5.2 collective-permute-start.4
  126.3 2.6 collective-permute-done.2.refs_1_
  128.9 10.7 %collective-permute-done.3.refs_2_ = bf16[256,512]{1,0:T(8,128)(2,1)S(1)} collective-permute-done((bf16[256,512]{1,0:T(8,128)(2,1)S(1)}, bf16[256,512]{1,0:T(8,128)(2,1)S(1)}, u32[]{:S(2)}, u32[]{:S(2)}) %collective-permute-start.3) | collective-permute-done | bytes 262176 | tf_op jit(solution)/shard_map/ppermute | solution.py:273
  139.6 4.1 collective-permute-done.4.refs_3_
  144.5 4.4 collective-permute-start.6
  148.9 4.4 collective-permute-start.7
  153.3 7.9 %collective-permute-start.8 = (bf16[256,512]{1,0:T(8,128)(2,1)S(1)}, bf16[256,512]{1,0:T(8,128)(2,1)S(1)}, u32[]{:S(2)}, u32[]{:S(2)}) collective-permute-start(bf16[256,512]{1,0:T(8,128)(2,1)S(1)} %pad_maximum_fusion.7), channel_id=1, source_target_pairs={{0,6},{1,7},{2,12},{3,13},{4,18},{5,19},{6,24},{7,25},{8,4},{9,5},... | collective-permute-start | bytes 786440 | tf_op jit(solution)/shard_map/ppermute | solution.py:273
  161.2 15.0 %precondition.4 = (bf16[256,512]{1,0:T(8,128)(2,1)}, bf16[256,512]{1,0:T(8,128)(2,1)}, bf16[256,512]{1,0:T(8,128)(2,1)}, bf16[256,512]{1,0:T(8,128)(2,1)}) custom-call(s32[3]{0:T(128)} %pad_add_fusion.place_ref, bf16[256,512]{1,0:T(8,128)(2,1)} %copy-done.9, bf16[256,512]{1,0:T(8,128)(2,1)} %copy-done.11, bf16[256,512]{1,0:T(8,128)(2,1)} %copy-done.13, ...), custom_call_target="tpu_custom_call" | custom-call | flops 8589934592 | bytes 14680064 | tf_op jit(solution)/shard_map/precondition/pallas_call | solution.py:205
  177.8 4.8 collective-permute-start.10
  184.0 14.9 %precondition.5 = (bf16[256,512]{1,0:T(8,128)(2,1)}, bf16[256,512]{1,0:T(8,128)(2,1)}, bf16[256,512]{1,0:T(8,128)(2,1)}, bf16[256,512]{1,0:T(8,128)(2,1)}) custom-call(s32[3]{0:T(128)} %pad_add_fusion.place_ref, bf16[256,512]{1,0:T(8,128)(2,1)} %copy-done.17, bf16[256,512]{1,0:T(8,128)(2,1)} %copy-done.19, bf16[256,512]{1,0:T(8,128)(2,1)} %copy-done.21, ...), custom_call_target="tpu_custom_call" | custom-call | flops 8589934592 | bytes 14680064 | tf_op jit(solution)/shard_map/precondition/pallas_call | solution.py:205
  206.4 8.1 %collective-permute-done.12.refs_3_ = bf16[256,512]{1,0:T(8,128)(2,1)S(1)} collective-permute-done((bf16[256,512]{1,0:T(8,128)(2,1)}, bf16[256,512]{1,0:T(8,128)(2,1)S(1)}, u32[]{:S(2)}, u32[]{:S(2)}) %collective-permute-start.12) | collective-permute-done | bytes 262176 | tf_op jit(solution)/shard_map/ppermute | solution.py:279
  215.2 4.4 collective-permute-start.51
  220.3 4.8 collective-permute-done.14.refs_1_
  226.8 10.9 %collective-permute-done.50 = bf16[128,512]{1,0:T(8,128)(2,1)S(1)} collective-permute-done((bf16[128,512]{1,0:T(8,128)(2,1)S(1)}, bf16[128,512]{1,0:T(8,128)(2,1)S(1)}, u32[]{:S(2)}, u32[]{:S(2)}) %collective-permute-start.50) | collective-permute-done | bytes 131104 | tf_op jit(solution)/shard_map/ppermute | solution.py:287
  241.4 2.2 collective-permute-start.55
  246.6 3.5 collective-permute-done.54
  254.0 3.6 collective-permute-done.56
  260.1 2.5 collective-permute-done.18
  263.3 8.1 %collective-permute-start.20 = (bf16[256,512]{1,0:T(8,128)(2,1)S(1)}, bf16[256,512]{1,0:T(8,128)(2,1)S(1)}, u32[]{:S(2)}, u32[]{:S(2)}) collective-permute-start(bf16[256,512]{1,0:T(8,128)(2,1)S(1)} %pad_maximum_fusion.9), channel_id=1, source_target_pairs={{0,2},{1,3},{2,8},{3,9},{4,22},{5,23},{6,28},{7,29},{8,0},{9,1},{1... | collective-permute-start | bytes 786440 | tf_op jit(solution)/shard_map/ppermute | solution.py:273
  271.4 4.2 collective-permute-start.21
  275.7 4.2 collective-permute-start.22
  279.9 2.9 collective-permute-done.20.refs_1_
  282.8 10.0 %collective-permute-done.21.refs_2_ = bf16[256,512]{1,0:T(8,128)(2,1)S(1)} collective-permute-done((bf16[256,512]{1,0:T(8,128)(2,1)S(1)}, bf16[256,512]{1,0:T(8,128)(2,1)S(1)}, u32[]{:S(2)}, u32[]{:S(2)}) %collective-permute-start.21) | collective-permute-done | bytes 262176 | tf_op jit(solution)/shard_map/ppermute | solution.py:273
  292.8 5.5 %collective-permute-done.22.refs_3_ = bf16[256,512]{1,0:T(8,128)(2,1)S(1)} collective-permute-done((bf16[256,512]{1,0:T(8,128)(2,1)S(1)}, bf16[256,512]{1,0:T(8,128)(2,1)S(1)}, u32[]{:S(2)}, u32[]{:S(2)}) %collective-permute-start.22) | collective-permute-done | bytes 262176 | tf_op jit(solution)/shard_map/ppermute | solution.py:273
  299.1 3.2 collective-permute-start.24
  302.4 2.6 collective-permute-start.25
  305.0 7.9 %collective-permute-start.26 = (bf16[256,512]{1,0:T(8,128)(2,1)S(1)}, bf16[256,512]{1,0:T(8,128)(2,1)S(1)}, u32[]{:S(2)}, u32[]{:S(2)}) collective-permute-start(bf16[256,512]{1,0:T(8,128)(2,1)S(1)} %pad_maximum_fusion.15), channel_id=1, source_target_pairs={{0,6},{1,7},{2,12},{3,13},{4,18},{5,19},{6,24},{7,25},{8,4},{9,5},... | collective-permute-start | bytes 786440 | tf_op jit(solution)/shard_map/ppermute | solution.py:273
  313.0 14.7 %precondition.6 = (bf16[256,512]{1,0:T(8,128)(2,1)}, bf16[256,512]{1,0:T(8,128)(2,1)}, bf16[256,512]{1,0:T(8,128)(2,1)}, bf16[256,512]{1,0:T(8,128)(2,1)}) custom-call(s32[3]{0:T(128)} %pad_add_fusion.place_ref, bf16[256,512]{1,0:T(8,128)(2,1)} %copy-done.8, bf16[256,512]{1,0:T(8,128)(2,1)} %copy-done.10, bf16[256,512]{1,0:T(8,128)(2,1)} %copy-done.12, ...), custom_call_target="tpu_custom_call" | custom-call | flops 8589934592 | bytes 14680064 | tf_op jit(solution)/shard_map/precondition/pallas_call | solution.py:205
  329.3 5.5 %collective-permute-start.28 = (bf16[256,512]{1,0:T(8,128)(2,1)}, bf16[256,512]{1,0:T(8,128)(2,1)S(1)}, u32[]{:S(2)}, u32[]{:S(2)}) collective-permute-start(bf16[256,512]{1,0:T(8,128)(2,1)} %get-tuple-element.182), channel_id=1, source_target_pairs={{0,16},{8,24},{16,0},{24,8},{1,17},{9,25},{17,1},{25,9},{2,18},{10... | collective-permute-start | bytes 786440 | tf_op jit(solution)/shard_map/ppermute | solution.py:279
  336.2 15.0 %precondition.7 = (bf16[256,512]{1,0:T(8,128)(2,1)}, bf16[256,512]{1,0:T(8,128)(2,1)}, bf16[256,512]{1,0:T(8,128)(2,1)}, bf16[256,512]{1,0:T(8,128)(2,1)}) custom-call(s32[3]{0:T(128)} %pad_add_fusion.place_ref, bf16[256,512]{1,0:T(8,128)(2,1)} %copy-done.14, bf16[256,512]{1,0:T(8,128)(2,1)} %copy-done.18, bf16[256,512]{1,0:T(8,128)(2,1)} %copy-done.20, ...), custom_call_target="tpu_custom_call" | custom-call | flops 8589934592 | bytes 14680064 | tf_op jit(solution)/shard_map/precondition/pallas_call | solution.py:205
  351.2 8.8 %collective-permute-done.29.refs_3_ = bf16[256,512]{1,0:T(8,128)(2,1)S(1)} collective-permute-done((bf16[256,512]{1,0:T(8,128)(2,1)}, bf16[256,512]{1,0:T(8,128)(2,1)S(1)}, u32[]{:S(2)}, u32[]{:S(2)}) %collective-permute-start.29) | collective-permute-done | bytes 262176 | tf_op jit(solution)/shard_map/ppermute | solution.py:279
  362.7 3.5 collective-permute-start.39
  366.2 9.6 %collective-permute-done.33.refs_3_ = bf16[256,512]{1,0:T(8,128)(2,1)S(1)} collective-permute-done((bf16[256,512]{1,0:T(8,128)(2,1)}, bf16[256,512]{1,0:T(8,128)(2,1)S(1)}, u32[]{:S(2)}, u32[]{:S(2)}) %collective-permute-start.33) | collective-permute-done | bytes 262176 | tf_op jit(solution)/shard_map/ppermute | solution.py:279
  377.5 6.2 %collective-permute-done.38.refs_1_ = bf16[256,512]{1,0:T(8,128)(2,1)S(1)} collective-permute-done((bf16[256,512]{1,0:T(8,128)(2,1)}, bf16[256,512]{1,0:T(8,128)(2,1)S(1)}, u32[]{:S(2)}, u32[]{:S(2)}) %collective-permute-start.38) | collective-permute-done | bytes 262176 | tf_op jit(solution)/shard_map/ppermute | solution.py:279
  383.7 2.4 collective-permute-start.36
  386.9 8.3 %collective-permute-start.41 = (bf16[128,512]{1,0:T(8,128)(2,1)S(1)}, bf16[128,512]{1,0:T(8,128)(2,1)S(1)}, u32[]{:S(2)}, u32[]{:S(2)}) collective-permute-start(bf16[128,512]{1,0:T(8,128)(2,1)S(1)} %get-tuple-element.219), channel_id=1, source_target_pairs={{0,2},{1,3},{2,0},{3,1},{4,6},{5,7},{6,4},{7,5},{8,10},{9,11},{10,... | collective-permute-start | bytes 393224 | tf_op jit(solution)/shard_map/ppermute | solution.py:287
  396.4 2.7 collective-permute-start.44
  399.7 2.7 collective-permute-start.46
  404.8 12.2 %collective-permute-done.44 = bf16[128,512]{1,0:T(8,128)(2,1)S(1)} collective-permute-done((bf16[128,512]{1,0:T(8,128)(2,1)S(1)}, bf16[128,512]{1,0:T(8,128)(2,1)S(1)}, u32[]{:S(2)}, u32[]{:S(2)}) %collective-permute-start.44) | collective-permute-done | bytes 131104 | tf_op jit(solution)/shard_map/ppermute | solution.py:287
  418.5 9.0 %unpack_slabs.2.rest_0_ = bf16[8,4,512,512]{3,2,1,0:T(8,128)(2,1)} custom-call(s32[3]{0:T(128)} %pad_add_fusion.place_ref, bf16[4,2,8,128,512]{4,3,2,1,0:T(8,128)(2,1)} %bitcast.13), custom_call_target="tpu_custom_call" | custom-call | bytes 16777216 | tf_op jit(solution)/shard_map/unpack_slabs/pallas_call | solution.py:107
  427.5 81.2 %all-gather.3.cloned.1.call-done = bf16[8192,512]{1,0:T(8,128)(2,1)} async-done(((bf16[2048,512]{1,0:T(8,128)(2,1)}), bf16[8192,512]{1,0:T(8,128)(2,1)}) %all-gather.3.cloned.1.call-update) | async-done | bytes 8388624 | tf_op jit(solution)/shard_map/all_gather | solution.py:317
  508.7 9.0 %unpack_slabs.3 = bf16[8,4,512,512]{3,2,1,0:T(8,128)(2,1)} custom-call(s32[3]{0:T(128)} %pad_add_fusion.place_ref, bf16[4,2,8,128,512]{4,3,2,1,0:T(8,128)(2,1)} %bitcast.14, bf16[8,4,512,512]{3,2,1,0:T(8,128)(2,1)} %unpack_slabs.2.rest_0_), custom_call_target="tpu_custom_call", output_to_operand_aliasing={{}: (2, {})} | custom-call | bytes 16777216 | tf_op jit(solution)/shard_map/unpack_slabs/pallas_call | solution.py:107
  (199 shorter events, 48.4 us)
Async XLA Ops:
  6.5 99.0 %reduce-scatter.3.cloned.1.call-start = ((), (), s32[]{:S(2)}) async-start(), calls=%async_computation.2 | async-start | bytes 10485760 | tf_op jit(solution)/shard_map/reduce_scatter | solution.py:255
  16.2 237.1 %reduce-scatter.5.cloned.1.call-start = ((), (), s32[]{:S(2)}) async-start(), calls=%async_computation.3 | async-start | bytes 10485760 | tf_op jit(solution)/shard_map/reduce_scatter | solution.py:255
  25.4 393.1 %all-gather.5.cloned.1.call-start = ((), (), s32[]{:S(2)}) async-start(), calls=%async_computation.5 | async-start | bytes 10485760 | tf_op jit(solution)/shard_map/all_gather | solution.py:317
  110.0 16.3 %collective-permute-start.1 = (bf16[256,512]{1,0:T(8,128)(2,1)S(1)}, bf16[256,512]{1,0:T(8,128)(2,1)S(1)}, u32[]{:S(2)}, u32[]{:S(2)}) collective-permute-start(bf16[256,512]{1,0:T(8,128)(2,1)S(1)} %pad_maximum_fusion), channel_id=1, source_target_pairs={{0,0},{1,1},{2,10},{3,11},{4,20},{5,21},{6,30},{7,31},{8,2},{9,3},... | collective-permute-start | bytes 786440 | tf_op jit(solution)/shard_map/ppermute | solution.py:273
  110.7 18.2 %collective-permute-start.2 = (bf16[256,512]{1,0:T(8,128)(2,1)S(1)}, bf16[256,512]{1,0:T(8,128)(2,1)S(1)}, u32[]{:S(2)}, u32[]{:S(2)}) collective-permute-start(bf16[256,512]{1,0:T(8,128)(2,1)S(1)} %pad_maximum_fusion.1), channel_id=1, source_target_pairs={{0,2},{1,3},{2,8},{3,9},{4,22},{5,23},{6,28},{7,29},{8,0},{9,1},{1... | collective-permute-start | bytes 786440 | tf_op jit(solution)/shard_map/ppermute | solution.py:273
  116.7 22.9 %collective-permute-start.3 = (bf16[256,512]{1,0:T(8,128)(2,1)S(1)}, bf16[256,512]{1,0:T(8,128)(2,1)S(1)}, u32[]{:S(2)}, u32[]{:S(2)}) collective-permute-start(bf16[256,512]{1,0:T(8,128)(2,1)S(1)} %pad_maximum_fusion.2), channel_id=1, source_target_pairs={{0,4},{1,5},{2,14},{3,15},{4,16},{5,17},{6,26},{7,27},{8,6},{9,7},... | collective-permute-start | bytes 786440 | tf_op jit(solution)/shard_map/ppermute | solution.py:273
  121.1 22.6 %collective-permute-start.4 = (bf16[256,512]{1,0:T(8,128)(2,1)S(1)}, bf16[256,512]{1,0:T(8,128)(2,1)S(1)}, u32[]{:S(2)}, u32[]{:S(2)}) collective-permute-start(bf16[256,512]{1,0:T(8,128)(2,1)S(1)} %pad_maximum_fusion.3), channel_id=1, source_target_pairs={{0,6},{1,7},{2,12},{3,13},{4,18},{5,19},{6,24},{7,25},{8,4},{9,5},... | collective-permute-start | bytes 786440 | tf_op jit(solution)/shard_map/ppermute | solution.py:273
  143.8 32.4 %collective-permute-start.5 = (bf16[256,512]{1,0:T(8,128)(2,1)S(1)}, bf16[256,512]{1,0:T(8,128)(2,1)S(1)}, u32[]{:S(2)}, u32[]{:S(2)}) collective-permute-start(bf16[256,512]{1,0:T(8,128)(2,1)S(1)} %pad_maximum_fusion.4), channel_id=1, source_target_pairs={{0,0},{1,1},{2,10},{3,11},{4,20},{5,21},{6,30},{7,31},{8,2},{9,3},... | collective-permute-start | bytes 786440 | tf_op jit(solution)/shard_map/ppermute | solution.py:273
  144.5 31.7 %collective-permute-start.6 = (bf16[256,512]{1,0:T(8,128)(2,1)S(1)}, bf16[256,512]{1,0:T(8,128)(2,1)S(1)}, u32[]{:S(2)}, u32[]{:S(2)}) collective-permute-start(bf16[256,512]{1,0:T(8,128)(2,1)S(1)} %pad_maximum_fusion.5), channel_id=1, source_target_pairs={{0,2},{1,3},{2,8},{3,9},{4,22},{5,23},{6,28},{7,29},{8,0},{9,1},{1... | collective-permute-start | bytes 786440 | tf_op jit(solution)/shard_map/ppermute | solution.py:273
  148.9 27.3 %collective-permute-start.7 = (bf16[256,512]{1,0:T(8,128)(2,1)S(1)}, bf16[256,512]{1,0:T(8,128)(2,1)S(1)}, u32[]{:S(2)}, u32[]{:S(2)}) collective-permute-start(bf16[256,512]{1,0:T(8,128)(2,1)S(1)} %pad_maximum_fusion.6), channel_id=1, source_target_pairs={{0,4},{1,5},{2,14},{3,15},{4,16},{5,17},{6,26},{7,27},{8,6},{9,7},... | collective-permute-start | bytes 786440 | tf_op jit(solution)/shard_map/ppermute | solution.py:273
  153.3 22.9 %collective-permute-start.8 = (bf16[256,512]{1,0:T(8,128)(2,1)S(1)}, bf16[256,512]{1,0:T(8,128)(2,1)S(1)}, u32[]{:S(2)}, u32[]{:S(2)}) collective-permute-start(bf16[256,512]{1,0:T(8,128)(2,1)S(1)} %pad_maximum_fusion.7), channel_id=1, source_target_pairs={{0,6},{1,7},{2,12},{3,13},{4,18},{5,19},{6,24},{7,25},{8,4},{9,5},... | collective-permute-start | bytes 786440 | tf_op jit(solution)/shard_map/ppermute | solution.py:273
  176.3 22.6 %collective-permute-start.9 = (bf16[256,512]{1,0:T(8,128)(2,1)}, bf16[256,512]{1,0:T(8,128)(2,1)S(1)}, u32[]{:S(2)}, u32[]{:S(2)}) collective-permute-start(bf16[256,512]{1,0:T(8,128)(2,1)} %get-tuple-element.138), channel_id=1, source_target_pairs={{0,8},{8,0},{16,24},{24,16},{1,9},{9,1},{17,25},{25,17},{2,10},{10... | collective-permute-start | bytes 786440 | tf_op jit(solution)/shard_map/ppermute | solution.py:279
  177.8 21.1 %collective-permute-start.10 = (bf16[256,512]{1,0:T(8,128)(2,1)}, bf16[256,512]{1,0:T(8,128)(2,1)S(1)}, u32[]{:S(2)}, u32[]{:S(2)}) collective-permute-start(bf16[256,512]{1,0:T(8,128)(2,1)} %get-tuple-element.139), channel_id=1, source_target_pairs={{0,16},{8,24},{16,0},{24,8},{1,17},{9,25},{17,1},{25,9},{2,18},{10... | collective-permute-start | bytes 786440 | tf_op jit(solution)/shard_map/ppermute | solution.py:279
  182.6 16.3 %collective-permute-start.11 = (bf16[256,512]{1,0:T(8,128)(2,1)}, bf16[256,512]{1,0:T(8,128)(2,1)S(1)}, u32[]{:S(2)}, u32[]{:S(2)}) collective-permute-start(bf16[256,512]{1,0:T(8,128)(2,1)} %get-tuple-element.140), channel_id=1, source_target_pairs={{0,24},{8,16},{16,8},{24,0},{1,25},{9,17},{17,9},{25,1},{2,26},{10... | collective-permute-start | bytes 786440 | tf_op jit(solution)/shard_map/ppermute | solution.py:279
  198.9 15.6 %collective-permute-start.12 = (bf16[256,512]{1,0:T(8,128)(2,1)}, bf16[256,512]{1,0:T(8,128)(2,1)S(1)}, u32[]{:S(2)}, u32[]{:S(2)}) collective-permute-start(bf16[256,512]{1,0:T(8,128)(2,1)} %get-tuple-element.157), channel_id=1, source_target_pairs={{0,24},{8,16},{16,8},{24,0},{1,25},{9,17},{17,9},{25,1},{2,26},{10... | collective-permute-start | bytes 786440 | tf_op jit(solution)/shard_map/ppermute | solution.py:279
  201.3 13.3 %collective-permute-start.48 = (bf16[128,512]{1,0:T(8,128)(2,1)S(1)}, bf16[128,512]{1,0:T(8,128)(2,1)S(1)}, u32[]{:S(2)}, u32[]{:S(2)}) collective-permute-start(bf16[128,512]{1,0:T(8,128)(2,1)S(1)} %get-tuple-element.227), channel_id=1, source_target_pairs={{0,2},{1,3},{2,0},{3,1},{4,6},{5,7},{6,4},{7,5},{8,10},{9,11},{10,... | collective-permute-start | bytes 393224 | tf_op jit(solution)/shard_map/ppermute | solution.py:287
  201.8 13.4 %collective-permute-start.49 = (bf16[128,512]{1,0:T(8,128)(2,1)S(1)}, bf16[128,512]{1,0:T(8,128)(2,1)S(1)}, u32[]{:S(2)}, u32[]{:S(2)}) collective-permute-start(bf16[128,512]{1,0:T(8,128)(2,1)S(1)} %get-tuple-element.228), channel_id=1, source_target_pairs={{0,3},{1,2},{2,1},{3,0},{4,7},{5,6},{6,5},{7,4},{8,11},{9,10},{10,... | collective-permute-start | bytes 393224 | tf_op jit(solution)/shard_map/ppermute | solution.py:287
  203.1 21.9 %collective-permute-start.14 = (bf16[256,512]{1,0:T(8,128)(2,1)}, bf16[256,512]{1,0:T(8,128)(2,1)S(1)}, u32[]{:S(2)}, u32[]{:S(2)}) collective-permute-start(bf16[256,512]{1,0:T(8,128)(2,1)} %get-tuple-element.160), channel_id=1, source_target_pairs={{0,8},{8,0},{16,24},{24,16},{1,9},{9,1},{17,25},{25,17},{2,10},{10... | collective-permute-start | bytes 786440 | tf_op jit(solution)/shard_map/ppermute | solution.py:279
  205.8 19.5 %collective-permute-start.15 = (bf16[256,512]{1,0:T(8,128)(2,1)}, bf16[256,512]{1,0:T(8,128)(2,1)S(1)}, u32[]{:S(2)}, u32[]{:S(2)}) collective-permute-start(bf16[256,512]{1,0:T(8,128)(2,1)} %get-tuple-element.161), channel_id=1, source_target_pairs={{0,16},{8,24},{16,0},{24,8},{1,17},{9,25},{17,1},{25,9},{2,18},{10... | collective-permute-start | bytes 786440 | tf_op jit(solution)/shard_map/ppermute | solution.py:279
  214.5 23.1 %collective-permute-start.50 = (bf16[128,512]{1,0:T(8,128)(2,1)S(1)}, bf16[128,512]{1,0:T(8,128)(2,1)S(1)}, u32[]{:S(2)}, u32[]{:S(2)}) collective-permute-start(bf16[128,512]{1,0:T(8,128)(2,1)S(1)} %get-tuple-element.229), channel_id=1, source_target_pairs={{0,4},{1,5},{2,6},{3,7},{4,0},{5,1},{6,2},{7,3},{8,12},{9,13},{10,... | collective-permute-start | bytes 393224 | tf_op jit(solution)/shard_map/ppermute | solution.py:287
  215.2 25.5 %collective-permute-start.51 = (bf16[128,512]{1,0:T(8,128)(2,1)S(1)}, bf16[128,512]{1,0:T(8,128)(2,1)S(1)}, u32[]{:S(2)}, u32[]{:S(2)}) collective-permute-start(bf16[128,512]{1,0:T(8,128)(2,1)S(1)} %get-tuple-element.230), channel_id=1, source_target_pairs={{0,5},{1,4},{2,7},{3,6},{4,1},{5,0},{6,3},{7,2},{8,13},{9,12},{10,... | collective-permute-start | bytes 393224 | tf_op jit(solution)/shard_map/ppermute | solution.py:287
  225.1 16.3 %collective-permute-start.52 = (bf16[128,512]{1,0:T(8,128)(2,1)S(1)}, bf16[128,512]{1,0:T(8,128)(2,1)S(1)}, u32[]{:S(2)}, u32[]{:S(2)}) collective-permute-start(bf16[128,512]{1,0:T(8,128)(2,1)S(1)} %get-tuple-element.231), channel_id=1, source_target_pairs={{0,6},{1,7},{2,4},{3,5},{4,2},{5,3},{6,0},{7,1},{8,14},{9,15},{10,... | collective-permute-start | bytes 393224 | tf_op jit(solution)/shard_map/ppermute | solution.py:287
  226.0 33.0 %collective-permute-start.16 = (bf16[128,512]{1,0:T(8,128)(2,1)S(1)}, bf16[128,512]{1,0:T(8,128)(2,1)S(1)}, u32[]{:S(2)}, u32[]{:S(2)}) collective-permute-start(bf16[128,512]{1,0:T(8,128)(2,1)S(1)} %get-tuple-element.167), channel_id=1, source_target_pairs={{0,7},{1,6},{2,5},{3,4},{4,3},{5,2},{6,1},{7,0},{8,15},{9,14},{10,... | collective-permute-start | bytes 393224 | tf_op jit(solution)/shard_map/ppermute | solution.py:287
  226.0 27.3 %collective-permute-start.17 = (bf16[128,512]{1,0:T(8,128)(2,1)S(1)}, bf16[128,512]{1,0:T(8,128)(2,1)S(1)}, u32[]{:S(2)}, u32[]{:S(2)}) collective-permute-start(bf16[128,512]{1,0:T(8,128)(2,1)S(1)} %get-tuple-element.168), channel_id=1, source_target_pairs={{0,4},{1,5},{2,6},{3,7},{4,0},{5,1},{6,2},{7,3},{8,12},{9,13},{10,... | collective-permute-start | bytes 393224 | tf_op jit(solution)/shard_map/ppermute | solution.py:287
  259.6 249.1 %all-gather.3.cloned.1.call-start = ((), (), s32[]{:S(2)}) async-start(), calls=%async_computation.4 | async-start | bytes 10485760 | tf_op jit(solution)/shard_map/all_gather | solution.py:317
  262.6 17.2 %collective-permute-start.19 = (bf16[256,512]{1,0:T(8,128)(2,1)S(1)}, bf16[256,512]{1,0:T(8,128)(2,1)S(1)}, u32[]{:S(2)}, u32[]{:S(2)}) collective-permute-start(bf16[256,512]{1,0:T(8,128)(2,1)S(1)} %pad_maximum_fusion.8), channel_id=1, source_target_pairs={{0,0},{1,1},{2,10},{3,11},{4,20},{5,21},{6,30},{7,31},{8,2},{9,3},... | collective-permute-start | bytes 786440 | tf_op jit(solution)/shard_map/ppermute | solution.py:273
  263.3 19.4 %collective-permute-start.20 = (bf16[256,512]{1,0:T(8,128)(2,1)S(1)}, bf16[256,512]{1,0:T(8,128)(2,1)S(1)}, u32[]{:S(2)}, u32[]{:S(2)}) collective-permute-start(bf16[256,512]{1,0:T(8,128)(2,1)S(1)} %pad_maximum_fusion.9), channel_id=1, source_target_pairs={{0,2},{1,3},{2,8},{3,9},{4,22},{5,23},{6,28},{7,29},{8,0},{9,1},{1... | collective-permute-start | bytes 786440 | tf_op jit(solution)/shard_map/ppermute | solution.py:273
  271.4 21.4 %collective-permute-start.21 = (bf16[256,512]{1,0:T(8,128)(2,1)S(1)}, bf16[256,512]{1,0:T(8,128)(2,1)S(1)}, u32[]{:S(2)}, u32[]{:S(2)}) collective-permute-start(bf16[256,512]{1,0:T(8,128)(2,1)S(1)} %pad_maximum_fusion.10), channel_id=1, source_target_pairs={{0,4},{1,5},{2,14},{3,15},{4,16},{5,17},{6,26},{7,27},{8,6},{9,7},... | collective-permute-start | bytes 786440 | tf_op jit(solution)/shard_map/ppermute | solution.py:273
  275.7 22.6 %collective-permute-start.22 = (bf16[256,512]{1,0:T(8,128)(2,1)S(1)}, bf16[256,512]{1,0:T(8,128)(2,1)S(1)}, u32[]{:S(2)}, u32[]{:S(2)}) collective-permute-start(bf16[256,512]{1,0:T(8,128)(2,1)S(1)} %pad_maximum_fusion.11), channel_id=1, source_target_pairs={{0,6},{1,7},{2,12},{3,13},{4,18},{5,19},{6,24},{7,25},{8,4},{9,5},... | collective-permute-start | bytes 786440 | tf_op jit(solution)/shard_map/ppermute | solution.py:273
  298.4 29.3 %collective-permute-start.23 = (bf16[256,512]{1,0:T(8,128)(2,1)S(1)}, bf16[256,512]{1,0:T(8,128)(2,1)S(1)}, u32[]{:S(2)}, u32[]{:S(2)}) collective-permute-start(bf16[256,512]{1,0:T(8,128)(2,1)S(1)} %pad_maximum_fusion.12), channel_id=1, source_target_pairs={{0,0},{1,1},{2,10},{3,11},{4,20},{5,21},{6,30},{7,31},{8,2},{9,3},... | collective-permute-start | bytes 786440 | tf_op jit(solution)/shard_map/ppermute | solution.py:273
  299.1 28.6 %collective-permute-start.24 = (bf16[256,512]{1,0:T(8,128)(2,1)S(1)}, bf16[256,512]{1,0:T(8,128)(2,1)S(1)}, u32[]{:S(2)}, u32[]{:S(2)}) collective-permute-start(bf16[256,512]{1,0:T(8,128)(2,1)S(1)} %pad_maximum_fusion.13), channel_id=1, source_target_pairs={{0,2},{1,3},{2,8},{3,9},{4,22},{5,23},{6,28},{7,29},{8,0},{9,1},{1... | collective-permute-start | bytes 786440 | tf_op jit(solution)/shard_map/ppermute | solution.py:273
  302.4 25.3 %collective-permute-start.25 = (bf16[256,512]{1,0:T(8,128)(2,1)S(1)}, bf16[256,512]{1,0:T(8,128)(2,1)S(1)}, u32[]{:S(2)}, u32[]{:S(2)}) collective-permute-start(bf16[256,512]{1,0:T(8,128)(2,1)S(1)} %pad_maximum_fusion.14), channel_id=1, source_target_pairs={{0,4},{1,5},{2,14},{3,15},{4,16},{5,17},{6,26},{7,27},{8,6},{9,7},... | collective-permute-start | bytes 786440 | tf_op jit(solution)/shard_map/ppermute | solution.py:273
  305.0 22.7 %collective-permute-start.26 = (bf16[256,512]{1,0:T(8,128)(2,1)S(1)}, bf16[256,512]{1,0:T(8,128)(2,1)S(1)}, u32[]{:S(2)}, u32[]{:S(2)}) collective-permute-start(bf16[256,512]{1,0:T(8,128)(2,1)S(1)} %pad_maximum_fusion.15), channel_id=1, source_target_pairs={{0,6},{1,7},{2,12},{3,13},{4,18},{5,19},{6,24},{7,25},{8,4},{9,5},... | collective-permute-start | bytes 786440 | tf_op jit(solution)/shard_map/ppermute | solution.py:273
  327.7 23.4 %collective-permute-start.27 = (bf16[256,512]{1,0:T(8,128)(2,1)}, bf16[256,512]{1,0:T(8,128)(2,1)S(1)}, u32[]{:S(2)}, u32[]{:S(2)}) collective-permute-start(bf16[256,512]{1,0:T(8,128)(2,1)} %get-tuple-element.181), channel_id=1, source_target_pairs={{0,8},{8,0},{16,24},{24,16},{1,9},{9,1},{17,25},{25,17},{2,10},{10... | collective-permute-start | bytes 786440 | tf_op jit(solution)/shard_map/ppermute | solution.py:279
  329.3 21.9 %collective-permute-start.28 = (bf16[256,512]{1,0:T(8,128)(2,1)}, bf16[256,512]{1,0:T(8,128)(2,1)S(1)}, u32[]{:S(2)}, u32[]{:S(2)}) collective-permute-start(bf16[256,512]{1,0:T(8,128)(2,1)} %get-tuple-element.182), channel_id=1, source_target_pairs={{0,16},{8,24},{16,0},{24,8},{1,17},{9,25},{17,1},{25,9},{2,18},{10... | collective-permute-start | bytes 786440 | tf_op jit(solution)/shard_map/ppermute | solution.py:279
  334.8 25.2 %collective-permute-start.29 = (bf16[256,512]{1,0:T(8,128)(2,1)}, bf16[256,512]{1,0:T(8,128)(2,1)S(1)}, u32[]{:S(2)}, u32[]{:S(2)}) collective-permute-start(bf16[256,512]{1,0:T(8,128)(2,1)} %get-tuple-element.183), channel_id=1, source_target_pairs={{0,24},{8,16},{16,8},{24,0},{1,25},{9,17},{17,9},{25,1},{2,26},{10... | collective-permute-start | bytes 786440 | tf_op jit(solution)/shard_map/ppermute | solution.py:279
  359.9 15.9 %collective-permute-start.33 = (bf16[256,512]{1,0:T(8,128)(2,1)}, bf16[256,512]{1,0:T(8,128)(2,1)S(1)}, u32[]{:S(2)}, u32[]{:S(2)}) collective-permute-start(bf16[256,512]{1,0:T(8,128)(2,1)} %get-tuple-element.204), channel_id=1, source_target_pairs={{0,24},{8,16},{16,8},{24,0},{1,25},{9,17},{17,9},{25,1},{2,26},{10... | collective-permute-start | bytes 786440 | tf_op jit(solution)/shard_map/ppermute | solution.py:279
  360.7 15.1 %collective-permute-start.31 = (bf16[128,512]{1,0:T(8,128)(2,1)S(1)}, bf16[128,512]{1,0:T(8,128)(2,1)S(1)}, u32[]{:S(2)}, u32[]{:S(2)}) collective-permute-start(bf16[128,512]{1,0:T(8,128)(2,1)S(1)} %get-tuple-element.198), channel_id=1, source_target_pairs={{0,2},{1,3},{2,0},{3,1},{4,6},{5,7},{6,4},{7,5},{8,10},{9,11},{10,... | collective-permute-start | bytes 393224 | tf_op jit(solution)/shard_map/ppermute | solution.py:287
  360.8 15.0 %collective-permute-start.32 = (bf16[128,512]{1,0:T(8,128)(2,1)S(1)}, bf16[128,512]{1,0:T(8,128)(2,1)S(1)}, u32[]{:S(2)}, u32[]{:S(2)}) collective-permute-start(bf16[128,512]{1,0:T(8,128)(2,1)S(1)} %get-tuple-element.199), channel_id=1, source_target_pairs={{0,3},{1,2},{2,1},{3,0},{4,7},{5,6},{6,5},{7,4},{8,11},{9,10},{10,... | collective-permute-start | bytes 393224 | tf_op jit(solution)/shard_map/ppermute | solution.py:287
  362.6 21.2 %collective-permute-start.38 = (bf16[256,512]{1,0:T(8,128)(2,1)}, bf16[256,512]{1,0:T(8,128)(2,1)S(1)}, u32[]{:S(2)}, u32[]{:S(2)}) collective-permute-start(bf16[256,512]{1,0:T(8,128)(2,1)} %get-tuple-element.210), channel_id=1, source_target_pairs={{0,8},{8,0},{16,24},{24,16},{1,9},{9,1},{17,25},{25,17},{2,10},{10... | collective-permute-start | bytes 786440 | tf_op jit(solution)/shard_map/ppermute | solution.py:279
  362.7 23.4 %collective-permute-start.39 = (bf16[256,512]{1,0:T(8,128)(2,1)}, bf16[256,512]{1,0:T(8,128)(2,1)S(1)}, u32[]{:S(2)}, u32[]{:S(2)}) collective-permute-start(bf16[256,512]{1,0:T(8,128)(2,1)} %get-tuple-element.211), channel_id=1, source_target_pairs={{0,16},{8,24},{16,0},{24,8},{1,17},{9,25},{17,1},{25,9},{2,18},{10... | collective-permute-start | bytes 786440 | tf_op jit(solution)/shard_map/ppermute | solution.py:279
  375.8 19.4 %collective-permute-start.34 = (bf16[128,512]{1,0:T(8,128)(2,1)S(1)}, bf16[128,512]{1,0:T(8,128)(2,1)S(1)}, u32[]{:S(2)}, u32[]{:S(2)}) collective-permute-start(bf16[128,512]{1,0:T(8,128)(2,1)S(1)} %get-tuple-element.205), channel_id=1, source_target_pairs={{0,4},{1,5},{2,6},{3,7},{4,0},{5,1},{6,2},{7,3},{8,12},{9,13},{10,... | collective-permute-start | bytes 393224 | tf_op jit(solution)/shard_map/ppermute | solution.py:287
  375.9 19.4 %collective-permute-start.35 = (bf16[128,512]{1,0:T(8,128)(2,1)S(1)}, bf16[128,512]{1,0:T(8,128)(2,1)S(1)}, u32[]{:S(2)}, u32[]{:S(2)}) collective-permute-start(bf16[128,512]{1,0:T(8,128)(2,1)S(1)} %get-tuple-element.206), channel_id=1, source_target_pairs={{0,5},{1,4},{2,7},{3,6},{4,1},{5,0},{6,3},{7,2},{8,13},{9,12},{10,... | collective-permute-start | bytes 393224 | tf_op jit(solution)/shard_map/ppermute | solution.py:287
  383.7 12.6 %collective-permute-start.36 = (bf16[128,512]{1,0:T(8,128)(2,1)S(1)}, bf16[128,512]{1,0:T(8,128)(2,1)S(1)}, u32[]{:S(2)}, u32[]{:S(2)}) collective-permute-start(bf16[128,512]{1,0:T(8,128)(2,1)S(1)} %get-tuple-element.207), channel_id=1, source_target_pairs={{0,6},{1,7},{2,4},{3,5},{4,2},{5,3},{6,0},{7,1},{8,14},{9,15},{10,... | collective-permute-start | bytes 393224 | tf_op jit(solution)/shard_map/ppermute | solution.py:287
  386.9 12.8 %collective-permute-start.41 = (bf16[128,512]{1,0:T(8,128)(2,1)S(1)}, bf16[128,512]{1,0:T(8,128)(2,1)S(1)}, u32[]{:S(2)}, u32[]{:S(2)}) collective-permute-start(bf16[128,512]{1,0:T(8,128)(2,1)S(1)} %get-tuple-element.219), channel_id=1, source_target_pairs={{0,2},{1,3},{2,0},{3,1},{4,6},{5,7},{6,4},{7,5},{8,10},{9,11},{10,... | collective-permute-start | bytes 393224 | tf_op jit(solution)/shard_map/ppermute | solution.py:287
  396.4 20.7 %collective-permute-start.44 = (bf16[128,512]{1,0:T(8,128)(2,1)S(1)}, bf16[128,512]{1,0:T(8,128)(2,1)S(1)}, u32[]{:S(2)}, u32[]{:S(2)}) collective-permute-start(bf16[128,512]{1,0:T(8,128)(2,1)S(1)} %get-tuple-element.222), channel_id=1, source_target_pairs={{0,5},{1,4},{2,7},{3,6},{4,1},{5,0},{6,3},{7,2},{8,13},{9,12},{10,... | collective-permute-start | bytes 393224 | tf_op jit(solution)/shard_map/ppermute | solution.py:287
  399.1 17.9 %collective-permute-start.45 = (bf16[128,512]{1,0:T(8,128)(2,1)S(1)}, bf16[128,512]{1,0:T(8,128)(2,1)S(1)}, u32[]{:S(2)}, u32[]{:S(2)}) collective-permute-start(bf16[128,512]{1,0:T(8,128)(2,1)S(1)} %get-tuple-element.223), channel_id=1, source_target_pairs={{0,6},{1,7},{2,4},{3,5},{4,2},{5,3},{6,0},{7,1},{8,14},{9,15},{10,... | collective-permute-start | bytes 393224 | tf_op jit(solution)/shard_map/ppermute | solution.py:287
  399.7 17.4 %collective-permute-start.46 = (bf16[128,512]{1,0:T(8,128)(2,1)S(1)}, bf16[128,512]{1,0:T(8,128)(2,1)S(1)}, u32[]{:S(2)}, u32[]{:S(2)}) collective-permute-start(bf16[128,512]{1,0:T(8,128)(2,1)S(1)} %get-tuple-element.224), channel_id=1, source_target_pairs={{0,7},{1,6},{2,5},{3,4},{4,3},{5,2},{6,1},{7,0},{8,15},{9,14},{10,... | collective-permute-start | bytes 393224 | tf_op jit(solution)/shard_map/ppermute | solution.py:287
  (38 other events, 501.0 us)
Sparse Core Ops, SparseCore 0:
  16.4 89.0 reduce-scatter.2
  108.9 128.5 reduce-scatter.4
  259.8 134.9 all-gather.4
  418.5 90.1 all-gather.2
